TPU v7x, 256 devices: a whole 4x4x8 slice. The times are simulated.
256 devices in a mesh: row: 8 (over z_lo, y), col: 32 (over x, z_hi, core).
Axes of the slice: x: 4, y: 4, z: 8 (z_hi: 4, z_lo: 2; z = z_hi * 2 + z_lo), core: 2. Of those that a mesh axis runs over, the one named last changes fastest.
Arguments:
- inputs: bfloat16 [512, 8192], P('col', 'row'), may hold values from -6 to 6
- teacher: bfloat16 [512, 8192], P('col', 'row'), may hold values from -6 to 6
- gate_weight: bfloat16 [8192, 16384], P('row', 'col'), may hold values from -0.125 to 0.125
- up_weight: bfloat16 [8192, 16384], P('row', 'col'), may hold values from -0.125 to 0.125
- down_weight: bfloat16 [16384, 8192], P('col', 'row'), may hold values from -0.078125 to 0.078125
- block_mask: int32 [3, 64, 128], P(None, 'row', 'col'), may hold values 0 or 1
Outputs:
- student: bfloat16 [512, 8192], P('col', 'row')
- loss: float32 [], replicated
- grad_gate: bfloat16 [8192, 16384], P('row', 'col')
- grad_up: bfloat16 [8192, 16384], P('row', 'col')
- grad_down: bfloat16 [16384, 8192], P('col', 'row')
- grad_in: bfloat16 [512, 8192], P('col', 'row')
All inputs are finite; a program needn't handle non-finite values. No bound on the sum of `block_mask` on one device may be relied on, other than what follows from the above.
Results may differ from a plain program's by a relative error of at most 0.0065.
Values may be sent and summed in bfloat16 or wider, within the bound.
No kernel may reach another device: no remote copies, remote signals or barrier semaphores. Data moves between devices by JAX's collectives and lax.ppermute only.
A program may use at most 64 MiB of HBM per device.

v0:
```python
import jax
import jax.numpy as jnp
from jax import lax
from jax.sharding import PartitionSpec as P

D = 8192
BLK = 128


def spread(blocks):
    return jnp.repeat(jnp.repeat(blocks, BLK, axis=0), BLK, axis=1).astype(jnp.bfloat16)


def contract_rows(left, right):
    return lax.dot_general(
        left, right, (((0,), (0,)), ((), ())), preferred_element_type=jnp.float32
    )


def contract_cols(left, right):
    return lax.dot_general(
        left, right, (((1,), (1,)), ((), ())), preferred_element_type=jnp.float32
    )


def act_grads(grad_hidden, gate, up, sig, act):
    grad_gate_act = (grad_hidden * up * sig * (1.0 + gate * (1.0 - sig))).astype(jnp.bfloat16)
    grad_up_act = (grad_hidden * act).astype(jnp.bfloat16)
    return (grad_gate_act, grad_up_act)


def per_device(inputs, teacher, gate_weight, up_weight, down_weight, block_mask):
    gate_keep = spread(block_mask[0])
    up_keep = spread(block_mask[1])
    down_keep = spread(block_mask[2]).T
    gate_kept = gate_weight * gate_keep
    up_kept = up_weight * up_keep
    down_kept = down_weight * down_keep
    hidden_cols = gate_weight.shape[1]
    paired = jnp.concatenate([gate_kept, up_kept], axis=1)
    rows_all = lax.all_gather(inputs, "col", axis=0, tiled=True)
    token_count = rows_all.shape[0]
    block = rows_all
    both = lax.psum_scatter(
        jnp.dot(block, paired, preferred_element_type=jnp.float32),
        "row",
        scatter_dimension=0,
        tiled=True,
    )
    gate = both[:, :hidden_cols]
    up = both[:, hidden_cols:]
    sig = jax.nn.sigmoid(gate)
    act = gate * sig
    hidden = (act * up).astype(jnp.bfloat16)
    hidden_all = lax.all_gather(hidden, "row", axis=0, tiled=True)
    block = hidden_all
    output = lax.psum_scatter(
        jnp.dot(block, down_kept, preferred_element_type=jnp.float32),
        "col",
        scatter_dimension=0,
        tiled=True,
    )
    diff = output - teacher.astype(jnp.float32)
    loss = lax.psum(jnp.sum(diff * diff), ("row", "col")) / (token_count * D)
    grad_out = (diff / jnp.sqrt(jnp.float32(token_count))).astype(jnp.bfloat16)
    grad_all = lax.all_gather(grad_out, "col", axis=0, tiled=True)
    block = grad_all
    grad_hidden = lax.psum_scatter(
        contract_cols(block, down_kept), "row", scatter_dimension=0, tiled=True
    )
    grad_gate_act, grad_up_act = act_grads(grad_hidden, gate, up, sig, act)
    gate_act_all, up_act_all = (
        lax.all_gather(grad_gate_act, "row", axis=0, tiled=True),
        lax.all_gather(grad_up_act, "row", axis=0, tiled=True),
    )
    grad_down = (contract_rows(hidden_all, grad_all) * down_keep).astype(jnp.bfloat16)
    grad_gate = (contract_rows(rows_all, gate_act_all) * gate_keep).astype(jnp.bfloat16)
    grad_up = (contract_rows(rows_all, up_act_all) * up_keep).astype(jnp.bfloat16)
    block = gate_act_all
    grad_in = lax.psum_scatter(
        contract_cols(block, gate_kept), "col", scatter_dimension=0, tiled=True
    )
    block = up_act_all
    grad_in = grad_in + lax.psum_scatter(
        contract_cols(block, up_kept), "col", scatter_dimension=0, tiled=True
    )
    return (
        output.astype(jnp.bfloat16),
        loss,
        grad_gate,
        grad_up,
        grad_down,
        grad_in.astype(jnp.bfloat16),
    )


def solution(mesh):
    return jax.shard_map(
        per_device,
        mesh=mesh,
        in_specs=(
            P("col", "row"),
            P("col", "row"),
            P("row", "col"),
            P("row", "col"),
            P("col", "row"),
            P(None, "row", "col"),
        ),
        out_specs=(
            P("col", "row"),
            P(),
            P("row", "col"),
            P("row", "col"),
            P("col", "row"),
            P("col", "row"),
        ),
        check_vma=False,
    )
```

profile of v0, /device:TPU:6, one launch (start us, length us, event | category | flops | bytes accessed | tf_op | source)
XLA Modules:
  0.0 494.4 jit_solution(4472042617715974865)
XLA Ops:
  7.2 0.7 all-gather.3.cloned.1.call-update
  8.0 0.7 convert.5
  8.7 1.5 copy.26
  10.3 0.5 copy.25
  11.0 53.1 %all-gather.3.cloned.1.call-done = bf16[512,1024]{1,0:T(8,128)(2,1)} async-done(((bf16[16,1024]{1,0:T(8,128)(2,1)}), bf16[512,1024]{1,0:T(8,128)(2,1)}) %all-gather.3.cloned.1.call-update) | async-done | bytes 1048592 | tf_op jit(solution)/shard_map/all_gather | solution.py:41
  64.2 3.8 fusion.6
  68.0 2.9 copy.35
  71.0 1.3 bitcast_multiply_fusion.2
  72.3 42.8 %reduce-scatter.13.cloned.1.call-done = f32[64,1024]{1,0:T(8,128)} async-done(((f32[512,1024]{1,0:T(8,128)}), f32[64,1024]{1,0:T(8,128)}) %reduce-scatter.13.cloned.1.call-update) | async-done | bytes 262160 | tf_op jit(solution)/shard_map/reduce_scatter | solution.py:44
  115.1 1.0 multiply_convert_fusion.3
  116.1 29.1 %all_gather.16 = bf16[512,512]{1,0:T(8,128)(2,1)S(1)} all-gather(bf16[64,512]{1,0:T(8,128)(2,1)S(1)} %multiply_convert_fusion.3), channel_id=1, replica_groups=mesh['row'=8,'col'=32] {'row'}, dimensions={0}, use_global_device_ids=true | all-gather | bytes 589824 | tf_op jit(solution)/shard_map/all_gather | solution.py:55
  145.2 0.8 copy-done
  146.0 2.0 fusion.11
  148.1 89.7 %reduce-scatter.9.cloned.1.call-done = f32[16,1024]{1,0:T(8,128)} async-done(((f32[512,1024]{1,0:T(8,128)}), f32[16,1024]{1,0:T(8,128)}) %reduce-scatter.9.cloned.1.call-update) | async-done | bytes 65552 | tf_op jit(solution)/shard_map/reduce_scatter | solution.py:57
  237.8 2.2 multiply_convert_fusion.4
  240.1 49.9 %all-gather.5.cloned.1.call-done = bf16[512,1024]{1,0:T(8,128)(2,1)} async-done(((bf16[16,1024]{1,0:T(8,128)(2,1)}), bf16[512,1024]{1,0:T(8,128)(2,1)}) %all-gather.5.cloned.1.call-update) | async-done | bytes 1048592 | tf_op jit(solution)/shard_map/all_gather | solution.py:66
  289.9 2.9 fusion.12
  292.9 40.6 %reduce-scatter.15.cloned.1.call-done = f32[64,512]{1,0:T(8,128)} async-done(((f32[512,512]{1,0:T(8,128)}), f32[64,512]{1,0:T(8,128)}) %reduce-scatter.15.cloned.1.call-update) | async-done | bytes 131088 | tf_op jit(solution)/shard_map/reduce_scatter | solution.py:68
  333.6 1.0 multiply_convert_fusion.1
  334.5 29.1 %all_gather.18 = bf16[512,512]{1,0:T(8,128)(2,1)S(1)} all-gather(bf16[64,512]{1,0:T(8,128)(2,1)S(1)} %get-tuple-element.25), channel_id=1, replica_groups=mesh['row'=8,'col'=32] {'row'}, dimensions={0}, use_global_device_ids=true | all-gather | bytes 589824 | tf_op jit(solution)/shard_map/all_gather | solution.py:73
  363.6 0.7 fusion.13
  364.3 29.0 %all_gather.19 = bf16[512,512]{1,0:T(8,128)(2,1)S(1)} all-gather(bf16[64,512]{1,0:T(8,128)(2,1)S(1)} %get-tuple-element.24), channel_id=1, replica_groups=mesh['row'=8,'col'=32] {'row'}, dimensions={0}, use_global_device_ids=true | all-gather | bytes 589824 | tf_op jit(solution)/shard_map/all_gather | solution.py:74
  393.3 2.0 convolution_add_fusion
  395.4 73.8 %psum.7 = f32[]{:T(128)} all-reduce(f32[]{:T(128)} %get-tuple-element.27), channel_id=1, replica_groups=mesh['row'=8,'col'=32] {'row','col'}, use_global_device_ids=true, to_apply=%region_3.0 | all-reduce | flops 1 | bytes 8 | tf_op jit(solution)/shard_map/psum | solution.py:64
  469.9 0.1 broadcast_in_dim.23
  470.0 3.0 multiply_convert_fusion
  473.2 1.7 fusion.4
  474.9 2.3 copy.33
  477.3 2.0 fusion.5
  479.3 1.3 copy.32
  480.6 4.4 reduce-scatter.11.cloned.1.call-done
  485.0 1.5 convert_element_type.96
  (32 shorter events, 0.9 us)
Async XLA Ops:
  7.2 3.2 copy-start.3
  7.2 57.0 %all-gather.3.cloned.1.call-start = ((), (), s32[]{:S(2)}) async-start(), calls=%async_computation.4 | async-start | bytes 1081344 | tf_op jit(solution)/shard_map/all_gather | solution.py:41
  7.9 107.2 %reduce-scatter.13.cloned.1.call-start = ((), (), s32[]{:S(2)}) async-start(), calls=%async_computation.8 | async-start | bytes 2359296 | tf_op jit(solution)/shard_map/reduce_scatter | solution.py:44
  70.9 166.9 %reduce-scatter.9.cloned.1.call-start = ((), (), s32[]{:S(2)}) async-start(), calls=%async_computation.5 | async-start | bytes 2162688 | tf_op jit(solution)/shard_map/reduce_scatter | solution.py:57
  145.2 0.8 copy-start
  146.0 91.8 %copy-start.4 = (bf16[16,1024]{1,0:T(8,128)(2,1)S(1)}, bf16[16,1024]{1,0:T(8,128)(2,1)}, u32[]{:S(2)}) copy-start(bf16[16,1024]{1,0:T(8,128)(2,1)} %param.7) | copy-start | bytes 98308
  148.1 141.8 %all-gather.5.cloned.1.call-start = ((), (), s32[]{:S(2)}) async-start(), calls=%async_computation.6 | async-start | bytes 1081344 | tf_op jit(solution)/shard_map/all_gather | solution.py:66
  240.0 93.6 %copy-start.2 = (f32[64,1024]{1,0:T(8,128)S(1)}, f32[64,1024]{1,0:T(8,128)}, u32[]{:S(2)}) copy-start(f32[64,1024]{1,0:T(8,128)} %reduce-scatter.13.cloned.1.call-done) | copy-start | bytes 786436
  240.0 93.5 %reduce-scatter.15.cloned.1.call-start = ((), (), s32[]{:S(2)}) async-start(), calls=%async_computation.9 | async-start | bytes 1179648 | tf_op jit(solution)/shard_map/reduce_scatter | solution.py:68
  292.9 192.1 %reduce-scatter.11.cloned.1.call-start = ((), (), s32[]{:S(2)}) async-start(), calls=%async_computation.7 | async-start | bytes 2162688 | tf_op jit(solution)/shard_map/reduce_scatter | solution.py:80
  395.4 74.6 %copy-start.1 = (bf16[512,512]{1,0:T(8,128)(2,1)S(1)}, bf16[512,512]{1,0:T(8,128)(2,1)}, u32[]{:S(2)}) copy-start(bf16[512,512]{1,0:T(8,128)(2,1)} %copy-done) | copy-start | bytes 1572868
  470.0 3.2 copy-start.5
Sparse Core Ops, SparseCore 0:
  10.6 53.5 all-gather.2
  71.1 43.9 reduce-scatter.12
  148.2 89.5 reduce-scatter.8
  240.8 49.0 all-gather.4
  293.0 40.5 reduce-scatter.14
  395.5 89.3 reduce-scatter.10
where the time goes:
time: 496 us; the launch traced here: 494 us
  waiting for transfers between devices  281 us (57%)
  blocking collectives  161 us (32%)
  matrix products  18.3 us (4%)
  between operations  16 us (3%)
  local copies, waits for them, and re-layouts  9.89 us (2%)
  other arithmetic  7.74 us (2%)
    reduce_scatter x1, waiting for transfers between devices, per_device(): lax.psum_scatter(jnp.dot(block, down_kept, preferred_element_type=jnp.flo...  89.7 us
    psum x1, blocking collectives, per_device(): loss = lax.psum(jnp.sum(diff * diff), ('row', 'col')) / (token_count * D)  73.8 us
    all_gather x1, waiting for transfers between devices, per_device(): rows_all = lax.all_gather(inputs, 'col', axis=0, tiled=True)  53.1 us
    all_gather x1, waiting for transfers between devices, per_device(): grad_all = lax.all_gather(grad_out, 'col', axis=0, tiled=True)  49.9 us
    reduce_scatter x1, waiting for transfers between devices, per_device(): lax.psum_scatter(jnp.dot(block, paired, preferred_element_type=jnp.float3...  42.8 us
    reduce_scatter x1, waiting for transfers between devices, per_device(): lax.psum_scatter(contract_cols(block, down_kept), 'row', scatter_dimensio...  40.6 us
    all_gather x1, blocking collectives, per_device(): hidden_all = lax.all_gather(hidden, 'row', axis=0, tiled=True)  29.1 us
    all_gather x1, blocking collectives, per_device(): lax.all_gather(grad_gate_act, 'row', axis=0, tiled=True)  29.1 us
  transfers between devices with their start and end apart: 6, of which 6 were waited for; matrix products, arithmetic and copies ran while one was open for 3% of the time, Pallas kernels for 0%

commit v1 on v0

v1 whole, which is shorter than its diff:
```python
import functools

import jax
import jax.numpy as jnp
from jax import lax
from jax.experimental import pallas as pl
from jax.experimental.pallas import tpu as pltpu
from jax.sharding import PartitionSpec as P

D = 8192
BLK = 128
X, Z, CORES = 4, 4, 2
CHIPS = X * Z
ROWS = 8
TILE = 512
DOWN = 2
VMEM = pl.BlockSpec(memory_space=pltpu.VMEM)
SMEM = pl.BlockSpec(memory_space=pltpu.SMEM)
ANY = pl.BlockSpec(memory_space=pl.ANY)


def call(kernel, shapes, *args, flops=0, vmem=12, in_specs=None, after=(), beside=False, **kwargs):
    moved = sum(a.size * a.dtype.itemsize for a in args)
    moved += sum(s.size * s.dtype.itemsize for s in jax.tree.leaves(shapes))
    return pl.pallas_call(
        lambda *refs: kernel(*refs[: len(args)], *refs[len(args) + len(after) :]),
        out_shape=shapes,
        in_specs=(in_specs or [VMEM] * len(args)) + [ANY] * len(after),
        compiler_params=pltpu.CompilerParams(vmem_limit_bytes=vmem << 20),
        cost_estimate=pl.CostEstimate(
            flops=0 if beside else flops, bytes_accessed=0 if beside else moved, transcendentals=0
        ),
        **kwargs,
    )(*args, *after)


def shaped(shape, dtype=jnp.bfloat16):
    return jax.ShapeDtypeStruct(shape, dtype)


DONE = shaped((8, BLK), jnp.float32)


def join_kernel(*refs):
    joined_ref = refs[-1]
    size = refs[0].shape[0]
    for part, ref in enumerate(refs[:-1]):
        joined_ref[pl.ds(part * size, size), :] = ref[...]


def keep_kernel(mask_ref, gate_ref, up_ref, down_ref, *kept_refs):
    for which, (ref, kept_ref) in enumerate(zip((gate_ref, up_ref, down_ref), kept_refs)):
        for row in range(ref.shape[0] // BLK):
            for col in range(ref.shape[1] // BLK):
                at = (row, col) if which == DOWN else (col, row)
                keep = mask_ref[which, at[0], at[1]].astype(jnp.float32).astype(jnp.bfloat16)
                block = (pl.ds(row * BLK, BLK), pl.ds(col * BLK, BLK))
                kept_ref[block] = ref[block] * keep


def plain_dot(left, right):
    return jnp.dot(left, right, preferred_element_type=jnp.float32)


def other_turned_dot(left, right):
    return lax.dot_general(left, right, (((1,), (1,)), ((), ())), preferred_element_type=jnp.float32)


def gate_up_kernel(*refs):
    slabs, weights, (out_ref, rows_ref) = refs[:X], refs[X:-2], refs[-2:]
    join_kernel(*slabs, rows_ref)
    for which, ref in enumerate(weights):
        units = ref.shape[1]
        value = plain_dot(rows_ref[...], ref[...])
        out_ref[:, pl.ds(which * units, units)] = value.astype(out_ref.dtype)


def put_slabs(out_refs, cols, value):
    size = out_refs[0].shape[0]
    for part, ref in enumerate(out_refs):
        ref[:, cols] = value[part * size : (part + 1) * size].astype(ref.dtype)


def output_kernel(hidden_ref, down_ref, down_other_ref, *out_refs):
    units, width = down_ref.shape
    for at in range(0, width, TILE):
        cols = pl.ds(at, TILE)
        value = plain_dot(hidden_ref[:, :units], down_ref[:, cols])
        value = value + plain_dot(hidden_ref[:, units:], down_other_ref[:, cols])
        put_slabs(out_refs, cols, value)


def grad_hidden_kernel(*refs):
    slabs, (down_ref, down_other_ref, out_ref, grad_ref) = refs[:X], refs[X:]
    join_kernel(*slabs, grad_ref)
    units = down_ref.shape[0]
    squares = jnp.sum(jnp.square(grad_ref[...].astype(jnp.float32)), axis=0, keepdims=True)
    squares = jnp.sum(squares, axis=1, keepdims=True)
    lane = lax.broadcasted_iota(jnp.int32, (out_ref.shape[0], BLK), 1)
    terms = jnp.zeros(lane.shape, jnp.float32)
    for which in range(3):
        term = squares.astype(jnp.bfloat16).astype(jnp.float32)
        terms = jnp.where(lane == which, term, terms)
        squares = squares - term
    out_ref[:, pl.ds(2 * units, BLK)] = terms.astype(out_ref.dtype)
    for which, ref in enumerate((down_ref, down_other_ref)):
        value = other_turned_dot(grad_ref[...], ref[...])
        out_ref[:, pl.ds(which * units, units)] = value.astype(out_ref.dtype)


def grad_in_kernel(acts_ref, *refs):
    weights, out_refs = refs[:-X], refs[-X:]
    width, units = weights[0].shape
    for at in range(0, width, TILE):
        value = None
        for which, ref in enumerate(weights):
            term = other_turned_dot(acts_ref[:, pl.ds(which * units, units)], ref[pl.ds(at, TILE), :])
            value = term if value is None else value + term
        put_slabs(out_refs, pl.ds(at, TILE), value)


def multiply(kernel, shapes, left, weights, after=()):
    flops = 2 * sum(part.shape[0] for part in left) * sum(weight.size for weight in weights)
    return call(kernel, shapes, *left, *weights, flops=flops, vmem=16, after=after)


def summed(parts):
    total = parts[0][...].astype(jnp.float32)
    for part in parts[1:]:
        total = total + part[...].astype(jnp.float32)
    return total


def parts_of(parts_ref):
    return [parts_ref.at[part] for part in range(parts_ref.shape[0])]


def hidden_kernel(parts_ref, both_ref, copies_ref):
    both = summed(parts_of(parts_ref))
    half = both.shape[1] // 2
    gate, up = both[:, :half], both[:, half:]
    hidden = (gate * jax.nn.sigmoid(gate) * up).astype(jnp.bfloat16)
    both_ref[...] = both
    for part in range(copies_ref.shape[0]):
        copies_ref[part] = hidden


def error_kernel(scale, teacher_ref, *refs):
    parts, (student_ref, grad_ref) = refs[:-2], refs[-2:]
    output = summed(parts)
    student_ref[...] = output.astype(jnp.bfloat16)
    grad_ref[...] = ((output - teacher_ref[...].astype(jnp.float32)) / scale).astype(jnp.bfloat16)


def acts_kernel(parts_ref, both_ref, copies_ref, squares_ref):
    total = summed(parts_of(parts_ref))
    half = both_ref.shape[1] // 2
    grad_hidden = total[:, :half]
    squares_ref[...] = jnp.sum(total[:1, half:], axis=1, keepdims=True)
    gate, up = both_ref[:, :half], both_ref[:, half:]
    sig = jax.nn.sigmoid(gate)
    grad_gate_act = (grad_hidden * up * sig * (1.0 + gate * (1.0 - sig))).astype(jnp.bfloat16)
    grad_up_act = (grad_hidden * (gate * sig)).astype(jnp.bfloat16)
    for part in range(copies_ref.shape[0]):
        copies_ref[part, :, :half] = grad_gate_act
        copies_ref[part, :, half:] = grad_up_act


def sum_kernel(*refs):
    parts, out_refs = refs[:X], refs[X:]
    put_slabs(out_refs, slice(None), summed(parts))


def turned_dot(left, right):
    return lax.dot_general(left, right, (((0,), (0,)), ((), ())), preferred_element_type=jnp.float32)


def weights_kernel(which, mask_ref, rows_ref, rows_other_ref, acts_ref, acts_other_ref, out_ref, done_ref):
    width, units = out_ref.shape
    done_ref[...] = jnp.zeros_like(done_ref)
    for at in range(0, units, 2 * BLK):
        own = pl.ds(2 * which * units + at, 2 * BLK)
        other = pl.ds((2 * which + 1) * units + at, 2 * BLK)
        value = turned_dot(rows_ref[...], acts_ref[:, own])
        value = value + turned_dot(rows_other_ref[...], acts_other_ref[:, other])
        for row in range(width // BLK):
            for col in range(2):
                keep = mask_ref[which, at // BLK + col, row].astype(jnp.float32)
                block = value[row * BLK : (row + 1) * BLK, col * BLK : (col + 1) * BLK] * keep
                out_ref[pl.ds(row * BLK, BLK), pl.ds(at + col * BLK, BLK)] = block.astype(jnp.bfloat16)


def down_kernel(
    mask_ref,
    hidden_ref,
    hidden_other_ref,
    grad_ref,
    grad_other_ref,
    squares_ref,
    squares_other_ref,
    out_ref,
    loss_ref,
    done_ref,
):
    units, width = out_ref.shape
    loss_ref[...] = (squares_ref[...] + squares_other_ref[...]) * (1.0 / D)
    done_ref[...] = jnp.zeros_like(done_ref)
    for at in range(0, width, 2 * BLK):
        cols = pl.ds(at, 2 * BLK)
        value = turned_dot(hidden_ref[:, :units], grad_ref[:, cols])
        value = value + turned_dot(hidden_other_ref[:, units:], grad_other_ref[:, cols])
        for row in range(units // BLK):
            for col in range(2):
                keep = mask_ref[DOWN, row, at // BLK + col].astype(jnp.float32)
                block = value[row * BLK : (row + 1) * BLK, col * BLK : (col + 1) * BLK] * keep
                out_ref[pl.ds(row * BLK, BLK), pl.ds(at + col * BLK, BLK)] = block.astype(jnp.bfloat16)


def other_core(value):
    count = CHIPS * CORES
    return lax.ppermute(value, "col", [(device, device ^ 1) for device in range(count)])


def fetch(value, dx, dz):
    pairs = [
        ((((x + dx) % X * Z + (z + dz) % Z) * CORES + core), (x * Z + z) * CORES + core)
        for x in range(X)
        for z in range(Z)
        for core in range(CORES)
    ]
    return lax.ppermute(value, "col", pairs)


def gather_z(block):
    return [block] + [fetch(block, 0, step) for step in range(1, Z)]


def joined(parts):
    size, width = parts[0].shape
    return call(join_kernel, shaped((len(parts) * size, width)), *parts)


def gather_x(block):
    return [block] + [fetch(block, step, 0) for step in range(1, X)]


def spread_x(parts):
    return [parts[0]] + [fetch(parts[step], -step, 0) for step in range(1, X)]


def spread_z(parts):
    return [parts[0]] + [fetch(parts[step], 0, -step) for step in range(1, Z)]


def exchange_row(value):
    return lax.all_to_all(value, "row", 0, 0)


def flat(value):
    return value.reshape((-1,) + value.shape[2:])


def split(value, count):
    return value.reshape((count, -1) + value.shape[1:])


def per_device(inputs, teacher, gate_weight, up_weight, down_weight, block_mask):
    tokens, width = inputs.shape
    token_count = tokens * CHIPS * CORES
    units = gate_weight.shape[1]
    half = tokens * CHIPS
    scale = float(token_count) ** 0.5
    mask = jnp.transpose(block_mask, (0, 2, 1))
    slab = shaped((Z * tokens, width))
    piece = shaped((tokens, width))
    parts = gather_z(inputs)
    weights = call(
        keep_kernel,
        (shaped((width, units)),) * 2 + (shaped((units, width)),),
        mask,
        gate_weight,
        up_weight,
        down_weight,
        in_specs=[SMEM] + [VMEM] * 3,
        vmem=16,
        after=(parts[1],),
    )
    gates, ups, downs = ((value, other_core(value)) for value in weights)
    slabs = gather_x(joined(parts))
    partial, rows = multiply(
        gate_up_kernel, (shaped((half, 4 * units)), shaped((half, width))), slabs, gates + ups, downs[1:]
    )
    both, copies = call(
        hidden_kernel,
        (shaped((half // ROWS, 4 * units), jnp.float32), shaped((ROWS, half // ROWS, 2 * units))),
        exchange_row(split(partial, ROWS)),
    )
    hidden = flat(exchange_row(copies))
    slabs = spread_x(multiply(output_kernel, (slab,) * X, [hidden], downs))
    parts = spread_z(call(sum_kernel, (piece,) * Z, *slabs))
    student, grad_out = call(functools.partial(error_kernel, scale), (piece, piece), teacher, *parts)
    slabs = gather_x(joined(gather_z(grad_out)))
    partial, grad_rows = multiply(
        grad_hidden_kernel, (shaped((half, 2 * units + BLK)), shaped((half, width))), slabs, downs
    )
    copies, squares = call(
        acts_kernel,
        (shaped((ROWS, half // ROWS, 4 * units)), shaped((1, 1), jnp.float32)),
        exchange_row(split(partial, ROWS)),
        both,
    )
    acts = flat(exchange_row(copies))
    slabs = spread_x(multiply(grad_in_kernel, (slab,) * X, [acts], gates + ups))
    rows_other, hidden_other, grad_rows_other, acts_other, squares_other = (
        other_core(value) for value in (rows, hidden, grad_rows, acts, squares)
    )
    grad_down, loss, down_done = call(
        down_kernel,
        (shaped((units, width)), shaped((1, 1), jnp.float32), DONE),
        mask,
        hidden,
        hidden_other,
        grad_rows,
        grad_rows_other,
        squares,
        squares_other,
        in_specs=[SMEM] + [VMEM] * 6,
        flops=2 * token_count * width * units,
        vmem=16,
    )
    (grad_gate, gate_done), (grad_up, up_done) = (
        call(
            functools.partial(weights_kernel, which),
            (shaped((width, units)), DONE),
            mask,
            rows,
            rows_other,
            acts,
            acts_other,
            in_specs=[SMEM] + [VMEM] * 4,
            flops=2 * token_count * width * units,
            vmem=16,
        )
        for which in range(2)
    )
    parts = spread_z(call(sum_kernel, (piece,) * Z, *slabs, after=(down_done,)))
    (grad_in,) = call(sum_kernel, (piece,), *parts, after=(gate_done, up_done))
    return student, loss[0, 0], grad_gate, grad_up, grad_down, grad_in


def solution(mesh):
    return jax.shard_map(
        per_device,
        mesh=mesh,
        in_specs=(
            P("col", "row"),
            P("col", "row"),
            P("row", "col"),
            P("row", "col"),
            P("col", "row"),
            P(None, "row", "col"),
        ),
        out_specs=(
            P("col", "row"),
            P(),
            P("row", "col"),
            P("row", "col"),
            P("col", "row"),
            P("col", "row"),
        ),
        check_vma=False,
    )
```

time: 496 us -> 166 us (0.33)
  waiting for transfers between devices: 281 us -> 38.3 us
  blocking collectives: 161 us -> 56.8 us
  starting transfers between devices: 0.24 us -> 49.6 us
  matrix products: 18.3 us -> 0 us
  Pallas kernels: 0 us -> 16 us
  between operations: 16 us -> 0.75 us
  other arithmetic: 7.74 us -> 0 us
  local copies, waits for them, and re-layouts: 9.89 us -> 4.37 us
    reduce_scatter x4 -> x0, waiting for transfers between devices: 177 us -> none  [the longest x1 89.7 us: per_device(): lax.psum_scatter(jnp.dot(block, down_kept, preferred_element_type=jnp.flo...]
    all_gather x2 -> x0, waiting for transfers between devices: 103 us -> none  [the longest x1 53.1 us: per_device(): rows_all = lax.all_gather(inputs, 'col', axis=0, tiled=True)]
    all_gather x3 -> x0, blocking collectives: 87.2 us -> none  [the longest x1 29.1 us: per_device(): hidden_all = lax.all_gather(hidden, 'row', axis=0, tiled=True)]
    psum x1 -> x0, blocking collectives: 73.8 us -> none  [per_device(): loss = lax.psum(jnp.sum(diff * diff), ('row', 'col')) / (token_count * D)]
    all_to_all x0 -> x4, blocking collectives: none -> 56.8 us  [exchange_row(): return lax.all_to_all(value, 'row', 0, 0)]
    ppermute x0 -> x32, starting transfers between devices: none -> 49.6 us  [the longest x24 47.9 us: fetch(): return lax.ppermute(value, 'col', pairs)]
    ppermute x0 -> x32, waiting for transfers between devices: none -> 38.3 us  [the longest x24 37.2 us: fetch(): return lax.ppermute(value, 'col', pairs)]
    pallas_call x0 -> x16, Pallas kernels: none -> 16 us  [call(): pl.pallas_call(lambda *refs: kernel(*refs[:len(args)], *refs[len(args) +...]
  transfers between devices with their start and end apart: 6 -> 32, of which waited for: 6 -> 20; matrix products, arithmetic and copies ran while one was open for 3% -> 0% of each run, Pallas kernels for 0% -> 6%
where the time goes in v1:
time: 166 us
  blocking collectives  56.8 us (34%)
  starting transfers between devices  49.6 us (30%)
  waiting for transfers between devices  38.3 us (23%)
  Pallas kernels  16 us (10%)
  local copies, waits for them, and re-layouts  4.37 us (3%)
    all_to_all x4, blocking collectives, exchange_row(): return lax.all_to_all(value, 'row', 0, 0)  56.8 us
    ppermute x24, starting transfers between devices, fetch(): return lax.ppermute(value, 'col', pairs)  47.9 us
    ppermute x24, waiting for transfers between devices, fetch(): return lax.ppermute(value, 'col', pairs)  37.2 us
    pallas_call x16, Pallas kernels, call(): pl.pallas_call(lambda *refs: kernel(*refs[:len(args)], *refs[len(args) +...  16 us
    unnamed x14, local copies, waits for them, and re-layouts  4.37 us
  transfers between devices with their start and end apart: 32, of which 20 were waited for; matrix products, arithmetic and copies ran while one was open for 0% of the time, Pallas kernels for 6%

profile of v1, /device:TPU:6, one launch (start us, length us, event | category | flops | bytes accessed | tf_op | source)
XLA Modules:
  0.0 165.9 jit_solution(2873944623422412833)
XLA Ops:
  0.6 6.4 %collective-permute-start = (bf16[16,1024]{1,0:T(8,128)(2,1)}, bf16[16,1024]{1,0:T(8,128)(2,1)S(1)}, u32[]{:S(2)}, u32[]{:S(2)}) collective-permute-start(bf16[16,1024]{1,0:T(8,128)(2,1)} %refs_0_.2), channel_id=1, source_target_pairs={{2,0},{3,1},{4,2},{5,3},{6,4},{7,5},{0,6},{1,7},{10,8},{11,9},{12,... | collective-permute-start | bytes 98312 | tf_op jit(solution)/shard_map/ppermute | solution.py:231
  7.0 1.9 %collective-permute-done.refs_1_.refs_4_ = bf16[16,1024]{1,0:T(8,128)(2,1)S(1)} collective-permute-done((bf16[16,1024]{1,0:T(8,128)(2,1)}, bf16[16,1024]{1,0:T(8,128)(2,1)S(1)}, u32[]{:S(2)}, u32[]{:S(2)}) %collective-permute-start) | collective-permute-done | bytes 32800 | tf_op jit(solution)/shard_map/ppermute | solution.py:231
  15.3 4.0 %collective-permute-start.1 = (bf16[16,1024]{1,0:T(8,128)(2,1)S(1)}, bf16[16,1024]{1,0:T(8,128)(2,1)S(1)}, u32[]{:S(2)}, u32[]{:S(2)}) collective-permute-start(bf16[16,1024]{1,0:T(8,128)(2,1)S(1)} %copy-done.6), channel_id=1, source_target_pairs={{4,0},{5,1},{6,2},{7,3},{0,4},{1,5},{2,6},{3,7},{12,8},{13,9},{14,... | collective-permute-start | bytes 98312 | tf_op jit(solution)/shard_map/ppermute | solution.py:231
  19.3 2.7 %collective-permute-start.2 = (bf16[16,1024]{1,0:T(8,128)(2,1)S(1)}, bf16[16,1024]{1,0:T(8,128)(2,1)S(1)}, u32[]{:S(2)}, u32[]{:S(2)}) collective-permute-start(bf16[16,1024]{1,0:T(8,128)(2,1)S(1)} %copy-done.6), channel_id=1, source_target_pairs={{6,0},{7,1},{0,2},{1,3},{2,4},{3,5},{4,6},{5,7},{14,8},{15,9},{8,1... | collective-permute-start | bytes 98312 | tf_op jit(solution)/shard_map/ppermute | solution.py:231
  23.1 2.5 %collective-permute-done.2.refs_3_ = bf16[16,1024]{1,0:T(8,128)(2,1)S(1)} collective-permute-done((bf16[16,1024]{1,0:T(8,128)(2,1)S(1)}, bf16[16,1024]{1,0:T(8,128)(2,1)S(1)}, u32[]{:S(2)}, u32[]{:S(2)}) %collective-permute-start.2) | collective-permute-done | bytes 32800 | tf_op jit(solution)/shard_map/ppermute | solution.py:231
  26.3 2.4 %collective-permute-start.4 = (bf16[64,1024]{1,0:T(8,128)(2,1)S(1)}, bf16[64,1024]{1,0:T(8,128)(2,1)S(1)}, u32[]{:S(2)}, u32[]{:S(2)}) collective-permute-start(bf16[64,1024]{1,0:T(8,128)(2,1)S(1)} %shard_map.109.refs_0_), channel_id=1, source_target_pairs={{16,0},{17,1},{18,2},{19,3},{20,4},{21,5},{22,6},{23,7},{24,8},{25... | collective-permute-start | bytes 393224 | tf_op jit(solution)/shard_map/ppermute | solution.py:231
  28.7 3.0 %collective-permute-done.5.refs_3_ = bf16[64,1024]{1,0:T(8,128)(2,1)S(1)} collective-permute-done((bf16[64,1024]{1,0:T(8,128)(2,1)S(1)}, bf16[64,1024]{1,0:T(8,128)(2,1)S(1)}, u32[]{:S(2)}, u32[]{:S(2)}) %collective-permute-start.5) | collective-permute-done | bytes 131104 | tf_op jit(solution)/shard_map/ppermute | solution.py:231
  33.0 4.8 %collective-permute-done.3.refs_1_ = bf16[64,1024]{1,0:T(8,128)(2,1)S(1)} collective-permute-done((bf16[64,1024]{1,0:T(8,128)(2,1)S(1)}, bf16[64,1024]{1,0:T(8,128)(2,1)S(1)}, u32[]{:S(2)}, u32[]{:S(2)}) %collective-permute-start.3) | collective-permute-done | bytes 131104 | tf_op jit(solution)/shard_map/ppermute | solution.py:231
  39.1 16.6 %all_to_all.20.refs_0_ = bf16[8,32,2048]{2,1,0:T(8,128)(2,1)S(1)} all-to-all(bf16[8,32,2048]{2,1,0:T(8,128)(2,1)S(1)} %bitcast.13), channel_id=1, replica_groups=mesh['row'=8,'col'=32] {'row'}, dimensions={0} | all-to-all | bytes 2097152 | tf_op jit(solution)/shard_map/all_to_all | solution.py:256
  55.9 11.2 %all_to_all.21 = bf16[8,32,1024]{2,1,0:T(8,128)(2,1)S(1)} all-to-all(bf16[8,32,1024]{2,1,0:T(8,128)(2,1)S(1)} %get-tuple-element.46), channel_id=1, replica_groups=mesh['row'=8,'col'=32] {'row'}, dimensions={0} | all-to-all | bytes 1048576 | tf_op jit(solution)/shard_map/all_to_all | solution.py:256
  68.7 1.5 collective-permute-start.10
  70.2 2.6 %collective-permute-done.9.refs_1_ = bf16[64,1024]{1,0:T(8,128)(2,1)S(1)} collective-permute-done((bf16[64,1024]{1,0:T(8,128)(2,1)S(1)}, bf16[64,1024]{1,0:T(8,128)(2,1)S(1)}, u32[]{:S(2)}, u32[]{:S(2)}) %collective-permute-start.9) | collective-permute-done | bytes 131104 | tf_op jit(solution)/shard_map/ppermute | solution.py:231
  72.9 2.3 %collective-permute-done.10.refs_2_ = bf16[64,1024]{1,0:T(8,128)(2,1)S(1)} collective-permute-done((bf16[64,1024]{1,0:T(8,128)(2,1)S(1)}, bf16[64,1024]{1,0:T(8,128)(2,1)S(1)}, u32[]{:S(2)}, u32[]{:S(2)}) %collective-permute-start.10) | collective-permute-done | bytes 131104 | tf_op jit(solution)/shard_map/ppermute | solution.py:231
  76.6 1.4 collective-permute-start.12
  78.1 3.5 %collective-permute-start.13 = (bf16[16,1024]{1,0:T(8,128)(2,1)S(1)}, bf16[16,1024]{1,0:T(8,128)(2,1)S(1)}, u32[]{:S(2)}, u32[]{:S(2)}) collective-permute-start(bf16[16,1024]{1,0:T(8,128)(2,1)S(1)} %get-tuple-element.53), channel_id=1, source_target_pairs={{4,0},{5,1},{6,2},{7,3},{0,4},{1,5},{2,6},{3,7},{12,8},{13,9},{14,... | collective-permute-start | bytes 98312 | tf_op jit(solution)/shard_map/ppermute | solution.py:231
  81.6 3.9 %collective-permute-start.14 = (bf16[16,1024]{1,0:T(8,128)(2,1)S(1)}, bf16[16,1024]{1,0:T(8,128)(2,1)S(1)}, u32[]{:S(2)}, u32[]{:S(2)}) collective-permute-start(bf16[16,1024]{1,0:T(8,128)(2,1)S(1)} %get-tuple-element.54), channel_id=1, source_target_pairs={{2,0},{3,1},{4,2},{5,3},{6,4},{7,5},{0,6},{1,7},{10,8},{11,9},{12,... | collective-permute-start | bytes 98312 | tf_op jit(solution)/shard_map/ppermute | solution.py:231
  88.0 2.6 %collective-permute-start.18 = (bf16[16,1024]{1,0:T(8,128)(2,1)S(1)}, bf16[16,1024]{1,0:T(8,128)(2,1)S(1)}, u32[]{:S(2)}, u32[]{:S(2)}) collective-permute-start(bf16[16,1024]{1,0:T(8,128)(2,1)S(1)} %get-tuple-element.56.refs_0_), channel_id=1, source_target_pairs={{6,0},{7,1},{0,2},{1,3},{2,4},{3,5},{4,6},{5,7},{14,8},{15,9},{8,1... | collective-permute-start | bytes 98312 | tf_op jit(solution)/shard_map/ppermute | solution.py:231
  90.6 4.4 %collective-permute-start.17 = (bf16[16,1024]{1,0:T(8,128)(2,1)S(1)}, bf16[16,1024]{1,0:T(8,128)(2,1)S(1)}, u32[]{:S(2)}, u32[]{:S(2)}) collective-permute-start(bf16[16,1024]{1,0:T(8,128)(2,1)S(1)} %get-tuple-element.56.refs_0_), channel_id=1, source_target_pairs={{4,0},{5,1},{6,2},{7,3},{0,4},{1,5},{2,6},{3,7},{12,8},{13,9},{14,... | collective-permute-start | bytes 98312 | tf_op jit(solution)/shard_map/ppermute | solution.py:231
  95.3 3.1 %collective-permute-done.17.refs_2_ = bf16[16,1024]{1,0:T(8,128)(2,1)S(1)} collective-permute-done((bf16[16,1024]{1,0:T(8,128)(2,1)S(1)}, bf16[16,1024]{1,0:T(8,128)(2,1)S(1)}, u32[]{:S(2)}, u32[]{:S(2)}) %collective-permute-start.17) | collective-permute-done | bytes 32800 | tf_op jit(solution)/shard_map/ppermute | solution.py:231
  98.4 1.5 collective-permute-done.16.refs_1_
  102.7 2.3 %collective-permute-done.21.refs_3_ = bf16[64,1024]{1,0:T(8,128)(2,1)S(1)} collective-permute-done((bf16[64,1024]{1,0:T(8,128)(2,1)S(1)}, bf16[64,1024]{1,0:T(8,128)(2,1)S(1)}, u32[]{:S(2)}, u32[]{:S(2)}) %collective-permute-start.21) | collective-permute-done | bytes 131104 | tf_op jit(solution)/shard_map/ppermute | solution.py:231
  104.9 2.6 %collective-permute-done.20.refs_2_ = bf16[64,1024]{1,0:T(8,128)(2,1)S(1)} collective-permute-done((bf16[64,1024]{1,0:T(8,128)(2,1)S(1)}, bf16[64,1024]{1,0:T(8,128)(2,1)S(1)}, u32[]{:S(2)}, u32[]{:S(2)}) %collective-permute-start.20) | collective-permute-done | bytes 131104 | tf_op jit(solution)/shard_map/ppermute | solution.py:231
  109.6 14.3 %all_to_all.22.refs_0_ = bf16[8,32,1152]{2,1,0:T(8,128)(2,1)S(1)} all-to-all(bf16[8,32,1152]{2,1,0:T(8,128)(2,1)S(1)} %bitcast.14), channel_id=1, replica_groups=mesh['row'=8,'col'=32] {'row'}, dimensions={0} | all-to-all | bytes 1179648 | tf_op jit(solution)/shard_map/all_to_all | solution.py:256
  124.6 14.8 %all_to_all.23 = bf16[8,32,2048]{2,1,0:T(8,128)(2,1)S(1)} all-to-all(bf16[8,32,2048]{2,1,0:T(8,128)(2,1)S(1)} %get-tuple-element.63), channel_id=1, replica_groups=mesh['row'=8,'col'=32] {'row'}, dimensions={0} | all-to-all | bytes 2097152 | tf_op jit(solution)/shard_map/all_to_all | solution.py:256
  143.6 1.6 collective-permute-start.28
  145.2 3.7 %shard_map.119 = (bf16[512,1024]{1,0:T(8,128)(2,1)}, f32[1,1]{1,0:T(1,128)}, f32[8,128]{1,0:T(8,128)S(1)}) custom-call(s32[3,4,8]{2,1,0:T(4,128)S(1)} %bitcast.16, bf16[256,1024]{1,0:T(8,128)(2,1)S(1)} %bitcast.12, bf16[256,1024]{1,0:T(8,128)(2,1)S(1)} %collective-permute-done.15.refs_2_, bf16[256,1024]{1,0:T(8,128)(2,1)S(1)} %get-tuple-element.57.refs_3_, ...), custom_call_target="tpu_custom_call" | custom-call | flops 536870912 | bytes 3150220 | tf_op jit(solution)/shard_map/pallas_call | solution.py:25
  149.1 2.3 %collective-permute-done.27.refs_2_ = bf16[64,1024]{1,0:T(8,128)(2,1)S(1)} collective-permute-done((bf16[64,1024]{1,0:T(8,128)(2,1)S(1)}, bf16[64,1024]{1,0:T(8,128)(2,1)S(1)}, u32[]{:S(2)}, u32[]{:S(2)}) %collective-permute-start.27) | collective-permute-done | bytes 131104 | tf_op jit(solution)/shard_map/ppermute | solution.py:231
  151.4 1.9 %collective-permute-done.28.refs_3_ = bf16[64,1024]{1,0:T(8,128)(2,1)S(1)} collective-permute-done((bf16[64,1024]{1,0:T(8,128)(2,1)S(1)}, bf16[64,1024]{1,0:T(8,128)(2,1)S(1)}, u32[]{:S(2)}, u32[]{:S(2)}) %collective-permute-start.28) | collective-permute-done | bytes 131104 | tf_op jit(solution)/shard_map/ppermute | solution.py:231
  154.4 2.0 %collective-permute-start.30 = (bf16[16,1024]{1,0:T(8,128)(2,1)S(1)}, bf16[16,1024]{1,0:T(8,128)(2,1)S(1)}, u32[]{:S(2)}, u32[]{:S(2)}) collective-permute-start(bf16[16,1024]{1,0:T(8,128)(2,1)S(1)} %get-tuple-element.74), channel_id=1, source_target_pairs={{4,0},{5,1},{6,2},{7,3},{0,4},{1,5},{2,6},{3,7},{12,8},{13,9},{14,... | collective-permute-start | bytes 98312 | tf_op jit(solution)/shard_map/ppermute | solution.py:231
  156.4 4.0 %collective-permute-start.31 = (bf16[16,1024]{1,0:T(8,128)(2,1)S(1)}, bf16[16,1024]{1,0:T(8,128)(2,1)S(1)}, u32[]{:S(2)}, u32[]{:S(2)}) collective-permute-start(bf16[16,1024]{1,0:T(8,128)(2,1)S(1)} %get-tuple-element.75), channel_id=1, source_target_pairs={{2,0},{3,1},{4,2},{5,3},{6,4},{7,5},{0,6},{1,7},{10,8},{11,9},{12,... | collective-permute-start | bytes 98312 | tf_op jit(solution)/shard_map/ppermute | solution.py:231
  160.4 2.4 %shard_map.121 = (bf16[1024,512]{1,0:T(8,128)(2,1)}, f32[8,128]{1,0:T(8,128)S(1)}) custom-call(s32[3,4,8]{2,1,0:T(4,128)S(1)} %bitcast.17, bf16[256,1024]{1,0:T(8,128)(2,1)S(1)} %get-tuple-element.62.refs_1_, bf16[256,1024]{1,0:T(8,128)(2,1)S(1)} %collective-permute-done.24.refs_2_, bf16[256,2048]{1,0:T(8,128)(2,1)S(1)} %bitcast.8, ...), custom_call_target="tpu_custom_call" | custom-call | flops 536870912 | bytes 4198784 | tf_op jit(solution)/shard_map/pallas_call | solution.py:25
  162.8 2.4 %shard_map.120 = (bf16[1024,512]{1,0:T(8,128)(2,1)}, f32[8,128]{1,0:T(8,128)S(1)}) custom-call(s32[3,4,8]{2,1,0:T(4,128)S(1)} %bitcast.18, bf16[256,1024]{1,0:T(8,128)(2,1)S(1)} %get-tuple-element.62.refs_1_, bf16[256,1024]{1,0:T(8,128)(2,1)S(1)} %collective-permute-done.24.refs_2_, bf16[256,2048]{1,0:T(8,128)(2,1)S(1)} %bitcast.9, ...), custom_call_target="tpu_custom_call" | custom-call | flops 536870912 | bytes 4198784 | tf_op jit(solution)/shard_map/pallas_call | solution.py:25
  (66 shorter events, 28.4 us)
Async XLA Ops:
  0.6 8.3 %collective-permute-start = (bf16[16,1024]{1,0:T(8,128)(2,1)}, bf16[16,1024]{1,0:T(8,128)(2,1)S(1)}, u32[]{:S(2)}, u32[]{:S(2)}) collective-permute-start(bf16[16,1024]{1,0:T(8,128)(2,1)} %refs_0_.2), channel_id=1, source_target_pairs={{2,0},{3,1},{4,2},{5,3},{6,4},{7,5},{0,6},{1,7},{10,8},{11,9},{12,... | collective-permute-start | bytes 98312 | tf_op jit(solution)/shard_map/ppermute | solution.py:231
  14.6 23.3 %collective-permute-start.6 = (bf16[1024,512]{1,0:T(8,128)(2,1)S(1)}, bf16[1024,512]{1,0:T(8,128)(2,1)S(1)}, u32[]{:S(2)}, u32[]{:S(2)}) collective-permute-start(bf16[1024,512]{1,0:T(8,128)(2,1)S(1)} %get-tuple-element.42.refs_4_.refs_1_), channel_id=1, source_target_pairs={{0,1},{1,0},{2,3},{3,2},{4,5},{5,4},{6,7},{7,6},{8,9},{9,8},{10,11... | collective-permute-start | bytes 3145736 | tf_op jit(solution)/shard_map/ppermute | solution.py:221
  14.7 23.2 %collective-permute-start.7 = (bf16[1024,512]{1,0:T(8,128)(2,1)S(1)}, bf16[1024,512]{1,0:T(8,128)(2,1)S(1)}, u32[]{:S(2)}, u32[]{:S(2)}) collective-permute-start(bf16[1024,512]{1,0:T(8,128)(2,1)S(1)} %get-tuple-element.43.refs_6_.refs_3_), channel_id=1, source_target_pairs={{0,1},{1,0},{2,3},{3,2},{4,5},{5,4},{6,7},{7,6},{8,9},{9,8},{10,11... | collective-permute-start | bytes 3145736 | tf_op jit(solution)/shard_map/ppermute | solution.py:221
  15.2 22.7 %collective-permute-start.8 = (bf16[512,1024]{1,0:T(8,128)(2,1)S(1)}, bf16[512,1024]{1,0:T(8,128)(2,1)S(1)}, u32[]{:S(2)}, u32[]{:S(2)}) collective-permute-start(bf16[512,1024]{1,0:T(8,128)(2,1)S(1)} %get-tuple-element.44.refs_1_.refs_4_), channel_id=1, source_target_pairs={{0,1},{1,0},{2,3},{3,2},{4,5},{5,4},{6,7},{7,6},{8,9},{9,8},{10,11... | collective-permute-start | bytes 3145736 | tf_op jit(solution)/shard_map/ppermute | solution.py:221
  15.3 7.8 %collective-permute-start.1 = (bf16[16,1024]{1,0:T(8,128)(2,1)S(1)}, bf16[16,1024]{1,0:T(8,128)(2,1)S(1)}, u32[]{:S(2)}, u32[]{:S(2)}) collective-permute-start(bf16[16,1024]{1,0:T(8,128)(2,1)S(1)} %copy-done.6), channel_id=1, source_target_pairs={{4,0},{5,1},{6,2},{7,3},{0,4},{1,5},{2,6},{3,7},{12,8},{13,9},{14,... | collective-permute-start | bytes 98312 | tf_op jit(solution)/shard_map/ppermute | solution.py:231
  19.3 6.4 %collective-permute-start.2 = (bf16[16,1024]{1,0:T(8,128)(2,1)S(1)}, bf16[16,1024]{1,0:T(8,128)(2,1)S(1)}, u32[]{:S(2)}, u32[]{:S(2)}) collective-permute-start(bf16[16,1024]{1,0:T(8,128)(2,1)S(1)} %copy-done.6), channel_id=1, source_target_pairs={{6,0},{7,1},{0,2},{1,3},{2,4},{3,5},{4,6},{5,7},{14,8},{15,9},{8,1... | collective-permute-start | bytes 98312 | tf_op jit(solution)/shard_map/ppermute | solution.py:231
  25.7 6.0 %collective-permute-start.5 = (bf16[64,1024]{1,0:T(8,128)(2,1)S(1)}, bf16[64,1024]{1,0:T(8,128)(2,1)S(1)}, u32[]{:S(2)}, u32[]{:S(2)}) collective-permute-start(bf16[64,1024]{1,0:T(8,128)(2,1)S(1)} %shard_map.109.refs_0_), channel_id=1, source_target_pairs={{24,0},{25,1},{26,2},{27,3},{28,4},{29,5},{30,6},{31,7},{0,8},{1,9... | collective-permute-start | bytes 393224 | tf_op jit(solution)/shard_map/ppermute | solution.py:231
  26.3 6.8 %collective-permute-start.4 = (bf16[64,1024]{1,0:T(8,128)(2,1)S(1)}, bf16[64,1024]{1,0:T(8,128)(2,1)S(1)}, u32[]{:S(2)}, u32[]{:S(2)}) collective-permute-start(bf16[64,1024]{1,0:T(8,128)(2,1)S(1)} %shard_map.109.refs_0_), channel_id=1, source_target_pairs={{16,0},{17,1},{18,2},{19,3},{20,4},{21,5},{22,6},{23,7},{24,8},{25... | collective-permute-start | bytes 393224 | tf_op jit(solution)/shard_map/ppermute | solution.py:231
  31.7 6.2 %collective-permute-start.3 = (bf16[64,1024]{1,0:T(8,128)(2,1)S(1)}, bf16[64,1024]{1,0:T(8,128)(2,1)S(1)}, u32[]{:S(2)}, u32[]{:S(2)}) collective-permute-start(bf16[64,1024]{1,0:T(8,128)(2,1)S(1)} %shard_map.109.refs_0_), channel_id=1, source_target_pairs={{8,0},{9,1},{10,2},{11,3},{12,4},{13,5},{14,6},{15,7},{16,8},{17,9... | collective-permute-start | bytes 393224 | tf_op jit(solution)/shard_map/ppermute | solution.py:231
  67.8 5.0 %collective-permute-start.9 = (bf16[64,1024]{1,0:T(8,128)(2,1)S(1)}, bf16[64,1024]{1,0:T(8,128)(2,1)S(1)}, u32[]{:S(2)}, u32[]{:S(2)}) collective-permute-start(bf16[64,1024]{1,0:T(8,128)(2,1)S(1)} %get-tuple-element.48), channel_id=1, source_target_pairs={{24,0},{25,1},{26,2},{27,3},{28,4},{29,5},{30,6},{31,7},{0,8},{1,9... | collective-permute-start | bytes 393224 | tf_op jit(solution)/shard_map/ppermute | solution.py:231
  68.7 6.5 %collective-permute-start.10 = (bf16[64,1024]{1,0:T(8,128)(2,1)S(1)}, bf16[64,1024]{1,0:T(8,128)(2,1)S(1)}, u32[]{:S(2)}, u32[]{:S(2)}) collective-permute-start(bf16[64,1024]{1,0:T(8,128)(2,1)S(1)} %get-tuple-element.49), channel_id=1, source_target_pairs={{16,0},{17,1},{18,2},{19,3},{20,4},{21,5},{22,6},{23,7},{24,8},{25... | collective-permute-start | bytes 393224 | tf_op jit(solution)/shard_map/ppermute | solution.py:231
  70.2 6.3 %collective-permute-start.11 = (bf16[64,1024]{1,0:T(8,128)(2,1)S(1)}, bf16[64,1024]{1,0:T(8,128)(2,1)S(1)}, u32[]{:S(2)}, u32[]{:S(2)}) collective-permute-start(bf16[64,1024]{1,0:T(8,128)(2,1)S(1)} %get-tuple-element.50), channel_id=1, source_target_pairs={{8,0},{9,1},{10,2},{11,3},{12,4},{13,5},{14,6},{15,7},{16,8},{17,9... | collective-permute-start | bytes 393224 | tf_op jit(solution)/shard_map/ppermute | solution.py:231
  76.6 8.9 %collective-permute-start.12 = (bf16[16,1024]{1,0:T(8,128)(2,1)S(1)}, bf16[16,1024]{1,0:T(8,128)(2,1)S(1)}, u32[]{:S(2)}, u32[]{:S(2)}) collective-permute-start(bf16[16,1024]{1,0:T(8,128)(2,1)S(1)} %get-tuple-element.52), channel_id=1, source_target_pairs={{6,0},{7,1},{0,2},{1,3},{2,4},{3,5},{4,6},{5,7},{14,8},{15,9},{8,1... | collective-permute-start | bytes 98312 | tf_op jit(solution)/shard_map/ppermute | solution.py:231
  78.1 8.2 %collective-permute-start.13 = (bf16[16,1024]{1,0:T(8,128)(2,1)S(1)}, bf16[16,1024]{1,0:T(8,128)(2,1)S(1)}, u32[]{:S(2)}, u32[]{:S(2)}) collective-permute-start(bf16[16,1024]{1,0:T(8,128)(2,1)S(1)} %get-tuple-element.53), channel_id=1, source_target_pairs={{4,0},{5,1},{6,2},{7,3},{0,4},{1,5},{2,6},{3,7},{12,8},{13,9},{14,... | collective-permute-start | bytes 98312 | tf_op jit(solution)/shard_map/ppermute | solution.py:231
  81.6 5.7 %collective-permute-start.14 = (bf16[16,1024]{1,0:T(8,128)(2,1)S(1)}, bf16[16,1024]{1,0:T(8,128)(2,1)S(1)}, u32[]{:S(2)}, u32[]{:S(2)}) collective-permute-start(bf16[16,1024]{1,0:T(8,128)(2,1)S(1)} %get-tuple-element.54), channel_id=1, source_target_pairs={{2,0},{3,1},{4,2},{5,3},{6,4},{7,5},{0,6},{1,7},{10,8},{11,9},{12,... | collective-permute-start | bytes 98312 | tf_op jit(solution)/shard_map/ppermute | solution.py:231
  88.0 7.3 %collective-permute-start.18 = (bf16[16,1024]{1,0:T(8,128)(2,1)S(1)}, bf16[16,1024]{1,0:T(8,128)(2,1)S(1)}, u32[]{:S(2)}, u32[]{:S(2)}) collective-permute-start(bf16[16,1024]{1,0:T(8,128)(2,1)S(1)} %get-tuple-element.56.refs_0_), channel_id=1, source_target_pairs={{6,0},{7,1},{0,2},{1,3},{2,4},{3,5},{4,6},{5,7},{14,8},{15,9},{8,1... | collective-permute-start | bytes 98312 | tf_op jit(solution)/shard_map/ppermute | solution.py:231
  90.6 7.8 %collective-permute-start.17 = (bf16[16,1024]{1,0:T(8,128)(2,1)S(1)}, bf16[16,1024]{1,0:T(8,128)(2,1)S(1)}, u32[]{:S(2)}, u32[]{:S(2)}) collective-permute-start(bf16[16,1024]{1,0:T(8,128)(2,1)S(1)} %get-tuple-element.56.refs_0_), channel_id=1, source_target_pairs={{4,0},{5,1},{6,2},{7,3},{0,4},{1,5},{2,6},{3,7},{12,8},{13,9},{14,... | collective-permute-start | bytes 98312 | tf_op jit(solution)/shard_map/ppermute | solution.py:231
  95.0 4.9 %collective-permute-start.16 = (bf16[16,1024]{1,0:T(8,128)(2,1)S(1)}, bf16[16,1024]{1,0:T(8,128)(2,1)S(1)}, u32[]{:S(2)}, u32[]{:S(2)}) collective-permute-start(bf16[16,1024]{1,0:T(8,128)(2,1)S(1)} %get-tuple-element.56.refs_0_), channel_id=1, source_target_pairs={{2,0},{3,1},{4,2},{5,3},{6,4},{7,5},{0,6},{1,7},{10,8},{11,9},{12,... | collective-permute-start | bytes 98312 | tf_op jit(solution)/shard_map/ppermute | solution.py:231
  99.9 5.0 %collective-permute-start.21 = (bf16[64,1024]{1,0:T(8,128)(2,1)S(1)}, bf16[64,1024]{1,0:T(8,128)(2,1)S(1)}, u32[]{:S(2)}, u32[]{:S(2)}) collective-permute-start(bf16[64,1024]{1,0:T(8,128)(2,1)S(1)} %shard_map.116.refs_0_), channel_id=1, source_target_pairs={{24,0},{25,1},{26,2},{27,3},{28,4},{29,5},{30,6},{31,7},{0,8},{1,9... | collective-permute-start | bytes 393224 | tf_op jit(solution)/shard_map/ppermute | solution.py:231
  101.0 6.6 %collective-permute-start.20 = (bf16[64,1024]{1,0:T(8,128)(2,1)S(1)}, bf16[64,1024]{1,0:T(8,128)(2,1)S(1)}, u32[]{:S(2)}, u32[]{:S(2)}) collective-permute-start(bf16[64,1024]{1,0:T(8,128)(2,1)S(1)} %shard_map.116.refs_0_), channel_id=1, source_target_pairs={{16,0},{17,1},{18,2},{19,3},{20,4},{21,5},{22,6},{23,7},{24,8},{25... | collective-permute-start | bytes 393224 | tf_op jit(solution)/shard_map/ppermute | solution.py:231
  101.9 7.0 %collective-permute-start.19 = (bf16[64,1024]{1,0:T(8,128)(2,1)S(1)}, bf16[64,1024]{1,0:T(8,128)(2,1)S(1)}, u32[]{:S(2)}, u32[]{:S(2)}) collective-permute-start(bf16[64,1024]{1,0:T(8,128)(2,1)S(1)} %shard_map.116.refs_0_), channel_id=1, source_target_pairs={{8,0},{9,1},{10,2},{11,3},{12,4},{13,5},{14,6},{15,7},{16,8},{17,9... | collective-permute-start | bytes 393224 | tf_op jit(solution)/shard_map/ppermute | solution.py:231
  139.4 21.1 %collective-permute-start.25 = (bf16[256,2048]{1,0:T(8,128)(2,1)S(1)}, bf16[256,2048]{1,0:T(8,128)(2,1)S(1)}, u32[]{:S(2)}, u32[]{:S(2)}) collective-permute-start(bf16[256,2048]{1,0:T(8,128)(2,1)S(1)} %bitcast.6), channel_id=1, source_target_pairs={{0,1},{1,0},{2,3},{3,2},{4,5},{5,4},{6,7},{7,6},{8,9},{9,8},{10,11... | collective-permute-start | bytes 3145736 | tf_op jit(solution)/shard_map/ppermute | solution.py:221
  139.4 3.4 %collective-permute-start.15 = (bf16[256,1024]{1,0:T(8,128)(2,1)S(1)}, bf16[256,1024]{1,0:T(8,128)(2,1)S(1)}, u32[]{:S(2)}, u32[]{:S(2)}) collective-permute-start(bf16[256,1024]{1,0:T(8,128)(2,1)S(1)} %bitcast.11), channel_id=1, source_target_pairs={{0,1},{1,0},{2,3},{3,2},{4,5},{5,4},{6,7},{7,6},{8,9},{9,8},{10,11... | collective-permute-start | bytes 1572872 | tf_op jit(solution)/shard_map/ppermute | solution.py:221
  139.9 3.7 %collective-permute-start.22 = (bf16[256,1024]{1,0:T(8,128)(2,1)S(1)}, bf16[256,1024]{1,0:T(8,128)(2,1)S(1)}, u32[]{:S(2)}, u32[]{:S(2)}) collective-permute-start(bf16[256,1024]{1,0:T(8,128)(2,1)S(1)} %get-tuple-element.57.refs_3_), channel_id=1, source_target_pairs={{0,1},{1,0},{2,3},{3,2},{4,5},{5,4},{6,7},{7,6},{8,9},{9,8},{10,11... | collective-permute-start | bytes 1572872 | tf_op jit(solution)/shard_map/ppermute | solution.py:221
  139.9 20.6 %collective-permute-start.24 = (bf16[256,1024]{1,0:T(8,128)(2,1)S(1)}, bf16[256,1024]{1,0:T(8,128)(2,1)S(1)}, u32[]{:S(2)}, u32[]{:S(2)}) collective-permute-start(bf16[256,1024]{1,0:T(8,128)(2,1)S(1)} %get-tuple-element.62.refs_1_), channel_id=1, source_target_pairs={{0,1},{1,0},{2,3},{3,2},{4,5},{5,4},{6,7},{7,6},{8,9},{9,8},{10,11... | collective-permute-start | bytes 1572872 | tf_op jit(solution)/shard_map/ppermute | solution.py:221
  140.4 3.2 %collective-permute-start.23 = (f32[1,1]{1,0:T(1,128)}, f32[1,1]{1,0:T(1,128)}, u32[]{:S(2)}, u32[]{:S(2)}) collective-permute-start(f32[1,1]{1,0:T(1,128)} %get-tuple-element.60.refs_5_), channel_id=1, source_target_pairs={{0,1},{1,0},{2,3},{3,2},{4,5},{5,4},{6,7},{7,6},{8,9},{9,8},{10,11... | collective-permute-start | bytes 20 | tf_op jit(solution)/shard_map/ppermute | solution.py:221
  142.8 6.3 %collective-permute-start.26 = (bf16[64,1024]{1,0:T(8,128)(2,1)S(1)}, bf16[64,1024]{1,0:T(8,128)(2,1)S(1)}, u32[]{:S(2)}, u32[]{:S(2)}) collective-permute-start(bf16[64,1024]{1,0:T(8,128)(2,1)S(1)} %get-tuple-element.68), channel_id=1, source_target_pairs={{24,0},{25,1},{26,2},{27,3},{28,4},{29,5},{30,6},{31,7},{0,8},{1,9... | collective-permute-start | bytes 393224 | tf_op jit(solution)/shard_map/ppermute | solution.py:231
  143.6 7.9 %collective-permute-start.27 = (bf16[64,1024]{1,0:T(8,128)(2,1)S(1)}, bf16[64,1024]{1,0:T(8,128)(2,1)S(1)}, u32[]{:S(2)}, u32[]{:S(2)}) collective-permute-start(bf16[64,1024]{1,0:T(8,128)(2,1)S(1)} %get-tuple-element.69), channel_id=1, source_target_pairs={{16,0},{17,1},{18,2},{19,3},{20,4},{21,5},{22,6},{23,7},{24,8},{25... | collective-permute-start | bytes 393224 | tf_op jit(solution)/shard_map/ppermute | solution.py:231
  143.6 9.8 %collective-permute-start.28 = (bf16[64,1024]{1,0:T(8,128)(2,1)S(1)}, bf16[64,1024]{1,0:T(8,128)(2,1)S(1)}, u32[]{:S(2)}, u32[]{:S(2)}) collective-permute-start(bf16[64,1024]{1,0:T(8,128)(2,1)S(1)} %get-tuple-element.70), channel_id=1, source_target_pairs={{8,0},{9,1},{10,2},{11,3},{12,4},{13,5},{14,6},{15,7},{16,8},{17,9... | collective-permute-start | bytes 393224 | tf_op jit(solution)/shard_map/ppermute | solution.py:231
  153.4 11.8 %collective-permute-start.29 = (bf16[16,1024]{1,0:T(8,128)(2,1)S(1)}, bf16[16,1024]{1,0:T(8,128)(2,1)S(1)}, u32[]{:S(2)}, u32[]{:S(2)}) collective-permute-start(bf16[16,1024]{1,0:T(8,128)(2,1)S(1)} %get-tuple-element.73), channel_id=1, source_target_pairs={{6,0},{7,1},{0,2},{1,3},{2,4},{3,5},{4,6},{5,7},{14,8},{15,9},{8,1... | collective-permute-start | bytes 98312 | tf_op jit(solution)/shard_map/ppermute | solution.py:231
  154.4 10.8 %collective-permute-start.30 = (bf16[16,1024]{1,0:T(8,128)(2,1)S(1)}, bf16[16,1024]{1,0:T(8,128)(2,1)S(1)}, u32[]{:S(2)}, u32[]{:S(2)}) collective-permute-start(bf16[16,1024]{1,0:T(8,128)(2,1)S(1)} %get-tuple-element.74), channel_id=1, source_target_pairs={{4,0},{5,1},{6,2},{7,3},{0,4},{1,5},{2,6},{3,7},{12,8},{13,9},{14,... | collective-permute-start | bytes 98312 | tf_op jit(solution)/shard_map/ppermute | solution.py:231
  156.4 8.8 %collective-permute-start.31 = (bf16[16,1024]{1,0:T(8,128)(2,1)S(1)}, bf16[16,1024]{1,0:T(8,128)(2,1)S(1)}, u32[]{:S(2)}, u32[]{:S(2)}) collective-permute-start(bf16[16,1024]{1,0:T(8,128)(2,1)S(1)} %get-tuple-element.75), channel_id=1, source_target_pairs={{2,0},{3,1},{4,2},{5,3},{6,4},{7,5},{0,6},{1,7},{10,8},{11,9},{12,... | collective-permute-start | bytes 98312 | tf_op jit(solution)/shard_map/ppermute | solution.py:231
  (7 other events, 22.0 us)

commit v2 on v1

--- a/solution.py
+++ b/solution.py
@@ -14,6 +14,7 @@
 ROWS = 8
 TILE = 512
 DOWN = 2
+SAME_CORE = [[chip * CORES + core for chip in range(CHIPS)] for core in range(CORES)]
 VMEM = pl.BlockSpec(memory_space=pltpu.VMEM)
 SMEM = pl.BlockSpec(memory_space=pltpu.SMEM)
 ANY = pl.BlockSpec(memory_space=pl.ANY)
@@ -48,14 +49,22 @@
         joined_ref[pl.ds(part * size, size), :] = ref[...]
 
 
-def keep_kernel(mask_ref, gate_ref, up_ref, down_ref, *kept_refs):
-    for which, (ref, kept_ref) in enumerate(zip((gate_ref, up_ref, down_ref), kept_refs)):
-        for row in range(ref.shape[0] // BLK):
-            for col in range(ref.shape[1] // BLK):
-                at = (row, col) if which == DOWN else (col, row)
-                keep = mask_ref[which, at[0], at[1]].astype(jnp.float32).astype(jnp.bfloat16)
-                block = (pl.ds(row * BLK, BLK), pl.ds(col * BLK, BLK))
-                kept_ref[block] = ref[block] * keep
+def copies_kernel(block_ref, copies_ref):
+    for part in range(copies_ref.shape[0]):
+        copies_ref[part] = block_ref[...]
+
+
+def turn_kernel(ref, turned_ref):
+    turned_ref[...] = ref[...].T
+
+
+def keep(mask_ref, which, ref, kept_ref):
+    for row in range(ref.shape[0] // BLK):
+        for col in range(ref.shape[1] // BLK):
+            at = (row, col) if which == DOWN else (col, row)
+            factor = mask_ref[which, at[0], at[1]].astype(jnp.float32).astype(jnp.bfloat16)
+            block = (pl.ds(row * BLK, BLK), pl.ds(col * BLK, BLK))
+            kept_ref[block] = ref[block] * factor
 
 
 def plain_dot(left, right):
@@ -66,12 +75,18 @@
     return lax.dot_general(left, right, (((1,), (1,)), ((), ())), preferred_element_type=jnp.float32)
 
 
-def gate_up_kernel(*refs):
-    slabs, weights, (out_ref, rows_ref) = refs[:X], refs[X:-2], refs[-2:]
-    join_kernel(*slabs, rows_ref)
-    for which, ref in enumerate(weights):
+def gate_up_kernel(mask_ref, mask_other_ref, chips_ref, *refs):
+    weights, kept_refs, (out_ref, rows_ref) = refs[:4], refs[4:8], refs[8:]
+    chip = lax.axis_index("col") // CORES
+    size = chips_ref.shape[1]
+    for part in range(CHIPS):
+        x = lax.rem(chip // Z + part // Z, X)
+        z = lax.rem(chip + part % Z, Z)
+        rows_ref[pl.ds(part * size, size), :] = chips_ref[x * Z + z]
+    for which, (ref, kept_ref) in enumerate(zip(weights, kept_refs)):
         units = ref.shape[1]
-        value = plain_dot(rows_ref[...], ref[...])
+        keep((mask_ref, mask_other_ref)[which % 2], which // 2, ref, kept_ref)
+        value = plain_dot(rows_ref[...], kept_ref[...])
         out_ref[:, pl.ds(which * units, units)] = value.astype(out_ref.dtype)
 
 
@@ -81,12 +96,14 @@
         ref[:, cols] = value[part * size : (part + 1) * size].astype(ref.dtype)
 
 
-def output_kernel(hidden_ref, down_ref, down_other_ref, *out_refs):
+def output_kernel(mask_ref, mask_other_ref, hidden_ref, down_ref, down_other_ref, kept_ref, kept_other_ref, *out_refs):
     units, width = down_ref.shape
+    keep(mask_ref, DOWN, down_ref, kept_ref)
+    keep(mask_other_ref, DOWN, down_other_ref, kept_other_ref)
     for at in range(0, width, TILE):
         cols = pl.ds(at, TILE)
-        value = plain_dot(hidden_ref[:, :units], down_ref[:, cols])
-        value = value + plain_dot(hidden_ref[:, units:], down_other_ref[:, cols])
+        value = plain_dot(hidden_ref[:, :units], kept_ref[:, cols])
+        value = value + plain_dot(hidden_ref[:, units:], kept_other_ref[:, cols])
         put_slabs(out_refs, cols, value)
 
 
@@ -119,9 +136,10 @@
         put_slabs(out_refs, pl.ds(at, TILE), value)
 
 
-def multiply(kernel, shapes, left, weights, after=()):
-    flops = 2 * sum(part.shape[0] for part in left) * sum(weight.size for weight in weights)
-    return call(kernel, shapes, *left, *weights, flops=flops, vmem=16, after=after)
+def multiply(kernel, shapes, left, weights, masks=(), after=()):
+    flops = 2 * sum(part.size // part.shape[-1] for part in left) * sum(weight.size for weight in weights)
+    specs = [SMEM] * len(masks) + [VMEM] * (len(left) + len(weights))
+    return call(kernel, shapes, *masks, *left, *weights, flops=flops, vmem=16, in_specs=specs, after=after)
 
 
 def summed(parts):
@@ -145,11 +163,26 @@
         copies_ref[part] = hidden
 
 
-def error_kernel(scale, teacher_ref, *refs):
-    parts, (student_ref, grad_ref) = refs[:-2], refs[-2:]
-    output = summed(parts)
-    student_ref[...] = output.astype(jnp.bfloat16)
-    grad_ref[...] = ((output - teacher_ref[...].astype(jnp.float32)) / scale).astype(jnp.bfloat16)
+def lessen_kernel(teacher_ref, *refs):
+    parts, (own_ref, slab_ref) = refs[:X], refs[X:]
+    size = own_ref.shape[0]
+    total = summed(parts)
+    own_ref[...] = total[:size]
+    slab_ref[pl.ds(0, size), :] = (total[:size] - teacher_ref[...].astype(jnp.float32)).astype(jnp.bfloat16)
+    slab_ref[pl.ds(size, (Z - 1) * size), :] = total[size:].astype(jnp.bfloat16)
+
+
+def error_kernel(scale, own_ref, *refs):
+    slabs, (student_ref, grad_ref) = refs[:Z], refs[Z:]
+    size = own_ref.shape[0]
+    for part in range(Z):
+        terms = [
+            slabs[step][pl.ds((part - step) % Z * size, size), :].astype(jnp.float32) for step in range(Z)
+        ]
+        diff = (terms[0] + terms[2]) + (terms[1] + terms[3])
+        grad_ref[pl.ds(part * size, size), :] = (diff / scale).astype(jnp.bfloat16)
+        if part == 0:
+            student_ref[...] = (own_ref[...] + terms[2] + terms[1] + terms[3]).astype(jnp.bfloat16)
 
 
 def acts_kernel(parts_ref, both_ref, copies_ref, squares_ref):
@@ -171,18 +204,14 @@
     put_slabs(out_refs, slice(None), summed(parts))
 
 
-def turned_dot(left, right):
-    return lax.dot_general(left, right, (((0,), (0,)), ((), ())), preferred_element_type=jnp.float32)
-
-
 def weights_kernel(which, mask_ref, rows_ref, rows_other_ref, acts_ref, acts_other_ref, out_ref, done_ref):
     width, units = out_ref.shape
     done_ref[...] = jnp.zeros_like(done_ref)
     for at in range(0, units, 2 * BLK):
         own = pl.ds(2 * which * units + at, 2 * BLK)
         other = pl.ds((2 * which + 1) * units + at, 2 * BLK)
-        value = turned_dot(rows_ref[...], acts_ref[:, own])
-        value = value + turned_dot(rows_other_ref[...], acts_other_ref[:, other])
+        value = plain_dot(rows_ref[...], acts_ref[:, own])
+        value = value + plain_dot(rows_other_ref[...], acts_other_ref[:, other])
         for row in range(width // BLK):
             for col in range(2):
                 keep = mask_ref[which, at // BLK + col, row].astype(jnp.float32)
@@ -207,8 +236,8 @@
     done_ref[...] = jnp.zeros_like(done_ref)
     for at in range(0, width, 2 * BLK):
         cols = pl.ds(at, 2 * BLK)
-        value = turned_dot(hidden_ref[:, :units], grad_ref[:, cols])
-        value = value + turned_dot(hidden_other_ref[:, units:], grad_other_ref[:, cols])
+        value = plain_dot(hidden_ref[pl.ds(0, units), :], grad_ref[:, cols])
+        value = value + plain_dot(hidden_other_ref[pl.ds(units, units), :], grad_other_ref[:, cols])
         for row in range(units // BLK):
             for col in range(2):
                 keep = mask_ref[DOWN, row, at // BLK + col].astype(jnp.float32)
@@ -233,11 +262,6 @@
 
 def gather_z(block):
     return [block] + [fetch(block, 0, step) for step in range(1, Z)]
-
-
-def joined(parts):
-    size, width = parts[0].shape
-    return call(join_kernel, shaped((len(parts) * size, width)), *parts)
 
 
 def gather_x(block):
@@ -273,22 +297,19 @@
     mask = jnp.transpose(block_mask, (0, 2, 1))
     slab = shaped((Z * tokens, width))
     piece = shaped((tokens, width))
-    parts = gather_z(inputs)
-    weights = call(
-        keep_kernel,
-        (shaped((width, units)),) * 2 + (shaped((units, width)),),
-        mask,
-        gate_weight,
-        up_weight,
-        down_weight,
-        in_specs=[SMEM] + [VMEM] * 3,
-        vmem=16,
-        after=(parts[1],),
-    )
-    gates, ups, downs = ((value, other_core(value)) for value in weights)
-    slabs = gather_x(joined(parts))
-    partial, rows = multiply(
-        gate_up_kernel, (shaped((half, 4 * units)), shaped((half, width))), slabs, gates + ups, downs[1:]
+    wide, tall = shaped((width, units)), shaped((units, width))
+    gates, ups, downs, masks = (
+        (value, other_core(value)) for value in (gate_weight, up_weight, down_weight, mask)
+    )
+    copies = call(copies_kernel, shaped((CHIPS, tokens, width)), inputs, after=masks[1:])
+    chips = lax.all_to_all(copies, "col", 0, 0, axis_index_groups=SAME_CORE)
+    *gate_ups, partial, rows = multiply(
+        gate_up_kernel,
+        (wide,) * 4 + (shaped((half, 4 * units)), shaped((half, width))),
+        [chips],
+        gates + ups,
+        masks,
+        downs[1:],
     )
     both, copies = call(
         hidden_kernel,
@@ -296,12 +317,23 @@
         exchange_row(split(partial, ROWS)),
     )
     hidden = flat(exchange_row(copies))
-    slabs = spread_x(multiply(output_kernel, (slab,) * X, [hidden], downs))
-    parts = spread_z(call(sum_kernel, (piece,) * Z, *slabs))
-    student, grad_out = call(functools.partial(error_kernel, scale), (piece, piece), teacher, *parts)
-    slabs = gather_x(joined(gather_z(grad_out)))
+    *downs, first, second, third, fourth = multiply(
+        output_kernel, (tall,) * 2 + (slab,) * X, [hidden], downs, masks
+    )
+    slabs = spread_x([first, second, third, fourth])
+    own, lessened = call(lessen_kernel, (shaped((tokens, width), jnp.float32), slab), teacher, *slabs)
+    slabs = gather_z(lessened)
+    rows_turned, hidden_turned = (
+        call(turn_kernel, shaped(value.shape[::-1]), value, after=slabs[3:]) for value in (rows, hidden)
+    )
+    turned_other = [other_core(value) for value in (rows_turned, hidden_turned)]
+    student, grad_out = call(functools.partial(error_kernel, scale), (piece, slab), own, *slabs)
     partial, grad_rows = multiply(
-        grad_hidden_kernel, (shaped((half, 2 * units + BLK)), shaped((half, width))), slabs, downs
+        grad_hidden_kernel,
+        (shaped((half, 2 * units + BLK)), shaped((half, width))),
+        gather_x(grad_out),
+        downs,
+        after=turned_other,
     )
     copies, squares = call(
         acts_kernel,
@@ -310,16 +342,16 @@
         both,
     )
     acts = flat(exchange_row(copies))
-    slabs = spread_x(multiply(grad_in_kernel, (slab,) * X, [acts], gates + ups))
-    rows_other, hidden_other, grad_rows_other, acts_other, squares_other = (
-        other_core(value) for value in (rows, hidden, grad_rows, acts, squares)
+    slabs = spread_x(multiply(grad_in_kernel, (slab,) * X, [acts], gate_ups))
+    grad_rows_other, acts_other, squares_other = (
+        other_core(value) for value in (grad_rows, acts, squares)
     )
     grad_down, loss, down_done = call(
         down_kernel,
         (shaped((units, width)), shaped((1, 1), jnp.float32), DONE),
         mask,
-        hidden,
-        hidden_other,
+        hidden_turned,
+        turned_other[1],
         grad_rows,
         grad_rows_other,
         squares,
@@ -333,8 +365,8 @@
             functools.partial(weights_kernel, which),
             (shaped((width, units)), DONE),
             mask,
-            rows,
-            rows_other,
+            rows_turned,
+            turned_other[0],
             acts,
             acts_other,
             in_specs=[SMEM] + [VMEM] * 4,

time: 166 us -> 173 us (1.042)
  blocking collectives: 56.8 us -> 87.8 us
  starting transfers between devices: 49.6 us -> 31.7 us
  waiting for transfers between devices: 38.3 us -> 33.5 us
  local copies, waits for them, and re-layouts: 4.37 us -> 2 us
    all_to_all x0 -> x1, blocking collectives: none -> 26.9 us  [per_device(): chips = lax.all_to_all(copies, 'col', 0, 0, axis_index_groups=SAME_CORE)]
    ppermute x24 -> x15, starting transfers between devices: 47.9 us -> 29.4 us  [fetch(): return lax.ppermute(value, 'col', pairs)]
    ppermute x24 -> x15, waiting for transfers between devices: 37.2 us -> 27.3 us  [fetch(): return lax.ppermute(value, 'col', pairs)]
    ppermute x8 -> x9, waiting for transfers between devices: 1.12 us -> 6.26 us  [other_core(): lax.ppermute(value, 'col', [(device, device ^ 1) for device in range(coun...]
    all_to_all x4, blocking collectives: 56.8 us -> 60.9 us  [exchange_row(): return lax.all_to_all(value, 'row', 0, 0)]
    unnamed x14 -> x12, local copies, waits for them, and re-layouts: 4.37 us -> 2 us
  transfers between devices with their start and end apart: 32 -> 24, of which waited for: 20 -> 12; matrix products, arithmetic and copies ran while one was open for 0% -> 0% of each run, Pallas kernels for 6% -> 6%
where the time goes in v2:
time: 173 us; the launch traced here: 172 us
  blocking collectives  87.8 us (51%)
  waiting for transfers between devices  33.5 us (19%)
  starting transfers between devices  31.7 us (18%)
  Pallas kernels  16.6 us (10%)
  local copies, waits for them, and re-layouts  2 us (1%)
    all_to_all x4, blocking collectives, exchange_row(): return lax.all_to_all(value, 'row', 0, 0)  60.9 us
    ppermute x15, starting transfers between devices, fetch(): return lax.ppermute(value, 'col', pairs)  29.4 us
    ppermute x15, waiting for transfers between devices, fetch(): return lax.ppermute(value, 'col', pairs)  27.3 us
    all_to_all x1, blocking collectives, per_device(): chips = lax.all_to_all(copies, 'col', 0, 0, axis_index_groups=SAME_CORE)  26.9 us
    pallas_call x16, Pallas kernels, call(): pl.pallas_call(lambda *refs: kernel(*refs[:len(args)], *refs[len(args) +...  16.6 us
    ppermute x9, waiting for transfers between devices, other_core(): lax.ppermute(value, 'col', [(device, device ^ 1) for device in range(coun...  6.26 us
  transfers between devices with their start and end apart: 24, of which 12 were waited for; matrix products, arithmetic and copies ran while one was open for 0% of the time, Pallas kernels for 6%

profile of v2, /device:TPU:6, one launch (start us, length us, event | category | flops | bytes accessed | tf_op | source)
XLA Modules:
  0.0 172.3 jit_solution(16273286081009918693)
XLA Ops:
  1.8 4.9 %collective-permute-done.refs_1_ = s32[3,4,8]{2,1,0:T(4,128)S(1)} collective-permute-done((s32[3,4,8]{2,1,0:T(4,128)}, s32[3,4,8]{2,1,0:T(4,128)S(1)}, u32[]{:S(2)}, u32[]{:S(2)}) %collective-permute-start) | collective-permute-done | bytes 416 | tf_op jit(solution)/shard_map/ppermute | solution.py:250
  7.4 26.9 %all_to_all.25.refs_2_ = bf16[16,16,1024]{2,1,0:T(8,128)(2,1)S(1)} all-to-all(bf16[16,16,1024]{2,1,0:T(8,128)(2,1)S(1)} %shard_map.109), channel_id=1, replica_groups={{0,2,4,6,8,10,12,14,16,18,20,22,24,26,28,30},{1,3,5,7,9,11,13,15,17,19,..., dimensions={0} | all-to-all | bytes 1048576 | tf_op jit(solution)/shard_map/all_to_all | solution.py:305
  35.6 2.1 %shard_map.110 = (bf16[1024,512]{1,0:T(8,128)(2,1)S(1)}, bf16[1024,512]{1,0:T(8,128)(2,1)S(1)}, bf16[1024,512]{1,0:T(8,128)(2,1)S(1)}, bf16[1024,512]{1,0:T(8,12...) custom-call(s32[3,4,8]{2,1,0:T(4,128)S(1)} %bitcast.15, ...), custom_call_target="tpu_custom_call" | custom-call | flops 1073741824 | bytes 10486528 | tf_op jit(solution)/shard_map/pallas_call | solution.py:26
  37.7 19.4 %all_to_all.26.refs_0_ = bf16[8,32,2048]{2,1,0:T(8,128)(2,1)S(1)} all-to-all(bf16[8,32,2048]{2,1,0:T(8,128)(2,1)S(1)} %bitcast.12), channel_id=1, replica_groups=mesh['row'=8,'col'=32] {'row'}, dimensions={0} | all-to-all | bytes 2097152 | tf_op jit(solution)/shard_map/all_to_all | solution.py:280
  57.2 11.4 %all_to_all.27 = bf16[8,32,1024]{2,1,0:T(8,128)(2,1)S(1)} all-to-all(bf16[8,32,1024]{2,1,0:T(8,128)(2,1)S(1)} %get-tuple-element.44), channel_id=1, replica_groups=mesh['row'=8,'col'=32] {'row'}, dimensions={0} | all-to-all | bytes 1048576 | tf_op jit(solution)/shard_map/all_to_all | solution.py:280
  68.6 1.5 shard_map.112
  70.1 2.5 %collective-permute-start.4 = (bf16[64,1024]{1,0:T(8,128)(2,1)S(1)}, bf16[64,1024]{1,0:T(8,128)(2,1)S(1)}, u32[]{:S(2)}, u32[]{:S(2)}) collective-permute-start(bf16[64,1024]{1,0:T(8,128)(2,1)S(1)} %get-tuple-element.46), channel_id=1, source_target_pairs={{24,0},{25,1},{26,2},{27,3},{28,4},{29,5},{30,6},{31,7},{0,8},{1,9... | collective-permute-start | bytes 393224 | tf_op jit(solution)/shard_map/ppermute | solution.py:260
  73.5 3.0 %collective-permute-done.4.refs_2_ = bf16[64,1024]{1,0:T(8,128)(2,1)S(1)} collective-permute-done((bf16[64,1024]{1,0:T(8,128)(2,1)S(1)}, bf16[64,1024]{1,0:T(8,128)(2,1)S(1)}, u32[]{:S(2)}, u32[]{:S(2)}) %collective-permute-start.4) | collective-permute-done | bytes 131104 | tf_op jit(solution)/shard_map/ppermute | solution.py:260
  76.5 2.7 %collective-permute-done.5.refs_3_ = bf16[64,1024]{1,0:T(8,128)(2,1)S(1)} collective-permute-done((bf16[64,1024]{1,0:T(8,128)(2,1)S(1)}, bf16[64,1024]{1,0:T(8,128)(2,1)S(1)}, u32[]{:S(2)}, u32[]{:S(2)}) %collective-permute-start.5) | collective-permute-done | bytes 131104 | tf_op jit(solution)/shard_map/ppermute | solution.py:260
  79.1 1.3 collective-permute-done.6.refs_4_
  80.5 3.5 %collective-permute-start.9 = (bf16[64,1024]{1,0:T(8,128)(2,1)S(1)}, bf16[64,1024]{1,0:T(8,128)(2,1)S(1)}, u32[]{:S(2)}, u32[]{:S(2)}) collective-permute-start(bf16[64,1024]{1,0:T(8,128)(2,1)S(1)} %get-tuple-element.50.refs_1_), channel_id=1, source_target_pairs={{6,0},{7,1},{0,2},{1,3},{2,4},{3,5},{4,6},{5,7},{14,8},{15,9},{8,1... | collective-permute-start | bytes 393224 | tf_op jit(solution)/shard_map/ppermute | solution.py:260
  84.0 4.2 %collective-permute-done.9.refs_4_.refs_1_ = bf16[64,1024]{1,0:T(8,128)(2,1)S(1)} collective-permute-done((bf16[64,1024]{1,0:T(8,128)(2,1)S(1)}, bf16[64,1024]{1,0:T(8,128)(2,1)S(1)}, u32[]{:S(2)}, u32[]{:S(2)}) %collective-permute-start.9) | collective-permute-done | bytes 131104 | tf_op jit(solution)/shard_map/ppermute | solution.py:260
  89.3 2.5 %collective-permute-start.8 = (bf16[64,1024]{1,0:T(8,128)(2,1)S(1)}, bf16[64,1024]{1,0:T(8,128)(2,1)S(1)}, u32[]{:S(2)}, u32[]{:S(2)}) collective-permute-start(bf16[64,1024]{1,0:T(8,128)(2,1)S(1)} %get-tuple-element.50.refs_1_), channel_id=1, source_target_pairs={{4,0},{5,1},{6,2},{7,3},{0,4},{1,5},{2,6},{3,7},{12,8},{13,9},{14,... | collective-permute-start | bytes 393224 | tf_op jit(solution)/shard_map/ppermute | solution.py:260
  91.7 3.6 %collective-permute-start.7 = (bf16[64,1024]{1,0:T(8,128)(2,1)S(1)}, bf16[64,1024]{1,0:T(8,128)(2,1)S(1)}, u32[]{:S(2)}, u32[]{:S(2)}) collective-permute-start(bf16[64,1024]{1,0:T(8,128)(2,1)S(1)} %get-tuple-element.50.refs_1_), channel_id=1, source_target_pairs={{2,0},{3,1},{4,2},{5,3},{6,4},{7,5},{0,6},{1,7},{10,8},{11,9},{12,... | collective-permute-start | bytes 393224 | tf_op jit(solution)/shard_map/ppermute | solution.py:260
  95.3 5.5 %collective-permute-done.8.refs_3_ = bf16[64,1024]{1,0:T(8,128)(2,1)S(1)} collective-permute-done((bf16[64,1024]{1,0:T(8,128)(2,1)S(1)}, bf16[64,1024]{1,0:T(8,128)(2,1)S(1)}, u32[]{:S(2)}, u32[]{:S(2)}) %collective-permute-start.8) | collective-permute-done | bytes 131104 | tf_op jit(solution)/shard_map/ppermute | solution.py:260
  100.8 3.3 %collective-permute-done.7.refs_2_ = bf16[64,1024]{1,0:T(8,128)(2,1)S(1)} collective-permute-done((bf16[64,1024]{1,0:T(8,128)(2,1)S(1)}, bf16[64,1024]{1,0:T(8,128)(2,1)S(1)}, u32[]{:S(2)}, u32[]{:S(2)}) %collective-permute-start.7) | collective-permute-done | bytes 131104 | tf_op jit(solution)/shard_map/ppermute | solution.py:260
  105.1 1.7 collective-permute-start.12
  106.8 1.3 collective-permute-start.11
  108.1 3.0 %collective-permute-done.13.refs_3_ = bf16[64,1024]{1,0:T(8,128)(2,1)S(1)} collective-permute-done((bf16[64,1024]{1,0:T(8,128)(2,1)S(1)}, bf16[64,1024]{1,0:T(8,128)(2,1)S(1)}, u32[]{:S(2)}, u32[]{:S(2)}) %collective-permute-start.13) | collective-permute-done | bytes 131104 | tf_op jit(solution)/shard_map/ppermute | solution.py:260
  111.1 1.3 collective-permute-done.12.refs_2_
  112.4 2.0 %collective-permute-done.11.refs_1_ = bf16[64,1024]{1,0:T(8,128)(2,1)S(1)} collective-permute-done((bf16[64,1024]{1,0:T(8,128)(2,1)S(1)}, bf16[64,1024]{1,0:T(8,128)(2,1)S(1)}, u32[]{:S(2)}, u32[]{:S(2)}) %collective-permute-start.11) | collective-permute-done | bytes 131104 | tf_op jit(solution)/shard_map/ppermute | solution.py:260
  115.2 13.5 %all_to_all.28.refs_0_ = bf16[8,32,1152]{2,1,0:T(8,128)(2,1)S(1)} all-to-all(bf16[8,32,1152]{2,1,0:T(8,128)(2,1)S(1)} %bitcast.13), channel_id=1, replica_groups=mesh['row'=8,'col'=32] {'row'}, dimensions={0} | all-to-all | bytes 1179648 | tf_op jit(solution)/shard_map/all_to_all | solution.py:280
  129.4 16.6 %all_to_all.29 = bf16[8,32,2048]{2,1,0:T(8,128)(2,1)S(1)} all-to-all(bf16[8,32,2048]{2,1,0:T(8,128)(2,1)S(1)} %get-tuple-element.61), channel_id=1, replica_groups=mesh['row'=8,'col'=32] {'row'}, dimensions={0} | all-to-all | bytes 2097152 | tf_op jit(solution)/shard_map/all_to_all | solution.py:280
  148.5 2.2 %collective-permute-start.19 = (bf16[64,1024]{1,0:T(8,128)(2,1)S(1)}, bf16[64,1024]{1,0:T(8,128)(2,1)S(1)}, u32[]{:S(2)}, u32[]{:S(2)}) collective-permute-start(bf16[64,1024]{1,0:T(8,128)(2,1)S(1)} %get-tuple-element.71), channel_id=1, source_target_pairs={{16,0},{17,1},{18,2},{19,3},{20,4},{21,5},{22,6},{23,7},{24,8},{25... | collective-permute-start | bytes 393224 | tf_op jit(solution)/shard_map/ppermute | solution.py:260
  150.6 1.3 collective-permute-start.20
  151.9 1.4 collective-permute-done.16.refs_6_
  153.3 3.6 %shard_map.119 = (bf16[512,1024]{1,0:T(8,128)(2,1)}, f32[1,1]{1,0:T(1,128)}, f32[8,128]{1,0:T(8,128)S(1)}) custom-call(s32[3,4,8]{2,1,0:T(4,128)S(1)} %bitcast.17, bf16[1024,256]{1,0:T(8,128)(2,1)S(1)} %shard_map.115.refs_1_, bf16[1024,256]{1,0:T(8,128)(2,1)S(1)} %collective-permute-done.10.refs_7_.refs_2_, bf16[256,1024]{1,0:T(8,128)(2,1)S(1)} %get-tuple-element.56.refs_3_, ...), custom_call_target="tpu_custom_call" | custom-call | flops 536870912 | bytes 3150220 | tf_op jit(solution)/shard_map/pallas_call | solution.py:26
  158.0 3.8 %collective-permute-start.21 = (bf16[16,1024]{1,0:T(8,128)(2,1)S(1)}, bf16[16,1024]{1,0:T(8,128)(2,1)S(1)}, u32[]{:S(2)}, u32[]{:S(2)}) collective-permute-start(bf16[16,1024]{1,0:T(8,128)(2,1)S(1)} %get-tuple-element.75), channel_id=1, source_target_pairs={{6,0},{7,1},{0,2},{1,3},{2,4},{3,5},{4,6},{5,7},{14,8},{15,9},{8,1... | collective-permute-start | bytes 98312 | tf_op jit(solution)/shard_map/ppermute | solution.py:260
  161.8 3.7 %collective-permute-start.22 = (bf16[16,1024]{1,0:T(8,128)(2,1)S(1)}, bf16[16,1024]{1,0:T(8,128)(2,1)S(1)}, u32[]{:S(2)}, u32[]{:S(2)}) collective-permute-start(bf16[16,1024]{1,0:T(8,128)(2,1)S(1)} %get-tuple-element.76), channel_id=1, source_target_pairs={{4,0},{5,1},{6,2},{7,3},{0,4},{1,5},{2,6},{3,7},{12,8},{13,9},{14,... | collective-permute-start | bytes 98312 | tf_op jit(solution)/shard_map/ppermute | solution.py:260
  165.6 1.5 collective-permute-start.23
  167.1 2.3 %shard_map.121 = (bf16[1024,512]{1,0:T(8,128)(2,1)}, f32[8,128]{1,0:T(8,128)S(1)}) custom-call(s32[3,4,8]{2,1,0:T(4,128)S(1)} %bitcast.18, bf16[1024,256]{1,0:T(8,128)(2,1)S(1)} %shard_map.116.refs_1_, bf16[1024,256]{1,0:T(8,128)(2,1)S(1)} %collective-permute-done.14.refs_6_.refs_2_, bf16[256,2048]{1,0:T(8,128)(2,1)S(1)} %bitcast.8, ...), custom_call_target="tpu_custom_call" | custom-call | flops 536870912 | bytes 4198784 | tf_op jit(solution)/shard_map/pallas_call | solution.py:26
  169.4 2.3 %shard_map.120 = (bf16[1024,512]{1,0:T(8,128)(2,1)}, f32[8,128]{1,0:T(8,128)S(1)}) custom-call(s32[3,4,8]{2,1,0:T(4,128)S(1)} %bitcast.19, bf16[1024,256]{1,0:T(8,128)(2,1)S(1)} %shard_map.116.refs_1_, bf16[1024,256]{1,0:T(8,128)(2,1)S(1)} %collective-permute-done.14.refs_6_.refs_2_, bf16[256,2048]{1,0:T(8,128)(2,1)S(1)} %bitcast.9, ...), custom_call_target="tpu_custom_call" | custom-call | flops 536870912 | bytes 4198784 | tf_op jit(solution)/shard_map/pallas_call | solution.py:26
  (49 shorter events, 12.0 us)
Async XLA Ops:
  0.6 33.7 %copy-start = (bf16[1024,512]{1,0:T(8,128)(2,1)S(1)}, bf16[1024,512]{1,0:T(8,128)(2,1)}, u32[]{:S(2)}) copy-start(bf16[1024,512]{1,0:T(8,128)(2,1)} %refs_3_.2) | copy-start | bytes 3145732
  0.6 33.7 %collective-permute-start.1 = (bf16[1024,512]{1,0:T(8,128)(2,1)}, bf16[1024,512]{1,0:T(8,128)(2,1)S(1)}, u32[]{:S(2)}, u32[]{:S(2)}) collective-permute-start(bf16[1024,512]{1,0:T(8,128)(2,1)} %refs_3_.2), channel_id=1, source_target_pairs={{0,1},{1,0},{2,3},{3,2},{4,5},{5,4},{6,7},{7,6},{8,9},{9,8},{10,11... | collective-permute-start | bytes 3145736 | tf_op jit(solution)/shard_map/ppermute | solution.py:250
  0.7 33.6 %collective-permute-start.2 = (bf16[1024,512]{1,0:T(8,128)(2,1)}, bf16[1024,512]{1,0:T(8,128)(2,1)S(1)}, u32[]{:S(2)}, u32[]{:S(2)}) collective-permute-start(bf16[1024,512]{1,0:T(8,128)(2,1)} %refs_5_.1), channel_id=1, source_target_pairs={{0,1},{1,0},{2,3},{3,2},{4,5},{5,4},{6,7},{7,6},{8,9},{9,8},{10,11... | collective-permute-start | bytes 3145736 | tf_op jit(solution)/shard_map/ppermute | solution.py:250
  1.2 33.1 %collective-permute-start.3 = (bf16[512,1024]{1,0:T(8,128)(2,1)}, bf16[512,1024]{1,0:T(8,128)(2,1)S(1)}, u32[]{:S(2)}, u32[]{:S(2)}) collective-permute-start(bf16[512,1024]{1,0:T(8,128)(2,1)} %refs_3_.3), channel_id=1, source_target_pairs={{0,1},{1,0},{2,3},{3,2},{4,5},{5,4},{6,7},{7,6},{8,9},{9,8},{10,11... | collective-permute-start | bytes 3145736 | tf_op jit(solution)/shard_map/ppermute | solution.py:250
  1.3 5.3 %collective-permute-start = (s32[3,4,8]{2,1,0:T(4,128)}, s32[3,4,8]{2,1,0:T(4,128)S(1)}, u32[]{:S(2)}, u32[]{:S(2)}) collective-permute-start(s32[3,4,8]{2,1,0:T(4,128)} %bitcast.14), channel_id=1, source_target_pairs={{0,1},{1,0},{2,3},{3,2},{4,5},{5,4},{6,7},{7,6},{8,9},{9,8},{10,11... | collective-permute-start | bytes 1160 | tf_op jit(solution)/shard_map/ppermute | solution.py:250
  6.6 0.8 copy-start.4
  7.4 26.9 %copy-start.3 = (s32[3,8,4]{1,2,0:T(4,128)S(1)}, s32[3,8,4]{1,2,0:T(4,128)}, u32[]{:S(2)}) copy-start(s32[3,8,4]{1,2,0:T(4,128)} %param.11) | copy-start | bytes 1156
  34.3 1.2 copy-start.1
  57.1 11.5 %copy-start.2 = (bf16[512,1024]{1,0:T(8,128)(2,1)S(1)}, bf16[512,1024]{1,0:T(8,128)(2,1)}, u32[]{:S(2)}) copy-start(bf16[512,1024]{1,0:T(8,128)(2,1)} %refs_3_.3) | copy-start | bytes 3145732
  68.6 11.9 %copy-start.5 = (bf16[16,1024]{1,0:T(8,128)(2,1)S(1)}, bf16[16,1024]{1,0:T(8,128)(2,1)}, u32[]{:S(2)}) copy-start(bf16[16,1024]{1,0:T(8,128)(2,1)} %refs_0_.3) | copy-start | bytes 98308
  70.1 6.4 %collective-permute-start.4 = (bf16[64,1024]{1,0:T(8,128)(2,1)S(1)}, bf16[64,1024]{1,0:T(8,128)(2,1)S(1)}, u32[]{:S(2)}, u32[]{:S(2)}) collective-permute-start(bf16[64,1024]{1,0:T(8,128)(2,1)S(1)} %get-tuple-element.46), channel_id=1, source_target_pairs={{24,0},{25,1},{26,2},{27,3},{28,4},{29,5},{30,6},{31,7},{0,8},{1,9... | collective-permute-start | bytes 393224 | tf_op jit(solution)/shard_map/ppermute | solution.py:260
  72.6 6.6 %collective-permute-start.5 = (bf16[64,1024]{1,0:T(8,128)(2,1)S(1)}, bf16[64,1024]{1,0:T(8,128)(2,1)S(1)}, u32[]{:S(2)}, u32[]{:S(2)}) collective-permute-start(bf16[64,1024]{1,0:T(8,128)(2,1)S(1)} %get-tuple-element.47), channel_id=1, source_target_pairs={{16,0},{17,1},{18,2},{19,3},{20,4},{21,5},{22,6},{23,7},{24,8},{25... | collective-permute-start | bytes 393224 | tf_op jit(solution)/shard_map/ppermute | solution.py:260
  73.1 7.4 %collective-permute-start.6 = (bf16[64,1024]{1,0:T(8,128)(2,1)S(1)}, bf16[64,1024]{1,0:T(8,128)(2,1)S(1)}, u32[]{:S(2)}, u32[]{:S(2)}) collective-permute-start(bf16[64,1024]{1,0:T(8,128)(2,1)S(1)} %get-tuple-element.48), channel_id=1, source_target_pairs={{8,0},{9,1},{10,2},{11,3},{12,4},{13,5},{14,6},{15,7},{16,8},{17,9... | collective-permute-start | bytes 393224 | tf_op jit(solution)/shard_map/ppermute | solution.py:260
  80.5 7.7 %collective-permute-start.9 = (bf16[64,1024]{1,0:T(8,128)(2,1)S(1)}, bf16[64,1024]{1,0:T(8,128)(2,1)S(1)}, u32[]{:S(2)}, u32[]{:S(2)}) collective-permute-start(bf16[64,1024]{1,0:T(8,128)(2,1)S(1)} %get-tuple-element.50.refs_1_), channel_id=1, source_target_pairs={{6,0},{7,1},{0,2},{1,3},{2,4},{3,5},{4,6},{5,7},{14,8},{15,9},{8,1... | collective-permute-start | bytes 393224 | tf_op jit(solution)/shard_map/ppermute | solution.py:260
  88.4 26.1 %collective-permute-start.10 = (bf16[1024,256]{1,0:T(8,128)(2,1)S(1)}, bf16[1024,256]{1,0:T(8,128)(2,1)S(1)}, u32[]{:S(2)}, u32[]{:S(2)}) collective-permute-start(bf16[1024,256]{1,0:T(8,128)(2,1)S(1)} %shard_map.115.refs_1_), channel_id=1, source_target_pairs={{0,1},{1,0},{2,3},{3,2},{4,5},{5,4},{6,7},{7,6},{8,9},{9,8},{10,11... | collective-permute-start | bytes 1572872 | tf_op jit(solution)/shard_map/ppermute | solution.py:250
  88.7 25.8 %collective-permute-start.14 = (bf16[1024,256]{1,0:T(8,128)(2,1)S(1)}, bf16[1024,256]{1,0:T(8,128)(2,1)S(1)}, u32[]{:S(2)}, u32[]{:S(2)}) collective-permute-start(bf16[1024,256]{1,0:T(8,128)(2,1)S(1)} %shard_map.116.refs_1_), channel_id=1, source_target_pairs={{0,1},{1,0},{2,3},{3,2},{4,5},{5,4},{6,7},{7,6},{8,9},{9,8},{10,11... | collective-permute-start | bytes 1572872 | tf_op jit(solution)/shard_map/ppermute | solution.py:250
  89.3 11.5 %collective-permute-start.8 = (bf16[64,1024]{1,0:T(8,128)(2,1)S(1)}, bf16[64,1024]{1,0:T(8,128)(2,1)S(1)}, u32[]{:S(2)}, u32[]{:S(2)}) collective-permute-start(bf16[64,1024]{1,0:T(8,128)(2,1)S(1)} %get-tuple-element.50.refs_1_), channel_id=1, source_target_pairs={{4,0},{5,1},{6,2},{7,3},{0,4},{1,5},{2,6},{3,7},{12,8},{13,9},{14,... | collective-permute-start | bytes 393224 | tf_op jit(solution)/shard_map/ppermute | solution.py:260
  91.7 12.4 %collective-permute-start.7 = (bf16[64,1024]{1,0:T(8,128)(2,1)S(1)}, bf16[64,1024]{1,0:T(8,128)(2,1)S(1)}, u32[]{:S(2)}, u32[]{:S(2)}) collective-permute-start(bf16[64,1024]{1,0:T(8,128)(2,1)S(1)} %get-tuple-element.50.refs_1_), channel_id=1, source_target_pairs={{2,0},{3,1},{4,2},{5,3},{6,4},{7,5},{0,6},{1,7},{10,8},{11,9},{12,... | collective-permute-start | bytes 393224 | tf_op jit(solution)/shard_map/ppermute | solution.py:260
  104.7 6.4 %collective-permute-start.13 = (bf16[64,1024]{1,0:T(8,128)(2,1)S(1)}, bf16[64,1024]{1,0:T(8,128)(2,1)S(1)}, u32[]{:S(2)}, u32[]{:S(2)}) collective-permute-start(bf16[64,1024]{1,0:T(8,128)(2,1)S(1)} %get-tuple-element.52.refs_0_), channel_id=1, source_target_pairs={{24,0},{25,1},{26,2},{27,3},{28,4},{29,5},{30,6},{31,7},{0,8},{1,9... | collective-permute-start | bytes 393224 | tf_op jit(solution)/shard_map/ppermute | solution.py:260
  105.1 7.3 %collective-permute-start.12 = (bf16[64,1024]{1,0:T(8,128)(2,1)S(1)}, bf16[64,1024]{1,0:T(8,128)(2,1)S(1)}, u32[]{:S(2)}, u32[]{:S(2)}) collective-permute-start(bf16[64,1024]{1,0:T(8,128)(2,1)S(1)} %get-tuple-element.52.refs_0_), channel_id=1, source_target_pairs={{16,0},{17,1},{18,2},{19,3},{20,4},{21,5},{22,6},{23,7},{24,8},{25... | collective-permute-start | bytes 393224 | tf_op jit(solution)/shard_map/ppermute | solution.py:260
  106.8 7.7 %collective-permute-start.11 = (bf16[64,1024]{1,0:T(8,128)(2,1)S(1)}, bf16[64,1024]{1,0:T(8,128)(2,1)S(1)}, u32[]{:S(2)}, u32[]{:S(2)}) collective-permute-start(bf16[64,1024]{1,0:T(8,128)(2,1)S(1)} %get-tuple-element.52.refs_0_), channel_id=1, source_target_pairs={{8,0},{9,1},{10,2},{11,3},{12,4},{13,5},{14,6},{15,7},{16,8},{17,9... | collective-permute-start | bytes 393224 | tf_op jit(solution)/shard_map/ppermute | solution.py:260
  146.1 21.0 %collective-permute-start.17 = (bf16[256,2048]{1,0:T(8,128)(2,1)S(1)}, bf16[256,2048]{1,0:T(8,128)(2,1)S(1)}, u32[]{:S(2)}, u32[]{:S(2)}) collective-permute-start(bf16[256,2048]{1,0:T(8,128)(2,1)S(1)} %bitcast.6), channel_id=1, source_target_pairs={{0,1},{1,0},{2,3},{3,2},{4,5},{5,4},{6,7},{7,6},{8,9},{9,8},{10,11... | collective-permute-start | bytes 3145736 | tf_op jit(solution)/shard_map/ppermute | solution.py:250
  146.1 5.9 %collective-permute-start.15 = (bf16[256,1024]{1,0:T(8,128)(2,1)S(1)}, bf16[256,1024]{1,0:T(8,128)(2,1)S(1)}, u32[]{:S(2)}, u32[]{:S(2)}) collective-permute-start(bf16[256,1024]{1,0:T(8,128)(2,1)S(1)} %get-tuple-element.56.refs_3_), channel_id=1, source_target_pairs={{0,1},{1,0},{2,3},{3,2},{4,5},{5,4},{6,7},{7,6},{8,9},{9,8},{10,11... | collective-permute-start | bytes 1572872 | tf_op jit(solution)/shard_map/ppermute | solution.py:250
  147.9 9.1 %collective-permute-start.18 = (bf16[64,1024]{1,0:T(8,128)(2,1)S(1)}, bf16[64,1024]{1,0:T(8,128)(2,1)S(1)}, u32[]{:S(2)}, u32[]{:S(2)}) collective-permute-start(bf16[64,1024]{1,0:T(8,128)(2,1)S(1)} %get-tuple-element.70), channel_id=1, source_target_pairs={{24,0},{25,1},{26,2},{27,3},{28,4},{29,5},{30,6},{31,7},{0,8},{1,9... | collective-permute-start | bytes 393224 | tf_op jit(solution)/shard_map/ppermute | solution.py:260
  148.5 8.5 %collective-permute-start.19 = (bf16[64,1024]{1,0:T(8,128)(2,1)S(1)}, bf16[64,1024]{1,0:T(8,128)(2,1)S(1)}, u32[]{:S(2)}, u32[]{:S(2)}) collective-permute-start(bf16[64,1024]{1,0:T(8,128)(2,1)S(1)} %get-tuple-element.71), channel_id=1, source_target_pairs={{16,0},{17,1},{18,2},{19,3},{20,4},{21,5},{22,6},{23,7},{24,8},{25... | collective-permute-start | bytes 393224 | tf_op jit(solution)/shard_map/ppermute | solution.py:260
  150.6 7.3 %collective-permute-start.20 = (bf16[64,1024]{1,0:T(8,128)(2,1)S(1)}, bf16[64,1024]{1,0:T(8,128)(2,1)S(1)}, u32[]{:S(2)}, u32[]{:S(2)}) collective-permute-start(bf16[64,1024]{1,0:T(8,128)(2,1)S(1)} %get-tuple-element.72), channel_id=1, source_target_pairs={{8,0},{9,1},{10,2},{11,3},{12,4},{13,5},{14,6},{15,7},{16,8},{17,9... | collective-permute-start | bytes 393224 | tf_op jit(solution)/shard_map/ppermute | solution.py:260
  151.9 1.4 collective-permute-start.16
  158.0 13.7 %collective-permute-start.21 = (bf16[16,1024]{1,0:T(8,128)(2,1)S(1)}, bf16[16,1024]{1,0:T(8,128)(2,1)S(1)}, u32[]{:S(2)}, u32[]{:S(2)}) collective-permute-start(bf16[16,1024]{1,0:T(8,128)(2,1)S(1)} %get-tuple-element.75), channel_id=1, source_target_pairs={{6,0},{7,1},{0,2},{1,3},{2,4},{3,5},{4,6},{5,7},{14,8},{15,9},{8,1... | collective-permute-start | bytes 98312 | tf_op jit(solution)/shard_map/ppermute | solution.py:260
  161.8 9.9 %collective-permute-start.22 = (bf16[16,1024]{1,0:T(8,128)(2,1)S(1)}, bf16[16,1024]{1,0:T(8,128)(2,1)S(1)}, u32[]{:S(2)}, u32[]{:S(2)}) collective-permute-start(bf16[16,1024]{1,0:T(8,128)(2,1)S(1)} %get-tuple-element.76), channel_id=1, source_target_pairs={{4,0},{5,1},{6,2},{7,3},{0,4},{1,5},{2,6},{3,7},{12,8},{13,9},{14,... | collective-permute-start | bytes 98312 | tf_op jit(solution)/shard_map/ppermute | solution.py:260
  165.6 6.1 %collective-permute-start.23 = (bf16[16,1024]{1,0:T(8,128)(2,1)S(1)}, bf16[16,1024]{1,0:T(8,128)(2,1)S(1)}, u32[]{:S(2)}, u32[]{:S(2)}) collective-permute-start(bf16[16,1024]{1,0:T(8,128)(2,1)S(1)} %get-tuple-element.77), channel_id=1, source_target_pairs={{2,0},{3,1},{4,2},{5,3},{6,4},{7,5},{0,6},{1,7},{10,8},{11,9},{12,... | collective-permute-start | bytes 98312 | tf_op jit(solution)/shard_map/ppermute | solution.py:260

commit v3 on v2

--- a/solution.py
+++ b/solution.py
@@ -47,15 +47,6 @@
     size = refs[0].shape[0]
     for part, ref in enumerate(refs[:-1]):
         joined_ref[pl.ds(part * size, size), :] = ref[...]
-
-
-def copies_kernel(block_ref, copies_ref):
-    for part in range(copies_ref.shape[0]):
-        copies_ref[part] = block_ref[...]
-
-
-def turn_kernel(ref, turned_ref):
-    turned_ref[...] = ref[...].T
 
 
 def keep(mask_ref, which, ref, kept_ref):
@@ -163,33 +154,18 @@
         copies_ref[part] = hidden
 
 
-def lessen_kernel(teacher_ref, *refs):
-    parts, (own_ref, slab_ref) = refs[:X], refs[X:]
-    size = own_ref.shape[0]
-    total = summed(parts)
-    own_ref[...] = total[:size]
-    slab_ref[pl.ds(0, size), :] = (total[:size] - teacher_ref[...].astype(jnp.float32)).astype(jnp.bfloat16)
-    slab_ref[pl.ds(size, (Z - 1) * size), :] = total[size:].astype(jnp.bfloat16)
-
-
-def error_kernel(scale, own_ref, *refs):
-    slabs, (student_ref, grad_ref) = refs[:Z], refs[Z:]
-    size = own_ref.shape[0]
-    for part in range(Z):
-        terms = [
-            slabs[step][pl.ds((part - step) % Z * size, size), :].astype(jnp.float32) for step in range(Z)
-        ]
-        diff = (terms[0] + terms[2]) + (terms[1] + terms[3])
-        grad_ref[pl.ds(part * size, size), :] = (diff / scale).astype(jnp.bfloat16)
-        if part == 0:
-            student_ref[...] = (own_ref[...] + terms[2] + terms[1] + terms[3]).astype(jnp.bfloat16)
+def error_kernel(scale, teacher_ref, *refs):
+    parts, (student_ref, grad_ref) = refs[:-2], refs[-2:]
+    output = summed(parts)
+    student_ref[...] = output.astype(jnp.bfloat16)
+    grad_ref[...] = ((output - teacher_ref[...].astype(jnp.float32)) / scale).astype(jnp.bfloat16)
 
 
 def acts_kernel(parts_ref, both_ref, copies_ref, squares_ref):
     total = summed(parts_of(parts_ref))
     half = both_ref.shape[1] // 2
     grad_hidden = total[:, :half]
-    squares_ref[...] = jnp.sum(total[:1, half:], axis=1, keepdims=True)
+    squares_ref[...] = jnp.broadcast_to(jnp.sum(total[:1, half:], axis=1, keepdims=True), squares_ref.shape)
     gate, up = both_ref[:, :half], both_ref[:, half:]
     sig = jax.nn.sigmoid(gate)
     grad_gate_act = (grad_hidden * up * sig * (1.0 + gate * (1.0 - sig))).astype(jnp.bfloat16)
@@ -204,45 +180,63 @@
     put_slabs(out_refs, slice(None), summed(parts))
 
 
-def weights_kernel(which, mask_ref, rows_ref, rows_other_ref, acts_ref, acts_other_ref, out_ref, done_ref):
-    width, units = out_ref.shape
-    done_ref[...] = jnp.zeros_like(done_ref)
-    for at in range(0, units, 2 * BLK):
-        own = pl.ds(2 * which * units + at, 2 * BLK)
-        other = pl.ds((2 * which + 1) * units + at, 2 * BLK)
-        value = plain_dot(rows_ref[...], acts_ref[:, own])
-        value = value + plain_dot(rows_other_ref[...], acts_other_ref[:, other])
-        for row in range(width // BLK):
-            for col in range(2):
-                keep = mask_ref[which, at // BLK + col, row].astype(jnp.float32)
-                block = value[row * BLK : (row + 1) * BLK, col * BLK : (col + 1) * BLK] * keep
-                out_ref[pl.ds(row * BLK, BLK), pl.ds(at + col * BLK, BLK)] = block.astype(jnp.bfloat16)
-
-
-def down_kernel(
+def put_kept(mask_ref, which, value, col, scratch_ref):
+    for row in range(value.shape[0] // BLK):
+        for step in range(value.shape[1] // BLK):
+            at = (row, col + step) if which == DOWN else (col + step, row)
+            factor = mask_ref[which, at[0], at[1]].astype(jnp.float32)
+            block = value[row * BLK : (row + 1) * BLK, step * BLK : (step + 1) * BLK] * factor
+            scratch_ref[pl.ds(row * BLK, BLK), pl.ds((col + step) * BLK, BLK)] = block.astype(jnp.bfloat16)
+
+
+def weights_kernel(
     mask_ref,
+    rows_ref,
+    rows_other_ref,
+    acts_ref,
+    acts_other_ref,
     hidden_ref,
     hidden_other_ref,
     grad_ref,
     grad_other_ref,
     squares_ref,
     squares_other_ref,
-    out_ref,
+    gate_ref,
+    up_ref,
+    down_ref,
     loss_ref,
     done_ref,
+    gate_scratch,
+    up_scratch,
+    down_scratch,
+    sems,
 ):
-    units, width = out_ref.shape
-    loss_ref[...] = (squares_ref[...] + squares_other_ref[...]) * (1.0 / D)
+    units = gate_ref.shape[1]
+    loss_ref[...] = (squares_ref[:1, :1] + squares_other_ref[:1, :1]) * (1.0 / D)
     done_ref[...] = jnp.zeros_like(done_ref)
-    for at in range(0, width, 2 * BLK):
-        cols = pl.ds(at, 2 * BLK)
-        value = plain_dot(hidden_ref[pl.ds(0, units), :], grad_ref[:, cols])
-        value = value + plain_dot(hidden_other_ref[pl.ds(units, units), :], grad_other_ref[:, cols])
-        for row in range(units // BLK):
-            for col in range(2):
-                keep = mask_ref[DOWN, row, at // BLK + col].astype(jnp.float32)
-                block = value[row * BLK : (row + 1) * BLK, col * BLK : (col + 1) * BLK] * keep
-                out_ref[pl.ds(row * BLK, BLK), pl.ds(at + col * BLK, BLK)] = block.astype(jnp.bfloat16)
+    copies = []
+
+    def put(which, value, col, scratch, out_ref):
+        put_kept(mask_ref, which, value, col, scratch)
+        cols = pl.ds(col * BLK, value.shape[1])
+        copy = pltpu.make_async_copy(scratch.at[:, cols], out_ref.at[:, cols], sems.at[len(copies)])
+        copy.start()
+        copies.append(copy)
+
+    turned, turned_other = hidden_ref[:, :units].T, hidden_other_ref[:, units:].T
+    for col in range(0, down_ref.shape[1] // BLK, 4):
+        cols = pl.ds(col * BLK, 4 * BLK)
+        value = plain_dot(turned, grad_ref[:, cols]) + plain_dot(turned_other, grad_other_ref[:, cols])
+        put(DOWN, value, col, down_scratch, down_ref)
+    turned, turned_other = rows_ref[...].T, rows_other_ref[...].T
+    for which, (scratch, out_ref) in enumerate(((gate_scratch, gate_ref), (up_scratch, up_ref))):
+        for col in range(0, units // BLK, 2):
+            own = pl.ds(2 * which * units + col * BLK, 2 * BLK)
+            other = pl.ds((2 * which + 1) * units + col * BLK, 2 * BLK)
+            value = plain_dot(turned, acts_ref[:, own]) + plain_dot(turned_other, acts_other_ref[:, other])
+            put(which, value, col, scratch, out_ref)
+    for copy in copies:
+        copy.wait()
 
 
 def other_core(value):
@@ -262,6 +256,11 @@
 
 def gather_z(block):
     return [block] + [fetch(block, 0, step) for step in range(1, Z)]
+
+
+def joined(parts):
+    size, width = parts[0].shape
+    return call(join_kernel, shaped((len(parts) * size, width)), *parts)
 
 
 def gather_x(block):
@@ -301,7 +300,7 @@
     gates, ups, downs, masks = (
         (value, other_core(value)) for value in (gate_weight, up_weight, down_weight, mask)
     )
-    copies = call(copies_kernel, shaped((CHIPS, tokens, width)), inputs, after=masks[1:])
+    copies = jnp.broadcast_to(inputs[None], (CHIPS, tokens, width))
     chips = lax.all_to_all(copies, "col", 0, 0, axis_index_groups=SAME_CORE)
     *gate_ups, partial, rows = multiply(
         gate_up_kernel,
@@ -321,62 +320,46 @@
         output_kernel, (tall,) * 2 + (slab,) * X, [hidden], downs, masks
     )
     slabs = spread_x([first, second, third, fourth])
-    own, lessened = call(lessen_kernel, (shaped((tokens, width), jnp.float32), slab), teacher, *slabs)
-    slabs = gather_z(lessened)
-    rows_turned, hidden_turned = (
-        call(turn_kernel, shaped(value.shape[::-1]), value, after=slabs[3:]) for value in (rows, hidden)
-    )
-    turned_other = [other_core(value) for value in (rows_turned, hidden_turned)]
-    student, grad_out = call(functools.partial(error_kernel, scale), (piece, slab), own, *slabs)
+    parts = spread_z(call(sum_kernel, (piece,) * Z, *slabs))
+    student, grad_out = call(functools.partial(error_kernel, scale), (piece, piece), teacher, *parts)
+    slabs = gather_x(joined(gather_z(grad_out)))
     partial, grad_rows = multiply(
-        grad_hidden_kernel,
-        (shaped((half, 2 * units + BLK)), shaped((half, width))),
-        gather_x(grad_out),
-        downs,
-        after=turned_other,
+        grad_hidden_kernel, (shaped((half, 2 * units + BLK)), shaped((half, width))), slabs, downs
     )
     copies, squares = call(
         acts_kernel,
-        (shaped((ROWS, half // ROWS, 4 * units)), shaped((1, 1), jnp.float32)),
+        (shaped((ROWS, half // ROWS, 4 * units)), DONE),
         exchange_row(split(partial, ROWS)),
         both,
     )
     acts = flat(exchange_row(copies))
     slabs = spread_x(multiply(grad_in_kernel, (slab,) * X, [acts], gate_ups))
-    grad_rows_other, acts_other, squares_other = (
-        other_core(value) for value in (grad_rows, acts, squares)
-    )
-    grad_down, loss, down_done = call(
-        down_kernel,
-        (shaped((units, width)), shaped((1, 1), jnp.float32), DONE),
+    rows_other, hidden_other, grad_rows_other, acts_other, squares_other = (
+        other_core(value) for value in (rows, hidden, grad_rows, acts, squares)
+    )
+    grad_gate, grad_up, grad_down, loss, done = call(
+        weights_kernel,
+        (wide, wide, tall, shaped((1, 1), jnp.float32), DONE),
         mask,
-        hidden_turned,
-        turned_other[1],
+        rows,
+        rows_other,
+        acts,
+        acts_other,
+        hidden,
+        hidden_other,
         grad_rows,
         grad_rows_other,
         squares,
         squares_other,
-        in_specs=[SMEM] + [VMEM] * 6,
-        flops=2 * token_count * width * units,
-        vmem=16,
-    )
-    (grad_gate, gate_done), (grad_up, up_done) = (
-        call(
-            functools.partial(weights_kernel, which),
-            (shaped((width, units)), DONE),
-            mask,
-            rows_turned,
-            turned_other[0],
-            acts,
-            acts_other,
-            in_specs=[SMEM] + [VMEM] * 4,
-            flops=2 * token_count * width * units,
-            vmem=16,
-        )
-        for which in range(2)
-    )
-    parts = spread_z(call(sum_kernel, (piece,) * Z, *slabs, after=(down_done,)))
-    (grad_in,) = call(sum_kernel, (piece,), *parts, after=(gate_done, up_done))
+        in_specs=[SMEM] + [VMEM] * 10,
+        out_specs=(ANY,) * 3 + (VMEM,) * 2,
+        scratch_shapes=[pltpu.VMEM(value.shape, value.dtype) for value in (wide, wide, tall)]
+        + [pltpu.SemaphoreType.DMA((6,))],
+        flops=6 * token_count * width * units,
+        vmem=24,
+    )
+    parts = spread_z(call(sum_kernel, (piece,) * Z, *slabs, after=(done,)))
+    (grad_in,) = call(sum_kernel, (piece,), *parts)
     return student, loss[0, 0], grad_gate, grad_up, grad_down, grad_in
 
 

time: 173 us -> 167 us (0.965)
  blocking collectives: 87.8 us -> 59.2 us
  starting transfers between devices: 31.7 us -> 44.4 us
  waiting for transfers between devices: 33.5 us -> 46 us
  Pallas kernels: 16.6 us -> 12.6 us
    all_to_all x1 -> x0, blocking collectives: 26.9 us -> none  [per_device(): chips = lax.all_to_all(copies, 'col', 0, 0, axis_index_groups=SAME_CORE)]
    all_to_all x0 -> x1, waiting for transfers between devices: none -> 16.2 us  [per_device(): chips = lax.all_to_all(copies, 'col', 0, 0, axis_index_groups=SAME_CORE)]
    all_to_all x0 -> x1, starting transfers between devices: none -> 11.6 us  [per_device(): chips = lax.all_to_all(copies, 'col', 0, 0, axis_index_groups=SAME_CORE)]
    pallas_call x16 -> x12, Pallas kernels: 16.6 us -> 12.6 us  [call(): pl.pallas_call(lambda *refs: kernel(*refs[:len(args)], *refs[len(args) +...]
    ppermute x9, waiting for transfers between devices: 6.26 us -> 2.25 us  [other_core(): lax.ppermute(value, 'col', [(device, device ^ 1) for device in range(coun...]
    ppermute x15 -> x18, starting transfers between devices: 29.4 us -> 31 us  [fetch(): return lax.ppermute(value, 'col', pairs)]
    ppermute x15 -> x18, waiting for transfers between devices: 27.3 us -> 27.6 us  [fetch(): return lax.ppermute(value, 'col', pairs)]
  transfers between devices with their start and end apart: 24 -> 28, of which waited for: 12 -> 16; matrix products, arithmetic and copies ran while one was open for 0% -> 1% of each run, Pallas kernels for 6% -> 3%
where the time goes in v3:
time: 167 us; the launch traced here: 166 us
  blocking collectives  59.2 us (35%)
  waiting for transfers between devices  46 us (28%)
  starting transfers between devices  44.4 us (27%)
  Pallas kernels  12.6 us (8%)
  local copies, waits for them, and re-layouts  2.84 us (2%)
    all_to_all x4, blocking collectives, exchange_row(): return lax.all_to_all(value, 'row', 0, 0)  59.2 us
    ppermute x18, starting transfers between devices, fetch(): return lax.ppermute(value, 'col', pairs)  31 us
    ppermute x18, waiting for transfers between devices, fetch(): return lax.ppermute(value, 'col', pairs)  27.6 us
    all_to_all x1, waiting for transfers between devices, per_device(): chips = lax.all_to_all(copies, 'col', 0, 0, axis_index_groups=SAME_CORE)  16.2 us
    pallas_call x12, Pallas kernels, call(): pl.pallas_call(lambda *refs: kernel(*refs[:len(args)], *refs[len(args) +...  12.6 us
    all_to_all x1, starting transfers between devices, per_device(): chips = lax.all_to_all(copies, 'col', 0, 0, axis_index_groups=SAME_CORE)  11.6 us
  transfers between devices with their start and end apart: 28, of which 16 were waited for; matrix products, arithmetic and copies ran while one was open for 1% of the time, Pallas kernels for 3%

profile of v3, /device:TPU:6, one launch (start us, length us, event | category | flops | bytes accessed | tf_op | source)
XLA Modules:
  0.0 165.7 jit_solution(3981060208027844465)
XLA Ops:
  1.3 1.6 broadcast_in_dim.2
  3.0 11.6 %all-to-all-start = ((bf16[16,16,1024]{2,1,0:T(8,128)(2,1)}), bf16[16,16,1024]{2,1,0:T(8,128)(2,1)S(1)}, u32[]{:S(2)}, u32[]{:S(2)}) async-start(bf16[16,16,1024]{2,1,0:T(8,128)(2,1)} %broadcast_in_dim.2), calls=%async_computation | async-start | bytes 1048576 | tf_op jit(solution)/shard_map/all_to_all | solution.py:304
  14.6 1.2 collective-permute-done.refs_1_
  15.8 16.2 %all-to-all-done.refs_2_ = bf16[16,16,1024]{2,1,0:T(8,128)(2,1)S(1)} async-done(((bf16[16,16,1024]{2,1,0:T(8,128)(2,1)}), bf16[16,16,1024]{2,1,0:T(8,128)(2,1)S(1)}, u32[]{:S(2)}, u32[]{:S(2)}) %all-to-all-start) | async-done | bytes 524320 | tf_op jit(solution)/shard_map/all_to_all | solution.py:304
  32.0 1.2 copy-done.1
  33.2 3.0 %shard_map.109 = (bf16[1024,512]{1,0:T(8,128)(2,1)S(1)}, bf16[1024,512]{1,0:T(8,128)(2,1)S(1)}, bf16[1024,512]{1,0:T(8,128)(2,1)S(1)}, bf16[1024,512]{1,0:T(8,12...) custom-call(s32[3,4,8]{2,1,0:T(4,128)S(1)} %bitcast.15, ...), custom_call_target="tpu_custom_call" | custom-call | flops 1073741824 | bytes 10486528 | tf_op jit(solution)/shard_map/pallas_call | solution.py:26
  36.2 18.5 %all_to_all.25.refs_0_ = bf16[8,32,2048]{2,1,0:T(8,128)(2,1)S(1)} all-to-all(bf16[8,32,2048]{2,1,0:T(8,128)(2,1)S(1)} %bitcast.12), channel_id=1, replica_groups=mesh['row'=8,'col'=32] {'row'}, dimensions={0} | all-to-all | bytes 2097152 | tf_op jit(solution)/shard_map/all_to_all | solution.py:279
  54.8 11.3 %all_to_all.26 = bf16[8,32,1024]{2,1,0:T(8,128)(2,1)S(1)} all-to-all(bf16[8,32,1024]{2,1,0:T(8,128)(2,1)S(1)} %get-tuple-element.44), channel_id=1, replica_groups=mesh['row'=8,'col'=32] {'row'}, dimensions={0} | all-to-all | bytes 1048576 | tf_op jit(solution)/shard_map/all_to_all | solution.py:279
  66.1 1.6 shard_map.111
  67.7 2.5 %collective-permute-start.4 = (bf16[64,1024]{1,0:T(8,128)(2,1)S(1)}, bf16[64,1024]{1,0:T(8,128)(2,1)S(1)}, u32[]{:S(2)}, u32[]{:S(2)}) collective-permute-start(bf16[64,1024]{1,0:T(8,128)(2,1)S(1)} %get-tuple-element.46), channel_id=1, source_target_pairs={{24,0},{25,1},{26,2},{27,3},{28,4},{29,5},{30,6},{31,7},{0,8},{1,9... | collective-permute-start | bytes 393224 | tf_op jit(solution)/shard_map/ppermute | solution.py:254
  71.1 3.0 %collective-permute-done.4.refs_1_ = bf16[64,1024]{1,0:T(8,128)(2,1)S(1)} collective-permute-done((bf16[64,1024]{1,0:T(8,128)(2,1)S(1)}, bf16[64,1024]{1,0:T(8,128)(2,1)S(1)}, u32[]{:S(2)}, u32[]{:S(2)}) %collective-permute-start.4) | collective-permute-done | bytes 131104 | tf_op jit(solution)/shard_map/ppermute | solution.py:254
  74.1 2.7 %collective-permute-done.5.refs_2_ = bf16[64,1024]{1,0:T(8,128)(2,1)S(1)} collective-permute-done((bf16[64,1024]{1,0:T(8,128)(2,1)S(1)}, bf16[64,1024]{1,0:T(8,128)(2,1)S(1)}, u32[]{:S(2)}, u32[]{:S(2)}) %collective-permute-start.5) | collective-permute-done | bytes 131104 | tf_op jit(solution)/shard_map/ppermute | solution.py:254
  76.7 1.2 collective-permute-done.6.refs_3_
  78.0 3.2 %collective-permute-start.7 = (bf16[16,1024]{1,0:T(8,128)(2,1)S(1)}, bf16[16,1024]{1,0:T(8,128)(2,1)S(1)}, u32[]{:S(2)}, u32[]{:S(2)}) collective-permute-start(bf16[16,1024]{1,0:T(8,128)(2,1)S(1)} %get-tuple-element.50), channel_id=1, source_target_pairs={{6,0},{7,1},{0,2},{1,3},{2,4},{3,5},{4,6},{5,7},{14,8},{15,9},{8,1... | collective-permute-start | bytes 98312 | tf_op jit(solution)/shard_map/ppermute | solution.py:254
  81.6 3.3 %collective-permute-start.9 = (bf16[16,1024]{1,0:T(8,128)(2,1)S(1)}, bf16[16,1024]{1,0:T(8,128)(2,1)S(1)}, u32[]{:S(2)}, u32[]{:S(2)}) collective-permute-start(bf16[16,1024]{1,0:T(8,128)(2,1)S(1)} %get-tuple-element.52), channel_id=1, source_target_pairs={{2,0},{3,1},{4,2},{5,3},{6,4},{7,5},{0,6},{1,7},{10,8},{11,9},{12,... | collective-permute-start | bytes 98312 | tf_op jit(solution)/shard_map/ppermute | solution.py:254
  84.9 4.1 %collective-permute-done.8.refs_3_ = bf16[16,1024]{1,0:T(8,128)(2,1)S(1)} collective-permute-done((bf16[16,1024]{1,0:T(8,128)(2,1)S(1)}, bf16[16,1024]{1,0:T(8,128)(2,1)S(1)}, u32[]{:S(2)}, u32[]{:S(2)}) %collective-permute-start.8) | collective-permute-done | bytes 32800 | tf_op jit(solution)/shard_map/ppermute | solution.py:254
  89.7 2.7 %collective-permute-start.11 = (bf16[16,1024]{1,0:T(8,128)(2,1)S(1)}, bf16[16,1024]{1,0:T(8,128)(2,1)S(1)}, u32[]{:S(2)}, u32[]{:S(2)}) collective-permute-start(bf16[16,1024]{1,0:T(8,128)(2,1)S(1)} %get-tuple-element.55.refs_0_), channel_id=1, source_target_pairs={{2,0},{3,1},{4,2},{5,3},{6,4},{7,5},{0,6},{1,7},{10,8},{11,9},{12,... | collective-permute-start | bytes 98312 | tf_op jit(solution)/shard_map/ppermute | solution.py:254
  92.4 2.9 %collective-permute-start.12 = (bf16[16,1024]{1,0:T(8,128)(2,1)S(1)}, bf16[16,1024]{1,0:T(8,128)(2,1)S(1)}, u32[]{:S(2)}, u32[]{:S(2)}) collective-permute-start(bf16[16,1024]{1,0:T(8,128)(2,1)S(1)} %get-tuple-element.55.refs_0_), channel_id=1, source_target_pairs={{4,0},{5,1},{6,2},{7,3},{0,4},{1,5},{2,6},{3,7},{12,8},{13,9},{14,... | collective-permute-start | bytes 98312 | tf_op jit(solution)/shard_map/ppermute | solution.py:254
  95.9 4.3 %collective-permute-done.12.refs_2_ = bf16[16,1024]{1,0:T(8,128)(2,1)S(1)} collective-permute-done((bf16[16,1024]{1,0:T(8,128)(2,1)S(1)}, bf16[16,1024]{1,0:T(8,128)(2,1)S(1)}, u32[]{:S(2)}, u32[]{:S(2)}) %collective-permute-start.12) | collective-permute-done | bytes 32800 | tf_op jit(solution)/shard_map/ppermute | solution.py:254
  101.6 2.3 %collective-permute-start.15 = (bf16[64,1024]{1,0:T(8,128)(2,1)S(1)}, bf16[64,1024]{1,0:T(8,128)(2,1)S(1)}, u32[]{:S(2)}, u32[]{:S(2)}) collective-permute-start(bf16[64,1024]{1,0:T(8,128)(2,1)S(1)} %shard_map.114.refs_0_), channel_id=1, source_target_pairs={{16,0},{17,1},{18,2},{19,3},{20,4},{21,5},{22,6},{23,7},{24,8},{25... | collective-permute-start | bytes 393224 | tf_op jit(solution)/shard_map/ppermute | solution.py:254
  105.0 4.2 %collective-permute-done.14.refs_1_ = bf16[64,1024]{1,0:T(8,128)(2,1)S(1)} collective-permute-done((bf16[64,1024]{1,0:T(8,128)(2,1)S(1)}, bf16[64,1024]{1,0:T(8,128)(2,1)S(1)}, u32[]{:S(2)}, u32[]{:S(2)}) %collective-permute-start.14) | collective-permute-done | bytes 131104 | tf_op jit(solution)/shard_map/ppermute | solution.py:254
  110.8 14.5 %all_to_all.27.refs_0_ = bf16[8,32,1152]{2,1,0:T(8,128)(2,1)S(1)} all-to-all(bf16[8,32,1152]{2,1,0:T(8,128)(2,1)S(1)} %bitcast.13), channel_id=1, replica_groups=mesh['row'=8,'col'=32] {'row'}, dimensions={0} | all-to-all | bytes 1179648 | tf_op jit(solution)/shard_map/all_to_all | solution.py:279
  125.5 15.0 %all_to_all.28 = bf16[8,32,2048]{2,1,0:T(8,128)(2,1)S(1)} all-to-all(bf16[8,32,2048]{2,1,0:T(8,128)(2,1)S(1)} %get-tuple-element.60), channel_id=1, replica_groups=mesh['row'=8,'col'=32] {'row'}, dimensions={0} | all-to-all | bytes 2097152 | tf_op jit(solution)/shard_map/all_to_all | solution.py:279
  141.5 1.3 shard_map.118
  143.9 2.3 %collective-permute-start.21 = (bf16[64,1024]{1,0:T(8,128)(2,1)S(1)}, bf16[64,1024]{1,0:T(8,128)(2,1)S(1)}, u32[]{:S(2)}, u32[]{:S(2)}) collective-permute-start(bf16[64,1024]{1,0:T(8,128)(2,1)S(1)} %get-tuple-element.72), channel_id=1, source_target_pairs={{24,0},{25,1},{26,2},{27,3},{28,4},{29,5},{30,6},{31,7},{0,8},{1,9... | collective-permute-start | bytes 393224 | tf_op jit(solution)/shard_map/ppermute | solution.py:254
  146.6 1.3 collective-permute-start.23
  147.9 4.2 %shard_map.117 = (bf16[1024,512]{1,0:T(8,128)(2,1)}, bf16[1024,512]{1,0:T(8,128)(2,1)}, bf16[512,1024]{1,0:T(8,128)(2,1)}, f32[1,1]{1,0:T(1,128)}, f32[8,128]{1,0:T(8,128)S(1)}) custom-call(s32[3,4,8]{2,1,0:T(4,128)S(1)} %bitcast.17, bf16[256,1024]{1,0:T(8,128)(2,1)S(1)} %get-tuple-element.54.refs_1_, bf16[256,1024]{1,0:T(8,128)(2,1)S(1)} %collective-permute-done.10.refs_2_, ...), custom_call_target="tpu_custom_call" | custom-call | flops 1610612736 | bytes 8401284 | tf_op jit(solution)/shard_map/pallas_call | solution.py:26
  152.1 2.0 %collective-permute-done.22.refs_2_ = bf16[64,1024]{1,0:T(8,128)(2,1)S(1)} collective-permute-done((bf16[64,1024]{1,0:T(8,128)(2,1)S(1)}, bf16[64,1024]{1,0:T(8,128)(2,1)S(1)}, u32[]{:S(2)}, u32[]{:S(2)}) %collective-permute-start.22) | collective-permute-done | bytes 131104 | tf_op jit(solution)/shard_map/ppermute | solution.py:254
  154.1 1.5 collective-permute-done.23.refs_3_
  155.8 3.0 %collective-permute-start.25 = (bf16[16,1024]{1,0:T(8,128)(2,1)S(1)}, bf16[16,1024]{1,0:T(8,128)(2,1)S(1)}, u32[]{:S(2)}, u32[]{:S(2)}) collective-permute-start(bf16[16,1024]{1,0:T(8,128)(2,1)S(1)} %get-tuple-element.78), channel_id=1, source_target_pairs={{4,0},{5,1},{6,2},{7,3},{0,4},{1,5},{2,6},{3,7},{12,8},{13,9},{14,... | collective-permute-start | bytes 98312 | tf_op jit(solution)/shard_map/ppermute | solution.py:254
  158.8 3.8 %collective-permute-start.26 = (bf16[16,1024]{1,0:T(8,128)(2,1)S(1)}, bf16[16,1024]{1,0:T(8,128)(2,1)S(1)}, u32[]{:S(2)}, u32[]{:S(2)}) collective-permute-start(bf16[16,1024]{1,0:T(8,128)(2,1)S(1)} %get-tuple-element.79), channel_id=1, source_target_pairs={{2,0},{3,1},{4,2},{5,3},{6,4},{7,5},{0,6},{1,7},{10,8},{11,9},{12,... | collective-permute-start | bytes 98312 | tf_op jit(solution)/shard_map/ppermute | solution.py:254
  163.7 1.4 collective-permute-done.26.refs_3_
  (51 shorter events, 12.2 us)
Async XLA Ops:
  0.6 31.3 %copy-start = (bf16[1024,512]{1,0:T(8,128)(2,1)S(1)}, bf16[1024,512]{1,0:T(8,128)(2,1)}, u32[]{:S(2)}) copy-start(bf16[1024,512]{1,0:T(8,128)(2,1)} %refs_3_.2) | copy-start | bytes 3145732
  0.6 31.3 %collective-permute-start.3 = (bf16[512,1024]{1,0:T(8,128)(2,1)}, bf16[512,1024]{1,0:T(8,128)(2,1)S(1)}, u32[]{:S(2)}, u32[]{:S(2)}) collective-permute-start(bf16[512,1024]{1,0:T(8,128)(2,1)} %refs_3_.3), channel_id=1, source_target_pairs={{0,1},{1,0},{2,3},{3,2},{4,5},{5,4},{6,7},{7,6},{8,9},{9,8},{10,11... | collective-permute-start | bytes 3145736 | tf_op jit(solution)/shard_map/ppermute | solution.py:244
  0.7 31.2 %collective-permute-start.1 = (bf16[1024,512]{1,0:T(8,128)(2,1)}, bf16[1024,512]{1,0:T(8,128)(2,1)}, u32[]{:S(2)}, u32[]{:S(2)}) collective-permute-start(bf16[1024,512]{1,0:T(8,128)(2,1)} %refs_3_.2), channel_id=1, source_target_pairs={{0,1},{1,0},{2,3},{3,2},{4,5},{5,4},{6,7},{7,6},{8,9},{9,8},{10,11... | collective-permute-start | bytes 3145736 | tf_op jit(solution)/shard_map/ppermute | solution.py:244
  1.2 30.7 %collective-permute-start.2 = (bf16[1024,512]{1,0:T(8,128)(2,1)}, bf16[1024,512]{1,0:T(8,128)(2,1)}, u32[]{:S(2)}, u32[]{:S(2)}) collective-permute-start(bf16[1024,512]{1,0:T(8,128)(2,1)} %refs_5_.1), channel_id=1, source_target_pairs={{0,1},{1,0},{2,3},{3,2},{4,5},{5,4},{6,7},{7,6},{8,9},{9,8},{10,11... | collective-permute-start | bytes 3145736 | tf_op jit(solution)/shard_map/ppermute | solution.py:244
  3.0 11.6 %copy-start.4 = (s32[3,8,4]{1,2,0:T(4,128)S(1)}, s32[3,8,4]{1,2,0:T(4,128)}, u32[]{:S(2)}) copy-start(s32[3,8,4]{1,2,0:T(4,128)} %param.11) | copy-start | bytes 1156
  3.0 29.0 %all-to-all-start = ((bf16[16,16,1024]{2,1,0:T(8,128)(2,1)}), bf16[16,16,1024]{2,1,0:T(8,128)(2,1)S(1)}, u32[]{:S(2)}, u32[]{:S(2)}) async-start(bf16[16,16,1024]{2,1,0:T(8,128)(2,1)} %broadcast_in_dim.2), calls=%async_computation | async-start | bytes 1048576 | tf_op jit(solution)/shard_map/all_to_all | solution.py:304
  14.5 1.3 collective-permute-start
  54.7 11.4 %copy-start.2 = (bf16[512,1024]{1,0:T(8,128)(2,1)S(1)}, bf16[512,1024]{1,0:T(8,128)(2,1)}, u32[]{:S(2)}) copy-start(bf16[512,1024]{1,0:T(8,128)(2,1)} %refs_3_.3) | copy-start | bytes 3145732
  67.7 6.4 %collective-permute-start.4 = (bf16[64,1024]{1,0:T(8,128)(2,1)S(1)}, bf16[64,1024]{1,0:T(8,128)(2,1)S(1)}, u32[]{:S(2)}, u32[]{:S(2)}) collective-permute-start(bf16[64,1024]{1,0:T(8,128)(2,1)S(1)} %get-tuple-element.46), channel_id=1, source_target_pairs={{24,0},{25,1},{26,2},{27,3},{28,4},{29,5},{30,6},{31,7},{0,8},{1,9... | collective-permute-start | bytes 393224 | tf_op jit(solution)/shard_map/ppermute | solution.py:254
  70.1 6.6 %collective-permute-start.5 = (bf16[64,1024]{1,0:T(8,128)(2,1)S(1)}, bf16[64,1024]{1,0:T(8,128)(2,1)S(1)}, u32[]{:S(2)}, u32[]{:S(2)}) collective-permute-start(bf16[64,1024]{1,0:T(8,128)(2,1)S(1)} %get-tuple-element.47), channel_id=1, source_target_pairs={{16,0},{17,1},{18,2},{19,3},{20,4},{21,5},{22,6},{23,7},{24,8},{25... | collective-permute-start | bytes 393224 | tf_op jit(solution)/shard_map/ppermute | solution.py:254
  70.4 7.6 %collective-permute-start.6 = (bf16[64,1024]{1,0:T(8,128)(2,1)S(1)}, bf16[64,1024]{1,0:T(8,128)(2,1)S(1)}, u32[]{:S(2)}, u32[]{:S(2)}) collective-permute-start(bf16[64,1024]{1,0:T(8,128)(2,1)S(1)} %get-tuple-element.48), channel_id=1, source_target_pairs={{8,0},{9,1},{10,2},{11,3},{12,4},{13,5},{14,6},{15,7},{16,8},{17,9... | collective-permute-start | bytes 393224 | tf_op jit(solution)/shard_map/ppermute | solution.py:254
  78.0 11.1 %copy-start.3 = (bf16[16,1024]{1,0:T(8,128)(2,1)S(1)}, bf16[16,1024]{1,0:T(8,128)(2,1)}, u32[]{:S(2)}) copy-start(bf16[16,1024]{1,0:T(8,128)(2,1)} %refs_0_.1) | copy-start | bytes 98308
  78.0 6.9 %collective-permute-start.7 = (bf16[16,1024]{1,0:T(8,128)(2,1)S(1)}, bf16[16,1024]{1,0:T(8,128)(2,1)S(1)}, u32[]{:S(2)}, u32[]{:S(2)}) collective-permute-start(bf16[16,1024]{1,0:T(8,128)(2,1)S(1)} %get-tuple-element.50), channel_id=1, source_target_pairs={{6,0},{7,1},{0,2},{1,3},{2,4},{3,5},{4,6},{5,7},{14,8},{15,9},{8,1... | collective-permute-start | bytes 98312 | tf_op jit(solution)/shard_map/ppermute | solution.py:254
  81.2 7.8 %collective-permute-start.8 = (bf16[16,1024]{1,0:T(8,128)(2,1)S(1)}, bf16[16,1024]{1,0:T(8,128)(2,1)S(1)}, u32[]{:S(2)}, u32[]{:S(2)}) collective-permute-start(bf16[16,1024]{1,0:T(8,128)(2,1)S(1)} %get-tuple-element.51), channel_id=1, source_target_pairs={{4,0},{5,1},{6,2},{7,3},{0,4},{1,5},{2,6},{3,7},{12,8},{13,9},{14,... | collective-permute-start | bytes 98312 | tf_op jit(solution)/shard_map/ppermute | solution.py:254
  81.6 7.5 %collective-permute-start.9 = (bf16[16,1024]{1,0:T(8,128)(2,1)S(1)}, bf16[16,1024]{1,0:T(8,128)(2,1)S(1)}, u32[]{:S(2)}, u32[]{:S(2)}) collective-permute-start(bf16[16,1024]{1,0:T(8,128)(2,1)S(1)} %get-tuple-element.52), channel_id=1, source_target_pairs={{2,0},{3,1},{4,2},{5,3},{6,4},{7,5},{0,6},{1,7},{10,8},{11,9},{12,... | collective-permute-start | bytes 98312 | tf_op jit(solution)/shard_map/ppermute | solution.py:254
  89.7 6.2 %collective-permute-start.11 = (bf16[16,1024]{1,0:T(8,128)(2,1)S(1)}, bf16[16,1024]{1,0:T(8,128)(2,1)S(1)}, u32[]{:S(2)}, u32[]{:S(2)}) collective-permute-start(bf16[16,1024]{1,0:T(8,128)(2,1)S(1)} %get-tuple-element.55.refs_0_), channel_id=1, source_target_pairs={{2,0},{3,1},{4,2},{5,3},{6,4},{7,5},{0,6},{1,7},{10,8},{11,9},{12,... | collective-permute-start | bytes 98312 | tf_op jit(solution)/shard_map/ppermute | solution.py:254
  92.4 7.8 %collective-permute-start.12 = (bf16[16,1024]{1,0:T(8,128)(2,1)S(1)}, bf16[16,1024]{1,0:T(8,128)(2,1)S(1)}, u32[]{:S(2)}, u32[]{:S(2)}) collective-permute-start(bf16[16,1024]{1,0:T(8,128)(2,1)S(1)} %get-tuple-element.55.refs_0_), channel_id=1, source_target_pairs={{4,0},{5,1},{6,2},{7,3},{0,4},{1,5},{2,6},{3,7},{12,8},{13,9},{14,... | collective-permute-start | bytes 98312 | tf_op jit(solution)/shard_map/ppermute | solution.py:254
  95.3 6.0 %collective-permute-start.13 = (bf16[16,1024]{1,0:T(8,128)(2,1)S(1)}, bf16[16,1024]{1,0:T(8,128)(2,1)S(1)}, u32[]{:S(2)}, u32[]{:S(2)}) collective-permute-start(bf16[16,1024]{1,0:T(8,128)(2,1)S(1)} %get-tuple-element.55.refs_0_), channel_id=1, source_target_pairs={{6,0},{7,1},{0,2},{1,3},{2,4},{3,5},{4,6},{5,7},{14,8},{15,9},{8,1... | collective-permute-start | bytes 98312 | tf_op jit(solution)/shard_map/ppermute | solution.py:254
  101.3 7.8 %collective-permute-start.14 = (bf16[64,1024]{1,0:T(8,128)(2,1)S(1)}, bf16[64,1024]{1,0:T(8,128)(2,1)S(1)}, u32[]{:S(2)}, u32[]{:S(2)}) collective-permute-start(bf16[64,1024]{1,0:T(8,128)(2,1)S(1)} %shard_map.114.refs_0_), channel_id=1, source_target_pairs={{8,0},{9,1},{10,2},{11,3},{12,4},{13,5},{14,6},{15,7},{16,8},{17,9... | collective-permute-start | bytes 393224 | tf_op jit(solution)/shard_map/ppermute | solution.py:254
  101.6 7.6 %collective-permute-start.15 = (bf16[64,1024]{1,0:T(8,128)(2,1)S(1)}, bf16[64,1024]{1,0:T(8,128)(2,1)S(1)}, u32[]{:S(2)}, u32[]{:S(2)}) collective-permute-start(bf16[64,1024]{1,0:T(8,128)(2,1)S(1)} %shard_map.114.refs_0_), channel_id=1, source_target_pairs={{16,0},{17,1},{18,2},{19,3},{20,4},{21,5},{22,6},{23,7},{24,8},{25... | collective-permute-start | bytes 393224 | tf_op jit(solution)/shard_map/ppermute | solution.py:254
  104.0 6.1 %collective-permute-start.16 = (bf16[64,1024]{1,0:T(8,128)(2,1)S(1)}, bf16[64,1024]{1,0:T(8,128)(2,1)S(1)}, u32[]{:S(2)}, u32[]{:S(2)}) collective-permute-start(bf16[64,1024]{1,0:T(8,128)(2,1)S(1)} %shard_map.114.refs_0_), channel_id=1, source_target_pairs={{24,0},{25,1},{26,2},{27,3},{28,4},{29,5},{30,6},{31,7},{0,8},{1,9... | collective-permute-start | bytes 393224 | tf_op jit(solution)/shard_map/ppermute | solution.py:254
  140.5 7.4 %collective-permute-start.17 = (bf16[256,2048]{1,0:T(8,128)(2,1)S(1)}, bf16[256,2048]{1,0:T(8,128)(2,1)S(1)}, u32[]{:S(2)}, u32[]{:S(2)}) collective-permute-start(bf16[256,2048]{1,0:T(8,128)(2,1)S(1)} %bitcast.6), channel_id=1, source_target_pairs={{0,1},{1,0},{2,3},{3,2},{4,5},{5,4},{6,7},{7,6},{8,9},{9,8},{10,11... | collective-permute-start | bytes 3145736 | tf_op jit(solution)/shard_map/ppermute | solution.py:244
  140.5 3.4 %collective-permute-start.10 = (bf16[256,1024]{1,0:T(8,128)(2,1)S(1)}, bf16[256,1024]{1,0:T(8,128)(2,1)S(1)}, u32[]{:S(2)}, u32[]{:S(2)}) collective-permute-start(bf16[256,1024]{1,0:T(8,128)(2,1)S(1)} %get-tuple-element.54.refs_1_), channel_id=1, source_target_pairs={{0,1},{1,0},{2,3},{3,2},{4,5},{5,4},{6,7},{7,6},{8,9},{9,8},{10,11... | collective-permute-start | bytes 1572872 | tf_op jit(solution)/shard_map/ppermute | solution.py:244
  141.0 5.2 %collective-permute-start.18 = (bf16[256,1024]{1,0:T(8,128)(2,1)S(1)}, bf16[256,1024]{1,0:T(8,128)(2,1)S(1)}, u32[]{:S(2)}, u32[]{:S(2)}) collective-permute-start(bf16[256,1024]{1,0:T(8,128)(2,1)S(1)} %bitcast.10), channel_id=1, source_target_pairs={{0,1},{1,0},{2,3},{3,2},{4,5},{5,4},{6,7},{7,6},{8,9},{9,8},{10,11... | collective-permute-start | bytes 1572872 | tf_op jit(solution)/shard_map/ppermute | solution.py:244
  141.0 5.6 %collective-permute-start.19 = (bf16[256,1024]{1,0:T(8,128)(2,1)S(1)}, bf16[256,1024]{1,0:T(8,128)(2,1)S(1)}, u32[]{:S(2)}, u32[]{:S(2)}) collective-permute-start(bf16[256,1024]{1,0:T(8,128)(2,1)S(1)} %get-tuple-element.61.refs_7_), channel_id=1, source_target_pairs={{0,1},{1,0},{2,3},{3,2},{4,5},{5,4},{6,7},{7,6},{8,9},{9,8},{10,11... | collective-permute-start | bytes 1572872 | tf_op jit(solution)/shard_map/ppermute | solution.py:244
  141.5 6.3 %collective-permute-start.20 = (f32[8,128]{1,0:T(8,128)S(1)}, f32[8,128]{1,0:T(8,128)S(1)}, u32[]{:S(2)}, u32[]{:S(2)}) collective-permute-start(f32[8,128]{1,0:T(8,128)S(1)} %get-tuple-element.62.refs_9_), channel_id=1, source_target_pairs={{0,1},{1,0},{2,3},{3,2},{4,5},{5,4},{6,7},{7,6},{8,9},{9,8},{10,11... | collective-permute-start | bytes 12296 | tf_op jit(solution)/shard_map/ppermute | solution.py:244
  143.9 8.2 %collective-permute-start.21 = (bf16[64,1024]{1,0:T(8,128)(2,1)S(1)}, bf16[64,1024]{1,0:T(8,128)(2,1)S(1)}, u32[]{:S(2)}, u32[]{:S(2)}) collective-permute-start(bf16[64,1024]{1,0:T(8,128)(2,1)S(1)} %get-tuple-element.72), channel_id=1, source_target_pairs={{24,0},{25,1},{26,2},{27,3},{28,4},{29,5},{30,6},{31,7},{0,8},{1,9... | collective-permute-start | bytes 393224 | tf_op jit(solution)/shard_map/ppermute | solution.py:254
  146.2 7.9 %collective-permute-start.22 = (bf16[64,1024]{1,0:T(8,128)(2,1)S(1)}, bf16[64,1024]{1,0:T(8,128)(2,1)S(1)}, u32[]{:S(2)}, u32[]{:S(2)}) collective-permute-start(bf16[64,1024]{1,0:T(8,128)(2,1)S(1)} %get-tuple-element.73), channel_id=1, source_target_pairs={{16,0},{17,1},{18,2},{19,3},{20,4},{21,5},{22,6},{23,7},{24,8},{25... | collective-permute-start | bytes 393224 | tf_op jit(solution)/shard_map/ppermute | solution.py:254
  146.6 9.0 %collective-permute-start.23 = (bf16[64,1024]{1,0:T(8,128)(2,1)S(1)}, bf16[64,1024]{1,0:T(8,128)(2,1)S(1)}, u32[]{:S(2)}, u32[]{:S(2)}) collective-permute-start(bf16[64,1024]{1,0:T(8,128)(2,1)S(1)} %get-tuple-element.74), channel_id=1, source_target_pairs={{8,0},{9,1},{10,2},{11,3},{12,4},{13,5},{14,6},{15,7},{16,8},{17,9... | collective-permute-start | bytes 393224 | tf_op jit(solution)/shard_map/ppermute | solution.py:254
  155.7 7.0 %collective-permute-start.24 = (bf16[16,1024]{1,0:T(8,128)(2,1)S(1)}, bf16[16,1024]{1,0:T(8,128)(2,1)S(1)}, u32[]{:S(2)}, u32[]{:S(2)}) collective-permute-start(bf16[16,1024]{1,0:T(8,128)(2,1)S(1)} %get-tuple-element.77), channel_id=1, source_target_pairs={{6,0},{7,1},{0,2},{1,3},{2,4},{3,5},{4,6},{5,7},{14,8},{15,9},{8,1... | collective-permute-start | bytes 98312 | tf_op jit(solution)/shard_map/ppermute | solution.py:254
  155.8 7.9 %collective-permute-start.25 = (bf16[16,1024]{1,0:T(8,128)(2,1)S(1)}, bf16[16,1024]{1,0:T(8,128)(2,1)S(1)}, u32[]{:S(2)}, u32[]{:S(2)}) collective-permute-start(bf16[16,1024]{1,0:T(8,128)(2,1)S(1)} %get-tuple-element.78), channel_id=1, source_target_pairs={{4,0},{5,1},{6,2},{7,3},{0,4},{1,5},{2,6},{3,7},{12,8},{13,9},{14,... | collective-permute-start | bytes 98312 | tf_op jit(solution)/shard_map/ppermute | solution.py:254
  158.8 6.2 %collective-permute-start.26 = (bf16[16,1024]{1,0:T(8,128)(2,1)S(1)}, bf16[16,1024]{1,0:T(8,128)(2,1)S(1)}, u32[]{:S(2)}, u32[]{:S(2)}) collective-permute-start(bf16[16,1024]{1,0:T(8,128)(2,1)S(1)} %get-tuple-element.79), channel_id=1, source_target_pairs={{2,0},{3,1},{4,2},{5,3},{6,4},{7,5},{0,6},{1,7},{10,8},{11,9},{12,... | collective-permute-start | bytes 98312 | tf_op jit(solution)/shard_map/ppermute | solution.py:254
  (1 other events, 1.2 us)

commit v4 on v3

--- a/solution.py
+++ b/solution.py
@@ -49,13 +49,36 @@
         joined_ref[pl.ds(part * size, size), :] = ref[...]
 
 
-def keep(mask_ref, which, ref, kept_ref):
-    for row in range(ref.shape[0] // BLK):
+def keep_kernel(mask_ref, mask_other_ref, *refs):
+    step = pl.program_id(0)
+    gate_ups_ref, downs_ref = refs[-2:]
+    for at, ref in enumerate(refs[:-2]):
+        masks, which = (mask_ref, mask_other_ref)[at % 2], at // 2
+        kept_ref = downs_ref.at[at % 2] if which == DOWN else gate_ups_ref.at[at]
         for col in range(ref.shape[1] // BLK):
-            at = (row, col) if which == DOWN else (col, row)
-            factor = mask_ref[which, at[0], at[1]].astype(jnp.float32).astype(jnp.bfloat16)
-            block = (pl.ds(row * BLK, BLK), pl.ds(col * BLK, BLK))
-            kept_ref[block] = ref[block] * factor
+            block = (step // 2, col) if which == DOWN else (col, step)
+            factor = masks[which, block[0], block[1]].astype(jnp.float32).astype(jnp.bfloat16)
+            cols = pl.ds(col * BLK, BLK)
+            kept_ref[:, cols] = ref[:, cols] * factor
+
+
+def keep(masks, weights):
+    steps = weights[0].shape[0] // BLK
+    kept = [shaped((count,) + value.shape) for count, value in ((4, weights[0]), (2, weights[-1]))]
+    return call(
+        keep_kernel,
+        kept,
+        *masks,
+        *weights,
+        in_specs=[SMEM] * 2
+        + [pl.BlockSpec((value.shape[0] // steps, value.shape[1]), lambda i: (i, 0)) for value in weights],
+        out_specs=[
+            pl.BlockSpec((value.shape[0], value.shape[1] // steps, value.shape[2]), lambda i: (0, i, 0))
+            for value in kept
+        ],
+        grid=(steps,),
+        vmem=59,
+    )
 
 
 def plain_dot(left, right):
@@ -66,18 +89,23 @@
     return lax.dot_general(left, right, (((1,), (1,)), ((), ())), preferred_element_type=jnp.float32)
 
 
-def gate_up_kernel(mask_ref, mask_other_ref, chips_ref, *refs):
-    weights, kept_refs, (out_ref, rows_ref) = refs[:4], refs[4:8], refs[8:]
+def gate_up_kernel(chips_ref, weights_ref, out_ref, rows_ref, scratch, sems):
+    copies = [
+        pltpu.make_async_copy(weights_ref.at[which], scratch.at[which], sems.at[which])
+        for which in range(weights_ref.shape[0])
+    ]
+    for copy in copies:
+        copy.start()
     chip = lax.axis_index("col") // CORES
     size = chips_ref.shape[1]
     for part in range(CHIPS):
         x = lax.rem(chip // Z + part // Z, X)
         z = lax.rem(chip + part % Z, Z)
         rows_ref[pl.ds(part * size, size), :] = chips_ref[x * Z + z]
-    for which, (ref, kept_ref) in enumerate(zip(weights, kept_refs)):
-        units = ref.shape[1]
-        keep((mask_ref, mask_other_ref)[which % 2], which // 2, ref, kept_ref)
-        value = plain_dot(rows_ref[...], kept_ref[...])
+    for which, copy in enumerate(copies):
+        units = scratch.shape[2]
+        copy.wait()
+        value = plain_dot(rows_ref[...], scratch[which])
         out_ref[:, pl.ds(which * units, units)] = value.astype(out_ref.dtype)
 
 
@@ -87,21 +115,19 @@
         ref[:, cols] = value[part * size : (part + 1) * size].astype(ref.dtype)
 
 
-def output_kernel(mask_ref, mask_other_ref, hidden_ref, down_ref, down_other_ref, kept_ref, kept_other_ref, *out_refs):
-    units, width = down_ref.shape
-    keep(mask_ref, DOWN, down_ref, kept_ref)
-    keep(mask_other_ref, DOWN, down_other_ref, kept_other_ref)
+def output_kernel(hidden_ref, downs_ref, *out_refs):
+    _, units, width = downs_ref.shape
     for at in range(0, width, TILE):
         cols = pl.ds(at, TILE)
-        value = plain_dot(hidden_ref[:, :units], kept_ref[:, cols])
-        value = value + plain_dot(hidden_ref[:, units:], kept_other_ref[:, cols])
+        value = plain_dot(hidden_ref[:, :units], downs_ref[0, :, cols])
+        value = value + plain_dot(hidden_ref[:, units:], downs_ref[1, :, cols])
         put_slabs(out_refs, cols, value)
 
 
 def grad_hidden_kernel(*refs):
-    slabs, (down_ref, down_other_ref, out_ref, grad_ref) = refs[:X], refs[X:]
+    slabs, (downs_ref, out_ref, grad_ref) = refs[:X], refs[X:]
     join_kernel(*slabs, grad_ref)
-    units = down_ref.shape[0]
+    units = downs_ref.shape[1]
     squares = jnp.sum(jnp.square(grad_ref[...].astype(jnp.float32)), axis=0, keepdims=True)
     squares = jnp.sum(squares, axis=1, keepdims=True)
     lane = lax.broadcasted_iota(jnp.int32, (out_ref.shape[0], BLK), 1)
@@ -111,26 +137,25 @@
         terms = jnp.where(lane == which, term, terms)
         squares = squares - term
     out_ref[:, pl.ds(2 * units, BLK)] = terms.astype(out_ref.dtype)
-    for which, ref in enumerate((down_ref, down_other_ref)):
-        value = other_turned_dot(grad_ref[...], ref[...])
+    for which in range(2):
+        value = other_turned_dot(grad_ref[...], downs_ref[which])
         out_ref[:, pl.ds(which * units, units)] = value.astype(out_ref.dtype)
 
 
-def grad_in_kernel(acts_ref, *refs):
-    weights, out_refs = refs[:-X], refs[-X:]
-    width, units = weights[0].shape
+def grad_in_kernel(acts_ref, weights_ref, *out_refs):
+    count, width, units = weights_ref.shape
     for at in range(0, width, TILE):
         value = None
-        for which, ref in enumerate(weights):
-            term = other_turned_dot(acts_ref[:, pl.ds(which * units, units)], ref[pl.ds(at, TILE), :])
+        for which in range(count):
+            weight = weights_ref[which, pl.ds(at, TILE), :]
+            term = other_turned_dot(acts_ref[:, pl.ds(which * units, units)], weight)
             value = term if value is None else value + term
         put_slabs(out_refs, pl.ds(at, TILE), value)
 
 
-def multiply(kernel, shapes, left, weights, masks=(), after=()):
+def multiply(kernel, shapes, left, weights, after=()):
     flops = 2 * sum(part.size // part.shape[-1] for part in left) * sum(weight.size for weight in weights)
-    specs = [SMEM] * len(masks) + [VMEM] * (len(left) + len(weights))
-    return call(kernel, shapes, *masks, *left, *weights, flops=flops, vmem=16, in_specs=specs, after=after)
+    return call(kernel, shapes, *left, *weights, flops=flops, vmem=16, after=after)
 
 
 def summed(parts):
@@ -302,13 +327,16 @@
     )
     copies = jnp.broadcast_to(inputs[None], (CHIPS, tokens, width))
     chips = lax.all_to_all(copies, "col", 0, 0, axis_index_groups=SAME_CORE)
-    *gate_ups, partial, rows = multiply(
+    gate_ups, downs = keep(masks, gates + ups + downs)
+    partial, rows = call(
         gate_up_kernel,
-        (wide,) * 4 + (shaped((half, 4 * units)), shaped((half, width))),
-        [chips],
-        gates + ups,
-        masks,
-        downs[1:],
+        (shaped((half, 4 * units)), shaped((half, width))),
+        chips,
+        gate_ups,
+        in_specs=[VMEM, ANY],
+        scratch_shapes=[pltpu.VMEM(gate_ups.shape, gate_ups.dtype), pltpu.SemaphoreType.DMA((4,))],
+        flops=8 * half * width * units,
+        vmem=60,
     )
     both, copies = call(
         hidden_kernel,
@@ -316,15 +344,13 @@
         exchange_row(split(partial, ROWS)),
     )
     hidden = flat(exchange_row(copies))
-    *downs, first, second, third, fourth = multiply(
-        output_kernel, (tall,) * 2 + (slab,) * X, [hidden], downs, masks
-    )
-    slabs = spread_x([first, second, third, fourth])
+    slabs = spread_x(multiply(output_kernel, (slab,) * X, [hidden], [downs]))
+    rows_other, hidden_other = other_core(rows), other_core(hidden)
     parts = spread_z(call(sum_kernel, (piece,) * Z, *slabs))
     student, grad_out = call(functools.partial(error_kernel, scale), (piece, piece), teacher, *parts)
     slabs = gather_x(joined(gather_z(grad_out)))
     partial, grad_rows = multiply(
-        grad_hidden_kernel, (shaped((half, 2 * units + BLK)), shaped((half, width))), slabs, downs
+        grad_hidden_kernel, (shaped((half, 2 * units + BLK)), shaped((half, width))), slabs, [downs], (rows_other, hidden_other)
     )
     copies, squares = call(
         acts_kernel,
@@ -333,10 +359,8 @@
         both,
     )
     acts = flat(exchange_row(copies))
-    slabs = spread_x(multiply(grad_in_kernel, (slab,) * X, [acts], gate_ups))
-    rows_other, hidden_other, grad_rows_other, acts_other, squares_other = (
-        other_core(value) for value in (rows, hidden, grad_rows, acts, squares)
-    )
+    slabs = spread_x(multiply(grad_in_kernel, (slab,) * X, [acts], [gate_ups]))
+    grad_rows_other, acts_other, squares_other = (other_core(value) for value in (grad_rows, acts, squares))
     grad_gate, grad_up, grad_down, loss, done = call(
         weights_kernel,
         (wide, wide, tall, shaped((1, 1), jnp.float32), DONE),

time: 167 us -> 165 us (0.988)
  blocking collectives: 59.2 us -> 44.1 us
  Pallas kernels: 12.6 us -> 23.1 us
    all_to_all x4 -> x3, blocking collectives: 59.2 us -> 44.1 us  [exchange_row(): return lax.all_to_all(value, 'row', 0, 0)]
    pallas_call x12 -> x13, Pallas kernels: 12.6 us -> 23.1 us  [call(): pl.pallas_call(lambda *refs: kernel(*refs[:len(args)], *refs[len(args) +...]
    all_to_all x1, waiting for transfers between devices: 16.2 us -> 6.31 us  [per_device(): chips = lax.all_to_all(copies, 'col', 0, 0, axis_index_groups=SAME_CORE)]
    all_to_all x0 -> x1, waiting for transfers between devices: none -> 8.11 us  [exchange_row(): return lax.all_to_all(value, 'row', 0, 0)]
    ppermute x18, waiting for transfers between devices: 27.6 us -> 31.1 us  [fetch(): return lax.ppermute(value, 'col', pairs)]
    all_to_all x0 -> x1, starting transfers between devices: none -> 3.49 us  [exchange_row(): return lax.all_to_all(value, 'row', 0, 0)]
    ppermute x18, starting transfers between devices: 31 us -> 29.2 us  [fetch(): return lax.ppermute(value, 'col', pairs)]
  transfers between devices with their start and end apart: 28 -> 29, of which waited for: 16 -> 15; matrix products, arithmetic and copies ran while one was open for 1% -> 1% of each run, Pallas kernels for 3% -> 9%
where the time goes in v4:
time: 165 us; the launch traced here: 164 us
  waiting for transfers between devices  46.9 us (28%)
  starting transfers between devices  45.5 us (28%)
  blocking collectives  44.1 us (27%)
  Pallas kernels  23.1 us (14%)
  local copies, waits for them, and re-layouts  3.71 us (2%)
    all_to_all x3, blocking collectives, exchange_row(): return lax.all_to_all(value, 'row', 0, 0)  44.1 us
    ppermute x18, waiting for transfers between devices, fetch(): return lax.ppermute(value, 'col', pairs)  31.1 us
    ppermute x18, starting transfers between devices, fetch(): return lax.ppermute(value, 'col', pairs)  29.2 us
    pallas_call x13, Pallas kernels, call(): pl.pallas_call(lambda *refs: kernel(*refs[:len(args)], *refs[len(args) +...  23.1 us
    all_to_all x1, starting transfers between devices, per_device(): chips = lax.all_to_all(copies, 'col', 0, 0, axis_index_groups=SAME_CORE)  11.4 us
    all_to_all x1, waiting for transfers between devices, exchange_row(): return lax.all_to_all(value, 'row', 0, 0)  8.11 us
    all_to_all x1, waiting for transfers between devices, per_device(): chips = lax.all_to_all(copies, 'col', 0, 0, axis_index_groups=SAME_CORE)  6.31 us
    all_to_all x1, starting transfers between devices, exchange_row(): return lax.all_to_all(value, 'row', 0, 0)  3.49 us
  transfers between devices with their start and end apart: 29, of which 15 were waited for; matrix products, arithmetic and copies ran while one was open for 1% of the time, Pallas kernels for 9%

profile of v4, /device:TPU:6, one launch (start us, length us, event | category | flops | bytes accessed | tf_op | source)
XLA Modules:
  0.0 164.1 jit_solution(136018963871654488)
XLA Ops:
  1.3 1.6 broadcast_in_dim.2
  2.9 11.4 %all-to-all-start = ((bf16[16,16,1024]{2,1,0:T(8,128)(2,1)}), bf16[16,16,1024]{2,1,0:T(8,128)(2,1)S(1)}, u32[]{:S(2)}, u32[]{:S(2)}) async-start(bf16[16,16,1024]{2,1,0:T(8,128)(2,1)} %broadcast_in_dim.2), calls=%async_computation | async-start | bytes 1048576 | tf_op jit(solution)/shard_map/all_to_all | solution.py:329
  14.4 1.4 collective-permute-done.refs_1_
  17.1 8.4 %shard_map.109 = (bf16[4,1024,512]{2,1,0:T(8,128)(2,1)}, bf16[2,512,1024]{2,1,0:T(8,128)(2,1)}) custom-call(s32[3,4,8]{2,1,0:T(4,128)} %bitcast.14, s32[3,4,8]{2,1,0:T(4,128)} %copy-done.8, bf16[1024,512]{1,0:T(8,128)(2,1)} %refs_2_.1, bf16[1024,512]{1,0:T(8,128)(2,1)} %copy-done.6, bf16[1024,512]{1,0:T(8,128)(2,1)} %refs_4_.1, bf16[1024,512]{1,0:T(8,128)(2,1)} %copy-done.7, ...), custom_call_target="tpu_custom_call" | custom-call | bytes 12583680 | tf_op jit(solution)/shard_map/pallas_call | solution.py:26
  25.5 6.3 %all-to-all-done.refs_0_ = bf16[16,16,1024]{2,1,0:T(8,128)(2,1)S(1)} async-done(((bf16[16,16,1024]{2,1,0:T(8,128)(2,1)}), bf16[16,16,1024]{2,1,0:T(8,128)(2,1)S(1)}, u32[]{:S(2)}, u32[]{:S(2)}) %all-to-all-start) | async-done | bytes 524320 | tf_op jit(solution)/shard_map/all_to_all | solution.py:329
  32.6 5.2 %shard_map.110 = (bf16[256,2048]{1,0:T(8,128)(2,1)}, bf16[256,1024]{1,0:T(8,128)(2,1)}) custom-call(bf16[16,16,1024]{2,1,0:T(8,128)(2,1)} %copy-done.5, bf16[4,1024,512]{2,1,0:T(8,128)(2,1)} %get-tuple-element.39.refs_1_), custom_call_target="tpu_custom_call" | custom-call | flops 1073741824 | bytes 6291456 | tf_op jit(solution)/shard_map/pallas_call | solution.py:26
  37.8 18.7 %all_to_all.25.refs_0_ = bf16[8,32,2048]{2,1,0:T(8,128)(2,1)S(1)} all-to-all(bf16[8,32,2048]{2,1,0:T(8,128)(2,1)} %bitcast.16), channel_id=1, replica_groups=mesh['row'=8,'col'=32] {'row'}, dimensions={0} | all-to-all | bytes 2097152 | tf_op jit(solution)/shard_map/all_to_all | solution.py:304
  57.4 3.5 %all-to-all-start.2 = ((bf16[8,32,1024]{2,1,0:T(8,128)(2,1)}), bf16[8,32,1024]{2,1,0:T(8,128)(2,1)S(1)}, u32[]{:S(2)}, u32[]{:S(2)}) async-start(bf16[8,32,1024]{2,1,0:T(8,128)(2,1)} %get-tuple-element.41), calls=%async_computation.2 | async-start | bytes 1048576 | tf_op jit(solution)/shard_map/all_to_all | solution.py:304
  61.0 8.1 %all-to-all-done.2 = bf16[8,32,1024]{2,1,0:T(8,128)(2,1)S(1)} async-done(((bf16[8,32,1024]{2,1,0:T(8,128)(2,1)}), bf16[8,32,1024]{2,1,0:T(8,128)(2,1)S(1)}, u32[]{:S(2)}, u32[]{:S(2)}) %all-to-all-start.2) | async-done | bytes 524320 | tf_op jit(solution)/shard_map/all_to_all | solution.py:304
  69.8 2.5 %collective-permute-start.4 = (bf16[64,1024]{1,0:T(8,128)(2,1)S(1)}, bf16[64,1024]{1,0:T(8,128)(2,1)S(1)}, u32[]{:S(2)}, u32[]{:S(2)}) collective-permute-start(bf16[64,1024]{1,0:T(8,128)(2,1)S(1)} %get-tuple-element.44), channel_id=1, source_target_pairs={{24,0},{25,1},{26,2},{27,3},{28,4},{29,5},{30,6},{31,7},{0,8},{1,9... | collective-permute-start | bytes 393224 | tf_op jit(solution)/shard_map/ppermute | solution.py:279
  73.3 5.3 %collective-permute-done.4.refs_1_ = bf16[64,1024]{1,0:T(8,128)(2,1)S(1)} collective-permute-done((bf16[64,1024]{1,0:T(8,128)(2,1)S(1)}, bf16[64,1024]{1,0:T(8,128)(2,1)S(1)}, u32[]{:S(2)}, u32[]{:S(2)}) %collective-permute-start.4) | collective-permute-done | bytes 131104 | tf_op jit(solution)/shard_map/ppermute | solution.py:279
  78.6 1.6 collective-permute-done.5.refs_2_
  80.2 1.8 %collective-permute-done.6.refs_3_ = bf16[64,1024]{1,0:T(8,128)(2,1)S(1)} collective-permute-done((bf16[64,1024]{1,0:T(8,128)(2,1)S(1)}, bf16[64,1024]{1,0:T(8,128)(2,1)S(1)}, u32[]{:S(2)}, u32[]{:S(2)}) %collective-permute-start.6) | collective-permute-done | bytes 131104 | tf_op jit(solution)/shard_map/ppermute | solution.py:279
  82.0 2.9 %collective-permute-start.7 = (bf16[16,1024]{1,0:T(8,128)(2,1)S(1)}, bf16[16,1024]{1,0:T(8,128)(2,1)S(1)}, u32[]{:S(2)}, u32[]{:S(2)}) collective-permute-start(bf16[16,1024]{1,0:T(8,128)(2,1)S(1)} %get-tuple-element.48), channel_id=1, source_target_pairs={{6,0},{7,1},{0,2},{1,3},{2,4},{3,5},{4,6},{5,7},{14,8},{15,9},{8,1... | collective-permute-start | bytes 98312 | tf_op jit(solution)/shard_map/ppermute | solution.py:279
  85.6 3.0 %collective-permute-start.9 = (bf16[16,1024]{1,0:T(8,128)(2,1)S(1)}, bf16[16,1024]{1,0:T(8,128)(2,1)S(1)}, u32[]{:S(2)}, u32[]{:S(2)}) collective-permute-start(bf16[16,1024]{1,0:T(8,128)(2,1)S(1)} %get-tuple-element.50), channel_id=1, source_target_pairs={{2,0},{3,1},{4,2},{5,3},{6,4},{7,5},{0,6},{1,7},{10,8},{11,9},{12,... | collective-permute-start | bytes 98312 | tf_op jit(solution)/shard_map/ppermute | solution.py:279
  88.6 4.1 %collective-permute-done.8.refs_3_ = bf16[16,1024]{1,0:T(8,128)(2,1)S(1)} collective-permute-done((bf16[16,1024]{1,0:T(8,128)(2,1)S(1)}, bf16[16,1024]{1,0:T(8,128)(2,1)S(1)}, u32[]{:S(2)}, u32[]{:S(2)}) %collective-permute-start.8) | collective-permute-done | bytes 32800 | tf_op jit(solution)/shard_map/ppermute | solution.py:279
  93.4 1.9 %collective-permute-start.13 = (bf16[16,1024]{1,0:T(8,128)(2,1)S(1)}, bf16[16,1024]{1,0:T(8,128)(2,1)S(1)}, u32[]{:S(2)}, u32[]{:S(2)}) collective-permute-start(bf16[16,1024]{1,0:T(8,128)(2,1)S(1)} %get-tuple-element.53.refs_0_), channel_id=1, source_target_pairs={{6,0},{7,1},{0,2},{1,3},{2,4},{3,5},{4,6},{5,7},{14,8},{15,9},{8,1... | collective-permute-start | bytes 98312 | tf_op jit(solution)/shard_map/ppermute | solution.py:279
  95.3 2.9 %collective-permute-start.12 = (bf16[16,1024]{1,0:T(8,128)(2,1)S(1)}, bf16[16,1024]{1,0:T(8,128)(2,1)S(1)}, u32[]{:S(2)}, u32[]{:S(2)}) collective-permute-start(bf16[16,1024]{1,0:T(8,128)(2,1)S(1)} %get-tuple-element.53.refs_0_), channel_id=1, source_target_pairs={{4,0},{5,1},{6,2},{7,3},{0,4},{1,5},{2,6},{3,7},{12,8},{13,9},{14,... | collective-permute-start | bytes 98312 | tf_op jit(solution)/shard_map/ppermute | solution.py:279
  98.2 2.3 %collective-permute-start.11 = (bf16[16,1024]{1,0:T(8,128)(2,1)S(1)}, bf16[16,1024]{1,0:T(8,128)(2,1)S(1)}, u32[]{:S(2)}, u32[]{:S(2)}) collective-permute-start(bf16[16,1024]{1,0:T(8,128)(2,1)S(1)} %get-tuple-element.53.refs_0_), channel_id=1, source_target_pairs={{2,0},{3,1},{4,2},{5,3},{6,4},{7,5},{0,6},{1,7},{10,8},{11,9},{12,... | collective-permute-start | bytes 98312 | tf_op jit(solution)/shard_map/ppermute | solution.py:279
  100.5 2.6 %collective-permute-done.12.refs_2_ = bf16[16,1024]{1,0:T(8,128)(2,1)S(1)} collective-permute-done((bf16[16,1024]{1,0:T(8,128)(2,1)S(1)}, bf16[16,1024]{1,0:T(8,128)(2,1)S(1)}, u32[]{:S(2)}, u32[]{:S(2)}) %collective-permute-start.12) | collective-permute-done | bytes 32800 | tf_op jit(solution)/shard_map/ppermute | solution.py:279
  105.9 2.7 %collective-permute-done.16.refs_3_ = bf16[64,1024]{1,0:T(8,128)(2,1)S(1)} collective-permute-done((bf16[64,1024]{1,0:T(8,128)(2,1)S(1)}, bf16[64,1024]{1,0:T(8,128)(2,1)S(1)}, u32[]{:S(2)}, u32[]{:S(2)}) %collective-permute-start.16) | collective-permute-done | bytes 131104 | tf_op jit(solution)/shard_map/ppermute | solution.py:279
  108.6 2.5 %collective-permute-done.15.refs_2_ = bf16[64,1024]{1,0:T(8,128)(2,1)S(1)} collective-permute-done((bf16[64,1024]{1,0:T(8,128)(2,1)S(1)}, bf16[64,1024]{1,0:T(8,128)(2,1)S(1)}, u32[]{:S(2)}, u32[]{:S(2)}) %collective-permute-start.15) | collective-permute-done | bytes 131104 | tf_op jit(solution)/shard_map/ppermute | solution.py:279
  113.2 11.6 %all_to_all.26.refs_0_ = bf16[8,32,1152]{2,1,0:T(8,128)(2,1)S(1)} all-to-all(bf16[8,32,1152]{2,1,0:T(8,128)(2,1)S(1)} %bitcast.12), channel_id=1, replica_groups=mesh['row'=8,'col'=32] {'row'}, dimensions={0} | all-to-all | bytes 1179648 | tf_op jit(solution)/shard_map/all_to_all | solution.py:304
  125.0 13.9 %all_to_all.27 = bf16[8,32,2048]{2,1,0:T(8,128)(2,1)S(1)} all-to-all(bf16[8,32,2048]{2,1,0:T(8,128)(2,1)S(1)} %get-tuple-element.56), channel_id=1, replica_groups=mesh['row'=8,'col'=32] {'row'}, dimensions={0} | all-to-all | bytes 2097152 | tf_op jit(solution)/shard_map/all_to_all | solution.py:304
  141.7 1.5 collective-permute-start.22
  143.2 4.2 %shard_map.118 = (bf16[1024,512]{1,0:T(8,128)(2,1)}, bf16[1024,512]{1,0:T(8,128)(2,1)}, bf16[512,1024]{1,0:T(8,128)(2,1)}, f32[1,1]{1,0:T(1,128)}, f32[8,128]{1,0:T(8,128)S(1)}) custom-call(s32[3,4,8]{2,1,0:T(4,128)S(1)} %bitcast.15, bf16[256,1024]{1,0:T(8,128)(2,1)S(1)} %copy-done.4, bf16[256,1024]{1,0:T(8,128)(2,1)S(1)} %collective-permute-done.10.refs_5_.refs_2_, ...), custom_call_target="tpu_custom_call" | custom-call | flops 1610612736 | bytes 8401284 | tf_op jit(solution)/shard_map/pallas_call | solution.py:26
  147.4 2.1 %collective-permute-done.22.refs_2_ = bf16[64,1024]{1,0:T(8,128)(2,1)S(1)} collective-permute-done((bf16[64,1024]{1,0:T(8,128)(2,1)S(1)}, bf16[64,1024]{1,0:T(8,128)(2,1)S(1)}, u32[]{:S(2)}, u32[]{:S(2)}) %collective-permute-start.22) | collective-permute-done | bytes 131104 | tf_op jit(solution)/shard_map/ppermute | solution.py:279
  149.5 2.1 %collective-permute-done.23.refs_3_ = bf16[64,1024]{1,0:T(8,128)(2,1)S(1)} collective-permute-done((bf16[64,1024]{1,0:T(8,128)(2,1)S(1)}, bf16[64,1024]{1,0:T(8,128)(2,1)S(1)}, u32[]{:S(2)}, u32[]{:S(2)}) %collective-permute-start.23) | collective-permute-done | bytes 131104 | tf_op jit(solution)/shard_map/ppermute | solution.py:279
  151.7 3.7 %collective-permute-start.24 = (bf16[16,1024]{1,0:T(8,128)(2,1)S(1)}, bf16[16,1024]{1,0:T(8,128)(2,1)S(1)}, u32[]{:S(2)}, u32[]{:S(2)}) collective-permute-start(bf16[16,1024]{1,0:T(8,128)(2,1)S(1)} %get-tuple-element.69), channel_id=1, source_target_pairs={{6,0},{7,1},{0,2},{1,3},{2,4},{3,5},{4,6},{5,7},{14,8},{15,9},{8,1... | collective-permute-start | bytes 98312 | tf_op jit(solution)/shard_map/ppermute | solution.py:279
  155.4 2.3 %collective-permute-start.25 = (bf16[16,1024]{1,0:T(8,128)(2,1)S(1)}, bf16[16,1024]{1,0:T(8,128)(2,1)S(1)}, u32[]{:S(2)}, u32[]{:S(2)}) collective-permute-start(bf16[16,1024]{1,0:T(8,128)(2,1)S(1)} %get-tuple-element.70), channel_id=1, source_target_pairs={{4,0},{5,1},{6,2},{7,3},{0,4},{1,5},{2,6},{3,7},{12,8},{13,9},{14,... | collective-permute-start | bytes 98312 | tf_op jit(solution)/shard_map/ppermute | solution.py:279
  157.7 1.4 collective-permute-start.26
  159.1 4.4 %collective-permute-done.25.refs_2_ = bf16[16,1024]{1,0:T(8,128)(2,1)S(1)} collective-permute-done((bf16[16,1024]{1,0:T(8,128)(2,1)S(1)}, bf16[16,1024]{1,0:T(8,128)(2,1)S(1)}, u32[]{:S(2)}, u32[]{:S(2)}) %collective-permute-start.25) | collective-permute-done | bytes 32800 | tf_op jit(solution)/shard_map/ppermute | solution.py:279
  (61 shorter events, 15.5 us)
Async XLA Ops:
  0.6 15.1 %collective-permute-start.1 = (bf16[1024,512]{1,0:T(8,128)(2,1)}, bf16[1024,512]{1,0:T(8,128)(2,1)S(1)}, u32[]{:S(2)}, u32[]{:S(2)}) collective-permute-start(bf16[1024,512]{1,0:T(8,128)(2,1)} %refs_2_.1), channel_id=1, source_target_pairs={{0,1},{1,0},{2,3},{3,2},{4,5},{5,4},{6,7},{7,6},{8,9},{9,8},{10,11... | collective-permute-start | bytes 3145736 | tf_op jit(solution)/shard_map/ppermute | solution.py:269
  0.7 15.0 %collective-permute-start.2 = (bf16[1024,512]{1,0:T(8,128)(2,1)}, bf16[1024,512]{1,0:T(8,128)(2,1)S(1)}, u32[]{:S(2)}, u32[]{:S(2)}) collective-permute-start(bf16[1024,512]{1,0:T(8,128)(2,1)} %refs_4_.1), channel_id=1, source_target_pairs={{0,1},{1,0},{2,3},{3,2},{4,5},{5,4},{6,7},{7,6},{8,9},{9,8},{10,11... | collective-permute-start | bytes 3145736 | tf_op jit(solution)/shard_map/ppermute | solution.py:269
  1.2 14.5 %collective-permute-start.3 = (bf16[512,1024]{1,0:T(8,128)(2,1)}, bf16[512,1024]{1,0:T(8,128)(2,1)}, u32[]{:S(2)}, u32[]{:S(2)}) collective-permute-start(bf16[512,1024]{1,0:T(8,128)(2,1)} %refs_6_.1), channel_id=1, source_target_pairs={{0,1},{1,0},{2,3},{3,2},{4,5},{5,4},{6,7},{7,6},{8,9},{9,8},{10,11... | collective-permute-start | bytes 3145736 | tf_op jit(solution)/shard_map/ppermute | solution.py:269
  2.9 28.8 %all-to-all-start = ((bf16[16,16,1024]{2,1,0:T(8,128)(2,1)}), bf16[16,16,1024]{2,1,0:T(8,128)(2,1)S(1)}, u32[]{:S(2)}, u32[]{:S(2)}) async-start(bf16[16,16,1024]{2,1,0:T(8,128)(2,1)} %broadcast_in_dim.2), calls=%async_computation | async-start | bytes 1048576 | tf_op jit(solution)/shard_map/all_to_all | solution.py:329
  14.4 1.4 collective-permute-start
  32.6 36.5 %copy-start.1 = (bf16[2,512,1024]{2,1,0:T(8,128)(2,1)S(1)}, bf16[2,512,1024]{2,1,0:T(8,128)(2,1)}, u32[]{:S(2)}) copy-start(bf16[2,512,1024]{2,1,0:T(8,128)(2,1)} %get-tuple-element.42.refs_1_.refs_4_) | copy-start | bytes 6291460
  37.8 55.0 %copy-start.2 = (bf16[16,1024]{1,0:T(8,128)(2,1)S(1)}, bf16[16,1024]{1,0:T(8,128)(2,1)}, u32[]{:S(2)}) copy-start(bf16[16,1024]{1,0:T(8,128)(2,1)} %refs_0_.1) | copy-start | bytes 98308
  57.4 11.7 %all-to-all-start.2 = ((bf16[8,32,1024]{2,1,0:T(8,128)(2,1)}), bf16[8,32,1024]{2,1,0:T(8,128)(2,1)S(1)}, u32[]{:S(2)}, u32[]{:S(2)}) async-start(bf16[8,32,1024]{2,1,0:T(8,128)(2,1)} %get-tuple-element.41), calls=%async_computation.2 | async-start | bytes 1048576 | tf_op jit(solution)/shard_map/all_to_all | solution.py:304
  60.9 45.0 %collective-permute-start.10 = (bf16[256,1024]{1,0:T(8,128)(2,1)}, bf16[256,1024]{1,0:T(8,128)(2,1)S(1)}, u32[]{:S(2)}, u32[]{:S(2)}) collective-permute-start(bf16[256,1024]{1,0:T(8,128)(2,1)} %get-tuple-element.52.refs_1_), channel_id=1, source_target_pairs={{0,1},{1,0},{2,3},{3,2},{4,5},{5,4},{6,7},{7,6},{8,9},{9,8},{10,11... | collective-permute-start | bytes 1572872 | tf_op jit(solution)/shard_map/ppermute | solution.py:269
  69.1 43.3 %collective-permute-start.17 = (bf16[256,1024]{1,0:T(8,128)(2,1)S(1)}, bf16[256,1024]{1,0:T(8,128)(2,1)S(1)}, u32[]{:S(2)}, u32[]{:S(2)}) collective-permute-start(bf16[256,1024]{1,0:T(8,128)(2,1)S(1)} %bitcast.9), channel_id=1, source_target_pairs={{0,1},{1,0},{2,3},{3,2},{4,5},{5,4},{6,7},{7,6},{8,9},{9,8},{10,11... | collective-permute-start | bytes 1572872 | tf_op jit(solution)/shard_map/ppermute | solution.py:269
  69.8 8.7 %collective-permute-start.4 = (bf16[64,1024]{1,0:T(8,128)(2,1)S(1)}, bf16[64,1024]{1,0:T(8,128)(2,1)S(1)}, u32[]{:S(2)}, u32[]{:S(2)}) collective-permute-start(bf16[64,1024]{1,0:T(8,128)(2,1)S(1)} %get-tuple-element.44), channel_id=1, source_target_pairs={{24,0},{25,1},{26,2},{27,3},{28,4},{29,5},{30,6},{31,7},{0,8},{1,9... | collective-permute-start | bytes 393224 | tf_op jit(solution)/shard_map/ppermute | solution.py:279
  72.3 7.9 %collective-permute-start.5 = (bf16[64,1024]{1,0:T(8,128)(2,1)S(1)}, bf16[64,1024]{1,0:T(8,128)(2,1)S(1)}, u32[]{:S(2)}, u32[]{:S(2)}) collective-permute-start(bf16[64,1024]{1,0:T(8,128)(2,1)S(1)} %get-tuple-element.45), channel_id=1, source_target_pairs={{16,0},{17,1},{18,2},{19,3},{20,4},{21,5},{22,6},{23,7},{24,8},{25... | collective-permute-start | bytes 393224 | tf_op jit(solution)/shard_map/ppermute | solution.py:279
  72.5 9.4 %collective-permute-start.6 = (bf16[64,1024]{1,0:T(8,128)(2,1)S(1)}, bf16[64,1024]{1,0:T(8,128)(2,1)S(1)}, u32[]{:S(2)}, u32[]{:S(2)}) collective-permute-start(bf16[64,1024]{1,0:T(8,128)(2,1)S(1)} %get-tuple-element.46), channel_id=1, source_target_pairs={{8,0},{9,1},{10,2},{11,3},{12,4},{13,5},{14,6},{15,7},{16,8},{17,9... | collective-permute-start | bytes 393224 | tf_op jit(solution)/shard_map/ppermute | solution.py:279
  82.0 57.4 %copy-start = (bf16[4,1024,512]{2,1,0:T(8,128)(2,1)S(1)}, bf16[4,1024,512]{2,1,0:T(8,128)(2,1)}, u32[]{:S(2)}) copy-start(bf16[4,1024,512]{2,1,0:T(8,128)(2,1)} %get-tuple-element.39.refs_1_) | copy-start | bytes 12582916
  82.0 6.6 %collective-permute-start.7 = (bf16[16,1024]{1,0:T(8,128)(2,1)S(1)}, bf16[16,1024]{1,0:T(8,128)(2,1)S(1)}, u32[]{:S(2)}, u32[]{:S(2)}) collective-permute-start(bf16[16,1024]{1,0:T(8,128)(2,1)S(1)} %get-tuple-element.48), channel_id=1, source_target_pairs={{6,0},{7,1},{0,2},{1,3},{2,4},{3,5},{4,6},{5,7},{14,8},{15,9},{8,1... | collective-permute-start | bytes 98312 | tf_op jit(solution)/shard_map/ppermute | solution.py:279
  84.9 7.8 %collective-permute-start.8 = (bf16[16,1024]{1,0:T(8,128)(2,1)S(1)}, bf16[16,1024]{1,0:T(8,128)(2,1)S(1)}, u32[]{:S(2)}, u32[]{:S(2)}) collective-permute-start(bf16[16,1024]{1,0:T(8,128)(2,1)S(1)} %get-tuple-element.49), channel_id=1, source_target_pairs={{4,0},{5,1},{6,2},{7,3},{0,4},{1,5},{2,6},{3,7},{12,8},{13,9},{14,... | collective-permute-start | bytes 98312 | tf_op jit(solution)/shard_map/ppermute | solution.py:279
  85.6 7.1 %collective-permute-start.9 = (bf16[16,1024]{1,0:T(8,128)(2,1)S(1)}, bf16[16,1024]{1,0:T(8,128)(2,1)S(1)}, u32[]{:S(2)}, u32[]{:S(2)}) collective-permute-start(bf16[16,1024]{1,0:T(8,128)(2,1)S(1)} %get-tuple-element.50), channel_id=1, source_target_pairs={{2,0},{3,1},{4,2},{5,3},{6,4},{7,5},{0,6},{1,7},{10,8},{11,9},{12,... | collective-permute-start | bytes 98312 | tf_op jit(solution)/shard_map/ppermute | solution.py:279
  93.4 7.1 %collective-permute-start.13 = (bf16[16,1024]{1,0:T(8,128)(2,1)S(1)}, bf16[16,1024]{1,0:T(8,128)(2,1)S(1)}, u32[]{:S(2)}, u32[]{:S(2)}) collective-permute-start(bf16[16,1024]{1,0:T(8,128)(2,1)S(1)} %get-tuple-element.53.refs_0_), channel_id=1, source_target_pairs={{6,0},{7,1},{0,2},{1,3},{2,4},{3,5},{4,6},{5,7},{14,8},{15,9},{8,1... | collective-permute-start | bytes 98312 | tf_op jit(solution)/shard_map/ppermute | solution.py:279
  95.3 7.8 %collective-permute-start.12 = (bf16[16,1024]{1,0:T(8,128)(2,1)S(1)}, bf16[16,1024]{1,0:T(8,128)(2,1)S(1)}, u32[]{:S(2)}, u32[]{:S(2)}) collective-permute-start(bf16[16,1024]{1,0:T(8,128)(2,1)S(1)} %get-tuple-element.53.refs_0_), channel_id=1, source_target_pairs={{4,0},{5,1},{6,2},{7,3},{0,4},{1,5},{2,6},{3,7},{12,8},{13,9},{14,... | collective-permute-start | bytes 98312 | tf_op jit(solution)/shard_map/ppermute | solution.py:279
  98.2 5.4 %collective-permute-start.11 = (bf16[16,1024]{1,0:T(8,128)(2,1)S(1)}, bf16[16,1024]{1,0:T(8,128)(2,1)S(1)}, u32[]{:S(2)}, u32[]{:S(2)}) collective-permute-start(bf16[16,1024]{1,0:T(8,128)(2,1)S(1)} %get-tuple-element.53.refs_0_), channel_id=1, source_target_pairs={{2,0},{3,1},{4,2},{5,3},{6,4},{7,5},{0,6},{1,7},{10,8},{11,9},{12,... | collective-permute-start | bytes 98312 | tf_op jit(solution)/shard_map/ppermute | solution.py:279
  103.6 5.0 %collective-permute-start.16 = (bf16[64,1024]{1,0:T(8,128)(2,1)S(1)}, bf16[64,1024]{1,0:T(8,128)(2,1)S(1)}, u32[]{:S(2)}, u32[]{:S(2)}) collective-permute-start(bf16[64,1024]{1,0:T(8,128)(2,1)S(1)} %shard_map.115.refs_0_), channel_id=1, source_target_pairs={{24,0},{25,1},{26,2},{27,3},{28,4},{29,5},{30,6},{31,7},{0,8},{1,9... | collective-permute-start | bytes 393224 | tf_op jit(solution)/shard_map/ppermute | solution.py:279
  104.6 6.6 %collective-permute-start.15 = (bf16[64,1024]{1,0:T(8,128)(2,1)S(1)}, bf16[64,1024]{1,0:T(8,128)(2,1)S(1)}, u32[]{:S(2)}, u32[]{:S(2)}) collective-permute-start(bf16[64,1024]{1,0:T(8,128)(2,1)S(1)} %shard_map.115.refs_0_), channel_id=1, source_target_pairs={{16,0},{17,1},{18,2},{19,3},{20,4},{21,5},{22,6},{23,7},{24,8},{25... | collective-permute-start | bytes 393224 | tf_op jit(solution)/shard_map/ppermute | solution.py:279
  104.8 7.6 %collective-permute-start.14 = (bf16[64,1024]{1,0:T(8,128)(2,1)S(1)}, bf16[64,1024]{1,0:T(8,128)(2,1)S(1)}, u32[]{:S(2)}, u32[]{:S(2)}) collective-permute-start(bf16[64,1024]{1,0:T(8,128)(2,1)S(1)} %shard_map.115.refs_0_), channel_id=1, source_target_pairs={{8,0},{9,1},{10,2},{11,3},{12,4},{13,5},{14,6},{15,7},{16,8},{17,9... | collective-permute-start | bytes 393224 | tf_op jit(solution)/shard_map/ppermute | solution.py:279
  138.9 4.3 %collective-permute-start.18 = (bf16[256,2048]{1,0:T(8,128)(2,1)S(1)}, bf16[256,2048]{1,0:T(8,128)(2,1)S(1)}, u32[]{:S(2)}, u32[]{:S(2)}) collective-permute-start(bf16[256,2048]{1,0:T(8,128)(2,1)S(1)} %bitcast.6), channel_id=1, source_target_pairs={{0,1},{1,0},{2,3},{3,2},{4,5},{5,4},{6,7},{7,6},{8,9},{9,8},{10,11... | collective-permute-start | bytes 3145736 | tf_op jit(solution)/shard_map/ppermute | solution.py:269
  138.9 4.3 %collective-permute-start.19 = (bf16[256,1024]{1,0:T(8,128)(2,1)S(1)}, bf16[256,1024]{1,0:T(8,128)(2,1)S(1)}, u32[]{:S(2)}, u32[]{:S(2)}) collective-permute-start(bf16[256,1024]{1,0:T(8,128)(2,1)S(1)} %get-tuple-element.57.refs_7_), channel_id=1, source_target_pairs={{0,1},{1,0},{2,3},{3,2},{4,5},{5,4},{6,7},{7,6},{8,9},{9,8},{10,11... | collective-permute-start | bytes 1572872 | tf_op jit(solution)/shard_map/ppermute | solution.py:269
  139.4 3.8 %collective-permute-start.20 = (f32[8,128]{1,0:T(8,128)S(1)}, f32[8,128]{1,0:T(8,128)S(1)}, u32[]{:S(2)}, u32[]{:S(2)}) collective-permute-start(f32[8,128]{1,0:T(8,128)S(1)} %get-tuple-element.58.refs_9_), channel_id=1, source_target_pairs={{0,1},{1,0},{2,3},{3,2},{4,5},{5,4},{6,7},{7,6},{8,9},{9,8},{10,11... | collective-permute-start | bytes 12296 | tf_op jit(solution)/shard_map/ppermute | solution.py:269
  140.7 6.7 %collective-permute-start.21 = (bf16[64,1024]{1,0:T(8,128)(2,1)S(1)}, bf16[64,1024]{1,0:T(8,128)(2,1)S(1)}, u32[]{:S(2)}, u32[]{:S(2)}) collective-permute-start(bf16[64,1024]{1,0:T(8,128)(2,1)S(1)} %get-tuple-element.64), channel_id=1, source_target_pairs={{24,0},{25,1},{26,2},{27,3},{28,4},{29,5},{30,6},{31,7},{0,8},{1,9... | collective-permute-start | bytes 393224 | tf_op jit(solution)/shard_map/ppermute | solution.py:279
  141.7 7.8 %collective-permute-start.22 = (bf16[64,1024]{1,0:T(8,128)(2,1)S(1)}, bf16[64,1024]{1,0:T(8,128)(2,1)S(1)}, u32[]{:S(2)}, u32[]{:S(2)}) collective-permute-start(bf16[64,1024]{1,0:T(8,128)(2,1)S(1)} %get-tuple-element.65), channel_id=1, source_target_pairs={{16,0},{17,1},{18,2},{19,3},{20,4},{21,5},{22,6},{23,7},{24,8},{25... | collective-permute-start | bytes 393224 | tf_op jit(solution)/shard_map/ppermute | solution.py:279
  143.1 8.5 %collective-permute-start.23 = (bf16[64,1024]{1,0:T(8,128)(2,1)S(1)}, bf16[64,1024]{1,0:T(8,128)(2,1)S(1)}, u32[]{:S(2)}, u32[]{:S(2)}) collective-permute-start(bf16[64,1024]{1,0:T(8,128)(2,1)S(1)} %get-tuple-element.66), channel_id=1, source_target_pairs={{8,0},{9,1},{10,2},{11,3},{12,4},{13,5},{14,6},{15,7},{16,8},{17,9... | collective-permute-start | bytes 393224 | tf_op jit(solution)/shard_map/ppermute | solution.py:279
  151.7 7.4 %collective-permute-start.24 = (bf16[16,1024]{1,0:T(8,128)(2,1)S(1)}, bf16[16,1024]{1,0:T(8,128)(2,1)S(1)}, u32[]{:S(2)}, u32[]{:S(2)}) collective-permute-start(bf16[16,1024]{1,0:T(8,128)(2,1)S(1)} %get-tuple-element.69), channel_id=1, source_target_pairs={{6,0},{7,1},{0,2},{1,3},{2,4},{3,5},{4,6},{5,7},{14,8},{15,9},{8,1... | collective-permute-start | bytes 98312 | tf_op jit(solution)/shard_map/ppermute | solution.py:279
  155.4 8.1 %collective-permute-start.25 = (bf16[16,1024]{1,0:T(8,128)(2,1)S(1)}, bf16[16,1024]{1,0:T(8,128)(2,1)S(1)}, u32[]{:S(2)}, u32[]{:S(2)}) collective-permute-start(bf16[16,1024]{1,0:T(8,128)(2,1)S(1)} %get-tuple-element.70), channel_id=1, source_target_pairs={{4,0},{5,1},{6,2},{7,3},{0,4},{1,5},{2,6},{3,7},{12,8},{13,9},{14,... | collective-permute-start | bytes 98312 | tf_op jit(solution)/shard_map/ppermute | solution.py:279
  157.7 5.8 %collective-permute-start.26 = (bf16[16,1024]{1,0:T(8,128)(2,1)S(1)}, bf16[16,1024]{1,0:T(8,128)(2,1)S(1)}, u32[]{:S(2)}, u32[]{:S(2)}) collective-permute-start(bf16[16,1024]{1,0:T(8,128)(2,1)S(1)} %get-tuple-element.71), channel_id=1, source_target_pairs={{2,0},{3,1},{4,2},{5,3},{6,4},{7,5},{0,6},{1,7},{10,8},{11,9},{12,... | collective-permute-start | bytes 98312 | tf_op jit(solution)/shard_map/ppermute | solution.py:279
  (6 other events, 40.4 us)

commit v5 on v3

--- a/solution.py
+++ b/solution.py
@@ -49,13 +49,37 @@
         joined_ref[pl.ds(part * size, size), :] = ref[...]
 
 
-def keep(mask_ref, which, ref, kept_ref):
-    for row in range(ref.shape[0] // BLK):
-        for col in range(ref.shape[1] // BLK):
-            at = (row, col) if which == DOWN else (col, row)
-            factor = mask_ref[which, at[0], at[1]].astype(jnp.float32).astype(jnp.bfloat16)
-            block = (pl.ds(row * BLK, BLK), pl.ds(col * BLK, BLK))
-            kept_ref[block] = ref[block] * factor
+def fetched(pairs, sems):
+    copies = [pltpu.make_async_copy(src, dst, sems.at[at]) for at, (src, dst) in enumerate(pairs)]
+    for copy in copies:
+        copy.start()
+    return copies
+
+
+def keep_kernel(mask_ref, mask_other_ref, *refs):
+    raw_refs, kept_refs, scratches, sems = refs[:6], refs[6:12], refs[12:18], refs[18]
+    for at, copy in enumerate(fetched(zip(raw_refs, scratches), sems)):
+        masks, which = (mask_ref, mask_other_ref)[at % 2], at // 2
+        copy.wait()
+        for row in range(raw_refs[at].shape[0] // BLK):
+            for col in range(raw_refs[at].shape[1] // BLK):
+                block = (row, col) if which == DOWN else (col, row)
+                factor = masks[which, block[0], block[1]].astype(jnp.float32).astype(jnp.bfloat16)
+                place = (pl.ds(row * BLK, BLK), pl.ds(col * BLK, BLK))
+                kept_refs[at][place] = scratches[at][place] * factor
+
+
+def keep(masks, weights):
+    return call(
+        keep_kernel,
+        [shaped(value.shape) for value in weights],
+        *masks,
+        *weights,
+        in_specs=[SMEM] * 2 + [ANY] * 6,
+        scratch_shapes=[pltpu.VMEM(value.shape, value.dtype) for value in weights]
+        + [pltpu.SemaphoreType.DMA((6,))],
+        vmem=24,
+    )
 
 
 def plain_dot(left, right):
@@ -66,18 +90,20 @@
     return lax.dot_general(left, right, (((1,), (1,)), ((), ())), preferred_element_type=jnp.float32)
 
 
-def gate_up_kernel(mask_ref, mask_other_ref, chips_ref, *refs):
-    weights, kept_refs, (out_ref, rows_ref) = refs[:4], refs[4:8], refs[8:]
+def gate_up_kernel(chips_ref, *refs):
+    weights, (out_ref, rows_ref, sems) = refs[:4], refs[4:]
     chip = lax.axis_index("col") // CORES
     size = chips_ref.shape[1]
+    pairs = []
     for part in range(CHIPS):
         x = lax.rem(chip // Z + part // Z, X)
         z = lax.rem(chip + part % Z, Z)
-        rows_ref[pl.ds(part * size, size), :] = chips_ref[x * Z + z]
-    for which, (ref, kept_ref) in enumerate(zip(weights, kept_refs)):
+        pairs.append((chips_ref.at[x * Z + z], rows_ref.at[pl.ds(part * size, size), :]))
+    for copy in fetched(pairs, sems):
+        copy.wait()
+    for which, ref in enumerate(weights):
         units = ref.shape[1]
-        keep((mask_ref, mask_other_ref)[which % 2], which // 2, ref, kept_ref)
-        value = plain_dot(rows_ref[...], kept_ref[...])
+        value = plain_dot(rows_ref[...], ref[...])
         out_ref[:, pl.ds(which * units, units)] = value.astype(out_ref.dtype)
 
 
@@ -87,14 +113,12 @@
         ref[:, cols] = value[part * size : (part + 1) * size].astype(ref.dtype)
 
 
-def output_kernel(mask_ref, mask_other_ref, hidden_ref, down_ref, down_other_ref, kept_ref, kept_other_ref, *out_refs):
+def output_kernel(hidden_ref, down_ref, down_other_ref, *out_refs):
     units, width = down_ref.shape
-    keep(mask_ref, DOWN, down_ref, kept_ref)
-    keep(mask_other_ref, DOWN, down_other_ref, kept_other_ref)
     for at in range(0, width, TILE):
         cols = pl.ds(at, TILE)
-        value = plain_dot(hidden_ref[:, :units], kept_ref[:, cols])
-        value = value + plain_dot(hidden_ref[:, units:], kept_other_ref[:, cols])
+        value = plain_dot(hidden_ref[:, :units], down_ref[:, cols])
+        value = value + plain_dot(hidden_ref[:, units:], down_other_ref[:, cols])
         put_slabs(out_refs, cols, value)
 
 
@@ -127,10 +151,9 @@
         put_slabs(out_refs, pl.ds(at, TILE), value)
 
 
-def multiply(kernel, shapes, left, weights, masks=(), after=()):
+def multiply(kernel, shapes, left, weights, after=()):
     flops = 2 * sum(part.size // part.shape[-1] for part in left) * sum(weight.size for weight in weights)
-    specs = [SMEM] * len(masks) + [VMEM] * (len(left) + len(weights))
-    return call(kernel, shapes, *masks, *left, *weights, flops=flops, vmem=16, in_specs=specs, after=after)
+    return call(kernel, shapes, *left, *weights, flops=flops, vmem=16, after=after)
 
 
 def summed(parts):
@@ -144,7 +167,9 @@
     return [parts_ref.at[part] for part in range(parts_ref.shape[0])]
 
 
-def hidden_kernel(parts_ref, both_ref, copies_ref):
+def hidden_kernel(sent_ref, both_ref, copies_ref, parts_ref, sems):
+    for copy in fetched([(sent_ref.at[part], parts_ref.at[part]) for part in range(ROWS)], sems):
+        copy.wait()
     both = summed(parts_of(parts_ref))
     half = both.shape[1] // 2
     gate, up = both[:, :half], both[:, half:]
@@ -239,6 +264,20 @@
         copy.wait()
 
 
+def hold_kernel(*refs):
+    pass
+
+
+def hold(values, after):
+    return pl.pallas_call(
+        hold_kernel,
+        out_shape=[shaped(value.shape) for value in values],
+        in_specs=[ANY] * (len(values) + len(after)),
+        out_specs=[ANY] * len(values),
+        input_output_aliases={at: at for at in range(len(values))},
+    )(*values, *after)
+
+
 def other_core(value):
     count = CHIPS * CORES
     return lax.ppermute(value, "col", [(device, device ^ 1) for device in range(count)])
@@ -277,6 +316,10 @@
 
 def exchange_row(value):
     return lax.all_to_all(value, "row", 0, 0)
+
+
+def in_hbm(value):
+    return pltpu.with_memory_space_constraint(value, pltpu.HBM)
 
 
 def flat(value):
@@ -302,29 +345,37 @@
     )
     copies = jnp.broadcast_to(inputs[None], (CHIPS, tokens, width))
     chips = lax.all_to_all(copies, "col", 0, 0, axis_index_groups=SAME_CORE)
-    *gate_ups, partial, rows = multiply(
+    chips = in_hbm(chips)
+    kept = keep(masks, [value for own, other in (gates, ups, downs) for value in (in_hbm(own), other)])
+    gate_ups, downs = kept[:4], kept[4:]
+    partial, rows = call(
         gate_up_kernel,
-        (wide,) * 4 + (shaped((half, 4 * units)), shaped((half, width))),
-        [chips],
-        gates + ups,
-        masks,
-        downs[1:],
-    )
+        (shaped((half, 4 * units)), shaped((half, width))),
+        chips,
+        *gate_ups,
+        in_specs=[ANY] + [VMEM] * 4,
+        scratch_shapes=[pltpu.SemaphoreType.DMA((CHIPS,))],
+        flops=8 * half * width * units,
+        vmem=16,
+    )
+    sent = in_hbm(exchange_row(split(partial, ROWS)))
     both, copies = call(
         hidden_kernel,
         (shaped((half // ROWS, 4 * units), jnp.float32), shaped((ROWS, half // ROWS, 2 * units))),
-        exchange_row(split(partial, ROWS)),
+        sent,
+        in_specs=[ANY],
+        scratch_shapes=[pltpu.VMEM(sent.shape, sent.dtype), pltpu.SemaphoreType.DMA((ROWS,))],
     )
     hidden = flat(exchange_row(copies))
-    *downs, first, second, third, fourth = multiply(
-        output_kernel, (tall,) * 2 + (slab,) * X, [hidden], downs, masks
-    )
-    slabs = spread_x([first, second, third, fourth])
-    parts = spread_z(call(sum_kernel, (piece,) * Z, *slabs))
+    slabs = spread_x(multiply(output_kernel, (slab,) * X, [hidden], downs))
+    parts = call(sum_kernel, (piece,) * Z, *slabs)
+    rows, hidden = hold((rows, hidden), parts[:1])
+    rows_other, hidden_other = other_core(rows), other_core(hidden)
+    parts = spread_z(parts)
     student, grad_out = call(functools.partial(error_kernel, scale), (piece, piece), teacher, *parts)
     slabs = gather_x(joined(gather_z(grad_out)))
     partial, grad_rows = multiply(
-        grad_hidden_kernel, (shaped((half, 2 * units + BLK)), shaped((half, width))), slabs, downs
+        grad_hidden_kernel, (shaped((half, 2 * units + BLK)), shaped((half, width))), slabs, downs, (rows_other, hidden_other)
     )
     copies, squares = call(
         acts_kernel,
@@ -334,9 +385,7 @@
     )
     acts = flat(exchange_row(copies))
     slabs = spread_x(multiply(grad_in_kernel, (slab,) * X, [acts], gate_ups))
-    rows_other, hidden_other, grad_rows_other, acts_other, squares_other = (
-        other_core(value) for value in (rows, hidden, grad_rows, acts, squares)
-    )
+    grad_rows_other, acts_other, squares_other = (other_core(value) for value in (grad_rows, acts, squares))
     grad_gate, grad_up, grad_down, loss, done = call(
         weights_kernel,
         (wide, wide, tall, shaped((1, 1), jnp.float32), DONE),

time: 167 us -> 168 us (level)
  waiting for transfers between devices: 46 us -> 29.8 us
  local copies, waits for them, and re-layouts: 2.84 us -> 17.7 us
  blocking collectives: 59.2 us -> 55.4 us
  Pallas kernels: 12.6 us -> 15.8 us
  starting transfers between devices: 44.4 us -> 47 us
    unnamed x10 -> x52, local copies, waits for them, and re-layouts: 1.24 us -> 16.1 us
    all_to_all x1, waiting for transfers between devices: 16.2 us -> 2.31 us  [per_device(): chips = lax.all_to_all(copies, 'col', 0, 0, axis_index_groups=SAME_CORE)]
    all_to_all x4, blocking collectives: 59.2 us -> 55.4 us  [exchange_row(): return lax.all_to_all(value, 'row', 0, 0)]
    pallas_call x12 -> x13, Pallas kernels: 12.6 us -> 15.8 us  [call(): pl.pallas_call(lambda *refs: kernel(*refs[:len(args)], *refs[len(args) +...]
    ppermute x18, starting transfers between devices: 31 us -> 33.6 us  [fetch(): return lax.ppermute(value, 'col', pairs)]
  transfers between devices with their start and end apart: 28 -> 28, of which waited for: 16 -> 16; matrix products, arithmetic and copies ran while one was open for 1% -> 1% of each run, Pallas kernels for 3% -> 6%
where the time goes in v5:
time: 168 us; the launch traced here: 167 us
  blocking collectives  55.4 us (33%)
  starting transfers between devices  47 us (28%)
  waiting for transfers between devices  29.8 us (18%)
  local copies, waits for them, and re-layouts  17.7 us (11%)
  Pallas kernels  15.8 us (9%)
    all_to_all x4, blocking collectives, exchange_row(): return lax.all_to_all(value, 'row', 0, 0)  55.4 us
    ppermute x18, starting transfers between devices, fetch(): return lax.ppermute(value, 'col', pairs)  33.6 us
    ppermute x18, waiting for transfers between devices, fetch(): return lax.ppermute(value, 'col', pairs)  26.3 us
    unnamed x52, local copies, waits for them, and re-layouts  16.1 us
    pallas_call x13, Pallas kernels, call(): pl.pallas_call(lambda *refs: kernel(*refs[:len(args)], *refs[len(args) +...  15.8 us
    all_to_all x1, starting transfers between devices, per_device(): chips = lax.all_to_all(copies, 'col', 0, 0, axis_index_groups=SAME_CORE)  11.6 us
  transfers between devices with their start and end apart: 28, of which 16 were waited for; matrix products, arithmetic and copies ran while one was open for 1% of the time, Pallas kernels for 6%

profile of v5, /device:TPU:6, one launch (start us, length us, event | category | flops | bytes accessed | tf_op | source)
XLA Modules:
  0.0 166.5 jit_solution(12440525572398628122)
XLA Ops:
  1.3 1.6 broadcast_in_dim.2
  3.0 11.6 %all-to-all-start = ((bf16[16,16,1024]{2,1,0:T(8,128)(2,1)}), bf16[16,16,1024]{2,1,0:T(8,128)(2,1)}, u32[]{:S(2)}, u32[]{:S(2)}) async-start(bf16[16,16,1024]{2,1,0:T(8,128)(2,1)} %broadcast_in_dim.2), calls=%async_computation | async-start | bytes 1048576 | tf_op jit(solution)/shard_map/all_to_all | solution.py:347
  22.4 3.4 %shard_map.109 = (bf16[1024,512]{1,0:T(8,128)(2,1)S(1)}, bf16[1024,512]{1,0:T(8,128)(2,1)S(1)}, bf16[1024,512]{1,0:T(8,128)(2,1)S(1)}, bf16[1024,512]{1,0:T(8,12...) custom-call(s32[3,4,8]{2,1,0:T(4,128)S(1)} %bitcast.14, ...), custom_call_target="tpu_custom_call" | custom-call | bytes 12583680 | tf_op jit(solution)/shard_map/pallas_call | solution.py:26
  29.7 2.3 %all-to-all-done.refs_0_ = bf16[16,16,1024]{2,1,0:T(8,128)(2,1)} async-done(((bf16[16,16,1024]{2,1,0:T(8,128)(2,1)}), bf16[16,16,1024]{2,1,0:T(8,128)(2,1)}, u32[]{:S(2)}, u32[]{:S(2)}) %all-to-all-start) | async-done | bytes 524320 | tf_op jit(solution)/shard_map/all_to_all | solution.py:347
  36.9 2.4 %shard_map.110 = (bf16[256,2048]{1,0:T(8,128)(2,1)S(1)}, bf16[256,1024]{1,0:T(8,128)(2,1)S(1)}) custom-call(bf16[16,16,1024]{2,1,0:T(8,128)(2,1)} %all-to-all-done.refs_0_, bf16[1024,512]{1,0:T(8,128)(2,1)S(1)} %copy-done.3, bf16[1024,512]{1,0:T(8,128)(2,1)S(1)} %copy-done.6, bf16[1024,512]{1,0:T(8,128)(2,1)S(1)} %copy-done.9, bf16[1024,512]{1,0:T(8,128)(2,1)S(1)} %copy-done.12), custom_call_target="tpu_custom_call" | custom-call | flops 1073741824 | bytes 6291456 | tf_op jit(solution)/shard_map/pallas_call | solution.py:26
  39.3 18.6 %all_to_all.25.refs_0_ = bf16[8,32,2048]{2,1,0:T(8,128)(2,1)} all-to-all(bf16[8,32,2048]{2,1,0:T(8,128)(2,1)S(1)} %bitcast.11), channel_id=1, replica_groups=mesh['row'=8,'col'=32] {'row'}, dimensions={0} | all-to-all | bytes 2097152 | tf_op jit(solution)/shard_map/all_to_all | solution.py:318
  57.9 1.5 shard_map.111
  59.4 11.1 %all_to_all.26 = bf16[8,32,1024]{2,1,0:T(8,128)(2,1)S(1)} all-to-all(bf16[8,32,1024]{2,1,0:T(8,128)(2,1)S(1)} %get-tuple-element.50), channel_id=1, replica_groups=mesh['row'=8,'col'=32] {'row'}, dimensions={0} | all-to-all | bytes 1048576 | tf_op jit(solution)/shard_map/all_to_all | solution.py:318
  71.4 2.4 %collective-permute-start.4 = (bf16[64,1024]{1,0:T(8,128)(2,1)S(1)}, bf16[64,1024]{1,0:T(8,128)(2,1)S(1)}, u32[]{:S(2)}, u32[]{:S(2)}) collective-permute-start(bf16[64,1024]{1,0:T(8,128)(2,1)S(1)} %get-tuple-element.54), channel_id=1, source_target_pairs={{24,0},{25,1},{26,2},{27,3},{28,4},{29,5},{30,6},{31,7},{0,8},{1,9... | collective-permute-start | bytes 393224 | tf_op jit(solution)/shard_map/ppermute | solution.py:293
  74.7 3.0 %collective-permute-done.4.refs_1_ = bf16[64,1024]{1,0:T(8,128)(2,1)S(1)} collective-permute-done((bf16[64,1024]{1,0:T(8,128)(2,1)S(1)}, bf16[64,1024]{1,0:T(8,128)(2,1)S(1)}, u32[]{:S(2)}, u32[]{:S(2)}) %collective-permute-start.4) | collective-permute-done | bytes 131104 | tf_op jit(solution)/shard_map/ppermute | solution.py:293
  77.7 2.7 %collective-permute-done.5.refs_2_ = bf16[64,1024]{1,0:T(8,128)(2,1)S(1)} collective-permute-done((bf16[64,1024]{1,0:T(8,128)(2,1)S(1)}, bf16[64,1024]{1,0:T(8,128)(2,1)S(1)}, u32[]{:S(2)}, u32[]{:S(2)}) %collective-permute-start.5) | collective-permute-done | bytes 131104 | tf_op jit(solution)/shard_map/ppermute | solution.py:293
  82.8 3.0 %collective-permute-start.7 = (bf16[16,1024]{1,0:T(8,128)(2,1)S(1)}, bf16[16,1024]{1,0:T(8,128)(2,1)S(1)}, u32[]{:S(2)}, u32[]{:S(2)}) collective-permute-start(bf16[16,1024]{1,0:T(8,128)(2,1)S(1)} %get-tuple-element.58), channel_id=1, source_target_pairs={{6,0},{7,1},{0,2},{1,3},{2,4},{3,5},{4,6},{5,7},{14,8},{15,9},{8,1... | collective-permute-start | bytes 98312 | tf_op jit(solution)/shard_map/ppermute | solution.py:293
  85.9 2.7 %collective-permute-start.8 = (bf16[16,1024]{1,0:T(8,128)(2,1)S(1)}, bf16[16,1024]{1,0:T(8,128)(2,1)S(1)}, u32[]{:S(2)}, u32[]{:S(2)}) collective-permute-start(bf16[16,1024]{1,0:T(8,128)(2,1)S(1)} %get-tuple-element.59), channel_id=1, source_target_pairs={{4,0},{5,1},{6,2},{7,3},{0,4},{1,5},{2,6},{3,7},{12,8},{13,9},{14,... | collective-permute-start | bytes 98312 | tf_op jit(solution)/shard_map/ppermute | solution.py:293
  88.6 3.6 %collective-permute-start.9 = (bf16[16,1024]{1,0:T(8,128)(2,1)S(1)}, bf16[16,1024]{1,0:T(8,128)(2,1)S(1)}, u32[]{:S(2)}, u32[]{:S(2)}) collective-permute-start(bf16[16,1024]{1,0:T(8,128)(2,1)S(1)} %get-tuple-element.60), channel_id=1, source_target_pairs={{2,0},{3,1},{4,2},{5,3},{6,4},{7,5},{0,6},{1,7},{10,8},{11,9},{12,... | collective-permute-start | bytes 98312 | tf_op jit(solution)/shard_map/ppermute | solution.py:293
  92.2 1.6 collective-permute-done.8.refs_3_
  94.8 2.4 %collective-permute-start.13 = (bf16[16,1024]{1,0:T(8,128)(2,1)S(1)}, bf16[16,1024]{1,0:T(8,128)(2,1)S(1)}, u32[]{:S(2)}, u32[]{:S(2)}) collective-permute-start(bf16[16,1024]{1,0:T(8,128)(2,1)S(1)} %get-tuple-element.64.refs_0_), channel_id=1, source_target_pairs={{6,0},{7,1},{0,2},{1,3},{2,4},{3,5},{4,6},{5,7},{14,8},{15,9},{8,1... | collective-permute-start | bytes 98312 | tf_op jit(solution)/shard_map/ppermute | solution.py:293
  97.2 4.4 %collective-permute-start.12 = (bf16[16,1024]{1,0:T(8,128)(2,1)S(1)}, bf16[16,1024]{1,0:T(8,128)(2,1)S(1)}, u32[]{:S(2)}, u32[]{:S(2)}) collective-permute-start(bf16[16,1024]{1,0:T(8,128)(2,1)S(1)} %get-tuple-element.64.refs_0_), channel_id=1, source_target_pairs={{4,0},{5,1},{6,2},{7,3},{0,4},{1,5},{2,6},{3,7},{12,8},{13,9},{14,... | collective-permute-start | bytes 98312 | tf_op jit(solution)/shard_map/ppermute | solution.py:293
  102.5 2.5 %collective-permute-done.12.refs_2_ = bf16[16,1024]{1,0:T(8,128)(2,1)S(1)} collective-permute-done((bf16[16,1024]{1,0:T(8,128)(2,1)S(1)}, bf16[16,1024]{1,0:T(8,128)(2,1)S(1)}, u32[]{:S(2)}, u32[]{:S(2)}) %collective-permute-start.12) | collective-permute-done | bytes 32800 | tf_op jit(solution)/shard_map/ppermute | solution.py:293
  105.0 1.6 collective-permute-done.11.refs_1_
  107.2 1.8 %collective-permute-start.15 = (bf16[64,1024]{1,0:T(8,128)(2,1)S(1)}, bf16[64,1024]{1,0:T(8,128)(2,1)S(1)}, u32[]{:S(2)}, u32[]{:S(2)}) collective-permute-start(bf16[64,1024]{1,0:T(8,128)(2,1)S(1)} %shard_map.116.refs_0_), channel_id=1, source_target_pairs={{16,0},{17,1},{18,2},{19,3},{20,4},{21,5},{22,6},{23,7},{24,8},{25... | collective-permute-start | bytes 393224 | tf_op jit(solution)/shard_map/ppermute | solution.py:293
  109.5 2.2 %collective-permute-done.16.refs_3_ = bf16[64,1024]{1,0:T(8,128)(2,1)S(1)} collective-permute-done((bf16[64,1024]{1,0:T(8,128)(2,1)S(1)}, bf16[64,1024]{1,0:T(8,128)(2,1)S(1)}, u32[]{:S(2)}, u32[]{:S(2)}) %collective-permute-start.16) | collective-permute-done | bytes 131104 | tf_op jit(solution)/shard_map/ppermute | solution.py:293
  111.6 2.1 %collective-permute-done.15.refs_2_ = bf16[64,1024]{1,0:T(8,128)(2,1)S(1)} collective-permute-done((bf16[64,1024]{1,0:T(8,128)(2,1)S(1)}, bf16[64,1024]{1,0:T(8,128)(2,1)S(1)}, u32[]{:S(2)}, u32[]{:S(2)}) %collective-permute-start.15) | collective-permute-done | bytes 131104 | tf_op jit(solution)/shard_map/ppermute | solution.py:293
  113.7 1.5 collective-permute-done.14.refs_1_
  116.0 11.7 %all_to_all.27.refs_0_ = bf16[8,32,1152]{2,1,0:T(8,128)(2,1)S(1)} all-to-all(bf16[8,32,1152]{2,1,0:T(8,128)(2,1)S(1)} %bitcast.12), channel_id=1, replica_groups=mesh['row'=8,'col'=32] {'row'}, dimensions={0} | all-to-all | bytes 1179648 | tf_op jit(solution)/shard_map/all_to_all | solution.py:318
  127.9 14.0 %all_to_all.28 = bf16[8,32,2048]{2,1,0:T(8,128)(2,1)S(1)} all-to-all(bf16[8,32,2048]{2,1,0:T(8,128)(2,1)S(1)} %get-tuple-element.68), channel_id=1, replica_groups=mesh['row'=8,'col'=32] {'row'}, dimensions={0} | all-to-all | bytes 2097152 | tf_op jit(solution)/shard_map/all_to_all | solution.py:318
  147.0 4.1 %shard_map.119 = (bf16[1024,512]{1,0:T(8,128)(2,1)}, bf16[1024,512]{1,0:T(8,128)(2,1)}, bf16[512,1024]{1,0:T(8,128)(2,1)}, f32[1,1]{1,0:T(1,128)}, f32[8,128]{1,0:T(8,128)S(1)}) custom-call(s32[3,4,8]{2,1,0:T(4,128)S(1)} %bitcast.15, bf16[256,1024]{1,0:T(8,128)(2,1)S(1)} %copy-done.21, bf16[256,1024]{1,0:T(8,128)(2,1)S(1)} %collective-permute-done.10.refs_6_.refs_2_, ...), custom_call_target="tpu_custom_call" | custom-call | flops 1610612736 | bytes 8401284 | tf_op jit(solution)/shard_map/pallas_call | solution.py:26
  151.2 1.6 collective-permute-done.22.refs_2_
  152.8 2.1 %collective-permute-done.23.refs_3_ = bf16[64,1024]{1,0:T(8,128)(2,1)S(1)} collective-permute-done((bf16[64,1024]{1,0:T(8,128)(2,1)S(1)}, bf16[64,1024]{1,0:T(8,128)(2,1)S(1)}, u32[]{:S(2)}, u32[]{:S(2)}) %collective-permute-start.23) | collective-permute-done | bytes 131104 | tf_op jit(solution)/shard_map/ppermute | solution.py:293
  156.1 4.6 %collective-permute-start.25 = (bf16[16,1024]{1,0:T(8,128)(2,1)S(1)}, bf16[16,1024]{1,0:T(8,128)(2,1)S(1)}, u32[]{:S(2)}, u32[]{:S(2)}) collective-permute-start(bf16[16,1024]{1,0:T(8,128)(2,1)S(1)} %get-tuple-element.82), channel_id=1, source_target_pairs={{4,0},{5,1},{6,2},{7,3},{0,4},{1,5},{2,6},{3,7},{12,8},{13,9},{14,... | collective-permute-start | bytes 98312 | tf_op jit(solution)/shard_map/ppermute | solution.py:293
  160.7 1.3 collective-permute-start.26
  162.0 2.0 %collective-permute-done.25.refs_2_ = bf16[16,1024]{1,0:T(8,128)(2,1)S(1)} collective-permute-done((bf16[16,1024]{1,0:T(8,128)(2,1)S(1)}, bf16[16,1024]{1,0:T(8,128)(2,1)S(1)}, u32[]{:S(2)}, u32[]{:S(2)}) %collective-permute-start.25) | collective-permute-done | bytes 32800 | tf_op jit(solution)/shard_map/ppermute | solution.py:293
  164.1 1.8 %collective-permute-done.26.refs_3_ = bf16[16,1024]{1,0:T(8,128)(2,1)S(1)} collective-permute-done((bf16[16,1024]{1,0:T(8,128)(2,1)S(1)}, bf16[16,1024]{1,0:T(8,128)(2,1)S(1)}, u32[]{:S(2)}, u32[]{:S(2)}) %collective-permute-start.26) | collective-permute-done | bytes 32800 | tf_op jit(solution)/shard_map/ppermute | solution.py:293
  (95 shorter events, 32.4 us)
Async XLA Ops:
  0.6 15.1 %collective-permute-start.1 = (bf16[1024,512]{1,0:T(8,128)(2,1)}, bf16[1024,512]{1,0:T(8,128)(2,1)S(1)}, u32[]{:S(2)}, u32[]{:S(2)}) collective-permute-start(bf16[1024,512]{1,0:T(8,128)(2,1)} %refs_2_.1), channel_id=1, source_target_pairs={{0,1},{1,0},{2,3},{3,2},{4,5},{5,4},{6,7},{7,6},{8,9},{9,8},{10,11... | collective-permute-start | bytes 3145736 | tf_op jit(solution)/shard_map/ppermute | solution.py:283
  0.7 16.0 %collective-permute-start.2 = (bf16[1024,512]{1,0:T(8,128)(2,1)}, bf16[1024,512]{1,0:T(8,128)(2,1)S(1)}, u32[]{:S(2)}, u32[]{:S(2)}) collective-permute-start(bf16[1024,512]{1,0:T(8,128)(2,1)} %refs_4_.1), channel_id=1, source_target_pairs={{0,1},{1,0},{2,3},{3,2},{4,5},{5,4},{6,7},{7,6},{8,9},{9,8},{10,11... | collective-permute-start | bytes 3145736 | tf_op jit(solution)/shard_map/ppermute | solution.py:283
  1.2 16.5 %collective-permute-start.3 = (bf16[512,1024]{1,0:T(8,128)(2,1)}, bf16[512,1024]{1,0:T(8,128)(2,1)S(1)}, u32[]{:S(2)}, u32[]{:S(2)}) collective-permute-start(bf16[512,1024]{1,0:T(8,128)(2,1)} %refs_6_.1), channel_id=1, source_target_pairs={{0,1},{1,0},{2,3},{3,2},{4,5},{5,4},{6,7},{7,6},{8,9},{9,8},{10,11... | collective-permute-start | bytes 3145736 | tf_op jit(solution)/shard_map/ppermute | solution.py:283
  3.0 29.1 %all-to-all-start = ((bf16[16,16,1024]{2,1,0:T(8,128)(2,1)}), bf16[16,16,1024]{2,1,0:T(8,128)(2,1)}, u32[]{:S(2)}, u32[]{:S(2)}) async-start(bf16[16,16,1024]{2,1,0:T(8,128)(2,1)} %broadcast_in_dim.2), calls=%async_computation | async-start | bytes 1048576 | tf_op jit(solution)/shard_map/all_to_all | solution.py:347
  14.5 1.3 collective-permute-start
  39.3 18.6 %copy-start.20 = (bf16[256,1024]{1,0:T(8,128)(2,1)}, bf16[256,1024]{1,0:T(8,128)(2,1)S(1)}, u32[]{:S(2)}) copy-start(bf16[256,1024]{1,0:T(8,128)(2,1)S(1)} %get-tuple-element.62.refs_0_) | copy-start | bytes 1572868
  71.4 6.3 %collective-permute-start.4 = (bf16[64,1024]{1,0:T(8,128)(2,1)S(1)}, bf16[64,1024]{1,0:T(8,128)(2,1)S(1)}, u32[]{:S(2)}, u32[]{:S(2)}) collective-permute-start(bf16[64,1024]{1,0:T(8,128)(2,1)S(1)} %get-tuple-element.54), channel_id=1, source_target_pairs={{24,0},{25,1},{26,2},{27,3},{28,4},{29,5},{30,6},{31,7},{0,8},{1,9... | collective-permute-start | bytes 393224 | tf_op jit(solution)/shard_map/ppermute | solution.py:293
  73.8 6.6 %collective-permute-start.5 = (bf16[64,1024]{1,0:T(8,128)(2,1)S(1)}, bf16[64,1024]{1,0:T(8,128)(2,1)S(1)}, u32[]{:S(2)}, u32[]{:S(2)}) collective-permute-start(bf16[64,1024]{1,0:T(8,128)(2,1)S(1)} %get-tuple-element.55), channel_id=1, source_target_pairs={{16,0},{17,1},{18,2},{19,3},{20,4},{21,5},{22,6},{23,7},{24,8},{25... | collective-permute-start | bytes 393224 | tf_op jit(solution)/shard_map/ppermute | solution.py:293
  74.3 7.3 %collective-permute-start.6 = (bf16[64,1024]{1,0:T(8,128)(2,1)S(1)}, bf16[64,1024]{1,0:T(8,128)(2,1)S(1)}, u32[]{:S(2)}, u32[]{:S(2)}) collective-permute-start(bf16[64,1024]{1,0:T(8,128)(2,1)S(1)} %get-tuple-element.56), channel_id=1, source_target_pairs={{8,0},{9,1},{10,2},{11,3},{12,4},{13,5},{14,6},{15,7},{16,8},{17,9... | collective-permute-start | bytes 393224 | tf_op jit(solution)/shard_map/ppermute | solution.py:293
  82.3 32.9 %collective-permute-start.10 = (bf16[256,1024]{1,0:T(8,128)(2,1)}, bf16[256,1024]{1,0:T(8,128)(2,1)S(1)}, u32[]{:S(2)}, u32[]{:S(2)}) collective-permute-start(bf16[256,1024]{1,0:T(8,128)(2,1)} %get-tuple-element.63.refs_1_), channel_id=1, source_target_pairs={{0,1},{1,0},{2,3},{3,2},{4,5},{5,4},{6,7},{7,6},{8,9},{9,8},{10,11... | collective-permute-start | bytes 1572872 | tf_op jit(solution)/shard_map/ppermute | solution.py:283
  82.3 32.9 %collective-permute-start.17 = (bf16[256,1024]{1,0:T(8,128)(2,1)}, bf16[256,1024]{1,0:T(8,128)(2,1)S(1)}, u32[]{:S(2)}, u32[]{:S(2)}) collective-permute-start(bf16[256,1024]{1,0:T(8,128)(2,1)} %get-tuple-element.65.refs_5_), channel_id=1, source_target_pairs={{0,1},{1,0},{2,3},{3,2},{4,5},{5,4},{6,7},{7,6},{8,9},{9,8},{10,11... | collective-permute-start | bytes 1572872 | tf_op jit(solution)/shard_map/ppermute | solution.py:283
  82.8 9.3 %collective-permute-start.7 = (bf16[16,1024]{1,0:T(8,128)(2,1)S(1)}, bf16[16,1024]{1,0:T(8,128)(2,1)S(1)}, u32[]{:S(2)}, u32[]{:S(2)}) collective-permute-start(bf16[16,1024]{1,0:T(8,128)(2,1)S(1)} %get-tuple-element.58), channel_id=1, source_target_pairs={{6,0},{7,1},{0,2},{1,3},{2,4},{3,5},{4,6},{5,7},{14,8},{15,9},{8,1... | collective-permute-start | bytes 98312 | tf_op jit(solution)/shard_map/ppermute | solution.py:293
  85.9 7.9 %collective-permute-start.8 = (bf16[16,1024]{1,0:T(8,128)(2,1)S(1)}, bf16[16,1024]{1,0:T(8,128)(2,1)S(1)}, u32[]{:S(2)}, u32[]{:S(2)}) collective-permute-start(bf16[16,1024]{1,0:T(8,128)(2,1)S(1)} %get-tuple-element.59), channel_id=1, source_target_pairs={{4,0},{5,1},{6,2},{7,3},{0,4},{1,5},{2,6},{3,7},{12,8},{13,9},{14,... | collective-permute-start | bytes 98312 | tf_op jit(solution)/shard_map/ppermute | solution.py:293
  88.6 5.5 %collective-permute-start.9 = (bf16[16,1024]{1,0:T(8,128)(2,1)S(1)}, bf16[16,1024]{1,0:T(8,128)(2,1)S(1)}, u32[]{:S(2)}, u32[]{:S(2)}) collective-permute-start(bf16[16,1024]{1,0:T(8,128)(2,1)S(1)} %get-tuple-element.60), channel_id=1, source_target_pairs={{2,0},{3,1},{4,2},{5,3},{6,4},{7,5},{0,6},{1,7},{10,8},{11,9},{12,... | collective-permute-start | bytes 98312 | tf_op jit(solution)/shard_map/ppermute | solution.py:293
  94.8 7.8 %collective-permute-start.13 = (bf16[16,1024]{1,0:T(8,128)(2,1)S(1)}, bf16[16,1024]{1,0:T(8,128)(2,1)S(1)}, u32[]{:S(2)}, u32[]{:S(2)}) collective-permute-start(bf16[16,1024]{1,0:T(8,128)(2,1)S(1)} %get-tuple-element.64.refs_0_), channel_id=1, source_target_pairs={{6,0},{7,1},{0,2},{1,3},{2,4},{3,5},{4,6},{5,7},{14,8},{15,9},{8,1... | collective-permute-start | bytes 98312 | tf_op jit(solution)/shard_map/ppermute | solution.py:293
  97.2 7.8 %collective-permute-start.12 = (bf16[16,1024]{1,0:T(8,128)(2,1)S(1)}, bf16[16,1024]{1,0:T(8,128)(2,1)S(1)}, u32[]{:S(2)}, u32[]{:S(2)}) collective-permute-start(bf16[16,1024]{1,0:T(8,128)(2,1)S(1)} %get-tuple-element.64.refs_0_), channel_id=1, source_target_pairs={{4,0},{5,1},{6,2},{7,3},{0,4},{1,5},{2,6},{3,7},{12,8},{13,9},{14,... | collective-permute-start | bytes 98312 | tf_op jit(solution)/shard_map/ppermute | solution.py:293
  101.6 5.0 %collective-permute-start.11 = (bf16[16,1024]{1,0:T(8,128)(2,1)S(1)}, bf16[16,1024]{1,0:T(8,128)(2,1)S(1)}, u32[]{:S(2)}, u32[]{:S(2)}) collective-permute-start(bf16[16,1024]{1,0:T(8,128)(2,1)S(1)} %get-tuple-element.64.refs_0_), channel_id=1, source_target_pairs={{2,0},{3,1},{4,2},{5,3},{6,4},{7,5},{0,6},{1,7},{10,8},{11,9},{12,... | collective-permute-start | bytes 98312 | tf_op jit(solution)/shard_map/ppermute | solution.py:293
  106.6 5.0 %collective-permute-start.16 = (bf16[64,1024]{1,0:T(8,128)(2,1)S(1)}, bf16[64,1024]{1,0:T(8,128)(2,1)S(1)}, u32[]{:S(2)}, u32[]{:S(2)}) collective-permute-start(bf16[64,1024]{1,0:T(8,128)(2,1)S(1)} %shard_map.116.refs_0_), channel_id=1, source_target_pairs={{24,0},{25,1},{26,2},{27,3},{28,4},{29,5},{30,6},{31,7},{0,8},{1,9... | collective-permute-start | bytes 393224 | tf_op jit(solution)/shard_map/ppermute | solution.py:293
  107.2 6.5 %collective-permute-start.15 = (bf16[64,1024]{1,0:T(8,128)(2,1)S(1)}, bf16[64,1024]{1,0:T(8,128)(2,1)S(1)}, u32[]{:S(2)}, u32[]{:S(2)}) collective-permute-start(bf16[64,1024]{1,0:T(8,128)(2,1)S(1)} %shard_map.116.refs_0_), channel_id=1, source_target_pairs={{16,0},{17,1},{18,2},{19,3},{20,4},{21,5},{22,6},{23,7},{24,8},{25... | collective-permute-start | bytes 393224 | tf_op jit(solution)/shard_map/ppermute | solution.py:293
  109.1 6.2 %collective-permute-start.14 = (bf16[64,1024]{1,0:T(8,128)(2,1)S(1)}, bf16[64,1024]{1,0:T(8,128)(2,1)S(1)}, u32[]{:S(2)}, u32[]{:S(2)}) collective-permute-start(bf16[64,1024]{1,0:T(8,128)(2,1)S(1)} %shard_map.116.refs_0_), channel_id=1, source_target_pairs={{8,0},{9,1},{10,2},{11,3},{12,4},{13,5},{14,6},{15,7},{16,8},{17,9... | collective-permute-start | bytes 393224 | tf_op jit(solution)/shard_map/ppermute | solution.py:293
  115.2 27.2 %copy-start.13 = (bf16[1024,512]{1,0:T(8,128)(2,1)S(1)}, bf16[1024,512]{1,0:T(8,128)(2,1)}, u32[]{:S(2)}) copy-start(bf16[1024,512]{1,0:T(8,128)(2,1)} %copy-done.11) | copy-start | bytes 3145732
  116.0 26.4 %copy-start.10 = (bf16[1024,512]{1,0:T(8,128)(2,1)S(1)}, bf16[1024,512]{1,0:T(8,128)(2,1)}, u32[]{:S(2)}) copy-start(bf16[1024,512]{1,0:T(8,128)(2,1)} %copy-done.8) | copy-start | bytes 3145732
  127.9 14.6 %copy-start.4 = (bf16[1024,512]{1,0:T(8,128)(2,1)S(1)}, bf16[1024,512]{1,0:T(8,128)(2,1)}, u32[]{:S(2)}) copy-start(bf16[1024,512]{1,0:T(8,128)(2,1)} %copy-done.2) | copy-start | bytes 3145732
  141.9 5.1 %collective-permute-start.18 = (bf16[256,2048]{1,0:T(8,128)(2,1)S(1)}, bf16[256,2048]{1,0:T(8,128)(2,1)S(1)}, u32[]{:S(2)}, u32[]{:S(2)}) collective-permute-start(bf16[256,2048]{1,0:T(8,128)(2,1)S(1)} %bitcast.8), channel_id=1, source_target_pairs={{0,1},{1,0},{2,3},{3,2},{4,5},{5,4},{6,7},{7,6},{8,9},{9,8},{10,11... | collective-permute-start | bytes 3145736 | tf_op jit(solution)/shard_map/ppermute | solution.py:283
  141.9 4.2 %collective-permute-start.19 = (bf16[256,1024]{1,0:T(8,128)(2,1)S(1)}, bf16[256,1024]{1,0:T(8,128)(2,1)S(1)}, u32[]{:S(2)}, u32[]{:S(2)}) collective-permute-start(bf16[256,1024]{1,0:T(8,128)(2,1)S(1)} %get-tuple-element.69.refs_7_), channel_id=1, source_target_pairs={{0,1},{1,0},{2,3},{3,2},{4,5},{5,4},{6,7},{7,6},{8,9},{9,8},{10,11... | collective-permute-start | bytes 1572872 | tf_op jit(solution)/shard_map/ppermute | solution.py:283
  142.4 4.5 %collective-permute-start.20 = (f32[8,128]{1,0:T(8,128)S(1)}, f32[8,128]{1,0:T(8,128)S(1)}, u32[]{:S(2)}, u32[]{:S(2)}) collective-permute-start(f32[8,128]{1,0:T(8,128)S(1)} %get-tuple-element.70.refs_9_), channel_id=1, source_target_pairs={{0,1},{1,0},{2,3},{3,2},{4,5},{5,4},{6,7},{7,6},{8,9},{9,8},{10,11... | collective-permute-start | bytes 12296 | tf_op jit(solution)/shard_map/ppermute | solution.py:283
  143.8 7.4 %collective-permute-start.21 = (bf16[64,1024]{1,0:T(8,128)(2,1)S(1)}, bf16[64,1024]{1,0:T(8,128)(2,1)S(1)}, u32[]{:S(2)}, u32[]{:S(2)}) collective-permute-start(bf16[64,1024]{1,0:T(8,128)(2,1)S(1)} %get-tuple-element.76), channel_id=1, source_target_pairs={{24,0},{25,1},{26,2},{27,3},{28,4},{29,5},{30,6},{31,7},{0,8},{1,9... | collective-permute-start | bytes 393224 | tf_op jit(solution)/shard_map/ppermute | solution.py:293
  144.9 7.8 %collective-permute-start.22 = (bf16[64,1024]{1,0:T(8,128)(2,1)S(1)}, bf16[64,1024]{1,0:T(8,128)(2,1)S(1)}, u32[]{:S(2)}, u32[]{:S(2)}) collective-permute-start(bf16[64,1024]{1,0:T(8,128)(2,1)S(1)} %get-tuple-element.77), channel_id=1, source_target_pairs={{16,0},{17,1},{18,2},{19,3},{20,4},{21,5},{22,6},{23,7},{24,8},{25... | collective-permute-start | bytes 393224 | tf_op jit(solution)/shard_map/ppermute | solution.py:293
  146.1 8.8 %collective-permute-start.23 = (bf16[64,1024]{1,0:T(8,128)(2,1)S(1)}, bf16[64,1024]{1,0:T(8,128)(2,1)S(1)}, u32[]{:S(2)}, u32[]{:S(2)}) collective-permute-start(bf16[64,1024]{1,0:T(8,128)(2,1)S(1)} %get-tuple-element.78), channel_id=1, source_target_pairs={{8,0},{9,1},{10,2},{11,3},{12,4},{13,5},{14,6},{15,7},{16,8},{17,9... | collective-permute-start | bytes 393224 | tf_op jit(solution)/shard_map/ppermute | solution.py:293
  154.9 7.1 %collective-permute-start.24 = (bf16[16,1024]{1,0:T(8,128)(2,1)S(1)}, bf16[16,1024]{1,0:T(8,128)(2,1)S(1)}, u32[]{:S(2)}, u32[]{:S(2)}) collective-permute-start(bf16[16,1024]{1,0:T(8,128)(2,1)S(1)} %get-tuple-element.81), channel_id=1, source_target_pairs={{6,0},{7,1},{0,2},{1,3},{2,4},{3,5},{4,6},{5,7},{14,8},{15,9},{8,1... | collective-permute-start | bytes 98312 | tf_op jit(solution)/shard_map/ppermute | solution.py:293
  156.1 7.9 %collective-permute-start.25 = (bf16[16,1024]{1,0:T(8,128)(2,1)S(1)}, bf16[16,1024]{1,0:T(8,128)(2,1)S(1)}, u32[]{:S(2)}, u32[]{:S(2)}) collective-permute-start(bf16[16,1024]{1,0:T(8,128)(2,1)S(1)} %get-tuple-element.82), channel_id=1, source_target_pairs={{4,0},{5,1},{6,2},{7,3},{0,4},{1,5},{2,6},{3,7},{12,8},{13,9},{14,... | collective-permute-start | bytes 98312 | tf_op jit(solution)/shard_map/ppermute | solution.py:293
  160.7 5.2 %collective-permute-start.26 = (bf16[16,1024]{1,0:T(8,128)(2,1)S(1)}, bf16[16,1024]{1,0:T(8,128)(2,1)S(1)}, u32[]{:S(2)}, u32[]{:S(2)}) collective-permute-start(bf16[16,1024]{1,0:T(8,128)(2,1)S(1)} %get-tuple-element.83), channel_id=1, source_target_pairs={{2,0},{3,1},{4,2},{5,3},{6,4},{7,5},{0,6},{1,7},{10,8},{11,9},{12,... | collective-permute-start | bytes 98312 | tf_op jit(solution)/shard_map/ppermute | solution.py:293
  (22 other events, 75.6 us)

commit v6 on v3

--- a/solution.py
+++ b/solution.py
@@ -67,18 +67,36 @@
 
 
 def gate_up_kernel(mask_ref, mask_other_ref, chips_ref, *refs):
-    weights, kept_refs, (out_ref, rows_ref) = refs[:4], refs[4:8], refs[8:]
+    weights, kept_refs, (out_ref, rows_ref, scratch, sems) = list(refs[:4]), refs[4:8], refs[8:]
     chip = lax.axis_index("col") // CORES
     size = chips_ref.shape[1]
+    pairs = [(weights[2], scratch)]
     for part in range(CHIPS):
         x = lax.rem(chip // Z + part // Z, X)
         z = lax.rem(chip + part % Z, Z)
-        rows_ref[pl.ds(part * size, size), :] = chips_ref[x * Z + z]
-    for which, (ref, kept_ref) in enumerate(zip(weights, kept_refs)):
-        units = ref.shape[1]
-        keep((mask_ref, mask_other_ref)[which % 2], which // 2, ref, kept_ref)
-        value = plain_dot(rows_ref[...], kept_ref[...])
+        pairs.append((chips_ref.at[x * Z + z], rows_ref.at[pl.ds(part * size, size), :]))
+    copies = [pltpu.make_async_copy(src, dst, sems.at[at]) for at, (src, dst) in enumerate(pairs)]
+    for copy in copies[1:] + copies[:1]:
+        copy.start()
+    weights[2] = scratch
+
+    def masked(which):
+        keep((mask_ref, mask_other_ref)[which % 2], which // 2, weights[which], kept_refs[which])
+
+    def multiplied(which):
+        units = scratch.shape[1]
+        value = plain_dot(rows_ref[...], kept_refs[which][...])
         out_ref[:, pl.ds(which * units, units)] = value.astype(out_ref.dtype)
+
+    for which in (0, 1, 3):
+        masked(which)
+    for copy in copies[1:]:
+        copy.wait()
+    for which in (0, 1, 3):
+        multiplied(which)
+    copies[0].wait()
+    masked(2)
+    multiplied(2)
 
 
 def put_slabs(out_refs, cols, value):
@@ -279,6 +297,10 @@
     return lax.all_to_all(value, "row", 0, 0)
 
 
+def in_hbm(value):
+    return pltpu.with_memory_space_constraint(value, pltpu.HBM)
+
+
 def flat(value):
     return value.reshape((-1,) + value.shape[2:])
 
@@ -302,13 +324,19 @@
     )
     copies = jnp.broadcast_to(inputs[None], (CHIPS, tokens, width))
     chips = lax.all_to_all(copies, "col", 0, 0, axis_index_groups=SAME_CORE)
-    *gate_ups, partial, rows = multiply(
+    *gate_ups, partial, rows = call(
         gate_up_kernel,
         (wide,) * 4 + (shaped((half, 4 * units)), shaped((half, width))),
-        [chips],
-        gates + ups,
-        masks,
-        downs[1:],
+        *masks,
+        in_hbm(chips),
+        *gates,
+        in_hbm(ups[0]),
+        ups[1],
+        in_specs=[SMEM] * 2 + [ANY] + [VMEM] * 2 + [ANY, VMEM],
+        scratch_shapes=[pltpu.VMEM(wide.shape, wide.dtype), pltpu.SemaphoreType.DMA((CHIPS + 1,))],
+        flops=8 * half * width * units,
+        vmem=16,
+        after=downs[1:],
     )
     both, copies = call(
         hidden_kernel,

time: 167 us -> 167 us (level)
  no operation moved by 1% of the time
where the time goes in v6:
time: 167 us; the launch traced here: 165 us
  blocking collectives  59.2 us (35%)
  waiting for transfers between devices  46.1 us (28%)
  starting transfers between devices  44.3 us (27%)
  Pallas kernels  13.5 us (8%)
    all_to_all x4, blocking collectives, exchange_row(): return lax.all_to_all(value, 'row', 0, 0)  59.2 us
    ppermute x18, starting transfers between devices, fetch(): return lax.ppermute(value, 'col', pairs)  31 us
    ppermute x18, waiting for transfers between devices, fetch(): return lax.ppermute(value, 'col', pairs)  27.6 us
    all_to_all x1, waiting for transfers between devices, per_device(): chips = lax.all_to_all(copies, 'col', 0, 0, axis_index_groups=SAME_CORE)  16.3 us
    pallas_call x12, Pallas kernels, call(): pl.pallas_call(lambda *refs: kernel(*refs[:len(args)], *refs[len(args) +...  13.5 us
    all_to_all x1, starting transfers between devices, per_device(): chips = lax.all_to_all(copies, 'col', 0, 0, axis_index_groups=SAME_CORE)  11.6 us
  transfers between devices with their start and end apart: 28, of which 16 were waited for; matrix products, arithmetic and copies ran while one was open for 1% of the time, Pallas kernels for 3%

profile of v6, /device:TPU:6, one launch (start us, length us, event | category | flops | bytes accessed | tf_op | source)
XLA Modules:
  0.0 165.5 jit_solution(8174378537649718314)
XLA Ops:
  1.3 1.6 broadcast_in_dim.2
  3.0 11.6 %all-to-all-start = ((bf16[16,16,1024]{2,1,0:T(8,128)(2,1)}), bf16[16,16,1024]{2,1,0:T(8,128)(2,1)}, u32[]{:S(2)}, u32[]{:S(2)}) async-start(bf16[16,16,1024]{2,1,0:T(8,128)(2,1)} %broadcast_in_dim.2), calls=%async_computation | async-start | bytes 1048576 | tf_op jit(solution)/shard_map/all_to_all | solution.py:326
  14.6 1.2 collective-permute-done.refs_1_
  15.8 16.3 %all-to-all-done.refs_2_ = bf16[16,16,1024]{2,1,0:T(8,128)(2,1)} async-done(((bf16[16,16,1024]{2,1,0:T(8,128)(2,1)}), bf16[16,16,1024]{2,1,0:T(8,128)(2,1)}, u32[]{:S(2)}, u32[]{:S(2)}) %all-to-all-start) | async-done | bytes 524320 | tf_op jit(solution)/shard_map/all_to_all | solution.py:326
  32.1 4.0 %shard_map.109 = (bf16[1024,512]{1,0:T(8,128)(2,1)S(1)}, bf16[1024,512]{1,0:T(8,128)(2,1)S(1)}, bf16[1024,512]{1,0:T(8,128)(2,1)S(1)}, bf16[1024,512]{1,0:T(8,12...) custom-call(s32[3,4,8]{2,1,0:T(4,128)S(1)} %bitcast.15, ...), custom_call_target="tpu_custom_call" | custom-call | flops 1073741824 | bytes 10486528 | tf_op jit(solution)/shard_map/pallas_call | solution.py:26
  36.0 18.5 %all_to_all.25.refs_0_ = bf16[8,32,2048]{2,1,0:T(8,128)(2,1)S(1)} all-to-all(bf16[8,32,2048]{2,1,0:T(8,128)(2,1)S(1)} %bitcast.12), channel_id=1, replica_groups=mesh['row'=8,'col'=32] {'row'}, dimensions={0} | all-to-all | bytes 2097152 | tf_op jit(solution)/shard_map/all_to_all | solution.py:297
  54.7 11.3 %all_to_all.26 = bf16[8,32,1024]{2,1,0:T(8,128)(2,1)S(1)} all-to-all(bf16[8,32,1024]{2,1,0:T(8,128)(2,1)S(1)} %get-tuple-element.44), channel_id=1, replica_groups=mesh['row'=8,'col'=32] {'row'}, dimensions={0} | all-to-all | bytes 1048576 | tf_op jit(solution)/shard_map/all_to_all | solution.py:297
  65.9 1.6 shard_map.111
  67.5 2.5 %collective-permute-start.4 = (bf16[64,1024]{1,0:T(8,128)(2,1)S(1)}, bf16[64,1024]{1,0:T(8,128)(2,1)S(1)}, u32[]{:S(2)}, u32[]{:S(2)}) collective-permute-start(bf16[64,1024]{1,0:T(8,128)(2,1)S(1)} %get-tuple-element.46), channel_id=1, source_target_pairs={{24,0},{25,1},{26,2},{27,3},{28,4},{29,5},{30,6},{31,7},{0,8},{1,9... | collective-permute-start | bytes 393224 | tf_op jit(solution)/shard_map/ppermute | solution.py:272
  70.9 3.0 %collective-permute-done.4.refs_1_ = bf16[64,1024]{1,0:T(8,128)(2,1)S(1)} collective-permute-done((bf16[64,1024]{1,0:T(8,128)(2,1)S(1)}, bf16[64,1024]{1,0:T(8,128)(2,1)S(1)}, u32[]{:S(2)}, u32[]{:S(2)}) %collective-permute-start.4) | collective-permute-done | bytes 131104 | tf_op jit(solution)/shard_map/ppermute | solution.py:272
  73.9 2.7 %collective-permute-done.5.refs_2_ = bf16[64,1024]{1,0:T(8,128)(2,1)S(1)} collective-permute-done((bf16[64,1024]{1,0:T(8,128)(2,1)S(1)}, bf16[64,1024]{1,0:T(8,128)(2,1)S(1)}, u32[]{:S(2)}, u32[]{:S(2)}) %collective-permute-start.5) | collective-permute-done | bytes 131104 | tf_op jit(solution)/shard_map/ppermute | solution.py:272
  76.5 1.3 collective-permute-done.6.refs_3_
  77.8 3.2 %collective-permute-start.7 = (bf16[16,1024]{1,0:T(8,128)(2,1)S(1)}, bf16[16,1024]{1,0:T(8,128)(2,1)S(1)}, u32[]{:S(2)}, u32[]{:S(2)}) collective-permute-start(bf16[16,1024]{1,0:T(8,128)(2,1)S(1)} %get-tuple-element.50), channel_id=1, source_target_pairs={{6,0},{7,1},{0,2},{1,3},{2,4},{3,5},{4,6},{5,7},{14,8},{15,9},{8,1... | collective-permute-start | bytes 98312 | tf_op jit(solution)/shard_map/ppermute | solution.py:272
  81.4 3.3 %collective-permute-start.9 = (bf16[16,1024]{1,0:T(8,128)(2,1)S(1)}, bf16[16,1024]{1,0:T(8,128)(2,1)S(1)}, u32[]{:S(2)}, u32[]{:S(2)}) collective-permute-start(bf16[16,1024]{1,0:T(8,128)(2,1)S(1)} %get-tuple-element.52), channel_id=1, source_target_pairs={{2,0},{3,1},{4,2},{5,3},{6,4},{7,5},{0,6},{1,7},{10,8},{11,9},{12,... | collective-permute-start | bytes 98312 | tf_op jit(solution)/shard_map/ppermute | solution.py:272
  84.7 4.1 %collective-permute-done.8.refs_3_ = bf16[16,1024]{1,0:T(8,128)(2,1)S(1)} collective-permute-done((bf16[16,1024]{1,0:T(8,128)(2,1)S(1)}, bf16[16,1024]{1,0:T(8,128)(2,1)S(1)}, u32[]{:S(2)}, u32[]{:S(2)}) %collective-permute-start.8) | collective-permute-done | bytes 32800 | tf_op jit(solution)/shard_map/ppermute | solution.py:272
  89.5 2.7 %collective-permute-start.11 = (bf16[16,1024]{1,0:T(8,128)(2,1)S(1)}, bf16[16,1024]{1,0:T(8,128)(2,1)S(1)}, u32[]{:S(2)}, u32[]{:S(2)}) collective-permute-start(bf16[16,1024]{1,0:T(8,128)(2,1)S(1)} %get-tuple-element.55.refs_0_), channel_id=1, source_target_pairs={{2,0},{3,1},{4,2},{5,3},{6,4},{7,5},{0,6},{1,7},{10,8},{11,9},{12,... | collective-permute-start | bytes 98312 | tf_op jit(solution)/shard_map/ppermute | solution.py:272
  92.2 2.9 %collective-permute-start.12 = (bf16[16,1024]{1,0:T(8,128)(2,1)S(1)}, bf16[16,1024]{1,0:T(8,128)(2,1)S(1)}, u32[]{:S(2)}, u32[]{:S(2)}) collective-permute-start(bf16[16,1024]{1,0:T(8,128)(2,1)S(1)} %get-tuple-element.55.refs_0_), channel_id=1, source_target_pairs={{4,0},{5,1},{6,2},{7,3},{0,4},{1,5},{2,6},{3,7},{12,8},{13,9},{14,... | collective-permute-start | bytes 98312 | tf_op jit(solution)/shard_map/ppermute | solution.py:272
  95.7 4.3 %collective-permute-done.12.refs_2_ = bf16[16,1024]{1,0:T(8,128)(2,1)S(1)} collective-permute-done((bf16[16,1024]{1,0:T(8,128)(2,1)S(1)}, bf16[16,1024]{1,0:T(8,128)(2,1)S(1)}, u32[]{:S(2)}, u32[]{:S(2)}) %collective-permute-start.12) | collective-permute-done | bytes 32800 | tf_op jit(solution)/shard_map/ppermute | solution.py:272
  100.0 1.1 collective-permute-done.13.refs_3_
  101.4 2.3 %collective-permute-start.15 = (bf16[64,1024]{1,0:T(8,128)(2,1)S(1)}, bf16[64,1024]{1,0:T(8,128)(2,1)S(1)}, u32[]{:S(2)}, u32[]{:S(2)}) collective-permute-start(bf16[64,1024]{1,0:T(8,128)(2,1)S(1)} %shard_map.114.refs_0_), channel_id=1, source_target_pairs={{16,0},{17,1},{18,2},{19,3},{20,4},{21,5},{22,6},{23,7},{24,8},{25... | collective-permute-start | bytes 393224 | tf_op jit(solution)/shard_map/ppermute | solution.py:272
  104.8 4.2 %collective-permute-done.14.refs_1_ = bf16[64,1024]{1,0:T(8,128)(2,1)S(1)} collective-permute-done((bf16[64,1024]{1,0:T(8,128)(2,1)S(1)}, bf16[64,1024]{1,0:T(8,128)(2,1)S(1)}, u32[]{:S(2)}, u32[]{:S(2)}) %collective-permute-start.14) | collective-permute-done | bytes 131104 | tf_op jit(solution)/shard_map/ppermute | solution.py:272
  110.6 14.5 %all_to_all.27.refs_0_ = bf16[8,32,1152]{2,1,0:T(8,128)(2,1)S(1)} all-to-all(bf16[8,32,1152]{2,1,0:T(8,128)(2,1)S(1)} %bitcast.13), channel_id=1, replica_groups=mesh['row'=8,'col'=32] {'row'}, dimensions={0} | all-to-all | bytes 1179648 | tf_op jit(solution)/shard_map/all_to_all | solution.py:297
  125.3 15.0 %all_to_all.28 = bf16[8,32,2048]{2,1,0:T(8,128)(2,1)S(1)} all-to-all(bf16[8,32,2048]{2,1,0:T(8,128)(2,1)S(1)} %get-tuple-element.60), channel_id=1, replica_groups=mesh['row'=8,'col'=32] {'row'}, dimensions={0} | all-to-all | bytes 2097152 | tf_op jit(solution)/shard_map/all_to_all | solution.py:297
  141.3 1.3 shard_map.118
  143.7 2.3 %collective-permute-start.21 = (bf16[64,1024]{1,0:T(8,128)(2,1)S(1)}, bf16[64,1024]{1,0:T(8,128)(2,1)S(1)}, u32[]{:S(2)}, u32[]{:S(2)}) collective-permute-start(bf16[64,1024]{1,0:T(8,128)(2,1)S(1)} %get-tuple-element.72), channel_id=1, source_target_pairs={{24,0},{25,1},{26,2},{27,3},{28,4},{29,5},{30,6},{31,7},{0,8},{1,9... | collective-permute-start | bytes 393224 | tf_op jit(solution)/shard_map/ppermute | solution.py:272
  146.4 1.3 collective-permute-start.23
  147.7 4.2 %shard_map.117 = (bf16[1024,512]{1,0:T(8,128)(2,1)}, bf16[1024,512]{1,0:T(8,128)(2,1)}, bf16[512,1024]{1,0:T(8,128)(2,1)}, f32[1,1]{1,0:T(1,128)}, f32[8,128]{1,0:T(8,128)S(1)}) custom-call(s32[3,4,8]{2,1,0:T(4,128)S(1)} %bitcast.17, bf16[256,1024]{1,0:T(8,128)(2,1)S(1)} %get-tuple-element.54.refs_1_, bf16[256,1024]{1,0:T(8,128)(2,1)S(1)} %collective-permute-done.10.refs_2_, ...), custom_call_target="tpu_custom_call" | custom-call | flops 1610612736 | bytes 8401284 | tf_op jit(solution)/shard_map/pallas_call | solution.py:26
  152.0 2.0 %collective-permute-done.22.refs_2_ = bf16[64,1024]{1,0:T(8,128)(2,1)S(1)} collective-permute-done((bf16[64,1024]{1,0:T(8,128)(2,1)S(1)}, bf16[64,1024]{1,0:T(8,128)(2,1)S(1)}, u32[]{:S(2)}, u32[]{:S(2)}) %collective-permute-start.22) | collective-permute-done | bytes 131104 | tf_op jit(solution)/shard_map/ppermute | solution.py:272
  153.9 1.5 collective-permute-done.23.refs_3_
  155.6 3.0 %collective-permute-start.25 = (bf16[16,1024]{1,0:T(8,128)(2,1)S(1)}, bf16[16,1024]{1,0:T(8,128)(2,1)S(1)}, u32[]{:S(2)}, u32[]{:S(2)}) collective-permute-start(bf16[16,1024]{1,0:T(8,128)(2,1)S(1)} %get-tuple-element.78), channel_id=1, source_target_pairs={{4,0},{5,1},{6,2},{7,3},{0,4},{1,5},{2,6},{3,7},{12,8},{13,9},{14,... | collective-permute-start | bytes 98312 | tf_op jit(solution)/shard_map/ppermute | solution.py:272
  158.6 3.8 %collective-permute-start.26 = (bf16[16,1024]{1,0:T(8,128)(2,1)S(1)}, bf16[16,1024]{1,0:T(8,128)(2,1)S(1)}, u32[]{:S(2)}, u32[]{:S(2)}) collective-permute-start(bf16[16,1024]{1,0:T(8,128)(2,1)S(1)} %get-tuple-element.79), channel_id=1, source_target_pairs={{2,0},{3,1},{4,2},{5,3},{6,4},{7,5},{0,6},{1,7},{10,8},{11,9},{12,... | collective-permute-start | bytes 98312 | tf_op jit(solution)/shard_map/ppermute | solution.py:272
  163.5 1.4 collective-permute-done.26.refs_3_
  (49 shorter events, 11.1 us)
Async XLA Ops:
  0.6 31.4 %copy-start = (bf16[1024,512]{1,0:T(8,128)(2,1)S(1)}, bf16[1024,512]{1,0:T(8,128)(2,1)}, u32[]{:S(2)}) copy-start(bf16[1024,512]{1,0:T(8,128)(2,1)} %refs_3_.2) | copy-start | bytes 3145732
  0.6 31.4 %collective-permute-start.3 = (bf16[512,1024]{1,0:T(8,128)(2,1)}, bf16[512,1024]{1,0:T(8,128)(2,1)S(1)}, u32[]{:S(2)}, u32[]{:S(2)}) collective-permute-start(bf16[512,1024]{1,0:T(8,128)(2,1)} %refs_3_.3), channel_id=1, source_target_pairs={{0,1},{1,0},{2,3},{3,2},{4,5},{5,4},{6,7},{7,6},{8,9},{9,8},{10,11... | collective-permute-start | bytes 3145736 | tf_op jit(solution)/shard_map/ppermute | solution.py:262
  0.7 31.3 %collective-permute-start.1 = (bf16[1024,512]{1,0:T(8,128)(2,1)}, bf16[1024,512]{1,0:T(8,128)(2,1)S(1)}, u32[]{:S(2)}, u32[]{:S(2)}) collective-permute-start(bf16[1024,512]{1,0:T(8,128)(2,1)} %refs_3_.2), channel_id=1, source_target_pairs={{0,1},{1,0},{2,3},{3,2},{4,5},{5,4},{6,7},{7,6},{8,9},{9,8},{10,11... | collective-permute-start | bytes 3145736 | tf_op jit(solution)/shard_map/ppermute | solution.py:262
  1.2 30.8 %collective-permute-start.2 = (bf16[1024,512]{1,0:T(8,128)(2,1)}, bf16[1024,512]{1,0:T(8,128)(2,1)}, u32[]{:S(2)}, u32[]{:S(2)}) collective-permute-start(bf16[1024,512]{1,0:T(8,128)(2,1)} %refs_5_.1), channel_id=1, source_target_pairs={{0,1},{1,0},{2,3},{3,2},{4,5},{5,4},{6,7},{7,6},{8,9},{9,8},{10,11... | collective-permute-start | bytes 3145736 | tf_op jit(solution)/shard_map/ppermute | solution.py:262
  3.0 11.6 %copy-start.3 = (s32[3,8,4]{1,2,0:T(4,128)S(1)}, s32[3,8,4]{1,2,0:T(4,128)}, u32[]{:S(2)}) copy-start(s32[3,8,4]{1,2,0:T(4,128)} %param.11) | copy-start | bytes 1156
  3.0 29.1 %all-to-all-start = ((bf16[16,16,1024]{2,1,0:T(8,128)(2,1)}), bf16[16,16,1024]{2,1,0:T(8,128)(2,1)}, u32[]{:S(2)}, u32[]{:S(2)}) async-start(bf16[16,16,1024]{2,1,0:T(8,128)(2,1)} %broadcast_in_dim.2), calls=%async_computation | async-start | bytes 1048576 | tf_op jit(solution)/shard_map/all_to_all | solution.py:326
  14.5 1.3 collective-permute-start
  54.5 11.4 %copy-start.1 = (bf16[512,1024]{1,0:T(8,128)(2,1)S(1)}, bf16[512,1024]{1,0:T(8,128)(2,1)}, u32[]{:S(2)}) copy-start(bf16[512,1024]{1,0:T(8,128)(2,1)} %refs_3_.3) | copy-start | bytes 3145732
  67.5 6.4 %collective-permute-start.4 = (bf16[64,1024]{1,0:T(8,128)(2,1)S(1)}, bf16[64,1024]{1,0:T(8,128)(2,1)S(1)}, u32[]{:S(2)}, u32[]{:S(2)}) collective-permute-start(bf16[64,1024]{1,0:T(8,128)(2,1)S(1)} %get-tuple-element.46), channel_id=1, source_target_pairs={{24,0},{25,1},{26,2},{27,3},{28,4},{29,5},{30,6},{31,7},{0,8},{1,9... | collective-permute-start | bytes 393224 | tf_op jit(solution)/shard_map/ppermute | solution.py:272
  69.9 6.6 %collective-permute-start.5 = (bf16[64,1024]{1,0:T(8,128)(2,1)S(1)}, bf16[64,1024]{1,0:T(8,128)(2,1)S(1)}, u32[]{:S(2)}, u32[]{:S(2)}) collective-permute-start(bf16[64,1024]{1,0:T(8,128)(2,1)S(1)} %get-tuple-element.47), channel_id=1, source_target_pairs={{16,0},{17,1},{18,2},{19,3},{20,4},{21,5},{22,6},{23,7},{24,8},{25... | collective-permute-start | bytes 393224 | tf_op jit(solution)/shard_map/ppermute | solution.py:272
  70.2 7.6 %collective-permute-start.6 = (bf16[64,1024]{1,0:T(8,128)(2,1)S(1)}, bf16[64,1024]{1,0:T(8,128)(2,1)S(1)}, u32[]{:S(2)}, u32[]{:S(2)}) collective-permute-start(bf16[64,1024]{1,0:T(8,128)(2,1)S(1)} %get-tuple-element.48), channel_id=1, source_target_pairs={{8,0},{9,1},{10,2},{11,3},{12,4},{13,5},{14,6},{15,7},{16,8},{17,9... | collective-permute-start | bytes 393224 | tf_op jit(solution)/shard_map/ppermute | solution.py:272
  77.8 11.1 %copy-start.2 = (bf16[16,1024]{1,0:T(8,128)(2,1)S(1)}, bf16[16,1024]{1,0:T(8,128)(2,1)}, u32[]{:S(2)}) copy-start(bf16[16,1024]{1,0:T(8,128)(2,1)} %refs_0_.1) | copy-start | bytes 98308
  77.8 6.8 %collective-permute-start.7 = (bf16[16,1024]{1,0:T(8,128)(2,1)S(1)}, bf16[16,1024]{1,0:T(8,128)(2,1)S(1)}, u32[]{:S(2)}, u32[]{:S(2)}) collective-permute-start(bf16[16,1024]{1,0:T(8,128)(2,1)S(1)} %get-tuple-element.50), channel_id=1, source_target_pairs={{6,0},{7,1},{0,2},{1,3},{2,4},{3,5},{4,6},{5,7},{14,8},{15,9},{8,1... | collective-permute-start | bytes 98312 | tf_op jit(solution)/shard_map/ppermute | solution.py:272
  81.0 7.8 %collective-permute-start.8 = (bf16[16,1024]{1,0:T(8,128)(2,1)S(1)}, bf16[16,1024]{1,0:T(8,128)(2,1)S(1)}, u32[]{:S(2)}, u32[]{:S(2)}) collective-permute-start(bf16[16,1024]{1,0:T(8,128)(2,1)S(1)} %get-tuple-element.51), channel_id=1, source_target_pairs={{4,0},{5,1},{6,2},{7,3},{0,4},{1,5},{2,6},{3,7},{12,8},{13,9},{14,... | collective-permute-start | bytes 98312 | tf_op jit(solution)/shard_map/ppermute | solution.py:272
  81.4 7.5 %collective-permute-start.9 = (bf16[16,1024]{1,0:T(8,128)(2,1)S(1)}, bf16[16,1024]{1,0:T(8,128)(2,1)S(1)}, u32[]{:S(2)}, u32[]{:S(2)}) collective-permute-start(bf16[16,1024]{1,0:T(8,128)(2,1)S(1)} %get-tuple-element.52), channel_id=1, source_target_pairs={{2,0},{3,1},{4,2},{5,3},{6,4},{7,5},{0,6},{1,7},{10,8},{11,9},{12,... | collective-permute-start | bytes 98312 | tf_op jit(solution)/shard_map/ppermute | solution.py:272
  89.5 6.2 %collective-permute-start.11 = (bf16[16,1024]{1,0:T(8,128)(2,1)S(1)}, bf16[16,1024]{1,0:T(8,128)(2,1)S(1)}, u32[]{:S(2)}, u32[]{:S(2)}) collective-permute-start(bf16[16,1024]{1,0:T(8,128)(2,1)S(1)} %get-tuple-element.55.refs_0_), channel_id=1, source_target_pairs={{2,0},{3,1},{4,2},{5,3},{6,4},{7,5},{0,6},{1,7},{10,8},{11,9},{12,... | collective-permute-start | bytes 98312 | tf_op jit(solution)/shard_map/ppermute | solution.py:272
  92.2 7.8 %collective-permute-start.12 = (bf16[16,1024]{1,0:T(8,128)(2,1)S(1)}, bf16[16,1024]{1,0:T(8,128)(2,1)S(1)}, u32[]{:S(2)}, u32[]{:S(2)}) collective-permute-start(bf16[16,1024]{1,0:T(8,128)(2,1)S(1)} %get-tuple-element.55.refs_0_), channel_id=1, source_target_pairs={{4,0},{5,1},{6,2},{7,3},{0,4},{1,5},{2,6},{3,7},{12,8},{13,9},{14,... | collective-permute-start | bytes 98312 | tf_op jit(solution)/shard_map/ppermute | solution.py:272
  95.1 6.0 %collective-permute-start.13 = (bf16[16,1024]{1,0:T(8,128)(2,1)S(1)}, bf16[16,1024]{1,0:T(8,128)(2,1)S(1)}, u32[]{:S(2)}, u32[]{:S(2)}) collective-permute-start(bf16[16,1024]{1,0:T(8,128)(2,1)S(1)} %get-tuple-element.55.refs_0_), channel_id=1, source_target_pairs={{6,0},{7,1},{0,2},{1,3},{2,4},{3,5},{4,6},{5,7},{14,8},{15,9},{8,1... | collective-permute-start | bytes 98312 | tf_op jit(solution)/shard_map/ppermute | solution.py:272
  101.1 7.8 %collective-permute-start.14 = (bf16[64,1024]{1,0:T(8,128)(2,1)S(1)}, bf16[64,1024]{1,0:T(8,128)(2,1)S(1)}, u32[]{:S(2)}, u32[]{:S(2)}) collective-permute-start(bf16[64,1024]{1,0:T(8,128)(2,1)S(1)} %shard_map.114.refs_0_), channel_id=1, source_target_pairs={{8,0},{9,1},{10,2},{11,3},{12,4},{13,5},{14,6},{15,7},{16,8},{17,9... | collective-permute-start | bytes 393224 | tf_op jit(solution)/shard_map/ppermute | solution.py:272
  101.4 7.6 %collective-permute-start.15 = (bf16[64,1024]{1,0:T(8,128)(2,1)S(1)}, bf16[64,1024]{1,0:T(8,128)(2,1)S(1)}, u32[]{:S(2)}, u32[]{:S(2)}) collective-permute-start(bf16[64,1024]{1,0:T(8,128)(2,1)S(1)} %shard_map.114.refs_0_), channel_id=1, source_target_pairs={{16,0},{17,1},{18,2},{19,3},{20,4},{21,5},{22,6},{23,7},{24,8},{25... | collective-permute-start | bytes 393224 | tf_op jit(solution)/shard_map/ppermute | solution.py:272
  103.8 6.1 %collective-permute-start.16 = (bf16[64,1024]{1,0:T(8,128)(2,1)S(1)}, bf16[64,1024]{1,0:T(8,128)(2,1)S(1)}, u32[]{:S(2)}, u32[]{:S(2)}) collective-permute-start(bf16[64,1024]{1,0:T(8,128)(2,1)S(1)} %shard_map.114.refs_0_), channel_id=1, source_target_pairs={{24,0},{25,1},{26,2},{27,3},{28,4},{29,5},{30,6},{31,7},{0,8},{1,9... | collective-permute-start | bytes 393224 | tf_op jit(solution)/shard_map/ppermute | solution.py:272
  140.3 7.4 %collective-permute-start.17 = (bf16[256,2048]{1,0:T(8,128)(2,1)S(1)}, bf16[256,2048]{1,0:T(8,128)(2,1)S(1)}, u32[]{:S(2)}, u32[]{:S(2)}) collective-permute-start(bf16[256,2048]{1,0:T(8,128)(2,1)S(1)} %bitcast.6), channel_id=1, source_target_pairs={{0,1},{1,0},{2,3},{3,2},{4,5},{5,4},{6,7},{7,6},{8,9},{9,8},{10,11... | collective-permute-start | bytes 3145736 | tf_op jit(solution)/shard_map/ppermute | solution.py:262
  140.3 3.4 %collective-permute-start.10 = (bf16[256,1024]{1,0:T(8,128)(2,1)S(1)}, bf16[256,1024]{1,0:T(8,128)(2,1)S(1)}, u32[]{:S(2)}, u32[]{:S(2)}) collective-permute-start(bf16[256,1024]{1,0:T(8,128)(2,1)S(1)} %get-tuple-element.54.refs_1_), channel_id=1, source_target_pairs={{0,1},{1,0},{2,3},{3,2},{4,5},{5,4},{6,7},{7,6},{8,9},{9,8},{10,11... | collective-permute-start | bytes 1572872 | tf_op jit(solution)/shard_map/ppermute | solution.py:262
  140.8 5.2 %collective-permute-start.18 = (bf16[256,1024]{1,0:T(8,128)(2,1)S(1)}, bf16[256,1024]{1,0:T(8,128)(2,1)S(1)}, u32[]{:S(2)}, u32[]{:S(2)}) collective-permute-start(bf16[256,1024]{1,0:T(8,128)(2,1)S(1)} %bitcast.10), channel_id=1, source_target_pairs={{0,1},{1,0},{2,3},{3,2},{4,5},{5,4},{6,7},{7,6},{8,9},{9,8},{10,11... | collective-permute-start | bytes 1572872 | tf_op jit(solution)/shard_map/ppermute | solution.py:262
  140.8 5.6 %collective-permute-start.19 = (bf16[256,1024]{1,0:T(8,128)(2,1)S(1)}, bf16[256,1024]{1,0:T(8,128)(2,1)S(1)}, u32[]{:S(2)}, u32[]{:S(2)}) collective-permute-start(bf16[256,1024]{1,0:T(8,128)(2,1)S(1)} %get-tuple-element.61.refs_7_), channel_id=1, source_target_pairs={{0,1},{1,0},{2,3},{3,2},{4,5},{5,4},{6,7},{7,6},{8,9},{9,8},{10,11... | collective-permute-start | bytes 1572872 | tf_op jit(solution)/shard_map/ppermute | solution.py:262
  141.3 6.3 %collective-permute-start.20 = (f32[8,128]{1,0:T(8,128)S(1)}, f32[8,128]{1,0:T(8,128)S(1)}, u32[]{:S(2)}, u32[]{:S(2)}) collective-permute-start(f32[8,128]{1,0:T(8,128)S(1)} %get-tuple-element.62.refs_9_), channel_id=1, source_target_pairs={{0,1},{1,0},{2,3},{3,2},{4,5},{5,4},{6,7},{7,6},{8,9},{9,8},{10,11... | collective-permute-start | bytes 12296 | tf_op jit(solution)/shard_map/ppermute | solution.py:262
  143.7 8.2 %collective-permute-start.21 = (bf16[64,1024]{1,0:T(8,128)(2,1)S(1)}, bf16[64,1024]{1,0:T(8,128)(2,1)S(1)}, u32[]{:S(2)}, u32[]{:S(2)}) collective-permute-start(bf16[64,1024]{1,0:T(8,128)(2,1)S(1)} %get-tuple-element.72), channel_id=1, source_target_pairs={{24,0},{25,1},{26,2},{27,3},{28,4},{29,5},{30,6},{31,7},{0,8},{1,9... | collective-permute-start | bytes 393224 | tf_op jit(solution)/shard_map/ppermute | solution.py:272
  146.1 7.9 %collective-permute-start.22 = (bf16[64,1024]{1,0:T(8,128)(2,1)S(1)}, bf16[64,1024]{1,0:T(8,128)(2,1)S(1)}, u32[]{:S(2)}, u32[]{:S(2)}) collective-permute-start(bf16[64,1024]{1,0:T(8,128)(2,1)S(1)} %get-tuple-element.73), channel_id=1, source_target_pairs={{16,0},{17,1},{18,2},{19,3},{20,4},{21,5},{22,6},{23,7},{24,8},{25... | collective-permute-start | bytes 393224 | tf_op jit(solution)/shard_map/ppermute | solution.py:272
  146.4 9.0 %collective-permute-start.23 = (bf16[64,1024]{1,0:T(8,128)(2,1)S(1)}, bf16[64,1024]{1,0:T(8,128)(2,1)S(1)}, u32[]{:S(2)}, u32[]{:S(2)}) collective-permute-start(bf16[64,1024]{1,0:T(8,128)(2,1)S(1)} %get-tuple-element.74), channel_id=1, source_target_pairs={{8,0},{9,1},{10,2},{11,3},{12,4},{13,5},{14,6},{15,7},{16,8},{17,9... | collective-permute-start | bytes 393224 | tf_op jit(solution)/shard_map/ppermute | solution.py:272
  155.5 7.0 %collective-permute-start.24 = (bf16[16,1024]{1,0:T(8,128)(2,1)S(1)}, bf16[16,1024]{1,0:T(8,128)(2,1)S(1)}, u32[]{:S(2)}, u32[]{:S(2)}) collective-permute-start(bf16[16,1024]{1,0:T(8,128)(2,1)S(1)} %get-tuple-element.77), channel_id=1, source_target_pairs={{6,0},{7,1},{0,2},{1,3},{2,4},{3,5},{4,6},{5,7},{14,8},{15,9},{8,1... | collective-permute-start | bytes 98312 | tf_op jit(solution)/shard_map/ppermute | solution.py:272
  155.6 7.9 %collective-permute-start.25 = (bf16[16,1024]{1,0:T(8,128)(2,1)S(1)}, bf16[16,1024]{1,0:T(8,128)(2,1)S(1)}, u32[]{:S(2)}, u32[]{:S(2)}) collective-permute-start(bf16[16,1024]{1,0:T(8,128)(2,1)S(1)} %get-tuple-element.78), channel_id=1, source_target_pairs={{4,0},{5,1},{6,2},{7,3},{0,4},{1,5},{2,6},{3,7},{12,8},{13,9},{14,... | collective-permute-start | bytes 98312 | tf_op jit(solution)/shard_map/ppermute | solution.py:272
  158.6 6.2 %collective-permute-start.26 = (bf16[16,1024]{1,0:T(8,128)(2,1)S(1)}, bf16[16,1024]{1,0:T(8,128)(2,1)S(1)}, u32[]{:S(2)}, u32[]{:S(2)}) collective-permute-start(bf16[16,1024]{1,0:T(8,128)(2,1)S(1)} %get-tuple-element.79), channel_id=1, source_target_pairs={{2,0},{3,1},{4,2},{5,3},{6,4},{7,5},{0,6},{1,7},{10,8},{11,9},{12,... | collective-permute-start | bytes 98312 | tf_op jit(solution)/shard_map/ppermute | solution.py:272

commit v7 on v6

--- a/solution.py
+++ b/solution.py
@@ -257,6 +257,22 @@
         copy.wait()
 
 
+def hold_kernel(*refs):
+    pass
+
+
+def hold(values, after):
+    return pl.pallas_call(
+        hold_kernel,
+        out_shape=[shaped(value.shape) for value in values],
+        in_specs=[ANY] * (len(values) + len(after)),
+        out_specs=[ANY] * len(values),
+        input_output_aliases={at: at for at in range(len(values))},
+        compiler_params=pltpu.CompilerParams(vmem_limit_bytes=1 << 20),
+        cost_estimate=pl.CostEstimate(flops=0, bytes_accessed=0, transcendentals=0),
+    )(*values, *after)
+
+
 def other_core(value):
     count = CHIPS * CORES
     return lax.ppermute(value, "col", [(device, device ^ 1) for device in range(count)])
@@ -348,11 +364,14 @@
         output_kernel, (tall,) * 2 + (slab,) * X, [hidden], downs, masks
     )
     slabs = spread_x([first, second, third, fourth])
-    parts = spread_z(call(sum_kernel, (piece,) * Z, *slabs))
+    parts = call(sum_kernel, (piece,) * Z, *slabs)
+    rows, hidden = hold((rows, hidden), parts[:1])
+    rows_other, hidden_other = other_core(rows), other_core(hidden)
+    parts = spread_z(parts)
     student, grad_out = call(functools.partial(error_kernel, scale), (piece, piece), teacher, *parts)
     slabs = gather_x(joined(gather_z(grad_out)))
     partial, grad_rows = multiply(
-        grad_hidden_kernel, (shaped((half, 2 * units + BLK)), shaped((half, width))), slabs, downs
+        grad_hidden_kernel, (shaped((half, 2 * units + BLK)), shaped((half, width))), slabs, downs, (), (rows_other, hidden_other)
     )
     copies, squares = call(
         acts_kernel,
@@ -362,9 +381,7 @@
     )
     acts = flat(exchange_row(copies))
     slabs = spread_x(multiply(grad_in_kernel, (slab,) * X, [acts], gate_ups))
-    rows_other, hidden_other, grad_rows_other, acts_other, squares_other = (
-        other_core(value) for value in (rows, hidden, grad_rows, acts, squares)
-    )
+    grad_rows_other, acts_other, squares_other = (other_core(value) for value in (grad_rows, acts, squares))
     grad_gate, grad_up, grad_down, loss, done = call(
         weights_kernel,
         (wide, wide, tall, shaped((1, 1), jnp.float32), DONE),

time: 167 us -> 161 us (0.964)
  blocking collectives: 59.2 us -> 55.4 us
    all_to_all x4, blocking collectives: 59.2 us -> 55.4 us  [exchange_row(): return lax.all_to_all(value, 'row', 0, 0)]
  transfers between devices with their start and end apart: 28 -> 28, of which waited for: 16 -> 15; matrix products, arithmetic and copies ran while one was open for 1% -> 1% of each run, Pallas kernels for 3% -> 4%
where the time goes in v7:
time: 161 us; the launch traced here: 160 us
  blocking collectives  55.4 us (34%)
  waiting for transfers between devices  45.6 us (28%)
  starting transfers between devices  43.3 us (27%)
  Pallas kernels  13.5 us (8%)
  local copies, waits for them, and re-layouts  1.63 us (1%)
    all_to_all x4, blocking collectives, exchange_row(): return lax.all_to_all(value, 'row', 0, 0)  55.4 us
    ppermute x18, starting transfers between devices, fetch(): return lax.ppermute(value, 'col', pairs)  29.9 us
    ppermute x18, waiting for transfers between devices, fetch(): return lax.ppermute(value, 'col', pairs)  28.1 us
    all_to_all x1, waiting for transfers between devices, per_device(): chips = lax.all_to_all(copies, 'col', 0, 0, axis_index_groups=SAME_CORE)  16.3 us
    pallas_call x12, Pallas kernels, call(): pl.pallas_call(lambda *refs: kernel(*refs[:len(args)], *refs[len(args) +...  13.5 us
    all_to_all x1, starting transfers between devices, per_device(): chips = lax.all_to_all(copies, 'col', 0, 0, axis_index_groups=SAME_CORE)  11.6 us
  transfers between devices with their start and end apart: 28, of which 15 were waited for; matrix products, arithmetic and copies ran while one was open for 1% of the time, Pallas kernels for 4%

profile of v7, /device:TPU:6, one launch (start us, length us, event | category | flops | bytes accessed | tf_op | source)
XLA Modules:
  0.0 160.3 jit_solution(473644376244318107)
XLA Ops:
  1.3 1.6 %broadcast_in_dim.2 = bf16[16,16,1024]{2,1,0:T(8,128)(2,1)} broadcast(bf16[16,1024]{1,0:T(8,128)(2,1)} %param.6), dimensions={1,2} | broadcast | bytes 557056 | tf_op jit(solution)/shard_map/broadcast_in_dim | solution.py:341
  3.0 11.6 %all-to-all-start = ((bf16[16,16,1024]{2,1,0:T(8,128)(2,1)}), bf16[16,16,1024]{2,1,0:T(8,128)(2,1)}, u32[]{:S(2)}, u32[]{:S(2)}) async-start(bf16[16,16,1024]{2,1,0:T(8,128)(2,1)} %broadcast_in_dim.2), calls=%async_computation | async-start | bytes 1048576 | tf_op jit(solution)/shard_map/all_to_all | solution.py:342
  15.8 16.3 %all-to-all-done.refs_2_ = bf16[16,16,1024]{2,1,0:T(8,128)(2,1)} async-done(((bf16[16,16,1024]{2,1,0:T(8,128)(2,1)}), bf16[16,16,1024]{2,1,0:T(8,128)(2,1)}, u32[]{:S(2)}, u32[]{:S(2)}) %all-to-all-start) | async-done | bytes 524320 | tf_op jit(solution)/shard_map/all_to_all | solution.py:342
  32.1 4.0 %shard_map.109 = (bf16[1024,512]{1,0:T(8,128)(2,1)S(1)}, bf16[1024,512]{1,0:T(8,128)(2,1)S(1)}, bf16[1024,512]{1,0:T(8,128)(2,1)S(1)}, bf16[1024,512]{1,0:T(8,12...) custom-call(s32[3,4,8]{2,1,0:T(4,128)S(1)} %bitcast.14, ...), custom_call_target="tpu_custom_call" | custom-call | flops 1073741824 | bytes 10486528 | tf_op jit(solution)/shard_map/pallas_call | solution.py:26
  36.0 18.5 %all_to_all.25.refs_0_ = bf16[8,32,2048]{2,1,0:T(8,128)(2,1)S(1)} all-to-all(bf16[8,32,2048]{2,1,0:T(8,128)(2,1)S(1)} %bitcast.11), channel_id=1, replica_groups=mesh['row'=8,'col'=32] {'row'}, dimensions={0} | all-to-all | bytes 2097152 | tf_op jit(solution)/shard_map/all_to_all | solution.py:313
  54.7 11.3 %all_to_all.26 = bf16[8,32,1024]{2,1,0:T(8,128)(2,1)S(1)} all-to-all(bf16[8,32,1024]{2,1,0:T(8,128)(2,1)S(1)} %get-tuple-element.46), channel_id=1, replica_groups=mesh['row'=8,'col'=32] {'row'}, dimensions={0} | all-to-all | bytes 1048576 | tf_op jit(solution)/shard_map/all_to_all | solution.py:313
  65.9 1.6 shard_map.111
  67.5 2.4 %collective-permute-start.4 = (bf16[64,1024]{1,0:T(8,128)(2,1)S(1)}, bf16[64,1024]{1,0:T(8,128)(2,1)S(1)}, u32[]{:S(2)}, u32[]{:S(2)}) collective-permute-start(bf16[64,1024]{1,0:T(8,128)(2,1)S(1)} %get-tuple-element.48), channel_id=1, source_target_pairs={{24,0},{25,1},{26,2},{27,3},{28,4},{29,5},{30,6},{31,7},{0,8},{1,9... | collective-permute-start | bytes 393224 | tf_op jit(solution)/shard_map/ppermute | solution.py:288
  70.9 3.0 %collective-permute-done.4.refs_1_ = bf16[64,1024]{1,0:T(8,128)(2,1)S(1)} collective-permute-done((bf16[64,1024]{1,0:T(8,128)(2,1)S(1)}, bf16[64,1024]{1,0:T(8,128)(2,1)S(1)}, u32[]{:S(2)}, u32[]{:S(2)}) %collective-permute-start.4) | collective-permute-done | bytes 131104 | tf_op jit(solution)/shard_map/ppermute | solution.py:288
  73.9 2.7 %collective-permute-done.5.refs_2_ = bf16[64,1024]{1,0:T(8,128)(2,1)S(1)} collective-permute-done((bf16[64,1024]{1,0:T(8,128)(2,1)S(1)}, bf16[64,1024]{1,0:T(8,128)(2,1)S(1)}, u32[]{:S(2)}, u32[]{:S(2)}) %collective-permute-start.5) | collective-permute-done | bytes 131104 | tf_op jit(solution)/shard_map/ppermute | solution.py:288
  78.5 3.1 %collective-permute-start.7 = (bf16[16,1024]{1,0:T(8,128)(2,1)S(1)}, bf16[16,1024]{1,0:T(8,128)(2,1)S(1)}, u32[]{:S(2)}, u32[]{:S(2)}) collective-permute-start(bf16[16,1024]{1,0:T(8,128)(2,1)S(1)} %get-tuple-element.52), channel_id=1, source_target_pairs={{6,0},{7,1},{0,2},{1,3},{2,4},{3,5},{4,6},{5,7},{14,8},{15,9},{8,1... | collective-permute-start | bytes 98312 | tf_op jit(solution)/shard_map/ppermute | solution.py:288
  81.9 3.2 %collective-permute-start.9 = (bf16[16,1024]{1,0:T(8,128)(2,1)S(1)}, bf16[16,1024]{1,0:T(8,128)(2,1)S(1)}, u32[]{:S(2)}, u32[]{:S(2)}) collective-permute-start(bf16[16,1024]{1,0:T(8,128)(2,1)S(1)} %get-tuple-element.54), channel_id=1, source_target_pairs={{2,0},{3,1},{4,2},{5,3},{6,4},{7,5},{0,6},{1,7},{10,8},{11,9},{12,... | collective-permute-start | bytes 98312 | tf_op jit(solution)/shard_map/ppermute | solution.py:288
  85.2 4.2 %collective-permute-done.8.refs_3_ = bf16[16,1024]{1,0:T(8,128)(2,1)S(1)} collective-permute-done((bf16[16,1024]{1,0:T(8,128)(2,1)S(1)}, bf16[16,1024]{1,0:T(8,128)(2,1)S(1)}, u32[]{:S(2)}, u32[]{:S(2)}) %collective-permute-start.8) | collective-permute-done | bytes 32800 | tf_op jit(solution)/shard_map/ppermute | solution.py:288
  90.0 2.0 %collective-permute-start.13 = (bf16[16,1024]{1,0:T(8,128)(2,1)S(1)}, bf16[16,1024]{1,0:T(8,128)(2,1)S(1)}, u32[]{:S(2)}, u32[]{:S(2)}) collective-permute-start(bf16[16,1024]{1,0:T(8,128)(2,1)S(1)} %get-tuple-element.58.refs_0_), channel_id=1, source_target_pairs={{6,0},{7,1},{0,2},{1,3},{2,4},{3,5},{4,6},{5,7},{14,8},{15,9},{8,1... | collective-permute-start | bytes 98312 | tf_op jit(solution)/shard_map/ppermute | solution.py:288
  92.0 2.5 %collective-permute-start.12 = (bf16[16,1024]{1,0:T(8,128)(2,1)S(1)}, bf16[16,1024]{1,0:T(8,128)(2,1)S(1)}, u32[]{:S(2)}, u32[]{:S(2)}) collective-permute-start(bf16[16,1024]{1,0:T(8,128)(2,1)S(1)} %get-tuple-element.58.refs_0_), channel_id=1, source_target_pairs={{4,0},{5,1},{6,2},{7,3},{0,4},{1,5},{2,6},{3,7},{12,8},{13,9},{14,... | collective-permute-start | bytes 98312 | tf_op jit(solution)/shard_map/ppermute | solution.py:288
  94.5 2.9 %collective-permute-start.11 = (bf16[16,1024]{1,0:T(8,128)(2,1)S(1)}, bf16[16,1024]{1,0:T(8,128)(2,1)S(1)}, u32[]{:S(2)}, u32[]{:S(2)}) collective-permute-start(bf16[16,1024]{1,0:T(8,128)(2,1)S(1)} %get-tuple-element.58.refs_0_), channel_id=1, source_target_pairs={{2,0},{3,1},{4,2},{5,3},{6,4},{7,5},{0,6},{1,7},{10,8},{11,9},{12,... | collective-permute-start | bytes 98312 | tf_op jit(solution)/shard_map/ppermute | solution.py:288
  97.5 2.4 %collective-permute-done.12.refs_2_ = bf16[16,1024]{1,0:T(8,128)(2,1)S(1)} collective-permute-done((bf16[16,1024]{1,0:T(8,128)(2,1)S(1)}, bf16[16,1024]{1,0:T(8,128)(2,1)S(1)}, u32[]{:S(2)}, u32[]{:S(2)}) %collective-permute-start.12) | collective-permute-done | bytes 32800 | tf_op jit(solution)/shard_map/ppermute | solution.py:288
  100.9 1.3 collective-permute-start.14
  102.2 2.9 %collective-permute-done.16.refs_3_ = bf16[64,1024]{1,0:T(8,128)(2,1)S(1)} collective-permute-done((bf16[64,1024]{1,0:T(8,128)(2,1)S(1)}, bf16[64,1024]{1,0:T(8,128)(2,1)S(1)}, u32[]{:S(2)}, u32[]{:S(2)}) %collective-permute-start.16) | collective-permute-done | bytes 131104 | tf_op jit(solution)/shard_map/ppermute | solution.py:288
  105.1 2.2 %collective-permute-done.15.refs_2_ = bf16[64,1024]{1,0:T(8,128)(2,1)S(1)} collective-permute-done((bf16[64,1024]{1,0:T(8,128)(2,1)S(1)}, bf16[64,1024]{1,0:T(8,128)(2,1)S(1)}, u32[]{:S(2)}, u32[]{:S(2)}) %collective-permute-start.15) | collective-permute-done | bytes 131104 | tf_op jit(solution)/shard_map/ppermute | solution.py:288
  107.3 1.3 collective-permute-done.14.refs_1_
  109.4 11.8 %all_to_all.27.refs_0_ = bf16[8,32,1152]{2,1,0:T(8,128)(2,1)S(1)} all-to-all(bf16[8,32,1152]{2,1,0:T(8,128)(2,1)S(1)} %bitcast.12), channel_id=1, replica_groups=mesh['row'=8,'col'=32] {'row'}, dimensions={0} | all-to-all | bytes 1179648 | tf_op jit(solution)/shard_map/all_to_all | solution.py:313
  121.4 13.9 %all_to_all.28 = bf16[8,32,2048]{2,1,0:T(8,128)(2,1)S(1)} all-to-all(bf16[8,32,2048]{2,1,0:T(8,128)(2,1)S(1)} %get-tuple-element.64), channel_id=1, replica_groups=mesh['row'=8,'col'=32] {'row'}, dimensions={0} | all-to-all | bytes 2097152 | tf_op jit(solution)/shard_map/all_to_all | solution.py:313
  135.8 1.3 shard_map.119
  138.3 2.0 %collective-permute-start.22 = (bf16[64,1024]{1,0:T(8,128)(2,1)S(1)}, bf16[64,1024]{1,0:T(8,128)(2,1)S(1)}, u32[]{:S(2)}, u32[]{:S(2)}) collective-permute-start(bf16[64,1024]{1,0:T(8,128)(2,1)S(1)} %get-tuple-element.77), channel_id=1, source_target_pairs={{16,0},{17,1},{18,2},{19,3},{20,4},{21,5},{22,6},{23,7},{24,8},{25... | collective-permute-start | bytes 393224 | tf_op jit(solution)/shard_map/ppermute | solution.py:288
  140.3 4.2 %shard_map.118 = (bf16[1024,512]{1,0:T(8,128)(2,1)}, bf16[1024,512]{1,0:T(8,128)(2,1)}, bf16[512,1024]{1,0:T(8,128)(2,1)}, f32[1,1]{1,0:T(1,128)}, f32[8,128]{1,0:T(8,128)S(1)}) custom-call(s32[3,4,8]{2,1,0:T(4,128)S(1)} %bitcast.16, bf16[256,1024]{1,0:T(8,128)(2,1)S(1)} %get-tuple-element.57.refs_1_, ...), custom_call_target="tpu_custom_call" | custom-call | flops 1610612736 | bytes 8401284 | tf_op jit(solution)/shard_map/pallas_call | solution.py:26
  144.4 1.7 %collective-permute-done.22.refs_2_ = bf16[64,1024]{1,0:T(8,128)(2,1)S(1)} collective-permute-done((bf16[64,1024]{1,0:T(8,128)(2,1)S(1)}, bf16[64,1024]{1,0:T(8,128)(2,1)S(1)}, u32[]{:S(2)}, u32[]{:S(2)}) %collective-permute-start.22) | collective-permute-done | bytes 131104 | tf_op jit(solution)/shard_map/ppermute | solution.py:288
  146.1 2.1 %collective-permute-done.23.refs_3_ = bf16[64,1024]{1,0:T(8,128)(2,1)S(1)} collective-permute-done((bf16[64,1024]{1,0:T(8,128)(2,1)S(1)}, bf16[64,1024]{1,0:T(8,128)(2,1)S(1)}, u32[]{:S(2)}, u32[]{:S(2)}) %collective-permute-start.23) | collective-permute-done | bytes 131104 | tf_op jit(solution)/shard_map/ppermute | solution.py:288
  148.3 3.3 %collective-permute-start.24 = (bf16[16,1024]{1,0:T(8,128)(2,1)S(1)}, bf16[16,1024]{1,0:T(8,128)(2,1)S(1)}, u32[]{:S(2)}, u32[]{:S(2)}) collective-permute-start(bf16[16,1024]{1,0:T(8,128)(2,1)S(1)} %get-tuple-element.81), channel_id=1, source_target_pairs={{6,0},{7,1},{0,2},{1,3},{2,4},{3,5},{4,6},{5,7},{14,8},{15,9},{8,1... | collective-permute-start | bytes 98312 | tf_op jit(solution)/shard_map/ppermute | solution.py:288
  151.6 2.6 %collective-permute-start.25 = (bf16[16,1024]{1,0:T(8,128)(2,1)S(1)}, bf16[16,1024]{1,0:T(8,128)(2,1)S(1)}, u32[]{:S(2)}, u32[]{:S(2)}) collective-permute-start(bf16[16,1024]{1,0:T(8,128)(2,1)S(1)} %get-tuple-element.82), channel_id=1, source_target_pairs={{4,0},{5,1},{6,2},{7,3},{0,4},{1,5},{2,6},{3,7},{12,8},{13,9},{14,... | collective-permute-start | bytes 98312 | tf_op jit(solution)/shard_map/ppermute | solution.py:288
  154.1 1.3 collective-permute-start.26
  155.4 4.0 %collective-permute-done.25.refs_2_ = bf16[16,1024]{1,0:T(8,128)(2,1)S(1)} collective-permute-done((bf16[16,1024]{1,0:T(8,128)(2,1)S(1)}, bf16[16,1024]{1,0:T(8,128)(2,1)S(1)}, u32[]{:S(2)}, u32[]{:S(2)}) %collective-permute-start.25) | collective-permute-done | bytes 32800 | tf_op jit(solution)/shard_map/ppermute | solution.py:288
  (50 shorter events, 10.7 us)
Async XLA Ops:
  0.6 31.4 %copy-start = (bf16[1024,512]{1,0:T(8,128)(2,1)S(1)}, bf16[1024,512]{1,0:T(8,128)(2,1)}, u32[]{:S(2)}) copy-start(bf16[1024,512]{1,0:T(8,128)(2,1)} %refs_3_.2) | copy-start | bytes 3145732
  0.6 31.4 %collective-permute-start.1 = (bf16[1024,512]{1,0:T(8,128)(2,1)}, bf16[1024,512]{1,0:T(8,128)(2,1)S(1)}, u32[]{:S(2)}, u32[]{:S(2)}) collective-permute-start(bf16[1024,512]{1,0:T(8,128)(2,1)} %refs_3_.2), channel_id=1, source_target_pairs={{0,1},{1,0},{2,3},{3,2},{4,5},{5,4},{6,7},{7,6},{8,9},{9,8},{10,11... | collective-permute-start | bytes 3145736 | tf_op jit(solution)/shard_map/ppermute | solution.py:278
  0.7 31.3 %collective-permute-start.2 = (bf16[1024,512]{1,0:T(8,128)(2,1)}, bf16[1024,512]{1,0:T(8,128)(2,1)}, u32[]{:S(2)}, u32[]{:S(2)}) collective-permute-start(bf16[1024,512]{1,0:T(8,128)(2,1)} %refs_5_.1), channel_id=1, source_target_pairs={{0,1},{1,0},{2,3},{3,2},{4,5},{5,4},{6,7},{7,6},{8,9},{9,8},{10,11... | collective-permute-start | bytes 3145736 | tf_op jit(solution)/shard_map/ppermute | solution.py:278
  1.2 30.8 %collective-permute-start.3 = (bf16[512,1024]{1,0:T(8,128)(2,1)}, bf16[512,1024]{1,0:T(8,128)(2,1)S(1)}, u32[]{:S(2)}, u32[]{:S(2)}) collective-permute-start(bf16[512,1024]{1,0:T(8,128)(2,1)} %refs_3_.3), channel_id=1, source_target_pairs={{0,1},{1,0},{2,3},{3,2},{4,5},{5,4},{6,7},{7,6},{8,9},{9,8},{10,11... | collective-permute-start | bytes 3145736 | tf_op jit(solution)/shard_map/ppermute | solution.py:278
  2.9 11.6 %copy-start.3 = (s32[3,8,4]{1,2,0:T(4,128)S(1)}, s32[3,8,4]{1,2,0:T(4,128)}, u32[]{:S(2)}) copy-start(s32[3,8,4]{1,2,0:T(4,128)} %param.11) | copy-start | bytes 1156
  3.0 29.1 %all-to-all-start = ((bf16[16,16,1024]{2,1,0:T(8,128)(2,1)}), bf16[16,16,1024]{2,1,0:T(8,128)(2,1)}, u32[]{:S(2)}, u32[]{:S(2)}) async-start(bf16[16,16,1024]{2,1,0:T(8,128)(2,1)} %broadcast_in_dim.2), calls=%async_computation | async-start | bytes 1048576 | tf_op jit(solution)/shard_map/all_to_all | solution.py:342
  14.5 1.3 collective-permute-start
  54.5 11.4 %copy-start.1 = (bf16[512,1024]{1,0:T(8,128)(2,1)S(1)}, bf16[512,1024]{1,0:T(8,128)(2,1)}, u32[]{:S(2)}) copy-start(bf16[512,1024]{1,0:T(8,128)(2,1)} %refs_3_.3) | copy-start | bytes 3145732
  67.5 6.4 %collective-permute-start.4 = (bf16[64,1024]{1,0:T(8,128)(2,1)S(1)}, bf16[64,1024]{1,0:T(8,128)(2,1)S(1)}, u32[]{:S(2)}, u32[]{:S(2)}) collective-permute-start(bf16[64,1024]{1,0:T(8,128)(2,1)S(1)} %get-tuple-element.48), channel_id=1, source_target_pairs={{24,0},{25,1},{26,2},{27,3},{28,4},{29,5},{30,6},{31,7},{0,8},{1,9... | collective-permute-start | bytes 393224 | tf_op jit(solution)/shard_map/ppermute | solution.py:288
  70.0 6.6 %collective-permute-start.5 = (bf16[64,1024]{1,0:T(8,128)(2,1)S(1)}, bf16[64,1024]{1,0:T(8,128)(2,1)S(1)}, u32[]{:S(2)}, u32[]{:S(2)}) collective-permute-start(bf16[64,1024]{1,0:T(8,128)(2,1)S(1)} %get-tuple-element.49), channel_id=1, source_target_pairs={{16,0},{17,1},{18,2},{19,3},{20,4},{21,5},{22,6},{23,7},{24,8},{25... | collective-permute-start | bytes 393224 | tf_op jit(solution)/shard_map/ppermute | solution.py:288
  70.2 7.6 %collective-permute-start.6 = (bf16[64,1024]{1,0:T(8,128)(2,1)S(1)}, bf16[64,1024]{1,0:T(8,128)(2,1)S(1)}, u32[]{:S(2)}, u32[]{:S(2)}) collective-permute-start(bf16[64,1024]{1,0:T(8,128)(2,1)S(1)} %get-tuple-element.50), channel_id=1, source_target_pairs={{8,0},{9,1},{10,2},{11,3},{12,4},{13,5},{14,6},{15,7},{16,8},{17,9... | collective-permute-start | bytes 393224 | tf_op jit(solution)/shard_map/ppermute | solution.py:288
  77.9 11.5 %copy-start.2 = (bf16[16,1024]{1,0:T(8,128)(2,1)S(1)}, bf16[16,1024]{1,0:T(8,128)(2,1)}, u32[]{:S(2)}) copy-start(bf16[16,1024]{1,0:T(8,128)(2,1)} %refs_0_.1) | copy-start | bytes 98308
  77.9 30.7 %collective-permute-start.10 = (bf16[256,1024]{1,0:T(8,128)(2,1)S(1)}, bf16[256,1024]{1,0:T(8,128)(2,1)S(1)}, u32[]{:S(2)}, u32[]{:S(2)}) collective-permute-start(bf16[256,1024]{1,0:T(8,128)(2,1)S(1)} %get-tuple-element.57.refs_1_), channel_id=1, source_target_pairs={{0,1},{1,0},{2,3},{3,2},{4,5},{5,4},{6,7},{7,6},{8,9},{9,8},{10,11... | collective-permute-start | bytes 1572872 | tf_op jit(solution)/shard_map/ppermute | solution.py:278
  78.0 30.6 %collective-permute-start.17 = (bf16[256,1024]{1,0:T(8,128)(2,1)S(1)}, bf16[256,1024]{1,0:T(8,128)(2,1)S(1)}, u32[]{:S(2)}, u32[]{:S(2)}) collective-permute-start(bf16[256,1024]{1,0:T(8,128)(2,1)S(1)} %get-tuple-element.61.refs_5_), channel_id=1, source_target_pairs={{0,1},{1,0},{2,3},{3,2},{4,5},{5,4},{6,7},{7,6},{8,9},{9,8},{10,11... | collective-permute-start | bytes 1572872 | tf_op jit(solution)/shard_map/ppermute | solution.py:278
  78.5 6.7 %collective-permute-start.7 = (bf16[16,1024]{1,0:T(8,128)(2,1)S(1)}, bf16[16,1024]{1,0:T(8,128)(2,1)S(1)}, u32[]{:S(2)}, u32[]{:S(2)}) collective-permute-start(bf16[16,1024]{1,0:T(8,128)(2,1)S(1)} %get-tuple-element.52), channel_id=1, source_target_pairs={{6,0},{7,1},{0,2},{1,3},{2,4},{3,5},{4,6},{5,7},{14,8},{15,9},{8,1... | collective-permute-start | bytes 98312 | tf_op jit(solution)/shard_map/ppermute | solution.py:288
  81.6 7.8 %collective-permute-start.8 = (bf16[16,1024]{1,0:T(8,128)(2,1)S(1)}, bf16[16,1024]{1,0:T(8,128)(2,1)S(1)}, u32[]{:S(2)}, u32[]{:S(2)}) collective-permute-start(bf16[16,1024]{1,0:T(8,128)(2,1)S(1)} %get-tuple-element.53), channel_id=1, source_target_pairs={{4,0},{5,1},{6,2},{7,3},{0,4},{1,5},{2,6},{3,7},{12,8},{13,9},{14,... | collective-permute-start | bytes 98312 | tf_op jit(solution)/shard_map/ppermute | solution.py:288
  81.9 7.5 %collective-permute-start.9 = (bf16[16,1024]{1,0:T(8,128)(2,1)S(1)}, bf16[16,1024]{1,0:T(8,128)(2,1)S(1)}, u32[]{:S(2)}, u32[]{:S(2)}) collective-permute-start(bf16[16,1024]{1,0:T(8,128)(2,1)S(1)} %get-tuple-element.54), channel_id=1, source_target_pairs={{2,0},{3,1},{4,2},{5,3},{6,4},{7,5},{0,6},{1,7},{10,8},{11,9},{12,... | collective-permute-start | bytes 98312 | tf_op jit(solution)/shard_map/ppermute | solution.py:288
  90.0 7.4 %collective-permute-start.13 = (bf16[16,1024]{1,0:T(8,128)(2,1)S(1)}, bf16[16,1024]{1,0:T(8,128)(2,1)S(1)}, u32[]{:S(2)}, u32[]{:S(2)}) collective-permute-start(bf16[16,1024]{1,0:T(8,128)(2,1)S(1)} %get-tuple-element.58.refs_0_), channel_id=1, source_target_pairs={{6,0},{7,1},{0,2},{1,3},{2,4},{3,5},{4,6},{5,7},{14,8},{15,9},{8,1... | collective-permute-start | bytes 98312 | tf_op jit(solution)/shard_map/ppermute | solution.py:288
  92.0 7.8 %collective-permute-start.12 = (bf16[16,1024]{1,0:T(8,128)(2,1)S(1)}, bf16[16,1024]{1,0:T(8,128)(2,1)S(1)}, u32[]{:S(2)}, u32[]{:S(2)}) collective-permute-start(bf16[16,1024]{1,0:T(8,128)(2,1)S(1)} %get-tuple-element.58.refs_0_), channel_id=1, source_target_pairs={{4,0},{5,1},{6,2},{7,3},{0,4},{1,5},{2,6},{3,7},{12,8},{13,9},{14,... | collective-permute-start | bytes 98312 | tf_op jit(solution)/shard_map/ppermute | solution.py:288
  94.5 5.5 %collective-permute-start.11 = (bf16[16,1024]{1,0:T(8,128)(2,1)S(1)}, bf16[16,1024]{1,0:T(8,128)(2,1)S(1)}, u32[]{:S(2)}, u32[]{:S(2)}) collective-permute-start(bf16[16,1024]{1,0:T(8,128)(2,1)S(1)} %get-tuple-element.58.refs_0_), channel_id=1, source_target_pairs={{2,0},{3,1},{4,2},{5,3},{6,4},{7,5},{0,6},{1,7},{10,8},{11,9},{12,... | collective-permute-start | bytes 98312 | tf_op jit(solution)/shard_map/ppermute | solution.py:288
  100.0 5.0 %collective-permute-start.16 = (bf16[64,1024]{1,0:T(8,128)(2,1)S(1)}, bf16[64,1024]{1,0:T(8,128)(2,1)S(1)}, u32[]{:S(2)}, u32[]{:S(2)}) collective-permute-start(bf16[64,1024]{1,0:T(8,128)(2,1)S(1)} %shard_map.115.refs_0_), channel_id=1, source_target_pairs={{24,0},{25,1},{26,2},{27,3},{28,4},{29,5},{30,6},{31,7},{0,8},{1,9... | collective-permute-start | bytes 393224 | tf_op jit(solution)/shard_map/ppermute | solution.py:288
  100.7 6.6 %collective-permute-start.15 = (bf16[64,1024]{1,0:T(8,128)(2,1)S(1)}, bf16[64,1024]{1,0:T(8,128)(2,1)S(1)}, u32[]{:S(2)}, u32[]{:S(2)}) collective-permute-start(bf16[64,1024]{1,0:T(8,128)(2,1)S(1)} %shard_map.115.refs_0_), channel_id=1, source_target_pairs={{16,0},{17,1},{18,2},{19,3},{20,4},{21,5},{22,6},{23,7},{24,8},{25... | collective-permute-start | bytes 393224 | tf_op jit(solution)/shard_map/ppermute | solution.py:288
  100.9 7.7 %collective-permute-start.14 = (bf16[64,1024]{1,0:T(8,128)(2,1)S(1)}, bf16[64,1024]{1,0:T(8,128)(2,1)S(1)}, u32[]{:S(2)}, u32[]{:S(2)}) collective-permute-start(bf16[64,1024]{1,0:T(8,128)(2,1)S(1)} %shard_map.115.refs_0_), channel_id=1, source_target_pairs={{8,0},{9,1},{10,2},{11,3},{12,4},{13,5},{14,6},{15,7},{16,8},{17,9... | collective-permute-start | bytes 393224 | tf_op jit(solution)/shard_map/ppermute | solution.py:288
  135.3 5.0 %collective-permute-start.18 = (bf16[256,2048]{1,0:T(8,128)(2,1)S(1)}, bf16[256,2048]{1,0:T(8,128)(2,1)S(1)}, u32[]{:S(2)}, u32[]{:S(2)}) collective-permute-start(bf16[256,2048]{1,0:T(8,128)(2,1)S(1)} %bitcast.8), channel_id=1, source_target_pairs={{0,1},{1,0},{2,3},{3,2},{4,5},{5,4},{6,7},{7,6},{8,9},{9,8},{10,11... | collective-permute-start | bytes 3145736 | tf_op jit(solution)/shard_map/ppermute | solution.py:278
  135.3 5.0 %collective-permute-start.19 = (bf16[256,1024]{1,0:T(8,128)(2,1)S(1)}, bf16[256,1024]{1,0:T(8,128)(2,1)S(1)}, u32[]{:S(2)}, u32[]{:S(2)}) collective-permute-start(bf16[256,1024]{1,0:T(8,128)(2,1)S(1)} %get-tuple-element.65.refs_7_), channel_id=1, source_target_pairs={{0,1},{1,0},{2,3},{3,2},{4,5},{5,4},{6,7},{7,6},{8,9},{9,8},{10,11... | collective-permute-start | bytes 1572872 | tf_op jit(solution)/shard_map/ppermute | solution.py:278
  135.8 4.5 %collective-permute-start.20 = (f32[8,128]{1,0:T(8,128)S(1)}, f32[8,128]{1,0:T(8,128)S(1)}, u32[]{:S(2)}, u32[]{:S(2)}) collective-permute-start(f32[8,128]{1,0:T(8,128)S(1)} %get-tuple-element.66.refs_9_), channel_id=1, source_target_pairs={{0,1},{1,0},{2,3},{3,2},{4,5},{5,4},{6,7},{7,6},{8,9},{9,8},{10,11... | collective-permute-start | bytes 12296 | tf_op jit(solution)/shard_map/ppermute | solution.py:278
  137.1 7.3 %collective-permute-start.21 = (bf16[64,1024]{1,0:T(8,128)(2,1)S(1)}, bf16[64,1024]{1,0:T(8,128)(2,1)S(1)}, u32[]{:S(2)}, u32[]{:S(2)}) collective-permute-start(bf16[64,1024]{1,0:T(8,128)(2,1)S(1)} %get-tuple-element.76), channel_id=1, source_target_pairs={{24,0},{25,1},{26,2},{27,3},{28,4},{29,5},{30,6},{31,7},{0,8},{1,9... | collective-permute-start | bytes 393224 | tf_op jit(solution)/shard_map/ppermute | solution.py:288
  138.3 7.8 %collective-permute-start.22 = (bf16[64,1024]{1,0:T(8,128)(2,1)S(1)}, bf16[64,1024]{1,0:T(8,128)(2,1)S(1)}, u32[]{:S(2)}, u32[]{:S(2)}) collective-permute-start(bf16[64,1024]{1,0:T(8,128)(2,1)S(1)} %get-tuple-element.77), channel_id=1, source_target_pairs={{16,0},{17,1},{18,2},{19,3},{20,4},{21,5},{22,6},{23,7},{24,8},{25... | collective-permute-start | bytes 393224 | tf_op jit(solution)/shard_map/ppermute | solution.py:288
  140.2 8.0 %collective-permute-start.23 = (bf16[64,1024]{1,0:T(8,128)(2,1)S(1)}, bf16[64,1024]{1,0:T(8,128)(2,1)S(1)}, u32[]{:S(2)}, u32[]{:S(2)}) collective-permute-start(bf16[64,1024]{1,0:T(8,128)(2,1)S(1)} %get-tuple-element.78), channel_id=1, source_target_pairs={{8,0},{9,1},{10,2},{11,3},{12,4},{13,5},{14,6},{15,7},{16,8},{17,9... | collective-permute-start | bytes 393224 | tf_op jit(solution)/shard_map/ppermute | solution.py:288
  148.3 7.1 %collective-permute-start.24 = (bf16[16,1024]{1,0:T(8,128)(2,1)S(1)}, bf16[16,1024]{1,0:T(8,128)(2,1)S(1)}, u32[]{:S(2)}, u32[]{:S(2)}) collective-permute-start(bf16[16,1024]{1,0:T(8,128)(2,1)S(1)} %get-tuple-element.81), channel_id=1, source_target_pairs={{6,0},{7,1},{0,2},{1,3},{2,4},{3,5},{4,6},{5,7},{14,8},{15,9},{8,1... | collective-permute-start | bytes 98312 | tf_op jit(solution)/shard_map/ppermute | solution.py:288
  151.6 7.8 %collective-permute-start.25 = (bf16[16,1024]{1,0:T(8,128)(2,1)S(1)}, bf16[16,1024]{1,0:T(8,128)(2,1)S(1)}, u32[]{:S(2)}, u32[]{:S(2)}) collective-permute-start(bf16[16,1024]{1,0:T(8,128)(2,1)S(1)} %get-tuple-element.82), channel_id=1, source_target_pairs={{4,0},{5,1},{6,2},{7,3},{0,4},{1,5},{2,6},{3,7},{12,8},{13,9},{14,... | collective-permute-start | bytes 98312 | tf_op jit(solution)/shard_map/ppermute | solution.py:288
  154.1 5.5 %collective-permute-start.26 = (bf16[16,1024]{1,0:T(8,128)(2,1)S(1)}, bf16[16,1024]{1,0:T(8,128)(2,1)S(1)}, u32[]{:S(2)}, u32[]{:S(2)}) collective-permute-start(bf16[16,1024]{1,0:T(8,128)(2,1)S(1)} %get-tuple-element.83), channel_id=1, source_target_pairs={{2,0},{3,1},{4,2},{5,3},{6,4},{7,5},{0,6},{1,7},{10,8},{11,9},{12,... | collective-permute-start | bytes 98312 | tf_op jit(solution)/shard_map/ppermute | solution.py:288

commit v8 on v7

--- a/solution.py
+++ b/solution.py
@@ -14,6 +14,7 @@
 ROWS = 8
 TILE = 512
 DOWN = 2
+PLACES = (0, 1, 3, 2)
 SAME_CORE = [[chip * CORES + core for chip in range(CHIPS)] for core in range(CORES)]
 VMEM = pl.BlockSpec(memory_space=pltpu.VMEM)
 SMEM = pl.BlockSpec(memory_space=pltpu.SMEM)
@@ -45,8 +46,8 @@
 def join_kernel(*refs):
     joined_ref = refs[-1]
     size = refs[0].shape[0]
-    for part, ref in enumerate(refs[:-1]):
-        joined_ref[pl.ds(part * size, size), :] = ref[...]
+    for place, ref in zip(PLACES, refs[:-1]):
+        joined_ref[pl.ds(place * size, size), :] = ref[...]
 
 
 def keep(mask_ref, which, ref, kept_ref):
@@ -289,7 +290,7 @@
 
 
 def gather_z(block):
-    return [block] + [fetch(block, 0, step) for step in range(1, Z)]
+    return [block] + [fetch(block, 0, step) for step in PLACES[1:]]
 
 
 def joined(parts):
@@ -298,15 +299,15 @@
 
 
 def gather_x(block):
-    return [block] + [fetch(block, step, 0) for step in range(1, X)]
+    return [block] + [fetch(block, step, 0) for step in PLACES[1:]]
 
 
 def spread_x(parts):
-    return [parts[0]] + [fetch(parts[step], -step, 0) for step in range(1, X)]
+    return [parts[0]] + [fetch(parts[step], -step, 0) for step in (2, 1, 3)]
 
 
 def spread_z(parts):
-    return [parts[0]] + [fetch(parts[step], 0, -step) for step in range(1, Z)]
+    return [parts[0]] + [fetch(parts[step], 0, -step) for step in (2, 1, 3)]
 
 
 def exchange_row(value):

time: 161 us -> 158 us (0.981)
  waiting for transfers between devices: 45.6 us -> 41.7 us
  starting transfers between devices: 43.3 us -> 45 us
    ppermute x18, waiting for transfers between devices: 28.1 us -> 24.3 us  [fetch(): return lax.ppermute(value, 'col', pairs)]
    ppermute x18, starting transfers between devices: 29.9 us -> 31.6 us  [fetch(): return lax.ppermute(value, 'col', pairs)]
  transfers between devices with their start and end apart: 28 -> 28, of which waited for: 15 -> 18; matrix products, arithmetic and copies ran while one was open for 1% -> 1% of each run, Pallas kernels for 4% -> 4%
where the time goes in v8:
time: 158 us
  blocking collectives  55.2 us (35%)
  starting transfers between devices  45 us (28%)
  waiting for transfers between devices  41.7 us (26%)
  Pallas kernels  13.5 us (9%)
  local copies, waits for them, and re-layouts  1.63 us (1%)
    all_to_all x4, blocking collectives, exchange_row(): return lax.all_to_all(value, 'row', 0, 0)  55.2 us
    ppermute x18, starting transfers between devices, fetch(): return lax.ppermute(value, 'col', pairs)  31.6 us
    ppermute x18, waiting for transfers between devices, fetch(): return lax.ppermute(value, 'col', pairs)  24.3 us
    all_to_all x1, waiting for transfers between devices, per_device(): chips = lax.all_to_all(copies, 'col', 0, 0, axis_index_groups=SAME_CORE)  16.3 us
    pallas_call x12, Pallas kernels, call(): pl.pallas_call(lambda *refs: kernel(*refs[:len(args)], *refs[len(args) +...  13.5 us
    all_to_all x1, starting transfers between devices, per_device(): chips = lax.all_to_all(copies, 'col', 0, 0, axis_index_groups=SAME_CORE)  11.6 us
  transfers between devices with their start and end apart: 28, of which 18 were waited for; matrix products, arithmetic and copies ran while one was open for 1% of the time, Pallas kernels for 4%

profile of v8, /device:TPU:6, one launch (start us, length us, event | category | flops | bytes accessed | tf_op | source)
XLA Modules:
  0.0 157.8 jit_solution(10452489613330262281)
XLA Ops:
  1.3 1.6 %broadcast_in_dim.2 = bf16[16,16,1024]{2,1,0:T(8,128)(2,1)} broadcast(bf16[16,1024]{1,0:T(8,128)(2,1)} %param.6), dimensions={1,2} | broadcast | bytes 557056 | tf_op jit(solution)/shard_map/broadcast_in_dim | solution.py:342
  3.0 11.6 %all-to-all-start = ((bf16[16,16,1024]{2,1,0:T(8,128)(2,1)}), bf16[16,16,1024]{2,1,0:T(8,128)(2,1)}, u32[]{:S(2)}, u32[]{:S(2)}) async-start(bf16[16,16,1024]{2,1,0:T(8,128)(2,1)} %broadcast_in_dim.2), calls=%async_computation | async-start | bytes 1048576 | tf_op jit(solution)/shard_map/all_to_all | solution.py:343
  14.6 1.2 collective-permute-done.refs_1_
  15.8 16.3 %all-to-all-done.refs_2_ = bf16[16,16,1024]{2,1,0:T(8,128)(2,1)} async-done(((bf16[16,16,1024]{2,1,0:T(8,128)(2,1)}), bf16[16,16,1024]{2,1,0:T(8,128)(2,1)}, u32[]{:S(2)}, u32[]{:S(2)}) %all-to-all-start) | async-done | bytes 524320 | tf_op jit(solution)/shard_map/all_to_all | solution.py:343
  32.1 4.0 %shard_map.109 = (bf16[1024,512]{1,0:T(8,128)(2,1)S(1)}, bf16[1024,512]{1,0:T(8,128)(2,1)S(1)}, bf16[1024,512]{1,0:T(8,128)(2,1)S(1)}, bf16[1024,512]{1,0:T(8,12...) custom-call(s32[3,4,8]{2,1,0:T(4,128)S(1)} %bitcast.14, ...), custom_call_target="tpu_custom_call" | custom-call | flops 1073741824 | bytes 10486528 | tf_op jit(solution)/shard_map/pallas_call | solution.py:27
  36.0 18.5 %all_to_all.25.refs_0_ = bf16[8,32,2048]{2,1,0:T(8,128)(2,1)S(1)} all-to-all(bf16[8,32,2048]{2,1,0:T(8,128)(2,1)S(1)} %bitcast.11), channel_id=1, replica_groups=mesh['row'=8,'col'=32] {'row'}, dimensions={0} | all-to-all | bytes 2097152 | tf_op jit(solution)/shard_map/all_to_all | solution.py:314
  54.7 11.3 %all_to_all.26 = bf16[8,32,1024]{2,1,0:T(8,128)(2,1)S(1)} all-to-all(bf16[8,32,1024]{2,1,0:T(8,128)(2,1)S(1)} %get-tuple-element.46), channel_id=1, replica_groups=mesh['row'=8,'col'=32] {'row'}, dimensions={0} | all-to-all | bytes 1048576 | tf_op jit(solution)/shard_map/all_to_all | solution.py:314
  65.9 1.6 shard_map.111
  68.5 2.3 %collective-permute-start.5 = (bf16[64,1024]{1,0:T(8,128)(2,1)S(1)}, bf16[64,1024]{1,0:T(8,128)(2,1)S(1)}, u32[]{:S(2)}, u32[]{:S(2)}) collective-permute-start(bf16[64,1024]{1,0:T(8,128)(2,1)S(1)} %get-tuple-element.49), channel_id=1, source_target_pairs={{24,0},{25,1},{26,2},{27,3},{28,4},{29,5},{30,6},{31,7},{0,8},{1,9... | collective-permute-start | bytes 393224 | tf_op jit(solution)/shard_map/ppermute | solution.py:289
  70.8 3.2 %collective-permute-done.4.refs_1_ = bf16[64,1024]{1,0:T(8,128)(2,1)S(1)} collective-permute-done((bf16[64,1024]{1,0:T(8,128)(2,1)S(1)}, bf16[64,1024]{1,0:T(8,128)(2,1)S(1)}, u32[]{:S(2)}, u32[]{:S(2)}) %collective-permute-start.4) | collective-permute-done | bytes 131104 | tf_op jit(solution)/shard_map/ppermute | solution.py:289
  75.2 1.8 %collective-permute-done.6.refs_3_ = bf16[64,1024]{1,0:T(8,128)(2,1)S(1)} collective-permute-done((bf16[64,1024]{1,0:T(8,128)(2,1)S(1)}, bf16[64,1024]{1,0:T(8,128)(2,1)S(1)}, u32[]{:S(2)}, u32[]{:S(2)}) %collective-permute-start.6) | collective-permute-done | bytes 131104 | tf_op jit(solution)/shard_map/ppermute | solution.py:289
  77.7 2.5 %collective-permute-start.7 = (bf16[16,1024]{1,0:T(8,128)(2,1)S(1)}, bf16[16,1024]{1,0:T(8,128)(2,1)S(1)}, u32[]{:S(2)}, u32[]{:S(2)}) collective-permute-start(bf16[16,1024]{1,0:T(8,128)(2,1)S(1)} %get-tuple-element.52), channel_id=1, source_target_pairs={{4,0},{5,1},{6,2},{7,3},{0,4},{1,5},{2,6},{3,7},{12,8},{13,9},{14,... | collective-permute-start | bytes 98312 | tf_op jit(solution)/shard_map/ppermute | solution.py:289
  80.2 2.3 %collective-permute-start.8 = (bf16[16,1024]{1,0:T(8,128)(2,1)S(1)}, bf16[16,1024]{1,0:T(8,128)(2,1)S(1)}, u32[]{:S(2)}, u32[]{:S(2)}) collective-permute-start(bf16[16,1024]{1,0:T(8,128)(2,1)S(1)} %get-tuple-element.53), channel_id=1, source_target_pairs={{6,0},{7,1},{0,2},{1,3},{2,4},{3,5},{4,6},{5,7},{14,8},{15,9},{8,1... | collective-permute-start | bytes 98312 | tf_op jit(solution)/shard_map/ppermute | solution.py:289
  82.6 1.8 %collective-permute-start.9 = (bf16[16,1024]{1,0:T(8,128)(2,1)S(1)}, bf16[16,1024]{1,0:T(8,128)(2,1)S(1)}, u32[]{:S(2)}, u32[]{:S(2)}) collective-permute-start(bf16[16,1024]{1,0:T(8,128)(2,1)S(1)} %get-tuple-element.54), channel_id=1, source_target_pairs={{2,0},{3,1},{4,2},{5,3},{6,4},{7,5},{0,6},{1,7},{10,8},{11,9},{12,... | collective-permute-start | bytes 98312 | tf_op jit(solution)/shard_map/ppermute | solution.py:289
  84.4 1.3 collective-permute-done.7.refs_2_
  85.6 1.5 collective-permute-done.8.refs_3_
  88.4 4.2 %collective-permute-start.13 = (bf16[16,1024]{1,0:T(8,128)(2,1)S(1)}, bf16[16,1024]{1,0:T(8,128)(2,1)S(1)}, u32[]{:S(2)}, u32[]{:S(2)}) collective-permute-start(bf16[16,1024]{1,0:T(8,128)(2,1)S(1)} %get-tuple-element.58.refs_0_), channel_id=1, source_target_pairs={{4,0},{5,1},{6,2},{7,3},{0,4},{1,5},{2,6},{3,7},{12,8},{13,9},{14,... | collective-permute-start | bytes 98312 | tf_op jit(solution)/shard_map/ppermute | solution.py:289
  92.5 1.2 collective-permute-start.12
  93.7 2.9 %collective-permute-start.11 = (bf16[16,1024]{1,0:T(8,128)(2,1)S(1)}, bf16[16,1024]{1,0:T(8,128)(2,1)S(1)}, u32[]{:S(2)}, u32[]{:S(2)}) collective-permute-start(bf16[16,1024]{1,0:T(8,128)(2,1)S(1)} %get-tuple-element.58.refs_0_), channel_id=1, source_target_pairs={{2,0},{3,1},{4,2},{5,3},{6,4},{7,5},{0,6},{1,7},{10,8},{11,9},{12,... | collective-permute-start | bytes 98312 | tf_op jit(solution)/shard_map/ppermute | solution.py:289
  96.7 1.9 %collective-permute-done.12.refs_2_ = bf16[16,1024]{1,0:T(8,128)(2,1)S(1)} collective-permute-done((bf16[16,1024]{1,0:T(8,128)(2,1)S(1)}, bf16[16,1024]{1,0:T(8,128)(2,1)S(1)}, u32[]{:S(2)}, u32[]{:S(2)}) %collective-permute-start.12) | collective-permute-done | bytes 32800 | tf_op jit(solution)/shard_map/ppermute | solution.py:289
  101.6 3.6 %collective-permute-done.16.refs_3_ = bf16[64,1024]{1,0:T(8,128)(2,1)S(1)} collective-permute-done((bf16[64,1024]{1,0:T(8,128)(2,1)S(1)}, bf16[64,1024]{1,0:T(8,128)(2,1)S(1)}, u32[]{:S(2)}, u32[]{:S(2)}) %collective-permute-start.16) | collective-permute-done | bytes 131104 | tf_op jit(solution)/shard_map/ppermute | solution.py:289
  105.2 1.7 %collective-permute-done.14.refs_1_ = bf16[64,1024]{1,0:T(8,128)(2,1)S(1)} collective-permute-done((bf16[64,1024]{1,0:T(8,128)(2,1)S(1)}, bf16[64,1024]{1,0:T(8,128)(2,1)S(1)}, u32[]{:S(2)}, u32[]{:S(2)}) %collective-permute-start.14) | collective-permute-done | bytes 131104 | tf_op jit(solution)/shard_map/ppermute | solution.py:289
  107.7 11.6 %all_to_all.27.refs_0_ = bf16[8,32,1152]{2,1,0:T(8,128)(2,1)S(1)} all-to-all(bf16[8,32,1152]{2,1,0:T(8,128)(2,1)S(1)} %bitcast.12), channel_id=1, replica_groups=mesh['row'=8,'col'=32] {'row'}, dimensions={0} | all-to-all | bytes 1179648 | tf_op jit(solution)/shard_map/all_to_all | solution.py:314
  119.4 13.9 %all_to_all.28 = bf16[8,32,2048]{2,1,0:T(8,128)(2,1)S(1)} all-to-all(bf16[8,32,2048]{2,1,0:T(8,128)(2,1)S(1)} %get-tuple-element.64), channel_id=1, replica_groups=mesh['row'=8,'col'=32] {'row'}, dimensions={0} | all-to-all | bytes 2097152 | tf_op jit(solution)/shard_map/all_to_all | solution.py:314
  133.8 1.3 shard_map.119
  136.1 1.8 %collective-permute-start.22 = (bf16[64,1024]{1,0:T(8,128)(2,1)S(1)}, bf16[64,1024]{1,0:T(8,128)(2,1)S(1)}, u32[]{:S(2)}, u32[]{:S(2)}) collective-permute-start(bf16[64,1024]{1,0:T(8,128)(2,1)S(1)} %get-tuple-element.77), channel_id=1, source_target_pairs={{24,0},{25,1},{26,2},{27,3},{28,4},{29,5},{30,6},{31,7},{0,8},{1,9... | collective-permute-start | bytes 393224 | tf_op jit(solution)/shard_map/ppermute | solution.py:289
  138.1 4.1 %shard_map.118 = (bf16[1024,512]{1,0:T(8,128)(2,1)}, bf16[1024,512]{1,0:T(8,128)(2,1)}, bf16[512,1024]{1,0:T(8,128)(2,1)}, f32[1,1]{1,0:T(1,128)}, f32[8,128]{1,0:T(8,128)S(1)}) custom-call(s32[3,4,8]{2,1,0:T(4,128)S(1)} %bitcast.16, bf16[256,1024]{1,0:T(8,128)(2,1)S(1)} %get-tuple-element.57.refs_1_, ...), custom_call_target="tpu_custom_call" | custom-call | flops 1610612736 | bytes 8401284 | tf_op jit(solution)/shard_map/pallas_call | solution.py:27
  144.0 1.5 collective-permute-done.23.refs_3_
  145.5 3.2 %collective-permute-start.24 = (bf16[16,1024]{1,0:T(8,128)(2,1)S(1)}, bf16[16,1024]{1,0:T(8,128)(2,1)S(1)}, u32[]{:S(2)}, u32[]{:S(2)}) collective-permute-start(bf16[16,1024]{1,0:T(8,128)(2,1)S(1)} %get-tuple-element.81), channel_id=1, source_target_pairs={{4,0},{5,1},{6,2},{7,3},{0,4},{1,5},{2,6},{3,7},{12,8},{13,9},{14,... | collective-permute-start | bytes 98312 | tf_op jit(solution)/shard_map/ppermute | solution.py:289
  148.7 3.3 %collective-permute-start.25 = (bf16[16,1024]{1,0:T(8,128)(2,1)S(1)}, bf16[16,1024]{1,0:T(8,128)(2,1)S(1)}, u32[]{:S(2)}, u32[]{:S(2)}) collective-permute-start(bf16[16,1024]{1,0:T(8,128)(2,1)S(1)} %get-tuple-element.82), channel_id=1, source_target_pairs={{6,0},{7,1},{0,2},{1,3},{2,4},{3,5},{4,6},{5,7},{14,8},{15,9},{8,1... | collective-permute-start | bytes 98312 | tf_op jit(solution)/shard_map/ppermute | solution.py:289
  153.5 1.2 collective-permute-done.25.refs_2_
  154.7 2.5 %collective-permute-done.26.refs_3_ = bf16[16,1024]{1,0:T(8,128)(2,1)S(1)} collective-permute-done((bf16[16,1024]{1,0:T(8,128)(2,1)S(1)}, bf16[16,1024]{1,0:T(8,128)(2,1)S(1)}, u32[]{:S(2)}, u32[]{:S(2)}) %collective-permute-start.26) | collective-permute-done | bytes 32800 | tf_op jit(solution)/shard_map/ppermute | solution.py:289
  (50 shorter events, 14.5 us)
Async XLA Ops:
  0.6 31.4 %copy-start = (bf16[1024,512]{1,0:T(8,128)(2,1)S(1)}, bf16[1024,512]{1,0:T(8,128)(2,1)}, u32[]{:S(2)}) copy-start(bf16[1024,512]{1,0:T(8,128)(2,1)} %refs_3_.2) | copy-start | bytes 3145732
  0.6 31.4 %collective-permute-start.1 = (bf16[1024,512]{1,0:T(8,128)(2,1)}, bf16[1024,512]{1,0:T(8,128)(2,1)S(1)}, u32[]{:S(2)}, u32[]{:S(2)}) collective-permute-start(bf16[1024,512]{1,0:T(8,128)(2,1)} %refs_3_.2), channel_id=1, source_target_pairs={{0,1},{1,0},{2,3},{3,2},{4,5},{5,4},{6,7},{7,6},{8,9},{9,8},{10,11... | collective-permute-start | bytes 3145736 | tf_op jit(solution)/shard_map/ppermute | solution.py:279
  0.7 31.3 %collective-permute-start.2 = (bf16[1024,512]{1,0:T(8,128)(2,1)}, bf16[1024,512]{1,0:T(8,128)(2,1)}, u32[]{:S(2)}, u32[]{:S(2)}) collective-permute-start(bf16[1024,512]{1,0:T(8,128)(2,1)} %refs_5_.1), channel_id=1, source_target_pairs={{0,1},{1,0},{2,3},{3,2},{4,5},{5,4},{6,7},{7,6},{8,9},{9,8},{10,11... | collective-permute-start | bytes 3145736 | tf_op jit(solution)/shard_map/ppermute | solution.py:279
  1.2 30.8 %collective-permute-start.3 = (bf16[512,1024]{1,0:T(8,128)(2,1)}, bf16[512,1024]{1,0:T(8,128)(2,1)S(1)}, u32[]{:S(2)}, u32[]{:S(2)}) collective-permute-start(bf16[512,1024]{1,0:T(8,128)(2,1)} %refs_3_.3), channel_id=1, source_target_pairs={{0,1},{1,0},{2,3},{3,2},{4,5},{5,4},{6,7},{7,6},{8,9},{9,8},{10,11... | collective-permute-start | bytes 3145736 | tf_op jit(solution)/shard_map/ppermute | solution.py:279
  2.9 11.6 %copy-start.3 = (s32[3,8,4]{1,2,0:T(4,128)S(1)}, s32[3,8,4]{1,2,0:T(4,128)}, u32[]{:S(2)}) copy-start(s32[3,8,4]{1,2,0:T(4,128)} %param.11) | copy-start | bytes 1156
  3.0 29.1 %all-to-all-start = ((bf16[16,16,1024]{2,1,0:T(8,128)(2,1)}), bf16[16,16,1024]{2,1,0:T(8,128)(2,1)}, u32[]{:S(2)}, u32[]{:S(2)}) async-start(bf16[16,16,1024]{2,1,0:T(8,128)(2,1)} %broadcast_in_dim.2), calls=%async_computation | async-start | bytes 1048576 | tf_op jit(solution)/shard_map/all_to_all | solution.py:343
  14.5 1.3 collective-permute-start
  54.5 11.4 %copy-start.1 = (bf16[512,1024]{1,0:T(8,128)(2,1)S(1)}, bf16[512,1024]{1,0:T(8,128)(2,1)}, u32[]{:S(2)}) copy-start(bf16[512,1024]{1,0:T(8,128)(2,1)} %refs_3_.3) | copy-start | bytes 3145732
  67.5 6.6 %collective-permute-start.4 = (bf16[64,1024]{1,0:T(8,128)(2,1)S(1)}, bf16[64,1024]{1,0:T(8,128)(2,1)S(1)}, u32[]{:S(2)}, u32[]{:S(2)}) collective-permute-start(bf16[64,1024]{1,0:T(8,128)(2,1)S(1)} %get-tuple-element.48), channel_id=1, source_target_pairs={{16,0},{17,1},{18,2},{19,3},{20,4},{21,5},{22,6},{23,7},{24,8},{25... | collective-permute-start | bytes 393224 | tf_op jit(solution)/shard_map/ppermute | solution.py:289
  68.5 6.7 %collective-permute-start.5 = (bf16[64,1024]{1,0:T(8,128)(2,1)S(1)}, bf16[64,1024]{1,0:T(8,128)(2,1)S(1)}, u32[]{:S(2)}, u32[]{:S(2)}) collective-permute-start(bf16[64,1024]{1,0:T(8,128)(2,1)S(1)} %get-tuple-element.49), channel_id=1, source_target_pairs={{24,0},{25,1},{26,2},{27,3},{28,4},{29,5},{30,6},{31,7},{0,8},{1,9... | collective-permute-start | bytes 393224 | tf_op jit(solution)/shard_map/ppermute | solution.py:289
  70.8 6.2 %collective-permute-start.6 = (bf16[64,1024]{1,0:T(8,128)(2,1)S(1)}, bf16[64,1024]{1,0:T(8,128)(2,1)S(1)}, u32[]{:S(2)}, u32[]{:S(2)}) collective-permute-start(bf16[64,1024]{1,0:T(8,128)(2,1)S(1)} %get-tuple-element.50), channel_id=1, source_target_pairs={{8,0},{9,1},{10,2},{11,3},{12,4},{13,5},{14,6},{15,7},{16,8},{17,9... | collective-permute-start | bytes 393224 | tf_op jit(solution)/shard_map/ppermute | solution.py:289
  77.1 10.6 %copy-start.2 = (bf16[16,1024]{1,0:T(8,128)(2,1)S(1)}, bf16[16,1024]{1,0:T(8,128)(2,1)}, u32[]{:S(2)}) copy-start(bf16[16,1024]{1,0:T(8,128)(2,1)} %refs_0_.1) | copy-start | bytes 98308
  77.1 29.8 %collective-permute-start.10 = (bf16[256,1024]{1,0:T(8,128)(2,1)S(1)}, bf16[256,1024]{1,0:T(8,128)(2,1)S(1)}, u32[]{:S(2)}, u32[]{:S(2)}) collective-permute-start(bf16[256,1024]{1,0:T(8,128)(2,1)S(1)} %get-tuple-element.57.refs_1_), channel_id=1, source_target_pairs={{0,1},{1,0},{2,3},{3,2},{4,5},{5,4},{6,7},{7,6},{8,9},{9,8},{10,11... | collective-permute-start | bytes 1572872 | tf_op jit(solution)/shard_map/ppermute | solution.py:279
  77.2 29.7 %collective-permute-start.17 = (bf16[256,1024]{1,0:T(8,128)(2,1)S(1)}, bf16[256,1024]{1,0:T(8,128)(2,1)S(1)}, u32[]{:S(2)}, u32[]{:S(2)}) collective-permute-start(bf16[256,1024]{1,0:T(8,128)(2,1)S(1)} %get-tuple-element.61.refs_5_), channel_id=1, source_target_pairs={{0,1},{1,0},{2,3},{3,2},{4,5},{5,4},{6,7},{7,6},{8,9},{9,8},{10,11... | collective-permute-start | bytes 1572872 | tf_op jit(solution)/shard_map/ppermute | solution.py:279
  77.7 7.9 %collective-permute-start.7 = (bf16[16,1024]{1,0:T(8,128)(2,1)S(1)}, bf16[16,1024]{1,0:T(8,128)(2,1)S(1)}, u32[]{:S(2)}, u32[]{:S(2)}) collective-permute-start(bf16[16,1024]{1,0:T(8,128)(2,1)S(1)} %get-tuple-element.52), channel_id=1, source_target_pairs={{4,0},{5,1},{6,2},{7,3},{0,4},{1,5},{2,6},{3,7},{12,8},{13,9},{14,... | collective-permute-start | bytes 98312 | tf_op jit(solution)/shard_map/ppermute | solution.py:289
  80.2 6.9 %collective-permute-start.8 = (bf16[16,1024]{1,0:T(8,128)(2,1)S(1)}, bf16[16,1024]{1,0:T(8,128)(2,1)S(1)}, u32[]{:S(2)}, u32[]{:S(2)}) collective-permute-start(bf16[16,1024]{1,0:T(8,128)(2,1)S(1)} %get-tuple-element.53), channel_id=1, source_target_pairs={{6,0},{7,1},{0,2},{1,3},{2,4},{3,5},{4,6},{5,7},{14,8},{15,9},{8,1... | collective-permute-start | bytes 98312 | tf_op jit(solution)/shard_map/ppermute | solution.py:289
  82.6 5.2 %collective-permute-start.9 = (bf16[16,1024]{1,0:T(8,128)(2,1)S(1)}, bf16[16,1024]{1,0:T(8,128)(2,1)S(1)}, u32[]{:S(2)}, u32[]{:S(2)}) collective-permute-start(bf16[16,1024]{1,0:T(8,128)(2,1)S(1)} %get-tuple-element.54), channel_id=1, source_target_pairs={{2,0},{3,1},{4,2},{5,3},{6,4},{7,5},{0,6},{1,7},{10,8},{11,9},{12,... | collective-permute-start | bytes 98312 | tf_op jit(solution)/shard_map/ppermute | solution.py:289
  88.4 8.3 %collective-permute-start.13 = (bf16[16,1024]{1,0:T(8,128)(2,1)S(1)}, bf16[16,1024]{1,0:T(8,128)(2,1)S(1)}, u32[]{:S(2)}, u32[]{:S(2)}) collective-permute-start(bf16[16,1024]{1,0:T(8,128)(2,1)S(1)} %get-tuple-element.58.refs_0_), channel_id=1, source_target_pairs={{4,0},{5,1},{6,2},{7,3},{0,4},{1,5},{2,6},{3,7},{12,8},{13,9},{14,... | collective-permute-start | bytes 98312 | tf_op jit(solution)/shard_map/ppermute | solution.py:289
  92.5 6.0 %collective-permute-start.12 = (bf16[16,1024]{1,0:T(8,128)(2,1)S(1)}, bf16[16,1024]{1,0:T(8,128)(2,1)S(1)}, u32[]{:S(2)}, u32[]{:S(2)}) collective-permute-start(bf16[16,1024]{1,0:T(8,128)(2,1)S(1)} %get-tuple-element.58.refs_0_), channel_id=1, source_target_pairs={{6,0},{7,1},{0,2},{1,3},{2,4},{3,5},{4,6},{5,7},{14,8},{15,9},{8,1... | collective-permute-start | bytes 98312 | tf_op jit(solution)/shard_map/ppermute | solution.py:289
  93.7 4.9 %collective-permute-start.11 = (bf16[16,1024]{1,0:T(8,128)(2,1)S(1)}, bf16[16,1024]{1,0:T(8,128)(2,1)S(1)}, u32[]{:S(2)}, u32[]{:S(2)}) collective-permute-start(bf16[16,1024]{1,0:T(8,128)(2,1)S(1)} %get-tuple-element.58.refs_0_), channel_id=1, source_target_pairs={{2,0},{3,1},{4,2},{5,3},{6,4},{7,5},{0,6},{1,7},{10,8},{11,9},{12,... | collective-permute-start | bytes 98312 | tf_op jit(solution)/shard_map/ppermute | solution.py:289
  98.6 6.6 %collective-permute-start.16 = (bf16[64,1024]{1,0:T(8,128)(2,1)S(1)}, bf16[64,1024]{1,0:T(8,128)(2,1)S(1)}, u32[]{:S(2)}, u32[]{:S(2)}) collective-permute-start(bf16[64,1024]{1,0:T(8,128)(2,1)S(1)} %shard_map.115.refs_0_), channel_id=1, source_target_pairs={{16,0},{17,1},{18,2},{19,3},{20,4},{21,5},{22,6},{23,7},{24,8},{25... | collective-permute-start | bytes 393224 | tf_op jit(solution)/shard_map/ppermute | solution.py:289
  99.6 5.6 %collective-permute-start.15 = (bf16[64,1024]{1,0:T(8,128)(2,1)S(1)}, bf16[64,1024]{1,0:T(8,128)(2,1)S(1)}, u32[]{:S(2)}, u32[]{:S(2)}) collective-permute-start(bf16[64,1024]{1,0:T(8,128)(2,1)S(1)} %shard_map.115.refs_0_), channel_id=1, source_target_pairs={{24,0},{25,1},{26,2},{27,3},{28,4},{29,5},{30,6},{31,7},{0,8},{1,9... | collective-permute-start | bytes 393224 | tf_op jit(solution)/shard_map/ppermute | solution.py:289
  100.7 6.2 %collective-permute-start.14 = (bf16[64,1024]{1,0:T(8,128)(2,1)S(1)}, bf16[64,1024]{1,0:T(8,128)(2,1)S(1)}, u32[]{:S(2)}, u32[]{:S(2)}) collective-permute-start(bf16[64,1024]{1,0:T(8,128)(2,1)S(1)} %shard_map.115.refs_0_), channel_id=1, source_target_pairs={{8,0},{9,1},{10,2},{11,3},{12,4},{13,5},{14,6},{15,7},{16,8},{17,9... | collective-permute-start | bytes 393224 | tf_op jit(solution)/shard_map/ppermute | solution.py:289
  133.3 4.8 %collective-permute-start.18 = (bf16[256,2048]{1,0:T(8,128)(2,1)S(1)}, bf16[256,2048]{1,0:T(8,128)(2,1)S(1)}, u32[]{:S(2)}, u32[]{:S(2)}) collective-permute-start(bf16[256,2048]{1,0:T(8,128)(2,1)S(1)} %bitcast.8), channel_id=1, source_target_pairs={{0,1},{1,0},{2,3},{3,2},{4,5},{5,4},{6,7},{7,6},{8,9},{9,8},{10,11... | collective-permute-start | bytes 3145736 | tf_op jit(solution)/shard_map/ppermute | solution.py:279
  133.3 4.6 %collective-permute-start.19 = (bf16[256,1024]{1,0:T(8,128)(2,1)S(1)}, bf16[256,1024]{1,0:T(8,128)(2,1)S(1)}, u32[]{:S(2)}, u32[]{:S(2)}) collective-permute-start(bf16[256,1024]{1,0:T(8,128)(2,1)S(1)} %get-tuple-element.65.refs_7_), channel_id=1, source_target_pairs={{0,1},{1,0},{2,3},{3,2},{4,5},{5,4},{6,7},{7,6},{8,9},{9,8},{10,11... | collective-permute-start | bytes 1572872 | tf_op jit(solution)/shard_map/ppermute | solution.py:279
  133.8 4.3 %collective-permute-start.20 = (f32[8,128]{1,0:T(8,128)S(1)}, f32[8,128]{1,0:T(8,128)S(1)}, u32[]{:S(2)}, u32[]{:S(2)}) collective-permute-start(f32[8,128]{1,0:T(8,128)S(1)} %get-tuple-element.66.refs_9_), channel_id=1, source_target_pairs={{0,1},{1,0},{2,3},{3,2},{4,5},{5,4},{6,7},{7,6},{8,9},{9,8},{10,11... | collective-permute-start | bytes 12296 | tf_op jit(solution)/shard_map/ppermute | solution.py:279
  135.1 7.9 %collective-permute-start.21 = (bf16[64,1024]{1,0:T(8,128)(2,1)S(1)}, bf16[64,1024]{1,0:T(8,128)(2,1)S(1)}, u32[]{:S(2)}, u32[]{:S(2)}) collective-permute-start(bf16[64,1024]{1,0:T(8,128)(2,1)S(1)} %get-tuple-element.76), channel_id=1, source_target_pairs={{16,0},{17,1},{18,2},{19,3},{20,4},{21,5},{22,6},{23,7},{24,8},{25... | collective-permute-start | bytes 393224 | tf_op jit(solution)/shard_map/ppermute | solution.py:289
  136.1 7.9 %collective-permute-start.22 = (bf16[64,1024]{1,0:T(8,128)(2,1)S(1)}, bf16[64,1024]{1,0:T(8,128)(2,1)S(1)}, u32[]{:S(2)}, u32[]{:S(2)}) collective-permute-start(bf16[64,1024]{1,0:T(8,128)(2,1)S(1)} %get-tuple-element.77), channel_id=1, source_target_pairs={{24,0},{25,1},{26,2},{27,3},{28,4},{29,5},{30,6},{31,7},{0,8},{1,9... | collective-permute-start | bytes 393224 | tf_op jit(solution)/shard_map/ppermute | solution.py:289
  137.9 7.6 %collective-permute-start.23 = (bf16[64,1024]{1,0:T(8,128)(2,1)S(1)}, bf16[64,1024]{1,0:T(8,128)(2,1)S(1)}, u32[]{:S(2)}, u32[]{:S(2)}) collective-permute-start(bf16[64,1024]{1,0:T(8,128)(2,1)S(1)} %get-tuple-element.78), channel_id=1, source_target_pairs={{8,0},{9,1},{10,2},{11,3},{12,4},{13,5},{14,6},{15,7},{16,8},{17,9... | collective-permute-start | bytes 393224 | tf_op jit(solution)/shard_map/ppermute | solution.py:289
  145.5 8.0 %collective-permute-start.24 = (bf16[16,1024]{1,0:T(8,128)(2,1)S(1)}, bf16[16,1024]{1,0:T(8,128)(2,1)S(1)}, u32[]{:S(2)}, u32[]{:S(2)}) collective-permute-start(bf16[16,1024]{1,0:T(8,128)(2,1)S(1)} %get-tuple-element.81), channel_id=1, source_target_pairs={{4,0},{5,1},{6,2},{7,3},{0,4},{1,5},{2,6},{3,7},{12,8},{13,9},{14,... | collective-permute-start | bytes 98312 | tf_op jit(solution)/shard_map/ppermute | solution.py:289
  148.7 6.0 %collective-permute-start.25 = (bf16[16,1024]{1,0:T(8,128)(2,1)S(1)}, bf16[16,1024]{1,0:T(8,128)(2,1)S(1)}, u32[]{:S(2)}, u32[]{:S(2)}) collective-permute-start(bf16[16,1024]{1,0:T(8,128)(2,1)S(1)} %get-tuple-element.82), channel_id=1, source_target_pairs={{6,0},{7,1},{0,2},{1,3},{2,4},{3,5},{4,6},{5,7},{14,8},{15,9},{8,1... | collective-permute-start | bytes 98312 | tf_op jit(solution)/shard_map/ppermute | solution.py:289
  152.0 5.2 %collective-permute-start.26 = (bf16[16,1024]{1,0:T(8,128)(2,1)S(1)}, bf16[16,1024]{1,0:T(8,128)(2,1)S(1)}, u32[]{:S(2)}, u32[]{:S(2)}) collective-permute-start(bf16[16,1024]{1,0:T(8,128)(2,1)S(1)} %get-tuple-element.83), channel_id=1, source_target_pairs={{2,0},{3,1},{4,2},{5,3},{6,4},{7,5},{0,6},{1,7},{10,8},{11,9},{12,... | collective-permute-start | bytes 98312 | tf_op jit(solution)/shard_map/ppermute | solution.py:289

commit v9 on v8

--- a/solution.py
+++ b/solution.py
@@ -15,7 +15,6 @@
 TILE = 512
 DOWN = 2
 PLACES = (0, 1, 3, 2)
-SAME_CORE = [[chip * CORES + core for chip in range(CHIPS)] for core in range(CORES)]
 VMEM = pl.BlockSpec(memory_space=pltpu.VMEM)
 SMEM = pl.BlockSpec(memory_space=pltpu.SMEM)
 ANY = pl.BlockSpec(memory_space=pl.ANY)
@@ -43,10 +42,10 @@
 DONE = shaped((8, BLK), jnp.float32)
 
 
-def join_kernel(*refs):
+def join_kernel(*refs, places=PLACES):
     joined_ref = refs[-1]
     size = refs[0].shape[0]
-    for place, ref in zip(PLACES, refs[:-1]):
+    for place, ref in zip(places, refs[:-1]):
         joined_ref[pl.ds(place * size, size), :] = ref[...]
 
 
@@ -67,37 +66,26 @@
     return lax.dot_general(left, right, (((1,), (1,)), ((), ())), preferred_element_type=jnp.float32)
 
 
-def gate_up_kernel(mask_ref, mask_other_ref, chips_ref, *refs):
-    weights, kept_refs, (out_ref, rows_ref, scratch, sems) = list(refs[:4]), refs[4:8], refs[8:]
-    chip = lax.axis_index("col") // CORES
-    size = chips_ref.shape[1]
-    pairs = [(weights[2], scratch)]
-    for part in range(CHIPS):
-        x = lax.rem(chip // Z + part // Z, X)
-        z = lax.rem(chip + part % Z, Z)
-        pairs.append((chips_ref.at[x * Z + z], rows_ref.at[pl.ds(part * size, size), :]))
-    copies = [pltpu.make_async_copy(src, dst, sems.at[at]) for at, (src, dst) in enumerate(pairs)]
-    for copy in copies[1:] + copies[:1]:
-        copy.start()
-    weights[2] = scratch
-
-    def masked(which):
+def gate_up_kernel(mask_ref, mask_other_ref, *refs):
+    slabs, weights, kept_refs = refs[:X], list(refs[X : X + 4]), refs[X + 4 : X + 8]
+    out_ref, rows_ref, scratch, sems = refs[X + 8 :]
+    copies = {}
+    for which in (0, 2):
+        copies[which] = pltpu.make_async_copy(weights[which], scratch.at[which // 2], sems.at[which // 2])
+        copies[which].start()
+        weights[which] = scratch.at[which // 2]
+    join_kernel(*slabs, rows_ref)
+    for which in (1, 3, 0, 2):
+        units = kept_refs[which].shape[1]
+        if which in copies:
+            copies[which].wait()
         keep((mask_ref, mask_other_ref)[which % 2], which // 2, weights[which], kept_refs[which])
-
-    def multiplied(which):
-        units = scratch.shape[1]
         value = plain_dot(rows_ref[...], kept_refs[which][...])
         out_ref[:, pl.ds(which * units, units)] = value.astype(out_ref.dtype)
 
-    for which in (0, 1, 3):
-        masked(which)
-    for copy in copies[1:]:
-        copy.wait()
-    for which in (0, 1, 3):
-        multiplied(which)
-    copies[0].wait()
-    masked(2)
-    multiplied(2)
+
+def keep_down_kernel(mask_ref, down_ref, kept_ref):
+    keep(mask_ref, DOWN, down_ref, kept_ref)
 
 
 def put_slabs(out_refs, cols, value):
@@ -106,14 +94,12 @@
         ref[:, cols] = value[part * size : (part + 1) * size].astype(ref.dtype)
 
 
-def output_kernel(mask_ref, mask_other_ref, hidden_ref, down_ref, down_other_ref, kept_ref, kept_other_ref, *out_refs):
+def output_kernel(hidden_ref, down_ref, down_other_ref, *out_refs):
     units, width = down_ref.shape
-    keep(mask_ref, DOWN, down_ref, kept_ref)
-    keep(mask_other_ref, DOWN, down_other_ref, kept_other_ref)
     for at in range(0, width, TILE):
         cols = pl.ds(at, TILE)
-        value = plain_dot(hidden_ref[:, :units], kept_ref[:, cols])
-        value = value + plain_dot(hidden_ref[:, units:], kept_other_ref[:, cols])
+        value = plain_dot(hidden_ref[:, :units], down_ref[:, cols])
+        value = value + plain_dot(hidden_ref[:, units:], down_other_ref[:, cols])
         put_slabs(out_refs, cols, value)
 
 
@@ -289,13 +275,14 @@
     return lax.ppermute(value, "col", pairs)
 
 
-def gather_z(block):
-    return [block] + [fetch(block, 0, step) for step in PLACES[1:]]
-
-
-def joined(parts):
+def gather_z(block, places=PLACES):
+    return [block] + [fetch(block, 0, step) for step in places[1:]]
+
+
+def joined(parts, places=PLACES, after=()):
     size, width = parts[0].shape
-    return call(join_kernel, shaped((len(parts) * size, width)), *parts)
+    kernel = functools.partial(join_kernel, places=places)
+    return call(kernel, shaped((len(parts) * size, width)), *parts, after=after)
 
 
 def gather_x(block):
@@ -336,21 +323,22 @@
     slab = shaped((Z * tokens, width))
     piece = shaped((tokens, width))
     wide, tall = shaped((width, units)), shaped((units, width))
-    gates, ups, downs, masks = (
-        (value, other_core(value)) for value in (gate_weight, up_weight, down_weight, mask)
-    )
-    copies = jnp.broadcast_to(inputs[None], (CHIPS, tokens, width))
-    chips = lax.all_to_all(copies, "col", 0, 0, axis_index_groups=SAME_CORE)
+    gates, ups, masks = ((value, other_core(value)) for value in (gate_weight, up_weight, mask))
+    places = (0, 2, 1, 3)
+    near = joined(gather_z(inputs, places), places, (gates[1], ups[1]))
+    down = call(keep_down_kernel, tall, mask, down_weight, in_specs=[SMEM, VMEM], after=(near,))
+    downs = (down, other_core(down))
     *gate_ups, partial, rows = call(
         gate_up_kernel,
         (wide,) * 4 + (shaped((half, 4 * units)), shaped((half, width))),
         *masks,
-        in_hbm(chips),
-        *gates,
+        *gather_x(near),
+        in_hbm(gates[0]),
+        gates[1],
         in_hbm(ups[0]),
         ups[1],
-        in_specs=[SMEM] * 2 + [ANY] + [VMEM] * 2 + [ANY, VMEM],
-        scratch_shapes=[pltpu.VMEM(wide.shape, wide.dtype), pltpu.SemaphoreType.DMA((CHIPS + 1,))],
+        in_specs=[SMEM] * 2 + [VMEM] * X + [ANY, VMEM] * 2,
+        scratch_shapes=[pltpu.VMEM((2,) + wide.shape, wide.dtype), pltpu.SemaphoreType.DMA((2,))],
         flops=8 * half * width * units,
         vmem=16,
         after=downs[1:],
@@ -361,10 +349,7 @@
         exchange_row(split(partial, ROWS)),
     )
     hidden = flat(exchange_row(copies))
-    *downs, first, second, third, fourth = multiply(
-        output_kernel, (tall,) * 2 + (slab,) * X, [hidden], downs, masks
-    )
-    slabs = spread_x([first, second, third, fourth])
+    slabs = spread_x(multiply(output_kernel, (slab,) * X, [hidden], downs))
     parts = call(sum_kernel, (piece,) * Z, *slabs)
     rows, hidden = hold((rows, hidden), parts[:1])
     rows_other, hidden_other = other_core(rows), other_core(hidden)

time: 158 us -> 157 us (level)
  waiting for transfers between devices: 41.7 us -> 37.5 us
  starting transfers between devices: 45 us -> 46.9 us
    all_to_all x1 -> x0, waiting for transfers between devices: 16.3 us -> none  [per_device(): chips = lax.all_to_all(copies, 'col', 0, 0, axis_index_groups=SAME_CORE)]
    ppermute x18 -> x24, starting transfers between devices: 31.6 us -> 45.1 us  [fetch(): return lax.ppermute(value, 'col', pairs)]
    ppermute x18 -> x24, waiting for transfers between devices: 24.3 us -> 36.3 us  [fetch(): return lax.ppermute(value, 'col', pairs)]
    all_to_all x1 -> x0, starting transfers between devices: 11.6 us -> none  [per_device(): chips = lax.all_to_all(copies, 'col', 0, 0, axis_index_groups=SAME_CORE)]
    broadcast_in_dim x1 -> x0, local copies, waits for them, and re-layouts: 1.61 us -> none  [per_device(): copies = jnp.broadcast_to(inputs[None], (CHIPS, tokens, width))]
    pallas_call x12 -> x14, Pallas kernels: 13.5 us -> 13.3 us  [call(): pl.pallas_call(lambda *refs: kernel(*refs[:len(args)], *refs[len(args) +...]
  transfers between devices with their start and end apart: 28 -> 33, of which waited for: 18 -> 21; matrix products, arithmetic and copies ran while one was open for 1% -> 0% of each run, Pallas kernels for 4% -> 4%
where the time goes in v9:
time: 157 us; the launch traced here: 156 us
  blocking collectives  56.5 us (36%)
  starting transfers between devices  46.9 us (30%)
  waiting for transfers between devices  37.5 us (24%)
  Pallas kernels  13.3 us (8%)
    all_to_all x4, blocking collectives, exchange_row(): return lax.all_to_all(value, 'row', 0, 0)  56.5 us
    ppermute x24, starting transfers between devices, fetch(): return lax.ppermute(value, 'col', pairs)  45.1 us
    ppermute x24, waiting for transfers between devices, fetch(): return lax.ppermute(value, 'col', pairs)  36.3 us
    pallas_call x14, Pallas kernels, call(): pl.pallas_call(lambda *refs: kernel(*refs[:len(args)], *refs[len(args) +...  13.3 us
  transfers between devices with their start and end apart: 33, of which 21 were waited for; matrix products, arithmetic and copies ran while one was open for 0% of the time, Pallas kernels for 4%

profile of v9, /device:TPU:6, one launch (start us, length us, event | category | flops | bytes accessed | tf_op | source)
XLA Modules:
  0.0 156.5 jit_solution(6087224764794372245)
XLA Ops:
  1.2 6.3 %collective-permute-start.2 = (bf16[16,1024]{1,0:T(8,128)(2,1)}, bf16[16,1024]{1,0:T(8,128)(2,1)S(1)}, u32[]{:S(2)}, u32[]{:S(2)}) collective-permute-start(bf16[16,1024]{1,0:T(8,128)(2,1)} %refs_0_.2), channel_id=1, source_target_pairs={{2,0},{3,1},{4,2},{5,3},{6,4},{7,5},{0,6},{1,7},{10,8},{11,9},{12,... | collective-permute-start | bytes 98312 | tf_op jit(solution)/shard_map/ppermute | solution.py:275
  8.4 2.9 %collective-permute-start.3 = (bf16[16,1024]{1,0:T(8,128)(2,1)}, bf16[16,1024]{1,0:T(8,128)(2,1)S(1)}, u32[]{:S(2)}, u32[]{:S(2)}) collective-permute-start(bf16[16,1024]{1,0:T(8,128)(2,1)} %refs_0_.2), channel_id=1, source_target_pairs={{6,0},{7,1},{0,2},{1,3},{2,4},{3,5},{4,6},{5,7},{14,8},{15,9},{8,1... | collective-permute-start | bytes 98312 | tf_op jit(solution)/shard_map/ppermute | solution.py:275
  11.4 4.4 %collective-permute-done.1.refs_1_ = bf16[16,1024]{1,0:T(8,128)(2,1)S(1)} collective-permute-done((bf16[16,1024]{1,0:T(8,128)(2,1)}, bf16[16,1024]{1,0:T(8,128)(2,1)S(1)}, u32[]{:S(2)}, u32[]{:S(2)}) %collective-permute-start.1) | collective-permute-done | bytes 32800 | tf_op jit(solution)/shard_map/ppermute | solution.py:275
  18.3 1.5 collective-permute-start.8
  19.7 2.1 %collective-permute-start.7 = (bf16[64,1024]{1,0:T(8,128)(2,1)S(1)}, bf16[64,1024]{1,0:T(8,128)(2,1)S(1)}, u32[]{:S(2)}, u32[]{:S(2)}) collective-permute-start(bf16[64,1024]{1,0:T(8,128)(2,1)S(1)} %shard_map.109.refs_2_), channel_id=1, source_target_pairs={{24,0},{25,1},{26,2},{27,3},{28,4},{29,5},{30,6},{31,7},{0,8},{1,9... | collective-permute-start | bytes 393224 | tf_op jit(solution)/shard_map/ppermute | solution.py:275
  23.0 3.1 %collective-permute-done.8.refs_5_ = bf16[64,1024]{1,0:T(8,128)(2,1)S(1)} collective-permute-done((bf16[64,1024]{1,0:T(8,128)(2,1)S(1)}, bf16[64,1024]{1,0:T(8,128)(2,1)S(1)}, u32[]{:S(2)}, u32[]{:S(2)}) %collective-permute-start.8) | collective-permute-done | bytes 131104 | tf_op jit(solution)/shard_map/ppermute | solution.py:275
  26.3 2.3 %collective-permute-done.6.refs_3_ = bf16[64,1024]{1,0:T(8,128)(2,1)S(1)} collective-permute-done((bf16[64,1024]{1,0:T(8,128)(2,1)S(1)}, bf16[64,1024]{1,0:T(8,128)(2,1)S(1)}, u32[]{:S(2)}, u32[]{:S(2)}) %collective-permute-start.6) | collective-permute-done | bytes 131104 | tf_op jit(solution)/shard_map/ppermute | solution.py:275
  28.6 3.7 %shard_map.111 = (bf16[1024,512]{1,0:T(8,128)(2,1)S(1)}, bf16[1024,512]{1,0:T(8,128)(2,1)S(1)}, bf16[1024,512]{1,0:T(8,128)(2,1)S(1)}, bf16[1024,512]{1,0:T(8,12...) custom-call(s32[3,4,8]{2,1,0:T(4,128)S(1)} %bitcast.15, ...), custom_call_target="tpu_custom_call" | custom-call | flops 1073741824 | bytes 10486528 | tf_op jit(solution)/shard_map/pallas_call | solution.py:26
  32.3 19.6 %all_to_all.20.refs_0_ = bf16[8,32,2048]{2,1,0:T(8,128)(2,1)S(1)} all-to-all(bf16[8,32,2048]{2,1,0:T(8,128)(2,1)S(1)} %bitcast.11), channel_id=1, replica_groups=mesh['row'=8,'col'=32] {'row'}, dimensions={0} | all-to-all | bytes 2097152 | tf_op jit(solution)/shard_map/all_to_all | solution.py:301
  52.2 11.3 %all_to_all.21 = bf16[8,32,1024]{2,1,0:T(8,128)(2,1)S(1)} all-to-all(bf16[8,32,1024]{2,1,0:T(8,128)(2,1)S(1)} %get-tuple-element.44), channel_id=1, replica_groups=mesh['row'=8,'col'=32] {'row'}, dimensions={0} | all-to-all | bytes 1048576 | tf_op jit(solution)/shard_map/all_to_all | solution.py:301
  64.2 2.2 %collective-permute-start.10 = (bf16[64,1024]{1,0:T(8,128)(2,1)S(1)}, bf16[64,1024]{1,0:T(8,128)(2,1)S(1)}, u32[]{:S(2)}, u32[]{:S(2)}) collective-permute-start(bf16[64,1024]{1,0:T(8,128)(2,1)S(1)} %get-tuple-element.46), channel_id=1, source_target_pairs={{16,0},{17,1},{18,2},{19,3},{20,4},{21,5},{22,6},{23,7},{24,8},{25... | collective-permute-start | bytes 393224 | tf_op jit(solution)/shard_map/ppermute | solution.py:275
  68.5 2.3 %collective-permute-done.10.refs_1_ = bf16[64,1024]{1,0:T(8,128)(2,1)S(1)} collective-permute-done((bf16[64,1024]{1,0:T(8,128)(2,1)S(1)}, bf16[64,1024]{1,0:T(8,128)(2,1)S(1)}, u32[]{:S(2)}, u32[]{:S(2)}) %collective-permute-start.10) | collective-permute-done | bytes 131104 | tf_op jit(solution)/shard_map/ppermute | solution.py:275
  71.4 1.9 %collective-permute-done.12.refs_3_ = bf16[64,1024]{1,0:T(8,128)(2,1)S(1)} collective-permute-done((bf16[64,1024]{1,0:T(8,128)(2,1)S(1)}, bf16[64,1024]{1,0:T(8,128)(2,1)S(1)}, u32[]{:S(2)}, u32[]{:S(2)}) %collective-permute-start.12) | collective-permute-done | bytes 131104 | tf_op jit(solution)/shard_map/ppermute | solution.py:275
  74.0 4.1 %collective-permute-start.13 = (bf16[16,1024]{1,0:T(8,128)(2,1)S(1)}, bf16[16,1024]{1,0:T(8,128)(2,1)S(1)}, u32[]{:S(2)}, u32[]{:S(2)}) collective-permute-start(bf16[16,1024]{1,0:T(8,128)(2,1)S(1)} %get-tuple-element.50), channel_id=1, source_target_pairs={{4,0},{5,1},{6,2},{7,3},{0,4},{1,5},{2,6},{3,7},{12,8},{13,9},{14,... | collective-permute-start | bytes 98312 | tf_op jit(solution)/shard_map/ppermute | solution.py:275
  78.1 4.1 %collective-permute-start.15 = (bf16[16,1024]{1,0:T(8,128)(2,1)S(1)}, bf16[16,1024]{1,0:T(8,128)(2,1)S(1)}, u32[]{:S(2)}, u32[]{:S(2)}) collective-permute-start(bf16[16,1024]{1,0:T(8,128)(2,1)S(1)} %get-tuple-element.52), channel_id=1, source_target_pairs={{2,0},{3,1},{4,2},{5,3},{6,4},{7,5},{0,6},{1,7},{10,8},{11,9},{12,... | collective-permute-start | bytes 98312 | tf_op jit(solution)/shard_map/ppermute | solution.py:275
  82.4 1.7 %collective-permute-done.14.refs_3_ = bf16[16,1024]{1,0:T(8,128)(2,1)S(1)} collective-permute-done((bf16[16,1024]{1,0:T(8,128)(2,1)S(1)}, bf16[16,1024]{1,0:T(8,128)(2,1)S(1)}, u32[]{:S(2)}, u32[]{:S(2)}) %collective-permute-start.14) | collective-permute-done | bytes 32800 | tf_op jit(solution)/shard_map/ppermute | solution.py:275
  84.8 3.0 %collective-permute-start.19 = (bf16[16,1024]{1,0:T(8,128)(2,1)S(1)}, bf16[16,1024]{1,0:T(8,128)(2,1)S(1)}, u32[]{:S(2)}, u32[]{:S(2)}) collective-permute-start(bf16[16,1024]{1,0:T(8,128)(2,1)S(1)} %get-tuple-element.56.refs_0_), channel_id=1, source_target_pairs={{4,0},{5,1},{6,2},{7,3},{0,4},{1,5},{2,6},{3,7},{12,8},{13,9},{14,... | collective-permute-start | bytes 98312 | tf_op jit(solution)/shard_map/ppermute | solution.py:275
  87.8 3.8 %collective-permute-start.18 = (bf16[16,1024]{1,0:T(8,128)(2,1)S(1)}, bf16[16,1024]{1,0:T(8,128)(2,1)S(1)}, u32[]{:S(2)}, u32[]{:S(2)}) collective-permute-start(bf16[16,1024]{1,0:T(8,128)(2,1)S(1)} %get-tuple-element.56.refs_0_), channel_id=1, source_target_pairs={{6,0},{7,1},{0,2},{1,3},{2,4},{3,5},{4,6},{5,7},{14,8},{15,9},{8,1... | collective-permute-start | bytes 98312 | tf_op jit(solution)/shard_map/ppermute | solution.py:275
  93.8 2.6 %collective-permute-done.17.refs_1_ = bf16[16,1024]{1,0:T(8,128)(2,1)S(1)} collective-permute-done((bf16[16,1024]{1,0:T(8,128)(2,1)S(1)}, bf16[16,1024]{1,0:T(8,128)(2,1)S(1)}, u32[]{:S(2)}, u32[]{:S(2)}) %collective-permute-start.17) | collective-permute-done | bytes 32800 | tf_op jit(solution)/shard_map/ppermute | solution.py:275
  97.7 1.8 %collective-permute-start.21 = (bf16[64,1024]{1,0:T(8,128)(2,1)S(1)}, bf16[64,1024]{1,0:T(8,128)(2,1)S(1)}, u32[]{:S(2)}, u32[]{:S(2)}) collective-permute-start(bf16[64,1024]{1,0:T(8,128)(2,1)S(1)} %shard_map.117.refs_0_), channel_id=1, source_target_pairs={{24,0},{25,1},{26,2},{27,3},{28,4},{29,5},{30,6},{31,7},{0,8},{1,9... | collective-permute-start | bytes 393224 | tf_op jit(solution)/shard_map/ppermute | solution.py:275
  99.7 3.4 %collective-permute-done.22.refs_3_ = bf16[64,1024]{1,0:T(8,128)(2,1)S(1)} collective-permute-done((bf16[64,1024]{1,0:T(8,128)(2,1)S(1)}, bf16[64,1024]{1,0:T(8,128)(2,1)S(1)}, u32[]{:S(2)}, u32[]{:S(2)}) %collective-permute-start.22) | collective-permute-done | bytes 131104 | tf_op jit(solution)/shard_map/ppermute | solution.py:275
  103.1 2.6 %collective-permute-done.20.refs_1_ = bf16[64,1024]{1,0:T(8,128)(2,1)S(1)} collective-permute-done((bf16[64,1024]{1,0:T(8,128)(2,1)S(1)}, bf16[64,1024]{1,0:T(8,128)(2,1)S(1)}, u32[]{:S(2)}, u32[]{:S(2)}) %collective-permute-start.20) | collective-permute-done | bytes 131104 | tf_op jit(solution)/shard_map/ppermute | solution.py:275
  106.4 11.6 %all_to_all.22.refs_0_ = bf16[8,32,1152]{2,1,0:T(8,128)(2,1)S(1)} all-to-all(bf16[8,32,1152]{2,1,0:T(8,128)(2,1)S(1)} %bitcast.12), channel_id=1, replica_groups=mesh['row'=8,'col'=32] {'row'}, dimensions={0} | all-to-all | bytes 1179648 | tf_op jit(solution)/shard_map/all_to_all | solution.py:301
  118.2 13.9 %all_to_all.23 = bf16[8,32,2048]{2,1,0:T(8,128)(2,1)S(1)} all-to-all(bf16[8,32,2048]{2,1,0:T(8,128)(2,1)S(1)} %get-tuple-element.60), channel_id=1, replica_groups=mesh['row'=8,'col'=32] {'row'}, dimensions={0} | all-to-all | bytes 2097152 | tf_op jit(solution)/shard_map/all_to_all | solution.py:301
  134.0 1.7 %collective-permute-start.28 = (bf16[64,1024]{1,0:T(8,128)(2,1)S(1)}, bf16[64,1024]{1,0:T(8,128)(2,1)S(1)}, u32[]{:S(2)}, u32[]{:S(2)}) collective-permute-start(bf16[64,1024]{1,0:T(8,128)(2,1)S(1)} %get-tuple-element.73), channel_id=1, source_target_pairs={{24,0},{25,1},{26,2},{27,3},{28,4},{29,5},{30,6},{31,7},{0,8},{1,9... | collective-permute-start | bytes 393224 | tf_op jit(solution)/shard_map/ppermute | solution.py:275
  136.1 4.2 %shard_map.120 = (bf16[1024,512]{1,0:T(8,128)(2,1)}, bf16[1024,512]{1,0:T(8,128)(2,1)}, bf16[512,1024]{1,0:T(8,128)(2,1)}, f32[1,1]{1,0:T(1,128)}, f32[8,128]{1,0:T(8,128)S(1)}) custom-call(s32[3,4,8]{2,1,0:T(4,128)S(1)} %bitcast.16, bf16[256,1024]{1,0:T(8,128)(2,1)S(1)} %get-tuple-element.55.refs_1_, ...), custom_call_target="tpu_custom_call" | custom-call | flops 1610612736 | bytes 8401284 | tf_op jit(solution)/shard_map/pallas_call | solution.py:26
  140.3 1.5 collective-permute-done.27.refs_1_
  142.8 1.4 collective-permute-done.29.refs_3_
  144.3 1.8 %collective-permute-start.30 = (bf16[16,1024]{1,0:T(8,128)(2,1)S(1)}, bf16[16,1024]{1,0:T(8,128)(2,1)S(1)}, u32[]{:S(2)}, u32[]{:S(2)}) collective-permute-start(bf16[16,1024]{1,0:T(8,128)(2,1)S(1)} %get-tuple-element.77), channel_id=1, source_target_pairs={{4,0},{5,1},{6,2},{7,3},{0,4},{1,5},{2,6},{3,7},{12,8},{13,9},{14,... | collective-permute-start | bytes 98312 | tf_op jit(solution)/shard_map/ppermute | solution.py:275
  146.1 4.6 %collective-permute-start.31 = (bf16[16,1024]{1,0:T(8,128)(2,1)S(1)}, bf16[16,1024]{1,0:T(8,128)(2,1)S(1)}, u32[]{:S(2)}, u32[]{:S(2)}) collective-permute-start(bf16[16,1024]{1,0:T(8,128)(2,1)S(1)} %get-tuple-element.78), channel_id=1, source_target_pairs={{6,0},{7,1},{0,2},{1,3},{2,4},{3,5},{4,6},{5,7},{14,8},{15,9},{8,1... | collective-permute-start | bytes 98312 | tf_op jit(solution)/shard_map/ppermute | solution.py:275
  150.7 1.7 %collective-permute-done.30.refs_1_ = bf16[16,1024]{1,0:T(8,128)(2,1)S(1)} collective-permute-done((bf16[16,1024]{1,0:T(8,128)(2,1)S(1)}, bf16[16,1024]{1,0:T(8,128)(2,1)S(1)}, u32[]{:S(2)}, u32[]{:S(2)}) %collective-permute-start.30) | collective-permute-done | bytes 32800 | tf_op jit(solution)/shard_map/ppermute | solution.py:275
  153.4 2.5 %collective-permute-done.32.refs_3_ = bf16[16,1024]{1,0:T(8,128)(2,1)S(1)} collective-permute-done((bf16[16,1024]{1,0:T(8,128)(2,1)S(1)}, bf16[16,1024]{1,0:T(8,128)(2,1)S(1)}, u32[]{:S(2)}, u32[]{:S(2)}) %collective-permute-start.32) | collective-permute-done | bytes 32800 | tf_op jit(solution)/shard_map/ppermute | solution.py:275
  (61 shorter events, 19.9 us)
Async XLA Ops:
  0.6 15.1 %collective-permute-start.4 = (bf16[1024,512]{1,0:T(8,128)(2,1)}, bf16[1024,512]{1,0:T(8,128)(2,1)S(1)}, u32[]{:S(2)}, u32[]{:S(2)}) collective-permute-start(bf16[1024,512]{1,0:T(8,128)(2,1)} %refs_6_.1), channel_id=1, source_target_pairs={{0,1},{1,0},{2,3},{3,2},{4,5},{5,4},{6,7},{7,6},{8,9},{9,8},{10,11... | collective-permute-start | bytes 3145736 | tf_op jit(solution)/shard_map/ppermute | solution.py:265
  0.7 15.0 %collective-permute-start.5 = (bf16[1024,512]{1,0:T(8,128)(2,1)}, bf16[1024,512]{1,0:T(8,128)(2,1)S(1)}, u32[]{:S(2)}, u32[]{:S(2)}) collective-permute-start(bf16[1024,512]{1,0:T(8,128)(2,1)} %refs_8_.1), channel_id=1, source_target_pairs={{0,1},{1,0},{2,3},{3,2},{4,5},{5,4},{6,7},{7,6},{8,9},{9,8},{10,11... | collective-permute-start | bytes 3145736 | tf_op jit(solution)/shard_map/ppermute | solution.py:265
  1.2 10.1 %collective-permute-start.2 = (bf16[16,1024]{1,0:T(8,128)(2,1)}, bf16[16,1024]{1,0:T(8,128)(2,1)S(1)}, u32[]{:S(2)}, u32[]{:S(2)}) collective-permute-start(bf16[16,1024]{1,0:T(8,128)(2,1)} %refs_0_.2), channel_id=1, source_target_pairs={{2,0},{3,1},{4,2},{5,3},{6,4},{7,5},{0,6},{1,7},{10,8},{11,9},{12,... | collective-permute-start | bytes 98312 | tf_op jit(solution)/shard_map/ppermute | solution.py:275
  7.5 8.2 %collective-permute-start.1 = (bf16[16,1024]{1,0:T(8,128)(2,1)}, bf16[16,1024]{1,0:T(8,128)(2,1)S(1)}, u32[]{:S(2)}, u32[]{:S(2)}) collective-permute-start(bf16[16,1024]{1,0:T(8,128)(2,1)} %refs_0_.2), channel_id=1, source_target_pairs={{4,0},{5,1},{6,2},{7,3},{0,4},{1,5},{2,6},{3,7},{12,8},{13,9},{14,... | collective-permute-start | bytes 98312 | tf_op jit(solution)/shard_map/ppermute | solution.py:275
  8.4 7.3 %collective-permute-start.3 = (bf16[16,1024]{1,0:T(8,128)(2,1)}, bf16[16,1024]{1,0:T(8,128)(2,1)S(1)}, u32[]{:S(2)}, u32[]{:S(2)}) collective-permute-start(bf16[16,1024]{1,0:T(8,128)(2,1)} %refs_0_.2), channel_id=1, source_target_pairs={{6,0},{7,1},{0,2},{1,3},{2,4},{3,5},{4,6},{5,7},{14,8},{15,9},{8,1... | collective-permute-start | bytes 98312 | tf_op jit(solution)/shard_map/ppermute | solution.py:275
  18.2 10.5 %collective-permute-start.9 = (bf16[512,1024]{1,0:T(8,128)(2,1)S(1)}, bf16[512,1024]{1,0:T(8,128)(2,1)S(1)}, u32[]{:S(2)}, u32[]{:S(2)}) collective-permute-start(bf16[512,1024]{1,0:T(8,128)(2,1)S(1)} %shard_map.110.refs_1_.refs_4_), channel_id=1, source_target_pairs={{0,1},{1,0},{2,3},{3,2},{4,5},{5,4},{6,7},{7,6},{8,9},{9,8},{10,11... | collective-permute-start | bytes 3145736 | tf_op jit(solution)/shard_map/ppermute | solution.py:265
  18.3 7.9 %collective-permute-start.8 = (bf16[64,1024]{1,0:T(8,128)(2,1)S(1)}, bf16[64,1024]{1,0:T(8,128)(2,1)S(1)}, u32[]{:S(2)}, u32[]{:S(2)}) collective-permute-start(bf16[64,1024]{1,0:T(8,128)(2,1)S(1)} %shard_map.109.refs_2_), channel_id=1, source_target_pairs={{16,0},{17,1},{18,2},{19,3},{20,4},{21,5},{22,6},{23,7},{24,8},{25... | collective-permute-start | bytes 393224 | tf_op jit(solution)/shard_map/ppermute | solution.py:275
  19.7 6.6 %collective-permute-start.7 = (bf16[64,1024]{1,0:T(8,128)(2,1)S(1)}, bf16[64,1024]{1,0:T(8,128)(2,1)S(1)}, u32[]{:S(2)}, u32[]{:S(2)}) collective-permute-start(bf16[64,1024]{1,0:T(8,128)(2,1)S(1)} %shard_map.109.refs_2_), channel_id=1, source_target_pairs={{24,0},{25,1},{26,2},{27,3},{28,4},{29,5},{30,6},{31,7},{0,8},{1,9... | collective-permute-start | bytes 393224 | tf_op jit(solution)/shard_map/ppermute | solution.py:275
  21.8 6.8 %collective-permute-start.6 = (bf16[64,1024]{1,0:T(8,128)(2,1)S(1)}, bf16[64,1024]{1,0:T(8,128)(2,1)S(1)}, u32[]{:S(2)}, u32[]{:S(2)}) collective-permute-start(bf16[64,1024]{1,0:T(8,128)(2,1)S(1)} %shard_map.109.refs_2_), channel_id=1, source_target_pairs={{8,0},{9,1},{10,2},{11,3},{12,4},{13,5},{14,6},{15,7},{16,8},{17,9... | collective-permute-start | bytes 393224 | tf_op jit(solution)/shard_map/ppermute | solution.py:275
  64.2 6.6 %collective-permute-start.10 = (bf16[64,1024]{1,0:T(8,128)(2,1)S(1)}, bf16[64,1024]{1,0:T(8,128)(2,1)S(1)}, u32[]{:S(2)}, u32[]{:S(2)}) collective-permute-start(bf16[64,1024]{1,0:T(8,128)(2,1)S(1)} %get-tuple-element.46), channel_id=1, source_target_pairs={{16,0},{17,1},{18,2},{19,3},{20,4},{21,5},{22,6},{23,7},{24,8},{25... | collective-permute-start | bytes 393224 | tf_op jit(solution)/shard_map/ppermute | solution.py:275
  66.4 5.0 %collective-permute-start.11 = (bf16[64,1024]{1,0:T(8,128)(2,1)S(1)}, bf16[64,1024]{1,0:T(8,128)(2,1)S(1)}, u32[]{:S(2)}, u32[]{:S(2)}) collective-permute-start(bf16[64,1024]{1,0:T(8,128)(2,1)S(1)} %get-tuple-element.47), channel_id=1, source_target_pairs={{24,0},{25,1},{26,2},{27,3},{28,4},{29,5},{30,6},{31,7},{0,8},{1,9... | collective-permute-start | bytes 393224 | tf_op jit(solution)/shard_map/ppermute | solution.py:275
  67.1 6.2 %collective-permute-start.12 = (bf16[64,1024]{1,0:T(8,128)(2,1)S(1)}, bf16[64,1024]{1,0:T(8,128)(2,1)S(1)}, u32[]{:S(2)}, u32[]{:S(2)}) collective-permute-start(bf16[64,1024]{1,0:T(8,128)(2,1)S(1)} %get-tuple-element.48), channel_id=1, source_target_pairs={{8,0},{9,1},{10,2},{11,3},{12,4},{13,5},{14,6},{15,7},{16,8},{17,9... | collective-permute-start | bytes 393224 | tf_op jit(solution)/shard_map/ppermute | solution.py:275
  73.4 32.3 %collective-permute-start.16 = (bf16[256,1024]{1,0:T(8,128)(2,1)S(1)}, bf16[256,1024]{1,0:T(8,128)(2,1)S(1)}, u32[]{:S(2)}, u32[]{:S(2)}) collective-permute-start(bf16[256,1024]{1,0:T(8,128)(2,1)S(1)} %get-tuple-element.55.refs_1_), channel_id=1, source_target_pairs={{0,1},{1,0},{2,3},{3,2},{4,5},{5,4},{6,7},{7,6},{8,9},{9,8},{10,11... | collective-permute-start | bytes 1572872 | tf_op jit(solution)/shard_map/ppermute | solution.py:265
  73.5 32.2 %collective-permute-start.23 = (bf16[256,1024]{1,0:T(8,128)(2,1)S(1)}, bf16[256,1024]{1,0:T(8,128)(2,1)S(1)}, u32[]{:S(2)}, u32[]{:S(2)}) collective-permute-start(bf16[256,1024]{1,0:T(8,128)(2,1)S(1)} %get-tuple-element.57.refs_5_), channel_id=1, source_target_pairs={{0,1},{1,0},{2,3},{3,2},{4,5},{5,4},{6,7},{7,6},{8,9},{9,8},{10,11... | collective-permute-start | bytes 1572872 | tf_op jit(solution)/shard_map/ppermute | solution.py:265
  74.0 8.4 %collective-permute-start.13 = (bf16[16,1024]{1,0:T(8,128)(2,1)S(1)}, bf16[16,1024]{1,0:T(8,128)(2,1)S(1)}, u32[]{:S(2)}, u32[]{:S(2)}) collective-permute-start(bf16[16,1024]{1,0:T(8,128)(2,1)S(1)} %get-tuple-element.50), channel_id=1, source_target_pairs={{4,0},{5,1},{6,2},{7,3},{0,4},{1,5},{2,6},{3,7},{12,8},{13,9},{14,... | collective-permute-start | bytes 98312 | tf_op jit(solution)/shard_map/ppermute | solution.py:275
  78.1 6.0 %collective-permute-start.14 = (bf16[16,1024]{1,0:T(8,128)(2,1)S(1)}, bf16[16,1024]{1,0:T(8,128)(2,1)S(1)}, u32[]{:S(2)}, u32[]{:S(2)}) collective-permute-start(bf16[16,1024]{1,0:T(8,128)(2,1)S(1)} %get-tuple-element.51), channel_id=1, source_target_pairs={{6,0},{7,1},{0,2},{1,3},{2,4},{3,5},{4,6},{5,7},{14,8},{15,9},{8,1... | collective-permute-start | bytes 98312 | tf_op jit(solution)/shard_map/ppermute | solution.py:275
  78.1 6.0 %collective-permute-start.15 = (bf16[16,1024]{1,0:T(8,128)(2,1)S(1)}, bf16[16,1024]{1,0:T(8,128)(2,1)S(1)}, u32[]{:S(2)}, u32[]{:S(2)}) collective-permute-start(bf16[16,1024]{1,0:T(8,128)(2,1)S(1)} %get-tuple-element.52), channel_id=1, source_target_pairs={{2,0},{3,1},{4,2},{5,3},{6,4},{7,5},{0,6},{1,7},{10,8},{11,9},{12,... | collective-permute-start | bytes 98312 | tf_op jit(solution)/shard_map/ppermute | solution.py:275
  84.8 8.2 %collective-permute-start.19 = (bf16[16,1024]{1,0:T(8,128)(2,1)S(1)}, bf16[16,1024]{1,0:T(8,128)(2,1)S(1)}, u32[]{:S(2)}, u32[]{:S(2)}) collective-permute-start(bf16[16,1024]{1,0:T(8,128)(2,1)S(1)} %get-tuple-element.56.refs_0_), channel_id=1, source_target_pairs={{4,0},{5,1},{6,2},{7,3},{0,4},{1,5},{2,6},{3,7},{12,8},{13,9},{14,... | collective-permute-start | bytes 98312 | tf_op jit(solution)/shard_map/ppermute | solution.py:275
  87.8 6.0 %collective-permute-start.18 = (bf16[16,1024]{1,0:T(8,128)(2,1)S(1)}, bf16[16,1024]{1,0:T(8,128)(2,1)S(1)}, u32[]{:S(2)}, u32[]{:S(2)}) collective-permute-start(bf16[16,1024]{1,0:T(8,128)(2,1)S(1)} %get-tuple-element.56.refs_0_), channel_id=1, source_target_pairs={{6,0},{7,1},{0,2},{1,3},{2,4},{3,5},{4,6},{5,7},{14,8},{15,9},{8,1... | collective-permute-start | bytes 98312 | tf_op jit(solution)/shard_map/ppermute | solution.py:275
  91.6 4.9 %collective-permute-start.17 = (bf16[16,1024]{1,0:T(8,128)(2,1)S(1)}, bf16[16,1024]{1,0:T(8,128)(2,1)S(1)}, u32[]{:S(2)}, u32[]{:S(2)}) collective-permute-start(bf16[16,1024]{1,0:T(8,128)(2,1)S(1)} %get-tuple-element.56.refs_0_), channel_id=1, source_target_pairs={{2,0},{3,1},{4,2},{5,3},{6,4},{7,5},{0,6},{1,7},{10,8},{11,9},{12,... | collective-permute-start | bytes 98312 | tf_op jit(solution)/shard_map/ppermute | solution.py:275
  96.5 6.6 %collective-permute-start.22 = (bf16[64,1024]{1,0:T(8,128)(2,1)S(1)}, bf16[64,1024]{1,0:T(8,128)(2,1)S(1)}, u32[]{:S(2)}, u32[]{:S(2)}) collective-permute-start(bf16[64,1024]{1,0:T(8,128)(2,1)S(1)} %shard_map.117.refs_0_), channel_id=1, source_target_pairs={{16,0},{17,1},{18,2},{19,3},{20,4},{21,5},{22,6},{23,7},{24,8},{25... | collective-permute-start | bytes 393224 | tf_op jit(solution)/shard_map/ppermute | solution.py:275
  97.7 5.4 %collective-permute-start.21 = (bf16[64,1024]{1,0:T(8,128)(2,1)S(1)}, bf16[64,1024]{1,0:T(8,128)(2,1)S(1)}, u32[]{:S(2)}, u32[]{:S(2)}) collective-permute-start(bf16[64,1024]{1,0:T(8,128)(2,1)S(1)} %shard_map.117.refs_0_), channel_id=1, source_target_pairs={{24,0},{25,1},{26,2},{27,3},{28,4},{29,5},{30,6},{31,7},{0,8},{1,9... | collective-permute-start | bytes 393224 | tf_op jit(solution)/shard_map/ppermute | solution.py:275
  99.4 6.2 %collective-permute-start.20 = (bf16[64,1024]{1,0:T(8,128)(2,1)S(1)}, bf16[64,1024]{1,0:T(8,128)(2,1)S(1)}, u32[]{:S(2)}, u32[]{:S(2)}) collective-permute-start(bf16[64,1024]{1,0:T(8,128)(2,1)S(1)} %shard_map.117.refs_0_), channel_id=1, source_target_pairs={{8,0},{9,1},{10,2},{11,3},{12,4},{13,5},{14,6},{15,7},{16,8},{17,9... | collective-permute-start | bytes 393224 | tf_op jit(solution)/shard_map/ppermute | solution.py:275
  132.1 4.0 %collective-permute-start.24 = (bf16[256,2048]{1,0:T(8,128)(2,1)S(1)}, bf16[256,2048]{1,0:T(8,128)(2,1)S(1)}, u32[]{:S(2)}, u32[]{:S(2)}) collective-permute-start(bf16[256,2048]{1,0:T(8,128)(2,1)S(1)} %bitcast.8), channel_id=1, source_target_pairs={{0,1},{1,0},{2,3},{3,2},{4,5},{5,4},{6,7},{7,6},{8,9},{9,8},{10,11... | collective-permute-start | bytes 3145736 | tf_op jit(solution)/shard_map/ppermute | solution.py:265
  132.1 3.6 %collective-permute-start.25 = (bf16[256,1024]{1,0:T(8,128)(2,1)S(1)}, bf16[256,1024]{1,0:T(8,128)(2,1)S(1)}, u32[]{:S(2)}, u32[]{:S(2)}) collective-permute-start(bf16[256,1024]{1,0:T(8,128)(2,1)S(1)} %get-tuple-element.61.refs_7_), channel_id=1, source_target_pairs={{0,1},{1,0},{2,3},{3,2},{4,5},{5,4},{6,7},{7,6},{8,9},{9,8},{10,11... | collective-permute-start | bytes 1572872 | tf_op jit(solution)/shard_map/ppermute | solution.py:265
  132.6 3.5 %collective-permute-start.26 = (f32[8,128]{1,0:T(8,128)S(1)}, f32[8,128]{1,0:T(8,128)S(1)}, u32[]{:S(2)}, u32[]{:S(2)}) collective-permute-start(f32[8,128]{1,0:T(8,128)S(1)} %get-tuple-element.62.refs_9_), channel_id=1, source_target_pairs={{0,1},{1,0},{2,3},{3,2},{4,5},{5,4},{6,7},{7,6},{8,9},{9,8},{10,11... | collective-permute-start | bytes 12296 | tf_op jit(solution)/shard_map/ppermute | solution.py:265
  133.9 7.9 %collective-permute-start.27 = (bf16[64,1024]{1,0:T(8,128)(2,1)S(1)}, bf16[64,1024]{1,0:T(8,128)(2,1)S(1)}, u32[]{:S(2)}, u32[]{:S(2)}) collective-permute-start(bf16[64,1024]{1,0:T(8,128)(2,1)S(1)} %get-tuple-element.72), channel_id=1, source_target_pairs={{16,0},{17,1},{18,2},{19,3},{20,4},{21,5},{22,6},{23,7},{24,8},{25... | collective-permute-start | bytes 393224 | tf_op jit(solution)/shard_map/ppermute | solution.py:275
  134.0 8.8 %collective-permute-start.28 = (bf16[64,1024]{1,0:T(8,128)(2,1)S(1)}, bf16[64,1024]{1,0:T(8,128)(2,1)S(1)}, u32[]{:S(2)}, u32[]{:S(2)}) collective-permute-start(bf16[64,1024]{1,0:T(8,128)(2,1)S(1)} %get-tuple-element.73), channel_id=1, source_target_pairs={{24,0},{25,1},{26,2},{27,3},{28,4},{29,5},{30,6},{31,7},{0,8},{1,9... | collective-permute-start | bytes 393224 | tf_op jit(solution)/shard_map/ppermute | solution.py:275
  135.7 8.5 %collective-permute-start.29 = (bf16[64,1024]{1,0:T(8,128)(2,1)S(1)}, bf16[64,1024]{1,0:T(8,128)(2,1)S(1)}, u32[]{:S(2)}, u32[]{:S(2)}) collective-permute-start(bf16[64,1024]{1,0:T(8,128)(2,1)S(1)} %get-tuple-element.74), channel_id=1, source_target_pairs={{8,0},{9,1},{10,2},{11,3},{12,4},{13,5},{14,6},{15,7},{16,8},{17,9... | collective-permute-start | bytes 393224 | tf_op jit(solution)/shard_map/ppermute | solution.py:275
  144.3 8.1 %collective-permute-start.30 = (bf16[16,1024]{1,0:T(8,128)(2,1)S(1)}, bf16[16,1024]{1,0:T(8,128)(2,1)S(1)}, u32[]{:S(2)}, u32[]{:S(2)}) collective-permute-start(bf16[16,1024]{1,0:T(8,128)(2,1)S(1)} %get-tuple-element.77), channel_id=1, source_target_pairs={{4,0},{5,1},{6,2},{7,3},{0,4},{1,5},{2,6},{3,7},{12,8},{13,9},{14,... | collective-permute-start | bytes 98312 | tf_op jit(solution)/shard_map/ppermute | solution.py:275
  146.1 7.3 %collective-permute-start.31 = (bf16[16,1024]{1,0:T(8,128)(2,1)S(1)}, bf16[16,1024]{1,0:T(8,128)(2,1)S(1)}, u32[]{:S(2)}, u32[]{:S(2)}) collective-permute-start(bf16[16,1024]{1,0:T(8,128)(2,1)S(1)} %get-tuple-element.78), channel_id=1, source_target_pairs={{6,0},{7,1},{0,2},{1,3},{2,4},{3,5},{4,6},{5,7},{14,8},{15,9},{8,1... | collective-permute-start | bytes 98312 | tf_op jit(solution)/shard_map/ppermute | solution.py:275
  150.7 5.2 %collective-permute-start.32 = (bf16[16,1024]{1,0:T(8,128)(2,1)S(1)}, bf16[16,1024]{1,0:T(8,128)(2,1)S(1)}, u32[]{:S(2)}, u32[]{:S(2)}) collective-permute-start(bf16[16,1024]{1,0:T(8,128)(2,1)S(1)} %get-tuple-element.79), channel_id=1, source_target_pairs={{2,0},{3,1},{4,2},{5,3},{6,4},{7,5},{0,6},{1,7},{10,8},{11,9},{12,... | collective-permute-start | bytes 98312 | tf_op jit(solution)/shard_map/ppermute | solution.py:275
  (5 other events, 29.3 us)

commit v10 on v9

--- a/solution.py
+++ b/solution.py
@@ -389,8 +389,8 @@
         flops=6 * token_count * width * units,
         vmem=24,
     )
-    parts = spread_z(call(sum_kernel, (piece,) * Z, *slabs, after=(done,)))
-    (grad_in,) = call(sum_kernel, (piece,), *parts)
+    parts = spread_z(call(sum_kernel, (piece,) * Z, *slabs))
+    (grad_in,) = call(sum_kernel, (piece,), *parts, after=(done,))
     return student, loss[0, 0], grad_gate, grad_up, grad_down, grad_in
 
 

time: 157 us -> 157 us (level)
  transfers between devices with their start and end apart: 33 -> 33, of which waited for: 21 -> 19; matrix products, arithmetic and copies ran while one was open for 0% -> 0% of each run, Pallas kernels for 4% -> 4%
where the time goes in v10:
time: 157 us; the launch traced here: 156 us
  blocking collectives  56.5 us (36%)
  starting transfers between devices  47.2 us (30%)
  waiting for transfers between devices  37 us (24%)
  Pallas kernels  13.3 us (8%)
    all_to_all x4, blocking collectives, exchange_row(): return lax.all_to_all(value, 'row', 0, 0)  56.5 us
    ppermute x24, starting transfers between devices, fetch(): return lax.ppermute(value, 'col', pairs)  45.4 us
    ppermute x24, waiting for transfers between devices, fetch(): return lax.ppermute(value, 'col', pairs)  35.8 us
    pallas_call x14, Pallas kernels, call(): pl.pallas_call(lambda *refs: kernel(*refs[:len(args)], *refs[len(args) +...  13.3 us
  transfers between devices with their start and end apart: 33, of which 19 were waited for; matrix products, arithmetic and copies ran while one was open for 0% of the time, Pallas kernels for 4%

profile of v10, /device:TPU:6, one launch (start us, length us, event | category | flops | bytes accessed | tf_op | source)
XLA Modules:
  0.0 156.2 jit_solution(10288064783773133399)
XLA Ops:
  1.2 6.3 %collective-permute-start.2 = (bf16[16,1024]{1,0:T(8,128)(2,1)}, bf16[16,1024]{1,0:T(8,128)(2,1)S(1)}, u32[]{:S(2)}, u32[]{:S(2)}) collective-permute-start(bf16[16,1024]{1,0:T(8,128)(2,1)} %refs_0_.2), channel_id=1, source_target_pairs={{2,0},{3,1},{4,2},{5,3},{6,4},{7,5},{0,6},{1,7},{10,8},{11,9},{12,... | collective-permute-start | bytes 98312 | tf_op jit(solution)/shard_map/ppermute | solution.py:275
  8.4 2.9 %collective-permute-start.3 = (bf16[16,1024]{1,0:T(8,128)(2,1)}, bf16[16,1024]{1,0:T(8,128)(2,1)S(1)}, u32[]{:S(2)}, u32[]{:S(2)}) collective-permute-start(bf16[16,1024]{1,0:T(8,128)(2,1)} %refs_0_.2), channel_id=1, source_target_pairs={{6,0},{7,1},{0,2},{1,3},{2,4},{3,5},{4,6},{5,7},{14,8},{15,9},{8,1... | collective-permute-start | bytes 98312 | tf_op jit(solution)/shard_map/ppermute | solution.py:275
  11.4 4.4 %collective-permute-done.1.refs_1_ = bf16[16,1024]{1,0:T(8,128)(2,1)S(1)} collective-permute-done((bf16[16,1024]{1,0:T(8,128)(2,1)}, bf16[16,1024]{1,0:T(8,128)(2,1)S(1)}, u32[]{:S(2)}, u32[]{:S(2)}) %collective-permute-start.1) | collective-permute-done | bytes 32800 | tf_op jit(solution)/shard_map/ppermute | solution.py:275
  18.3 1.5 collective-permute-start.8
  19.7 2.1 %collective-permute-start.7 = (bf16[64,1024]{1,0:T(8,128)(2,1)S(1)}, bf16[64,1024]{1,0:T(8,128)(2,1)S(1)}, u32[]{:S(2)}, u32[]{:S(2)}) collective-permute-start(bf16[64,1024]{1,0:T(8,128)(2,1)S(1)} %shard_map.109.refs_2_), channel_id=1, source_target_pairs={{24,0},{25,1},{26,2},{27,3},{28,4},{29,5},{30,6},{31,7},{0,8},{1,9... | collective-permute-start | bytes 393224 | tf_op jit(solution)/shard_map/ppermute | solution.py:275
  23.0 3.1 %collective-permute-done.8.refs_5_ = bf16[64,1024]{1,0:T(8,128)(2,1)S(1)} collective-permute-done((bf16[64,1024]{1,0:T(8,128)(2,1)S(1)}, bf16[64,1024]{1,0:T(8,128)(2,1)S(1)}, u32[]{:S(2)}, u32[]{:S(2)}) %collective-permute-start.8) | collective-permute-done | bytes 131104 | tf_op jit(solution)/shard_map/ppermute | solution.py:275
  26.3 2.3 %collective-permute-done.6.refs_3_ = bf16[64,1024]{1,0:T(8,128)(2,1)S(1)} collective-permute-done((bf16[64,1024]{1,0:T(8,128)(2,1)S(1)}, bf16[64,1024]{1,0:T(8,128)(2,1)S(1)}, u32[]{:S(2)}, u32[]{:S(2)}) %collective-permute-start.6) | collective-permute-done | bytes 131104 | tf_op jit(solution)/shard_map/ppermute | solution.py:275
  28.6 3.7 %shard_map.111 = (bf16[1024,512]{1,0:T(8,128)(2,1)S(1)}, bf16[1024,512]{1,0:T(8,128)(2,1)S(1)}, bf16[1024,512]{1,0:T(8,128)(2,1)S(1)}, bf16[1024,512]{1,0:T(8,12...) custom-call(s32[3,4,8]{2,1,0:T(4,128)S(1)} %bitcast.15, ...), custom_call_target="tpu_custom_call" | custom-call | flops 1073741824 | bytes 10486528 | tf_op jit(solution)/shard_map/pallas_call | solution.py:26
  32.3 19.6 %all_to_all.20.refs_0_ = bf16[8,32,2048]{2,1,0:T(8,128)(2,1)S(1)} all-to-all(bf16[8,32,2048]{2,1,0:T(8,128)(2,1)S(1)} %bitcast.11), channel_id=1, replica_groups=mesh['row'=8,'col'=32] {'row'}, dimensions={0} | all-to-all | bytes 2097152 | tf_op jit(solution)/shard_map/all_to_all | solution.py:301
  52.2 11.3 %all_to_all.21 = bf16[8,32,1024]{2,1,0:T(8,128)(2,1)S(1)} all-to-all(bf16[8,32,1024]{2,1,0:T(8,128)(2,1)S(1)} %get-tuple-element.44), channel_id=1, replica_groups=mesh['row'=8,'col'=32] {'row'}, dimensions={0} | all-to-all | bytes 1048576 | tf_op jit(solution)/shard_map/all_to_all | solution.py:301
  64.2 2.2 %collective-permute-start.10 = (bf16[64,1024]{1,0:T(8,128)(2,1)S(1)}, bf16[64,1024]{1,0:T(8,128)(2,1)S(1)}, u32[]{:S(2)}, u32[]{:S(2)}) collective-permute-start(bf16[64,1024]{1,0:T(8,128)(2,1)S(1)} %get-tuple-element.46), channel_id=1, source_target_pairs={{16,0},{17,1},{18,2},{19,3},{20,4},{21,5},{22,6},{23,7},{24,8},{25... | collective-permute-start | bytes 393224 | tf_op jit(solution)/shard_map/ppermute | solution.py:275
  67.1 1.4 collective-permute-start.12
  68.5 2.3 %collective-permute-done.10.refs_1_ = bf16[64,1024]{1,0:T(8,128)(2,1)S(1)} collective-permute-done((bf16[64,1024]{1,0:T(8,128)(2,1)S(1)}, bf16[64,1024]{1,0:T(8,128)(2,1)S(1)}, u32[]{:S(2)}, u32[]{:S(2)}) %collective-permute-start.10) | collective-permute-done | bytes 131104 | tf_op jit(solution)/shard_map/ppermute | solution.py:275
  71.4 1.9 %collective-permute-done.12.refs_3_ = bf16[64,1024]{1,0:T(8,128)(2,1)S(1)} collective-permute-done((bf16[64,1024]{1,0:T(8,128)(2,1)S(1)}, bf16[64,1024]{1,0:T(8,128)(2,1)S(1)}, u32[]{:S(2)}, u32[]{:S(2)}) %collective-permute-start.12) | collective-permute-done | bytes 131104 | tf_op jit(solution)/shard_map/ppermute | solution.py:275
  74.0 4.1 %collective-permute-start.13 = (bf16[16,1024]{1,0:T(8,128)(2,1)S(1)}, bf16[16,1024]{1,0:T(8,128)(2,1)S(1)}, u32[]{:S(2)}, u32[]{:S(2)}) collective-permute-start(bf16[16,1024]{1,0:T(8,128)(2,1)S(1)} %get-tuple-element.50), channel_id=1, source_target_pairs={{4,0},{5,1},{6,2},{7,3},{0,4},{1,5},{2,6},{3,7},{12,8},{13,9},{14,... | collective-permute-start | bytes 98312 | tf_op jit(solution)/shard_map/ppermute | solution.py:275
  78.1 4.1 %collective-permute-start.15 = (bf16[16,1024]{1,0:T(8,128)(2,1)S(1)}, bf16[16,1024]{1,0:T(8,128)(2,1)S(1)}, u32[]{:S(2)}, u32[]{:S(2)}) collective-permute-start(bf16[16,1024]{1,0:T(8,128)(2,1)S(1)} %get-tuple-element.52), channel_id=1, source_target_pairs={{2,0},{3,1},{4,2},{5,3},{6,4},{7,5},{0,6},{1,7},{10,8},{11,9},{12,... | collective-permute-start | bytes 98312 | tf_op jit(solution)/shard_map/ppermute | solution.py:275
  82.4 1.7 %collective-permute-done.14.refs_3_ = bf16[16,1024]{1,0:T(8,128)(2,1)S(1)} collective-permute-done((bf16[16,1024]{1,0:T(8,128)(2,1)S(1)}, bf16[16,1024]{1,0:T(8,128)(2,1)S(1)}, u32[]{:S(2)}, u32[]{:S(2)}) %collective-permute-start.14) | collective-permute-done | bytes 32800 | tf_op jit(solution)/shard_map/ppermute | solution.py:275
  84.8 3.0 %collective-permute-start.19 = (bf16[16,1024]{1,0:T(8,128)(2,1)S(1)}, bf16[16,1024]{1,0:T(8,128)(2,1)S(1)}, u32[]{:S(2)}, u32[]{:S(2)}) collective-permute-start(bf16[16,1024]{1,0:T(8,128)(2,1)S(1)} %get-tuple-element.56.refs_0_), channel_id=1, source_target_pairs={{4,0},{5,1},{6,2},{7,3},{0,4},{1,5},{2,6},{3,7},{12,8},{13,9},{14,... | collective-permute-start | bytes 98312 | tf_op jit(solution)/shard_map/ppermute | solution.py:275
  87.8 3.8 %collective-permute-start.18 = (bf16[16,1024]{1,0:T(8,128)(2,1)S(1)}, bf16[16,1024]{1,0:T(8,128)(2,1)S(1)}, u32[]{:S(2)}, u32[]{:S(2)}) collective-permute-start(bf16[16,1024]{1,0:T(8,128)(2,1)S(1)} %get-tuple-element.56.refs_0_), channel_id=1, source_target_pairs={{6,0},{7,1},{0,2},{1,3},{2,4},{3,5},{4,6},{5,7},{14,8},{15,9},{8,1... | collective-permute-start | bytes 98312 | tf_op jit(solution)/shard_map/ppermute | solution.py:275
  93.8 2.6 %collective-permute-done.17.refs_1_ = bf16[16,1024]{1,0:T(8,128)(2,1)S(1)} collective-permute-done((bf16[16,1024]{1,0:T(8,128)(2,1)S(1)}, bf16[16,1024]{1,0:T(8,128)(2,1)S(1)}, u32[]{:S(2)}, u32[]{:S(2)}) %collective-permute-start.17) | collective-permute-done | bytes 32800 | tf_op jit(solution)/shard_map/ppermute | solution.py:275
  97.7 1.8 %collective-permute-start.21 = (bf16[64,1024]{1,0:T(8,128)(2,1)S(1)}, bf16[64,1024]{1,0:T(8,128)(2,1)S(1)}, u32[]{:S(2)}, u32[]{:S(2)}) collective-permute-start(bf16[64,1024]{1,0:T(8,128)(2,1)S(1)} %shard_map.117.refs_0_), channel_id=1, source_target_pairs={{24,0},{25,1},{26,2},{27,3},{28,4},{29,5},{30,6},{31,7},{0,8},{1,9... | collective-permute-start | bytes 393224 | tf_op jit(solution)/shard_map/ppermute | solution.py:275
  99.7 3.4 %collective-permute-done.22.refs_3_ = bf16[64,1024]{1,0:T(8,128)(2,1)S(1)} collective-permute-done((bf16[64,1024]{1,0:T(8,128)(2,1)S(1)}, bf16[64,1024]{1,0:T(8,128)(2,1)S(1)}, u32[]{:S(2)}, u32[]{:S(2)}) %collective-permute-start.22) | collective-permute-done | bytes 131104 | tf_op jit(solution)/shard_map/ppermute | solution.py:275
  103.1 2.6 %collective-permute-done.20.refs_1_ = bf16[64,1024]{1,0:T(8,128)(2,1)S(1)} collective-permute-done((bf16[64,1024]{1,0:T(8,128)(2,1)S(1)}, bf16[64,1024]{1,0:T(8,128)(2,1)S(1)}, u32[]{:S(2)}, u32[]{:S(2)}) %collective-permute-start.20) | collective-permute-done | bytes 131104 | tf_op jit(solution)/shard_map/ppermute | solution.py:275
  106.4 11.6 %all_to_all.22.refs_0_ = bf16[8,32,1152]{2,1,0:T(8,128)(2,1)S(1)} all-to-all(bf16[8,32,1152]{2,1,0:T(8,128)(2,1)S(1)} %bitcast.12), channel_id=1, replica_groups=mesh['row'=8,'col'=32] {'row'}, dimensions={0} | all-to-all | bytes 1179648 | tf_op jit(solution)/shard_map/all_to_all | solution.py:301
  118.2 13.9 %all_to_all.23 = bf16[8,32,2048]{2,1,0:T(8,128)(2,1)S(1)} all-to-all(bf16[8,32,2048]{2,1,0:T(8,128)(2,1)S(1)} %get-tuple-element.60), channel_id=1, replica_groups=mesh['row'=8,'col'=32] {'row'}, dimensions={0} | all-to-all | bytes 2097152 | tf_op jit(solution)/shard_map/all_to_all | solution.py:301
  132.6 1.3 shard_map.121
  134.0 1.7 %collective-permute-start.28 = (bf16[64,1024]{1,0:T(8,128)(2,1)S(1)}, bf16[64,1024]{1,0:T(8,128)(2,1)S(1)}, u32[]{:S(2)}, u32[]{:S(2)}) collective-permute-start(bf16[64,1024]{1,0:T(8,128)(2,1)S(1)} %get-tuple-element.73), channel_id=1, source_target_pairs={{24,0},{25,1},{26,2},{27,3},{28,4},{29,5},{30,6},{31,7},{0,8},{1,9... | collective-permute-start | bytes 393224 | tf_op jit(solution)/shard_map/ppermute | solution.py:275
  136.1 5.8 %collective-permute-done.27.refs_1_ = bf16[64,1024]{1,0:T(8,128)(2,1)S(1)} collective-permute-done((bf16[64,1024]{1,0:T(8,128)(2,1)S(1)}, bf16[64,1024]{1,0:T(8,128)(2,1)S(1)}, u32[]{:S(2)}, u32[]{:S(2)}) %collective-permute-start.27) | collective-permute-done | bytes 131104 | tf_op jit(solution)/shard_map/ppermute | solution.py:275
  142.3 1.4 collective-permute-done.29.refs_3_
  143.8 2.0 %collective-permute-start.30 = (bf16[16,1024]{1,0:T(8,128)(2,1)S(1)}, bf16[16,1024]{1,0:T(8,128)(2,1)S(1)}, u32[]{:S(2)}, u32[]{:S(2)}) collective-permute-start(bf16[16,1024]{1,0:T(8,128)(2,1)S(1)} %get-tuple-element.76), channel_id=1, source_target_pairs={{4,0},{5,1},{6,2},{7,3},{0,4},{1,5},{2,6},{3,7},{12,8},{13,9},{14,... | collective-permute-start | bytes 98312 | tf_op jit(solution)/shard_map/ppermute | solution.py:275
  145.8 4.6 %collective-permute-start.31 = (bf16[16,1024]{1,0:T(8,128)(2,1)S(1)}, bf16[16,1024]{1,0:T(8,128)(2,1)S(1)}, u32[]{:S(2)}, u32[]{:S(2)}) collective-permute-start(bf16[16,1024]{1,0:T(8,128)(2,1)S(1)} %get-tuple-element.77), channel_id=1, source_target_pairs={{6,0},{7,1},{0,2},{1,3},{2,4},{3,5},{4,6},{5,7},{14,8},{15,9},{8,1... | collective-permute-start | bytes 98312 | tf_op jit(solution)/shard_map/ppermute | solution.py:275
  150.4 4.2 %shard_map.120 = (bf16[1024,512]{1,0:T(8,128)(2,1)}, bf16[1024,512]{1,0:T(8,128)(2,1)}, bf16[512,1024]{1,0:T(8,128)(2,1)}, f32[1,1]{1,0:T(1,128)}, f32[8,128]{1,0:T(8,128)S(1)}) custom-call(s32[3,4,8]{2,1,0:T(4,128)S(1)} %bitcast.16, bf16[256,1024]{1,0:T(8,128)(2,1)S(1)} %get-tuple-element.55.refs_1_, ...), custom_call_target="tpu_custom_call" | custom-call | flops 1610612736 | bytes 8401284 | tf_op jit(solution)/shard_map/pallas_call | solution.py:26
  (61 shorter events, 16.6 us)
Async XLA Ops:
  0.6 15.1 %collective-permute-start.4 = (bf16[1024,512]{1,0:T(8,128)(2,1)}, bf16[1024,512]{1,0:T(8,128)(2,1)S(1)}, u32[]{:S(2)}, u32[]{:S(2)}) collective-permute-start(bf16[1024,512]{1,0:T(8,128)(2,1)} %refs_6_.1), channel_id=1, source_target_pairs={{0,1},{1,0},{2,3},{3,2},{4,5},{5,4},{6,7},{7,6},{8,9},{9,8},{10,11... | collective-permute-start | bytes 3145736 | tf_op jit(solution)/shard_map/ppermute | solution.py:265
  0.7 15.0 %collective-permute-start.5 = (bf16[1024,512]{1,0:T(8,128)(2,1)}, bf16[1024,512]{1,0:T(8,128)(2,1)S(1)}, u32[]{:S(2)}, u32[]{:S(2)}) collective-permute-start(bf16[1024,512]{1,0:T(8,128)(2,1)} %refs_8_.1), channel_id=1, source_target_pairs={{0,1},{1,0},{2,3},{3,2},{4,5},{5,4},{6,7},{7,6},{8,9},{9,8},{10,11... | collective-permute-start | bytes 3145736 | tf_op jit(solution)/shard_map/ppermute | solution.py:265
  1.2 10.1 %collective-permute-start.2 = (bf16[16,1024]{1,0:T(8,128)(2,1)}, bf16[16,1024]{1,0:T(8,128)(2,1)S(1)}, u32[]{:S(2)}, u32[]{:S(2)}) collective-permute-start(bf16[16,1024]{1,0:T(8,128)(2,1)} %refs_0_.2), channel_id=1, source_target_pairs={{2,0},{3,1},{4,2},{5,3},{6,4},{7,5},{0,6},{1,7},{10,8},{11,9},{12,... | collective-permute-start | bytes 98312 | tf_op jit(solution)/shard_map/ppermute | solution.py:275
  7.5 8.2 %collective-permute-start.1 = (bf16[16,1024]{1,0:T(8,128)(2,1)}, bf16[16,1024]{1,0:T(8,128)(2,1)S(1)}, u32[]{:S(2)}, u32[]{:S(2)}) collective-permute-start(bf16[16,1024]{1,0:T(8,128)(2,1)} %refs_0_.2), channel_id=1, source_target_pairs={{4,0},{5,1},{6,2},{7,3},{0,4},{1,5},{2,6},{3,7},{12,8},{13,9},{14,... | collective-permute-start | bytes 98312 | tf_op jit(solution)/shard_map/ppermute | solution.py:275
  8.4 7.3 %collective-permute-start.3 = (bf16[16,1024]{1,0:T(8,128)(2,1)}, bf16[16,1024]{1,0:T(8,128)(2,1)S(1)}, u32[]{:S(2)}, u32[]{:S(2)}) collective-permute-start(bf16[16,1024]{1,0:T(8,128)(2,1)} %refs_0_.2), channel_id=1, source_target_pairs={{6,0},{7,1},{0,2},{1,3},{2,4},{3,5},{4,6},{5,7},{14,8},{15,9},{8,1... | collective-permute-start | bytes 98312 | tf_op jit(solution)/shard_map/ppermute | solution.py:275
  18.2 10.5 %collective-permute-start.9 = (bf16[512,1024]{1,0:T(8,128)(2,1)S(1)}, bf16[512,1024]{1,0:T(8,128)(2,1)S(1)}, u32[]{:S(2)}, u32[]{:S(2)}) collective-permute-start(bf16[512,1024]{1,0:T(8,128)(2,1)S(1)} %shard_map.110.refs_1_.refs_4_), channel_id=1, source_target_pairs={{0,1},{1,0},{2,3},{3,2},{4,5},{5,4},{6,7},{7,6},{8,9},{9,8},{10,11... | collective-permute-start | bytes 3145736 | tf_op jit(solution)/shard_map/ppermute | solution.py:265
  18.3 7.9 %collective-permute-start.8 = (bf16[64,1024]{1,0:T(8,128)(2,1)S(1)}, bf16[64,1024]{1,0:T(8,128)(2,1)S(1)}, u32[]{:S(2)}, u32[]{:S(2)}) collective-permute-start(bf16[64,1024]{1,0:T(8,128)(2,1)S(1)} %shard_map.109.refs_2_), channel_id=1, source_target_pairs={{16,0},{17,1},{18,2},{19,3},{20,4},{21,5},{22,6},{23,7},{24,8},{25... | collective-permute-start | bytes 393224 | tf_op jit(solution)/shard_map/ppermute | solution.py:275
  19.7 6.6 %collective-permute-start.7 = (bf16[64,1024]{1,0:T(8,128)(2,1)S(1)}, bf16[64,1024]{1,0:T(8,128)(2,1)S(1)}, u32[]{:S(2)}, u32[]{:S(2)}) collective-permute-start(bf16[64,1024]{1,0:T(8,128)(2,1)S(1)} %shard_map.109.refs_2_), channel_id=1, source_target_pairs={{24,0},{25,1},{26,2},{27,3},{28,4},{29,5},{30,6},{31,7},{0,8},{1,9... | collective-permute-start | bytes 393224 | tf_op jit(solution)/shard_map/ppermute | solution.py:275
  21.8 6.8 %collective-permute-start.6 = (bf16[64,1024]{1,0:T(8,128)(2,1)S(1)}, bf16[64,1024]{1,0:T(8,128)(2,1)S(1)}, u32[]{:S(2)}, u32[]{:S(2)}) collective-permute-start(bf16[64,1024]{1,0:T(8,128)(2,1)S(1)} %shard_map.109.refs_2_), channel_id=1, source_target_pairs={{8,0},{9,1},{10,2},{11,3},{12,4},{13,5},{14,6},{15,7},{16,8},{17,9... | collective-permute-start | bytes 393224 | tf_op jit(solution)/shard_map/ppermute | solution.py:275
  64.2 6.6 %collective-permute-start.10 = (bf16[64,1024]{1,0:T(8,128)(2,1)S(1)}, bf16[64,1024]{1,0:T(8,128)(2,1)S(1)}, u32[]{:S(2)}, u32[]{:S(2)}) collective-permute-start(bf16[64,1024]{1,0:T(8,128)(2,1)S(1)} %get-tuple-element.46), channel_id=1, source_target_pairs={{16,0},{17,1},{18,2},{19,3},{20,4},{21,5},{22,6},{23,7},{24,8},{25... | collective-permute-start | bytes 393224 | tf_op jit(solution)/shard_map/ppermute | solution.py:275
  66.4 5.0 %collective-permute-start.11 = (bf16[64,1024]{1,0:T(8,128)(2,1)S(1)}, bf16[64,1024]{1,0:T(8,128)(2,1)S(1)}, u32[]{:S(2)}, u32[]{:S(2)}) collective-permute-start(bf16[64,1024]{1,0:T(8,128)(2,1)S(1)} %get-tuple-element.47), channel_id=1, source_target_pairs={{24,0},{25,1},{26,2},{27,3},{28,4},{29,5},{30,6},{31,7},{0,8},{1,9... | collective-permute-start | bytes 393224 | tf_op jit(solution)/shard_map/ppermute | solution.py:275
  67.1 6.2 %collective-permute-start.12 = (bf16[64,1024]{1,0:T(8,128)(2,1)S(1)}, bf16[64,1024]{1,0:T(8,128)(2,1)S(1)}, u32[]{:S(2)}, u32[]{:S(2)}) collective-permute-start(bf16[64,1024]{1,0:T(8,128)(2,1)S(1)} %get-tuple-element.48), channel_id=1, source_target_pairs={{8,0},{9,1},{10,2},{11,3},{12,4},{13,5},{14,6},{15,7},{16,8},{17,9... | collective-permute-start | bytes 393224 | tf_op jit(solution)/shard_map/ppermute | solution.py:275
  73.4 32.3 %collective-permute-start.16 = (bf16[256,1024]{1,0:T(8,128)(2,1)S(1)}, bf16[256,1024]{1,0:T(8,128)(2,1)S(1)}, u32[]{:S(2)}, u32[]{:S(2)}) collective-permute-start(bf16[256,1024]{1,0:T(8,128)(2,1)S(1)} %get-tuple-element.55.refs_1_), channel_id=1, source_target_pairs={{0,1},{1,0},{2,3},{3,2},{4,5},{5,4},{6,7},{7,6},{8,9},{9,8},{10,11... | collective-permute-start | bytes 1572872 | tf_op jit(solution)/shard_map/ppermute | solution.py:265
  73.5 32.2 %collective-permute-start.23 = (bf16[256,1024]{1,0:T(8,128)(2,1)S(1)}, bf16[256,1024]{1,0:T(8,128)(2,1)S(1)}, u32[]{:S(2)}, u32[]{:S(2)}) collective-permute-start(bf16[256,1024]{1,0:T(8,128)(2,1)S(1)} %get-tuple-element.57.refs_5_), channel_id=1, source_target_pairs={{0,1},{1,0},{2,3},{3,2},{4,5},{5,4},{6,7},{7,6},{8,9},{9,8},{10,11... | collective-permute-start | bytes 1572872 | tf_op jit(solution)/shard_map/ppermute | solution.py:265
  74.0 8.4 %collective-permute-start.13 = (bf16[16,1024]{1,0:T(8,128)(2,1)S(1)}, bf16[16,1024]{1,0:T(8,128)(2,1)S(1)}, u32[]{:S(2)}, u32[]{:S(2)}) collective-permute-start(bf16[16,1024]{1,0:T(8,128)(2,1)S(1)} %get-tuple-element.50), channel_id=1, source_target_pairs={{4,0},{5,1},{6,2},{7,3},{0,4},{1,5},{2,6},{3,7},{12,8},{13,9},{14,... | collective-permute-start | bytes 98312 | tf_op jit(solution)/shard_map/ppermute | solution.py:275
  78.1 6.0 %collective-permute-start.14 = (bf16[16,1024]{1,0:T(8,128)(2,1)S(1)}, bf16[16,1024]{1,0:T(8,128)(2,1)S(1)}, u32[]{:S(2)}, u32[]{:S(2)}) collective-permute-start(bf16[16,1024]{1,0:T(8,128)(2,1)S(1)} %get-tuple-element.51), channel_id=1, source_target_pairs={{6,0},{7,1},{0,2},{1,3},{2,4},{3,5},{4,6},{5,7},{14,8},{15,9},{8,1... | collective-permute-start | bytes 98312 | tf_op jit(solution)/shard_map/ppermute | solution.py:275
  78.1 6.0 %collective-permute-start.15 = (bf16[16,1024]{1,0:T(8,128)(2,1)S(1)}, bf16[16,1024]{1,0:T(8,128)(2,1)S(1)}, u32[]{:S(2)}, u32[]{:S(2)}) collective-permute-start(bf16[16,1024]{1,0:T(8,128)(2,1)S(1)} %get-tuple-element.52), channel_id=1, source_target_pairs={{2,0},{3,1},{4,2},{5,3},{6,4},{7,5},{0,6},{1,7},{10,8},{11,9},{12,... | collective-permute-start | bytes 98312 | tf_op jit(solution)/shard_map/ppermute | solution.py:275
  84.8 8.2 %collective-permute-start.19 = (bf16[16,1024]{1,0:T(8,128)(2,1)S(1)}, bf16[16,1024]{1,0:T(8,128)(2,1)S(1)}, u32[]{:S(2)}, u32[]{:S(2)}) collective-permute-start(bf16[16,1024]{1,0:T(8,128)(2,1)S(1)} %get-tuple-element.56.refs_0_), channel_id=1, source_target_pairs={{4,0},{5,1},{6,2},{7,3},{0,4},{1,5},{2,6},{3,7},{12,8},{13,9},{14,... | collective-permute-start | bytes 98312 | tf_op jit(solution)/shard_map/ppermute | solution.py:275
  87.8 6.0 %collective-permute-start.18 = (bf16[16,1024]{1,0:T(8,128)(2,1)S(1)}, bf16[16,1024]{1,0:T(8,128)(2,1)S(1)}, u32[]{:S(2)}, u32[]{:S(2)}) collective-permute-start(bf16[16,1024]{1,0:T(8,128)(2,1)S(1)} %get-tuple-element.56.refs_0_), channel_id=1, source_target_pairs={{6,0},{7,1},{0,2},{1,3},{2,4},{3,5},{4,6},{5,7},{14,8},{15,9},{8,1... | collective-permute-start | bytes 98312 | tf_op jit(solution)/shard_map/ppermute | solution.py:275
  91.6 4.9 %collective-permute-start.17 = (bf16[16,1024]{1,0:T(8,128)(2,1)S(1)}, bf16[16,1024]{1,0:T(8,128)(2,1)S(1)}, u32[]{:S(2)}, u32[]{:S(2)}) collective-permute-start(bf16[16,1024]{1,0:T(8,128)(2,1)S(1)} %get-tuple-element.56.refs_0_), channel_id=1, source_target_pairs={{2,0},{3,1},{4,2},{5,3},{6,4},{7,5},{0,6},{1,7},{10,8},{11,9},{12,... | collective-permute-start | bytes 98312 | tf_op jit(solution)/shard_map/ppermute | solution.py:275
  96.5 6.6 %collective-permute-start.22 = (bf16[64,1024]{1,0:T(8,128)(2,1)S(1)}, bf16[64,1024]{1,0:T(8,128)(2,1)S(1)}, u32[]{:S(2)}, u32[]{:S(2)}) collective-permute-start(bf16[64,1024]{1,0:T(8,128)(2,1)S(1)} %shard_map.117.refs_0_), channel_id=1, source_target_pairs={{16,0},{17,1},{18,2},{19,3},{20,4},{21,5},{22,6},{23,7},{24,8},{25... | collective-permute-start | bytes 393224 | tf_op jit(solution)/shard_map/ppermute | solution.py:275
  97.7 5.4 %collective-permute-start.21 = (bf16[64,1024]{1,0:T(8,128)(2,1)S(1)}, bf16[64,1024]{1,0:T(8,128)(2,1)S(1)}, u32[]{:S(2)}, u32[]{:S(2)}) collective-permute-start(bf16[64,1024]{1,0:T(8,128)(2,1)S(1)} %shard_map.117.refs_0_), channel_id=1, source_target_pairs={{24,0},{25,1},{26,2},{27,3},{28,4},{29,5},{30,6},{31,7},{0,8},{1,9... | collective-permute-start | bytes 393224 | tf_op jit(solution)/shard_map/ppermute | solution.py:275
  99.4 6.2 %collective-permute-start.20 = (bf16[64,1024]{1,0:T(8,128)(2,1)S(1)}, bf16[64,1024]{1,0:T(8,128)(2,1)S(1)}, u32[]{:S(2)}, u32[]{:S(2)}) collective-permute-start(bf16[64,1024]{1,0:T(8,128)(2,1)S(1)} %shard_map.117.refs_0_), channel_id=1, source_target_pairs={{8,0},{9,1},{10,2},{11,3},{12,4},{13,5},{14,6},{15,7},{16,8},{17,9... | collective-permute-start | bytes 393224 | tf_op jit(solution)/shard_map/ppermute | solution.py:275
  132.1 18.3 %collective-permute-start.24 = (bf16[256,2048]{1,0:T(8,128)(2,1)S(1)}, bf16[256,2048]{1,0:T(8,128)(2,1)S(1)}, u32[]{:S(2)}, u32[]{:S(2)}) collective-permute-start(bf16[256,2048]{1,0:T(8,128)(2,1)S(1)} %bitcast.8), channel_id=1, source_target_pairs={{0,1},{1,0},{2,3},{3,2},{4,5},{5,4},{6,7},{7,6},{8,9},{9,8},{10,11... | collective-permute-start | bytes 3145736 | tf_op jit(solution)/shard_map/ppermute | solution.py:265
  132.1 18.3 %collective-permute-start.25 = (bf16[256,1024]{1,0:T(8,128)(2,1)S(1)}, bf16[256,1024]{1,0:T(8,128)(2,1)S(1)}, u32[]{:S(2)}, u32[]{:S(2)}) collective-permute-start(bf16[256,1024]{1,0:T(8,128)(2,1)S(1)} %get-tuple-element.61.refs_7_), channel_id=1, source_target_pairs={{0,1},{1,0},{2,3},{3,2},{4,5},{5,4},{6,7},{7,6},{8,9},{9,8},{10,11... | collective-permute-start | bytes 1572872 | tf_op jit(solution)/shard_map/ppermute | solution.py:265
  133.9 8.0 %collective-permute-start.27 = (bf16[64,1024]{1,0:T(8,128)(2,1)S(1)}, bf16[64,1024]{1,0:T(8,128)(2,1)S(1)}, u32[]{:S(2)}, u32[]{:S(2)}) collective-permute-start(bf16[64,1024]{1,0:T(8,128)(2,1)S(1)} %get-tuple-element.72), channel_id=1, source_target_pairs={{16,0},{17,1},{18,2},{19,3},{20,4},{21,5},{22,6},{23,7},{24,8},{25... | collective-permute-start | bytes 393224 | tf_op jit(solution)/shard_map/ppermute | solution.py:275
  134.0 8.3 %collective-permute-start.28 = (bf16[64,1024]{1,0:T(8,128)(2,1)S(1)}, bf16[64,1024]{1,0:T(8,128)(2,1)S(1)}, u32[]{:S(2)}, u32[]{:S(2)}) collective-permute-start(bf16[64,1024]{1,0:T(8,128)(2,1)S(1)} %get-tuple-element.73), channel_id=1, source_target_pairs={{24,0},{25,1},{26,2},{27,3},{28,4},{29,5},{30,6},{31,7},{0,8},{1,9... | collective-permute-start | bytes 393224 | tf_op jit(solution)/shard_map/ppermute | solution.py:275
  135.7 8.0 %collective-permute-start.29 = (bf16[64,1024]{1,0:T(8,128)(2,1)S(1)}, bf16[64,1024]{1,0:T(8,128)(2,1)S(1)}, u32[]{:S(2)}, u32[]{:S(2)}) collective-permute-start(bf16[64,1024]{1,0:T(8,128)(2,1)S(1)} %get-tuple-element.74), channel_id=1, source_target_pairs={{8,0},{9,1},{10,2},{11,3},{12,4},{13,5},{14,6},{15,7},{16,8},{17,9... | collective-permute-start | bytes 393224 | tf_op jit(solution)/shard_map/ppermute | solution.py:275
  141.9 8.5 %collective-permute-start.26 = (f32[8,128]{1,0:T(8,128)S(1)}, f32[8,128]{1,0:T(8,128)S(1)}, u32[]{:S(2)}, u32[]{:S(2)}) collective-permute-start(f32[8,128]{1,0:T(8,128)S(1)} %get-tuple-element.62.refs_9_), channel_id=1, source_target_pairs={{0,1},{1,0},{2,3},{3,2},{4,5},{5,4},{6,7},{7,6},{8,9},{9,8},{10,11... | collective-permute-start | bytes 12296 | tf_op jit(solution)/shard_map/ppermute | solution.py:265
  143.8 10.8 %collective-permute-start.30 = (bf16[16,1024]{1,0:T(8,128)(2,1)S(1)}, bf16[16,1024]{1,0:T(8,128)(2,1)S(1)}, u32[]{:S(2)}, u32[]{:S(2)}) collective-permute-start(bf16[16,1024]{1,0:T(8,128)(2,1)S(1)} %get-tuple-element.76), channel_id=1, source_target_pairs={{4,0},{5,1},{6,2},{7,3},{0,4},{1,5},{2,6},{3,7},{12,8},{13,9},{14,... | collective-permute-start | bytes 98312 | tf_op jit(solution)/shard_map/ppermute | solution.py:275
  145.8 8.8 %collective-permute-start.31 = (bf16[16,1024]{1,0:T(8,128)(2,1)S(1)}, bf16[16,1024]{1,0:T(8,128)(2,1)S(1)}, u32[]{:S(2)}, u32[]{:S(2)}) collective-permute-start(bf16[16,1024]{1,0:T(8,128)(2,1)S(1)} %get-tuple-element.77), channel_id=1, source_target_pairs={{6,0},{7,1},{0,2},{1,3},{2,4},{3,5},{4,6},{5,7},{14,8},{15,9},{8,1... | collective-permute-start | bytes 98312 | tf_op jit(solution)/shard_map/ppermute | solution.py:275
  150.4 5.2 %collective-permute-start.32 = (bf16[16,1024]{1,0:T(8,128)(2,1)S(1)}, bf16[16,1024]{1,0:T(8,128)(2,1)S(1)}, u32[]{:S(2)}, u32[]{:S(2)}) collective-permute-start(bf16[16,1024]{1,0:T(8,128)(2,1)S(1)} %get-tuple-element.78), channel_id=1, source_target_pairs={{2,0},{3,1},{4,2},{5,3},{6,4},{7,5},{0,6},{1,7},{10,8},{11,9},{12,... | collective-permute-start | bytes 98312 | tf_op jit(solution)/shard_map/ppermute | solution.py:275
  (5 other events, 29.3 us)

commit v11 on v10

--- a/solution.py
+++ b/solution.py
@@ -351,10 +351,10 @@
     hidden = flat(exchange_row(copies))
     slabs = spread_x(multiply(output_kernel, (slab,) * X, [hidden], downs))
     parts = call(sum_kernel, (piece,) * Z, *slabs)
-    rows, hidden = hold((rows, hidden), parts[:1])
-    rows_other, hidden_other = other_core(rows), other_core(hidden)
     parts = spread_z(parts)
     student, grad_out = call(functools.partial(error_kernel, scale), (piece, piece), teacher, *parts)
+    rows, hidden = hold((rows, hidden), (grad_out,))
+    rows_other, hidden_other = other_core(rows), other_core(hidden)
     slabs = gather_x(joined(gather_z(grad_out)))
     partial, grad_rows = multiply(
         grad_hidden_kernel, (shaped((half, 2 * units + BLK)), shaped((half, width))), slabs, downs, (), (rows_other, hidden_other)

time: 157 us -> 161 us (1.025)
  starting transfers between devices: 47.2 us -> 49.2 us
    ppermute x24, starting transfers between devices: 45.4 us -> 47.4 us  [fetch(): return lax.ppermute(value, 'col', pairs)]
  transfers between devices with their start and end apart: 33 -> 33, of which waited for: 19 -> 17; matrix products, arithmetic and copies ran while one was open for 0% -> 0% of each run, Pallas kernels for 4% -> 3%
where the time goes in v11:
time: 161 us; the launch traced here: 159 us
  blocking collectives  57.9 us (36%)
  starting transfers between devices  49.2 us (31%)
  waiting for transfers between devices  36.6 us (23%)
  Pallas kernels  13.3 us (8%)
    all_to_all x4, blocking collectives, exchange_row(): return lax.all_to_all(value, 'row', 0, 0)  57.9 us
    ppermute x24, starting transfers between devices, fetch(): return lax.ppermute(value, 'col', pairs)  47.4 us
    ppermute x24, waiting for transfers between devices, fetch(): return lax.ppermute(value, 'col', pairs)  35.4 us
    pallas_call x14, Pallas kernels, call(): pl.pallas_call(lambda *refs: kernel(*refs[:len(args)], *refs[len(args) +...  13.3 us
  transfers between devices with their start and end apart: 33, of which 17 were waited for; matrix products, arithmetic and copies ran while one was open for 0% of the time, Pallas kernels for 3%

profile of v11, /device:TPU:6, one launch (start us, length us, event | category | flops | bytes accessed | tf_op | source)
XLA Modules:
  0.0 159.2 jit_solution(14938653262422068245)
XLA Ops:
  1.2 6.3 %collective-permute-start.2 = (bf16[16,1024]{1,0:T(8,128)(2,1)}, bf16[16,1024]{1,0:T(8,128)(2,1)S(1)}, u32[]{:S(2)}, u32[]{:S(2)}) collective-permute-start(bf16[16,1024]{1,0:T(8,128)(2,1)} %refs_0_.2), channel_id=1, source_target_pairs={{2,0},{3,1},{4,2},{5,3},{6,4},{7,5},{0,6},{1,7},{10,8},{11,9},{12,... | collective-permute-start | bytes 98312 | tf_op jit(solution)/shard_map/ppermute | solution.py:275
  8.4 2.9 %collective-permute-start.3 = (bf16[16,1024]{1,0:T(8,128)(2,1)}, bf16[16,1024]{1,0:T(8,128)(2,1)S(1)}, u32[]{:S(2)}, u32[]{:S(2)}) collective-permute-start(bf16[16,1024]{1,0:T(8,128)(2,1)} %refs_0_.2), channel_id=1, source_target_pairs={{6,0},{7,1},{0,2},{1,3},{2,4},{3,5},{4,6},{5,7},{14,8},{15,9},{8,1... | collective-permute-start | bytes 98312 | tf_op jit(solution)/shard_map/ppermute | solution.py:275
  11.4 4.4 %collective-permute-done.1.refs_1_ = bf16[16,1024]{1,0:T(8,128)(2,1)S(1)} collective-permute-done((bf16[16,1024]{1,0:T(8,128)(2,1)}, bf16[16,1024]{1,0:T(8,128)(2,1)S(1)}, u32[]{:S(2)}, u32[]{:S(2)}) %collective-permute-start.1) | collective-permute-done | bytes 32800 | tf_op jit(solution)/shard_map/ppermute | solution.py:275
  18.3 1.5 collective-permute-start.8
  19.7 2.1 %collective-permute-start.7 = (bf16[64,1024]{1,0:T(8,128)(2,1)S(1)}, bf16[64,1024]{1,0:T(8,128)(2,1)S(1)}, u32[]{:S(2)}, u32[]{:S(2)}) collective-permute-start(bf16[64,1024]{1,0:T(8,128)(2,1)S(1)} %shard_map.109.refs_2_), channel_id=1, source_target_pairs={{24,0},{25,1},{26,2},{27,3},{28,4},{29,5},{30,6},{31,7},{0,8},{1,9... | collective-permute-start | bytes 393224 | tf_op jit(solution)/shard_map/ppermute | solution.py:275
  23.0 3.1 %collective-permute-done.8.refs_5_ = bf16[64,1024]{1,0:T(8,128)(2,1)S(1)} collective-permute-done((bf16[64,1024]{1,0:T(8,128)(2,1)S(1)}, bf16[64,1024]{1,0:T(8,128)(2,1)S(1)}, u32[]{:S(2)}, u32[]{:S(2)}) %collective-permute-start.8) | collective-permute-done | bytes 131104 | tf_op jit(solution)/shard_map/ppermute | solution.py:275
  26.3 2.3 %collective-permute-done.6.refs_3_ = bf16[64,1024]{1,0:T(8,128)(2,1)S(1)} collective-permute-done((bf16[64,1024]{1,0:T(8,128)(2,1)S(1)}, bf16[64,1024]{1,0:T(8,128)(2,1)S(1)}, u32[]{:S(2)}, u32[]{:S(2)}) %collective-permute-start.6) | collective-permute-done | bytes 131104 | tf_op jit(solution)/shard_map/ppermute | solution.py:275
  28.6 3.7 %shard_map.111 = (bf16[1024,512]{1,0:T(8,128)(2,1)S(1)}, bf16[1024,512]{1,0:T(8,128)(2,1)S(1)}, bf16[1024,512]{1,0:T(8,128)(2,1)S(1)}, bf16[1024,512]{1,0:T(8,12...) custom-call(s32[3,4,8]{2,1,0:T(4,128)S(1)} %bitcast.15, ...), custom_call_target="tpu_custom_call" | custom-call | flops 1073741824 | bytes 10486528 | tf_op jit(solution)/shard_map/pallas_call | solution.py:26
  32.3 19.6 %all_to_all.20.refs_0_ = bf16[8,32,2048]{2,1,0:T(8,128)(2,1)S(1)} all-to-all(bf16[8,32,2048]{2,1,0:T(8,128)(2,1)S(1)} %bitcast.11), channel_id=1, replica_groups=mesh['row'=8,'col'=32] {'row'}, dimensions={0} | all-to-all | bytes 2097152 | tf_op jit(solution)/shard_map/all_to_all | solution.py:301
  52.2 11.3 %all_to_all.21 = bf16[8,32,1024]{2,1,0:T(8,128)(2,1)S(1)} all-to-all(bf16[8,32,1024]{2,1,0:T(8,128)(2,1)S(1)} %get-tuple-element.44), channel_id=1, replica_groups=mesh['row'=8,'col'=32] {'row'}, dimensions={0} | all-to-all | bytes 1048576 | tf_op jit(solution)/shard_map/all_to_all | solution.py:301
  64.2 2.2 %collective-permute-start.10 = (bf16[64,1024]{1,0:T(8,128)(2,1)S(1)}, bf16[64,1024]{1,0:T(8,128)(2,1)S(1)}, u32[]{:S(2)}, u32[]{:S(2)}) collective-permute-start(bf16[64,1024]{1,0:T(8,128)(2,1)S(1)} %get-tuple-element.46), channel_id=1, source_target_pairs={{16,0},{17,1},{18,2},{19,3},{20,4},{21,5},{22,6},{23,7},{24,8},{25... | collective-permute-start | bytes 393224 | tf_op jit(solution)/shard_map/ppermute | solution.py:275
  67.1 1.4 collective-permute-start.12
  68.5 2.3 %collective-permute-done.10.refs_1_ = bf16[64,1024]{1,0:T(8,128)(2,1)S(1)} collective-permute-done((bf16[64,1024]{1,0:T(8,128)(2,1)S(1)}, bf16[64,1024]{1,0:T(8,128)(2,1)S(1)}, u32[]{:S(2)}, u32[]{:S(2)}) %collective-permute-start.10) | collective-permute-done | bytes 131104 | tf_op jit(solution)/shard_map/ppermute | solution.py:275
  71.4 1.9 %collective-permute-done.12.refs_3_ = bf16[64,1024]{1,0:T(8,128)(2,1)S(1)} collective-permute-done((bf16[64,1024]{1,0:T(8,128)(2,1)S(1)}, bf16[64,1024]{1,0:T(8,128)(2,1)S(1)}, u32[]{:S(2)}, u32[]{:S(2)}) %collective-permute-start.12) | collective-permute-done | bytes 131104 | tf_op jit(solution)/shard_map/ppermute | solution.py:275
  73.4 4.2 %collective-permute-start.13 = (bf16[16,1024]{1,0:T(8,128)(2,1)S(1)}, bf16[16,1024]{1,0:T(8,128)(2,1)S(1)}, u32[]{:S(2)}, u32[]{:S(2)}) collective-permute-start(bf16[16,1024]{1,0:T(8,128)(2,1)S(1)} %get-tuple-element.50), channel_id=1, source_target_pairs={{4,0},{5,1},{6,2},{7,3},{0,4},{1,5},{2,6},{3,7},{12,8},{13,9},{14,... | collective-permute-start | bytes 98312 | tf_op jit(solution)/shard_map/ppermute | solution.py:275
  77.6 4.1 %collective-permute-start.15 = (bf16[16,1024]{1,0:T(8,128)(2,1)S(1)}, bf16[16,1024]{1,0:T(8,128)(2,1)S(1)}, u32[]{:S(2)}, u32[]{:S(2)}) collective-permute-start(bf16[16,1024]{1,0:T(8,128)(2,1)S(1)} %get-tuple-element.52), channel_id=1, source_target_pairs={{2,0},{3,1},{4,2},{5,3},{6,4},{7,5},{0,6},{1,7},{10,8},{11,9},{12,... | collective-permute-start | bytes 98312 | tf_op jit(solution)/shard_map/ppermute | solution.py:275
  81.7 1.9 %collective-permute-done.14.refs_3_ = bf16[16,1024]{1,0:T(8,128)(2,1)S(1)} collective-permute-done((bf16[16,1024]{1,0:T(8,128)(2,1)S(1)}, bf16[16,1024]{1,0:T(8,128)(2,1)S(1)}, u32[]{:S(2)}, u32[]{:S(2)}) %collective-permute-start.14) | collective-permute-done | bytes 32800 | tf_op jit(solution)/shard_map/ppermute | solution.py:275
  84.7 2.7 %collective-permute-start.19 = (bf16[16,1024]{1,0:T(8,128)(2,1)S(1)}, bf16[16,1024]{1,0:T(8,128)(2,1)S(1)}, u32[]{:S(2)}, u32[]{:S(2)}) collective-permute-start(bf16[16,1024]{1,0:T(8,128)(2,1)S(1)} %get-tuple-element.55.refs_2_.refs_0_), channel_id=1, source_target_pairs={{4,0},{5,1},{6,2},{7,3},{0,4},{1,5},{2,6},{3,7},{12,8},{13,9},{14,... | collective-permute-start | bytes 98312 | tf_op jit(solution)/shard_map/ppermute | solution.py:275
  87.5 4.1 %collective-permute-start.18 = (bf16[16,1024]{1,0:T(8,128)(2,1)S(1)}, bf16[16,1024]{1,0:T(8,128)(2,1)S(1)}, u32[]{:S(2)}, u32[]{:S(2)}) collective-permute-start(bf16[16,1024]{1,0:T(8,128)(2,1)S(1)} %get-tuple-element.55.refs_2_.refs_0_), channel_id=1, source_target_pairs={{6,0},{7,1},{0,2},{1,3},{2,4},{3,5},{4,6},{5,7},{14,8},{15,9},{8,1... | collective-permute-start | bytes 98312 | tf_op jit(solution)/shard_map/ppermute | solution.py:275
  93.7 3.0 %collective-permute-done.17.refs_1_ = bf16[16,1024]{1,0:T(8,128)(2,1)S(1)} collective-permute-done((bf16[16,1024]{1,0:T(8,128)(2,1)S(1)}, bf16[16,1024]{1,0:T(8,128)(2,1)S(1)}, u32[]{:S(2)}, u32[]{:S(2)}) %collective-permute-start.17) | collective-permute-done | bytes 32800 | tf_op jit(solution)/shard_map/ppermute | solution.py:275
  97.8 1.8 %collective-permute-start.21 = (bf16[64,1024]{1,0:T(8,128)(2,1)S(1)}, bf16[64,1024]{1,0:T(8,128)(2,1)S(1)}, u32[]{:S(2)}, u32[]{:S(2)}) collective-permute-start(bf16[64,1024]{1,0:T(8,128)(2,1)S(1)} %shard_map.117.refs_0_), channel_id=1, source_target_pairs={{24,0},{25,1},{26,2},{27,3},{28,4},{29,5},{30,6},{31,7},{0,8},{1,9... | collective-permute-start | bytes 393224 | tf_op jit(solution)/shard_map/ppermute | solution.py:275
  99.9 3.6 %collective-permute-done.22.refs_3_ = bf16[64,1024]{1,0:T(8,128)(2,1)S(1)} collective-permute-done((bf16[64,1024]{1,0:T(8,128)(2,1)S(1)}, bf16[64,1024]{1,0:T(8,128)(2,1)S(1)}, u32[]{:S(2)}, u32[]{:S(2)}) %collective-permute-start.22) | collective-permute-done | bytes 131104 | tf_op jit(solution)/shard_map/ppermute | solution.py:275
  103.4 2.4 %collective-permute-done.20.refs_1_ = bf16[64,1024]{1,0:T(8,128)(2,1)S(1)} collective-permute-done((bf16[64,1024]{1,0:T(8,128)(2,1)S(1)}, bf16[64,1024]{1,0:T(8,128)(2,1)S(1)}, u32[]{:S(2)}, u32[]{:S(2)}) %collective-permute-start.20) | collective-permute-done | bytes 131104 | tf_op jit(solution)/shard_map/ppermute | solution.py:275
  106.6 11.6 %all_to_all.22.refs_0_ = bf16[8,32,1152]{2,1,0:T(8,128)(2,1)S(1)} all-to-all(bf16[8,32,1152]{2,1,0:T(8,128)(2,1)S(1)} %bitcast.12), channel_id=1, replica_groups=mesh['row'=8,'col'=32] {'row'}, dimensions={0} | all-to-all | bytes 1179648 | tf_op jit(solution)/shard_map/all_to_all | solution.py:301
  118.4 15.3 %all_to_all.23 = bf16[8,32,2048]{2,1,0:T(8,128)(2,1)S(1)} all-to-all(bf16[8,32,2048]{2,1,0:T(8,128)(2,1)S(1)} %get-tuple-element.60), channel_id=1, replica_groups=mesh['row'=8,'col'=32] {'row'}, dimensions={0} | all-to-all | bytes 2097152 | tf_op jit(solution)/shard_map/all_to_all | solution.py:301
  134.2 1.3 shard_map.121
  137.7 5.8 %collective-permute-done.27.refs_1_ = bf16[64,1024]{1,0:T(8,128)(2,1)S(1)} collective-permute-done((bf16[64,1024]{1,0:T(8,128)(2,1)S(1)}, bf16[64,1024]{1,0:T(8,128)(2,1)S(1)}, u32[]{:S(2)}, u32[]{:S(2)}) %collective-permute-start.27) | collective-permute-done | bytes 131104 | tf_op jit(solution)/shard_map/ppermute | solution.py:275
  143.6 1.7 %collective-permute-done.29.refs_3_ = bf16[64,1024]{1,0:T(8,128)(2,1)S(1)} collective-permute-done((bf16[64,1024]{1,0:T(8,128)(2,1)S(1)}, bf16[64,1024]{1,0:T(8,128)(2,1)S(1)}, u32[]{:S(2)}, u32[]{:S(2)}) %collective-permute-start.29) | collective-permute-done | bytes 131104 | tf_op jit(solution)/shard_map/ppermute | solution.py:275
  145.4 4.8 %collective-permute-start.30 = (bf16[16,1024]{1,0:T(8,128)(2,1)S(1)}, bf16[16,1024]{1,0:T(8,128)(2,1)S(1)}, u32[]{:S(2)}, u32[]{:S(2)}) collective-permute-start(bf16[16,1024]{1,0:T(8,128)(2,1)S(1)} %get-tuple-element.76), channel_id=1, source_target_pairs={{4,0},{5,1},{6,2},{7,3},{0,4},{1,5},{2,6},{3,7},{12,8},{13,9},{14,... | collective-permute-start | bytes 98312 | tf_op jit(solution)/shard_map/ppermute | solution.py:275
  150.2 2.2 %collective-permute-start.31 = (bf16[16,1024]{1,0:T(8,128)(2,1)S(1)}, bf16[16,1024]{1,0:T(8,128)(2,1)S(1)}, u32[]{:S(2)}, u32[]{:S(2)}) collective-permute-start(bf16[16,1024]{1,0:T(8,128)(2,1)S(1)} %get-tuple-element.77), channel_id=1, source_target_pairs={{6,0},{7,1},{0,2},{1,3},{2,4},{3,5},{4,6},{5,7},{14,8},{15,9},{8,1... | collective-permute-start | bytes 98312 | tf_op jit(solution)/shard_map/ppermute | solution.py:275
  152.4 1.9 %collective-permute-start.32 = (bf16[16,1024]{1,0:T(8,128)(2,1)S(1)}, bf16[16,1024]{1,0:T(8,128)(2,1)S(1)}, u32[]{:S(2)}, u32[]{:S(2)}) collective-permute-start(bf16[16,1024]{1,0:T(8,128)(2,1)S(1)} %get-tuple-element.78), channel_id=1, source_target_pairs={{2,0},{3,1},{4,2},{5,3},{6,4},{7,5},{0,6},{1,7},{10,8},{11,9},{12,... | collective-permute-start | bytes 98312 | tf_op jit(solution)/shard_map/ppermute | solution.py:275
  154.3 4.2 %shard_map.120 = (bf16[1024,512]{1,0:T(8,128)(2,1)}, bf16[1024,512]{1,0:T(8,128)(2,1)}, bf16[512,1024]{1,0:T(8,128)(2,1)}, f32[1,1]{1,0:T(1,128)}, f32[8,128]{1,0:T(8,128)S(1)}) custom-call(s32[3,4,8]{2,1,0:T(4,128)S(1)} %bitcast.16, bf16[256,1024]{1,0:T(8,128)(2,1)S(1)} %get-tuple-element.56.refs_1_, ...), custom_call_target="tpu_custom_call" | custom-call | flops 1610612736 | bytes 8401284 | tf_op jit(solution)/shard_map/pallas_call | solution.py:26
  (61 shorter events, 16.7 us)
Async XLA Ops:
  0.6 15.1 %collective-permute-start.4 = (bf16[1024,512]{1,0:T(8,128)(2,1)}, bf16[1024,512]{1,0:T(8,128)(2,1)S(1)}, u32[]{:S(2)}, u32[]{:S(2)}) collective-permute-start(bf16[1024,512]{1,0:T(8,128)(2,1)} %refs_6_.1), channel_id=1, source_target_pairs={{0,1},{1,0},{2,3},{3,2},{4,5},{5,4},{6,7},{7,6},{8,9},{9,8},{10,11... | collective-permute-start | bytes 3145736 | tf_op jit(solution)/shard_map/ppermute | solution.py:265
  0.7 15.0 %collective-permute-start.5 = (bf16[1024,512]{1,0:T(8,128)(2,1)}, bf16[1024,512]{1,0:T(8,128)(2,1)S(1)}, u32[]{:S(2)}, u32[]{:S(2)}) collective-permute-start(bf16[1024,512]{1,0:T(8,128)(2,1)} %refs_8_.1), channel_id=1, source_target_pairs={{0,1},{1,0},{2,3},{3,2},{4,5},{5,4},{6,7},{7,6},{8,9},{9,8},{10,11... | collective-permute-start | bytes 3145736 | tf_op jit(solution)/shard_map/ppermute | solution.py:265
  1.2 10.1 %collective-permute-start.2 = (bf16[16,1024]{1,0:T(8,128)(2,1)}, bf16[16,1024]{1,0:T(8,128)(2,1)S(1)}, u32[]{:S(2)}, u32[]{:S(2)}) collective-permute-start(bf16[16,1024]{1,0:T(8,128)(2,1)} %refs_0_.2), channel_id=1, source_target_pairs={{2,0},{3,1},{4,2},{5,3},{6,4},{7,5},{0,6},{1,7},{10,8},{11,9},{12,... | collective-permute-start | bytes 98312 | tf_op jit(solution)/shard_map/ppermute | solution.py:275
  7.5 8.2 %collective-permute-start.1 = (bf16[16,1024]{1,0:T(8,128)(2,1)}, bf16[16,1024]{1,0:T(8,128)(2,1)S(1)}, u32[]{:S(2)}, u32[]{:S(2)}) collective-permute-start(bf16[16,1024]{1,0:T(8,128)(2,1)} %refs_0_.2), channel_id=1, source_target_pairs={{4,0},{5,1},{6,2},{7,3},{0,4},{1,5},{2,6},{3,7},{12,8},{13,9},{14,... | collective-permute-start | bytes 98312 | tf_op jit(solution)/shard_map/ppermute | solution.py:275
  8.4 7.3 %collective-permute-start.3 = (bf16[16,1024]{1,0:T(8,128)(2,1)}, bf16[16,1024]{1,0:T(8,128)(2,1)S(1)}, u32[]{:S(2)}, u32[]{:S(2)}) collective-permute-start(bf16[16,1024]{1,0:T(8,128)(2,1)} %refs_0_.2), channel_id=1, source_target_pairs={{6,0},{7,1},{0,2},{1,3},{2,4},{3,5},{4,6},{5,7},{14,8},{15,9},{8,1... | collective-permute-start | bytes 98312 | tf_op jit(solution)/shard_map/ppermute | solution.py:275
  18.2 10.5 %collective-permute-start.9 = (bf16[512,1024]{1,0:T(8,128)(2,1)S(1)}, bf16[512,1024]{1,0:T(8,128)(2,1)S(1)}, u32[]{:S(2)}, u32[]{:S(2)}) collective-permute-start(bf16[512,1024]{1,0:T(8,128)(2,1)S(1)} %shard_map.110.refs_1_.refs_4_), channel_id=1, source_target_pairs={{0,1},{1,0},{2,3},{3,2},{4,5},{5,4},{6,7},{7,6},{8,9},{9,8},{10,11... | collective-permute-start | bytes 3145736 | tf_op jit(solution)/shard_map/ppermute | solution.py:265
  18.3 7.9 %collective-permute-start.8 = (bf16[64,1024]{1,0:T(8,128)(2,1)S(1)}, bf16[64,1024]{1,0:T(8,128)(2,1)S(1)}, u32[]{:S(2)}, u32[]{:S(2)}) collective-permute-start(bf16[64,1024]{1,0:T(8,128)(2,1)S(1)} %shard_map.109.refs_2_), channel_id=1, source_target_pairs={{16,0},{17,1},{18,2},{19,3},{20,4},{21,5},{22,6},{23,7},{24,8},{25... | collective-permute-start | bytes 393224 | tf_op jit(solution)/shard_map/ppermute | solution.py:275
  19.7 6.6 %collective-permute-start.7 = (bf16[64,1024]{1,0:T(8,128)(2,1)S(1)}, bf16[64,1024]{1,0:T(8,128)(2,1)S(1)}, u32[]{:S(2)}, u32[]{:S(2)}) collective-permute-start(bf16[64,1024]{1,0:T(8,128)(2,1)S(1)} %shard_map.109.refs_2_), channel_id=1, source_target_pairs={{24,0},{25,1},{26,2},{27,3},{28,4},{29,5},{30,6},{31,7},{0,8},{1,9... | collective-permute-start | bytes 393224 | tf_op jit(solution)/shard_map/ppermute | solution.py:275
  21.8 6.8 %collective-permute-start.6 = (bf16[64,1024]{1,0:T(8,128)(2,1)S(1)}, bf16[64,1024]{1,0:T(8,128)(2,1)S(1)}, u32[]{:S(2)}, u32[]{:S(2)}) collective-permute-start(bf16[64,1024]{1,0:T(8,128)(2,1)S(1)} %shard_map.109.refs_2_), channel_id=1, source_target_pairs={{8,0},{9,1},{10,2},{11,3},{12,4},{13,5},{14,6},{15,7},{16,8},{17,9... | collective-permute-start | bytes 393224 | tf_op jit(solution)/shard_map/ppermute | solution.py:275
  64.2 6.6 %collective-permute-start.10 = (bf16[64,1024]{1,0:T(8,128)(2,1)S(1)}, bf16[64,1024]{1,0:T(8,128)(2,1)S(1)}, u32[]{:S(2)}, u32[]{:S(2)}) collective-permute-start(bf16[64,1024]{1,0:T(8,128)(2,1)S(1)} %get-tuple-element.46), channel_id=1, source_target_pairs={{16,0},{17,1},{18,2},{19,3},{20,4},{21,5},{22,6},{23,7},{24,8},{25... | collective-permute-start | bytes 393224 | tf_op jit(solution)/shard_map/ppermute | solution.py:275
  66.4 5.0 %collective-permute-start.11 = (bf16[64,1024]{1,0:T(8,128)(2,1)S(1)}, bf16[64,1024]{1,0:T(8,128)(2,1)S(1)}, u32[]{:S(2)}, u32[]{:S(2)}) collective-permute-start(bf16[64,1024]{1,0:T(8,128)(2,1)S(1)} %get-tuple-element.47), channel_id=1, source_target_pairs={{24,0},{25,1},{26,2},{27,3},{28,4},{29,5},{30,6},{31,7},{0,8},{1,9... | collective-permute-start | bytes 393224 | tf_op jit(solution)/shard_map/ppermute | solution.py:275
  67.1 6.2 %collective-permute-start.12 = (bf16[64,1024]{1,0:T(8,128)(2,1)S(1)}, bf16[64,1024]{1,0:T(8,128)(2,1)S(1)}, u32[]{:S(2)}, u32[]{:S(2)}) collective-permute-start(bf16[64,1024]{1,0:T(8,128)(2,1)S(1)} %get-tuple-element.48), channel_id=1, source_target_pairs={{8,0},{9,1},{10,2},{11,3},{12,4},{13,5},{14,6},{15,7},{16,8},{17,9... | collective-permute-start | bytes 393224 | tf_op jit(solution)/shard_map/ppermute | solution.py:275
  73.4 8.3 %collective-permute-start.13 = (bf16[16,1024]{1,0:T(8,128)(2,1)S(1)}, bf16[16,1024]{1,0:T(8,128)(2,1)S(1)}, u32[]{:S(2)}, u32[]{:S(2)}) collective-permute-start(bf16[16,1024]{1,0:T(8,128)(2,1)S(1)} %get-tuple-element.50), channel_id=1, source_target_pairs={{4,0},{5,1},{6,2},{7,3},{0,4},{1,5},{2,6},{3,7},{12,8},{13,9},{14,... | collective-permute-start | bytes 98312 | tf_op jit(solution)/shard_map/ppermute | solution.py:275
  77.6 6.0 %collective-permute-start.14 = (bf16[16,1024]{1,0:T(8,128)(2,1)S(1)}, bf16[16,1024]{1,0:T(8,128)(2,1)S(1)}, u32[]{:S(2)}, u32[]{:S(2)}) collective-permute-start(bf16[16,1024]{1,0:T(8,128)(2,1)S(1)} %get-tuple-element.51), channel_id=1, source_target_pairs={{6,0},{7,1},{0,2},{1,3},{2,4},{3,5},{4,6},{5,7},{14,8},{15,9},{8,1... | collective-permute-start | bytes 98312 | tf_op jit(solution)/shard_map/ppermute | solution.py:275
  77.6 6.0 %collective-permute-start.15 = (bf16[16,1024]{1,0:T(8,128)(2,1)S(1)}, bf16[16,1024]{1,0:T(8,128)(2,1)S(1)}, u32[]{:S(2)}, u32[]{:S(2)}) collective-permute-start(bf16[16,1024]{1,0:T(8,128)(2,1)S(1)} %get-tuple-element.52), channel_id=1, source_target_pairs={{2,0},{3,1},{4,2},{5,3},{6,4},{7,5},{0,6},{1,7},{10,8},{11,9},{12,... | collective-permute-start | bytes 98312 | tf_op jit(solution)/shard_map/ppermute | solution.py:275
  84.2 21.6 %collective-permute-start.16 = (bf16[256,1024]{1,0:T(8,128)(2,1)S(1)}, bf16[256,1024]{1,0:T(8,128)(2,1)S(1)}, u32[]{:S(2)}, u32[]{:S(2)}) collective-permute-start(bf16[256,1024]{1,0:T(8,128)(2,1)S(1)} %get-tuple-element.56.refs_1_), channel_id=1, source_target_pairs={{0,1},{1,0},{2,3},{3,2},{4,5},{5,4},{6,7},{7,6},{8,9},{9,8},{10,11... | collective-permute-start | bytes 1572872 | tf_op jit(solution)/shard_map/ppermute | solution.py:265
  84.2 21.6 %collective-permute-start.23 = (bf16[256,1024]{1,0:T(8,128)(2,1)S(1)}, bf16[256,1024]{1,0:T(8,128)(2,1)S(1)}, u32[]{:S(2)}, u32[]{:S(2)}) collective-permute-start(bf16[256,1024]{1,0:T(8,128)(2,1)S(1)} %get-tuple-element.57.refs_5_), channel_id=1, source_target_pairs={{0,1},{1,0},{2,3},{3,2},{4,5},{5,4},{6,7},{7,6},{8,9},{9,8},{10,11... | collective-permute-start | bytes 1572872 | tf_op jit(solution)/shard_map/ppermute | solution.py:265
  84.7 8.0 %collective-permute-start.19 = (bf16[16,1024]{1,0:T(8,128)(2,1)S(1)}, bf16[16,1024]{1,0:T(8,128)(2,1)S(1)}, u32[]{:S(2)}, u32[]{:S(2)}) collective-permute-start(bf16[16,1024]{1,0:T(8,128)(2,1)S(1)} %get-tuple-element.55.refs_2_.refs_0_), channel_id=1, source_target_pairs={{4,0},{5,1},{6,2},{7,3},{0,4},{1,5},{2,6},{3,7},{12,8},{13,9},{14,... | collective-permute-start | bytes 98312 | tf_op jit(solution)/shard_map/ppermute | solution.py:275
  87.5 6.3 %collective-permute-start.18 = (bf16[16,1024]{1,0:T(8,128)(2,1)S(1)}, bf16[16,1024]{1,0:T(8,128)(2,1)S(1)}, u32[]{:S(2)}, u32[]{:S(2)}) collective-permute-start(bf16[16,1024]{1,0:T(8,128)(2,1)S(1)} %get-tuple-element.55.refs_2_.refs_0_), channel_id=1, source_target_pairs={{6,0},{7,1},{0,2},{1,3},{2,4},{3,5},{4,6},{5,7},{14,8},{15,9},{8,1... | collective-permute-start | bytes 98312 | tf_op jit(solution)/shard_map/ppermute | solution.py:275
  91.6 5.1 %collective-permute-start.17 = (bf16[16,1024]{1,0:T(8,128)(2,1)S(1)}, bf16[16,1024]{1,0:T(8,128)(2,1)S(1)}, u32[]{:S(2)}, u32[]{:S(2)}) collective-permute-start(bf16[16,1024]{1,0:T(8,128)(2,1)S(1)} %get-tuple-element.55.refs_2_.refs_0_), channel_id=1, source_target_pairs={{2,0},{3,1},{4,2},{5,3},{6,4},{7,5},{0,6},{1,7},{10,8},{11,9},{12,... | collective-permute-start | bytes 98312 | tf_op jit(solution)/shard_map/ppermute | solution.py:275
  96.7 6.8 %collective-permute-start.22 = (bf16[64,1024]{1,0:T(8,128)(2,1)S(1)}, bf16[64,1024]{1,0:T(8,128)(2,1)S(1)}, u32[]{:S(2)}, u32[]{:S(2)}) collective-permute-start(bf16[64,1024]{1,0:T(8,128)(2,1)S(1)} %shard_map.117.refs_0_), channel_id=1, source_target_pairs={{16,0},{17,1},{18,2},{19,3},{20,4},{21,5},{22,6},{23,7},{24,8},{25... | collective-permute-start | bytes 393224 | tf_op jit(solution)/shard_map/ppermute | solution.py:275
  97.8 5.6 %collective-permute-start.21 = (bf16[64,1024]{1,0:T(8,128)(2,1)S(1)}, bf16[64,1024]{1,0:T(8,128)(2,1)S(1)}, u32[]{:S(2)}, u32[]{:S(2)}) collective-permute-start(bf16[64,1024]{1,0:T(8,128)(2,1)S(1)} %shard_map.117.refs_0_), channel_id=1, source_target_pairs={{24,0},{25,1},{26,2},{27,3},{28,4},{29,5},{30,6},{31,7},{0,8},{1,9... | collective-permute-start | bytes 393224 | tf_op jit(solution)/shard_map/ppermute | solution.py:275
  99.6 6.2 %collective-permute-start.20 = (bf16[64,1024]{1,0:T(8,128)(2,1)S(1)}, bf16[64,1024]{1,0:T(8,128)(2,1)S(1)}, u32[]{:S(2)}, u32[]{:S(2)}) collective-permute-start(bf16[64,1024]{1,0:T(8,128)(2,1)S(1)} %shard_map.117.refs_0_), channel_id=1, source_target_pairs={{8,0},{9,1},{10,2},{11,3},{12,4},{13,5},{14,6},{15,7},{16,8},{17,9... | collective-permute-start | bytes 393224 | tf_op jit(solution)/shard_map/ppermute | solution.py:275
  133.7 20.6 %collective-permute-start.24 = (bf16[256,2048]{1,0:T(8,128)(2,1)S(1)}, bf16[256,2048]{1,0:T(8,128)(2,1)S(1)}, u32[]{:S(2)}, u32[]{:S(2)}) collective-permute-start(bf16[256,2048]{1,0:T(8,128)(2,1)S(1)} %bitcast.8), channel_id=1, source_target_pairs={{0,1},{1,0},{2,3},{3,2},{4,5},{5,4},{6,7},{7,6},{8,9},{9,8},{10,11... | collective-permute-start | bytes 3145736 | tf_op jit(solution)/shard_map/ppermute | solution.py:265
  133.7 18.7 %collective-permute-start.25 = (bf16[256,1024]{1,0:T(8,128)(2,1)S(1)}, bf16[256,1024]{1,0:T(8,128)(2,1)S(1)}, u32[]{:S(2)}, u32[]{:S(2)}) collective-permute-start(bf16[256,1024]{1,0:T(8,128)(2,1)S(1)} %get-tuple-element.61.refs_7_), channel_id=1, source_target_pairs={{0,1},{1,0},{2,3},{3,2},{4,5},{5,4},{6,7},{7,6},{8,9},{9,8},{10,11... | collective-permute-start | bytes 1572872 | tf_op jit(solution)/shard_map/ppermute | solution.py:265
  135.5 8.0 %collective-permute-start.27 = (bf16[64,1024]{1,0:T(8,128)(2,1)S(1)}, bf16[64,1024]{1,0:T(8,128)(2,1)S(1)}, u32[]{:S(2)}, u32[]{:S(2)}) collective-permute-start(bf16[64,1024]{1,0:T(8,128)(2,1)S(1)} %get-tuple-element.72), channel_id=1, source_target_pairs={{16,0},{17,1},{18,2},{19,3},{20,4},{21,5},{22,6},{23,7},{24,8},{25... | collective-permute-start | bytes 393224 | tf_op jit(solution)/shard_map/ppermute | solution.py:275
  135.6 8.0 %collective-permute-start.28 = (bf16[64,1024]{1,0:T(8,128)(2,1)S(1)}, bf16[64,1024]{1,0:T(8,128)(2,1)S(1)}, u32[]{:S(2)}, u32[]{:S(2)}) collective-permute-start(bf16[64,1024]{1,0:T(8,128)(2,1)S(1)} %get-tuple-element.73), channel_id=1, source_target_pairs={{24,0},{25,1},{26,2},{27,3},{28,4},{29,5},{30,6},{31,7},{0,8},{1,9... | collective-permute-start | bytes 393224 | tf_op jit(solution)/shard_map/ppermute | solution.py:275
  136.6 8.7 %collective-permute-start.29 = (bf16[64,1024]{1,0:T(8,128)(2,1)S(1)}, bf16[64,1024]{1,0:T(8,128)(2,1)S(1)}, u32[]{:S(2)}, u32[]{:S(2)}) collective-permute-start(bf16[64,1024]{1,0:T(8,128)(2,1)S(1)} %get-tuple-element.74), channel_id=1, source_target_pairs={{8,0},{9,1},{10,2},{11,3},{12,4},{13,5},{14,6},{15,7},{16,8},{17,9... | collective-permute-start | bytes 393224 | tf_op jit(solution)/shard_map/ppermute | solution.py:275
  143.5 10.8 %collective-permute-start.26 = (f32[8,128]{1,0:T(8,128)S(1)}, f32[8,128]{1,0:T(8,128)S(1)}, u32[]{:S(2)}, u32[]{:S(2)}) collective-permute-start(f32[8,128]{1,0:T(8,128)S(1)} %get-tuple-element.62.refs_9_), channel_id=1, source_target_pairs={{0,1},{1,0},{2,3},{3,2},{4,5},{5,4},{6,7},{7,6},{8,9},{9,8},{10,11... | collective-permute-start | bytes 12296 | tf_op jit(solution)/shard_map/ppermute | solution.py:265
  145.4 13.1 %collective-permute-start.30 = (bf16[16,1024]{1,0:T(8,128)(2,1)S(1)}, bf16[16,1024]{1,0:T(8,128)(2,1)S(1)}, u32[]{:S(2)}, u32[]{:S(2)}) collective-permute-start(bf16[16,1024]{1,0:T(8,128)(2,1)S(1)} %get-tuple-element.76), channel_id=1, source_target_pairs={{4,0},{5,1},{6,2},{7,3},{0,4},{1,5},{2,6},{3,7},{12,8},{13,9},{14,... | collective-permute-start | bytes 98312 | tf_op jit(solution)/shard_map/ppermute | solution.py:275
  150.2 8.3 %collective-permute-start.31 = (bf16[16,1024]{1,0:T(8,128)(2,1)S(1)}, bf16[16,1024]{1,0:T(8,128)(2,1)S(1)}, u32[]{:S(2)}, u32[]{:S(2)}) collective-permute-start(bf16[16,1024]{1,0:T(8,128)(2,1)S(1)} %get-tuple-element.77), channel_id=1, source_target_pairs={{6,0},{7,1},{0,2},{1,3},{2,4},{3,5},{4,6},{5,7},{14,8},{15,9},{8,1... | collective-permute-start | bytes 98312 | tf_op jit(solution)/shard_map/ppermute | solution.py:275
  152.4 6.1 %collective-permute-start.32 = (bf16[16,1024]{1,0:T(8,128)(2,1)S(1)}, bf16[16,1024]{1,0:T(8,128)(2,1)S(1)}, u32[]{:S(2)}, u32[]{:S(2)}) collective-permute-start(bf16[16,1024]{1,0:T(8,128)(2,1)S(1)} %get-tuple-element.78), channel_id=1, source_target_pairs={{2,0},{3,1},{4,2},{5,3},{6,4},{7,5},{0,6},{1,7},{10,8},{11,9},{12,... | collective-permute-start | bytes 98312 | tf_op jit(solution)/shard_map/ppermute | solution.py:275
  (5 other events, 28.9 us)
